TPU v7x, 32 devices: a whole 2x2x4 slice. The times are simulated.
32 devices in a mesh: dp: 8 (over z, y), rows: 4 (over x, core).
Axes of the slice: x: 2, y: 2, z: 4, core: 2. Of those that a mesh axis runs over, the one named last changes fastest.
Arguments:
- images: bfloat16 [16, 40, 48, 512], P('dp', 'rows'), may hold values from -6 to 6
- size_ids: int32 [16], replicated, may hold values from 0 to 1, as said below
- shared_conv: bfloat16 [2, 4608, 512], replicated, may hold values from -0.09375 to 0.09375
- task_conv: bfloat16 [3, 4608, 512], replicated, may hold values from -0.09375 to 0.09375
- task_down: bfloat16 [3, 512, 512], replicated, may hold values from -0.25 to 0.25
- task_up: bfloat16 [3, 512, 512], replicated, may hold values from -0.25 to 0.25
- shared_gain: float32 [2, 512], replicated, may hold values from 0.5 to 1.5
- shared_shift: float32 [2, 512], replicated, may hold values from -3 to 3
- down_gain: float32 [3, 512], replicated, may hold values from 0.5 to 1.5
- down_shift: float32 [3, 512], replicated, may hold values from -3 to 3
- up_gain: float32 [3, 512], replicated, may hold values from 0.5 to 1.5
- up_shift: float32 [3, 512], replicated, may hold values from -3 to 3
- conv_gain: float32 [3, 512], replicated, may hold values from 0.5 to 1.5
- conv_shift: float32 [3, 512], replicated, may hold values from -3 to 3
- cotangent: bfloat16 [3, 16, 20, 24, 512], P(None, 'dp', 'rows'), may hold values from -6 to 6
Outputs:
- task_maps: bfloat16 [3, 16, 20, 24, 512], P(None, 'dp', 'rows')
- input_grad: float32 [16, 40, 48, 512], P('dp', 'rows')
- shared_conv_grad: float32 [2, 4608, 512], P(None, 'dp')
- task_conv_grad: float32 [3, 4608, 512], P(None, 'dp')
- down_grad: float32 [3, 512, 512], P(None, 'dp')
- up_grad: float32 [3, 512, 512], P(None, None, 'dp')
- shared_gain_grad: float32 [2, 512], replicated
- shared_shift_grad: float32 [2, 512], replicated
- down_gain_grad: float32 [3, 512], replicated
- down_shift_grad: float32 [3, 512], replicated
- up_gain_grad: float32 [3, 512], replicated
- up_shift_grad: float32 [3, 512], replicated
- conv_gain_grad: float32 [3, 512], replicated
- conv_shift_grad: float32 [3, 512], replicated
Inputs may be any that keep to these rules, and one draw needn't show every extreme that they name: `size_ids`: 0 names a 36 x 48 map and 1 a 18 x 24 map, each placed at the frame's first rows and columns; every aligned group of 2 slots holds at least one map of the first kind.
All inputs are finite; a program needn't handle non-finite values.
Results may differ from a plain program's by a relative error of at most 0.02.
Values may be sent and summed in bfloat16 or wider, within the bound.
No kernel may reach another device: no remote copies, remote signals or barrier semaphores. Data moves between devices by JAX's collectives and lax.ppermute only.
A program may use at most 256 MiB of HBM per device.

v0:
```python
import jax
import jax.numpy as jnp
from jax import lax
from jax.sharding import PartitionSpec as P

H_BIG = 36
W_BIG = 48
H_SMALL = 18
W_SMALL = 24


EPSILON = 1e-05


def with_halo(cells, sides, width):
    for axis, dim in sides:
        count = lax.axis_size(axis)
        ends = count - 1
        head = lax.slice_in_dim(cells, 0, width, axis=dim)
        tail = lax.slice_in_dim(cells, cells.shape[dim] - width, cells.shape[dim], axis=dim)
        cells = jnp.concatenate(
            [
                lax.ppermute(tail, axis, [(i, (i + 1) % count) for i in range(ends)]),
                cells,
                lax.ppermute(head, axis, [((i + 1) % count, i) for i in range(ends)]),
            ],
            axis=dim,
        )
    return cells


def silu_slope(values):
    logistic = jax.nn.sigmoid(values)
    return logistic * (1.0 + values * (1.0 - logistic))


def widen(values):
    padded = with_halo(values, (("rows", 1),), 1)
    return jnp.pad(padded, ((0, 0), (0, 0), (1, 1), (0, 0)))


def windows(padded, height, breadth, flipped):
    pieces = []
    for tap_row in range(3):
        for tap_col in range(3):
            top_row = 2 - tap_row if flipped else tap_row
            left_col = 2 - tap_col if flipped else tap_col
            pieces.append(padded[:, top_row : top_row + height, left_col : left_col + breadth])
    return jnp.concatenate(pieces, axis=-1)


def conv_apply(values, weight):
    slot_count, height, breadth, channels = values.shape
    padded = widen(values)
    columns = windows(padded, height, breadth, False).reshape(-1, 9 * channels)
    result = jnp.dot(columns, weight, preferred_element_type=jnp.float32)
    return (result.reshape(slot_count, height, breadth, weight.shape[1]), padded)


def conv_back(grad_out, weight, padded):
    slot_count, height, breadth, out_channels = grad_out.shape
    channels = weight.shape[0] // 9
    columns = windows(padded, height, breadth, False).reshape(-1, 9 * channels)
    weight_grad = lax.dot_general(
        columns,
        grad_out.reshape(-1, out_channels),
        (((0,), (0,)), ((), ())),
        preferred_element_type=jnp.float32,
    )
    grad_padded = widen(grad_out)
    grad_columns = windows(grad_padded, height, breadth, True).reshape(-1, 9 * out_channels)
    turned = (
        weight.reshape(9, channels, out_channels)
        .transpose(0, 2, 1)
        .reshape(9 * out_channels, channels)
    )
    grad_in = jnp.dot(grad_columns, turned, preferred_element_type=jnp.float32)
    return (weight_grad, grad_in.reshape(slot_count, height, breadth, channels))


def moment_totals(stacked):
    return lax.psum(stacked, ("dp", "rows"))


def slope_totals(stacked):
    return lax.psum(stacked, ("dp", "rows"))


def reduce_groups(partials, reducer):
    totals = jnp.concatenate(
        [
            reducer(partials[2 * member : 2 * member + 2])
            for member in range(partials.shape[0] // 2)
        ],
        axis=0,
    )
    return totals


def normalize(arrays, gains, shifts, valid_mask, pixel_count):
    partials = []
    for values in arrays:
        masked = values * valid_mask
        partials.append(jnp.sum(masked, axis=(0, 1, 2)))
        partials.append(jnp.sum(masked * values, axis=(0, 1, 2)))
    totals = reduce_groups(jnp.stack(partials), moment_totals)
    outputs = []
    saved = []
    for member, values in enumerate(arrays):
        average = totals[2 * member] / pixel_count
        variance = totals[2 * member + 1] / pixel_count - average * average
        inverse = lax.rsqrt(variance + EPSILON)
        centred = (values - average) * inverse
        outputs.append(gains[member] * centred + shifts[member])
        saved.append((centred, inverse))
    return (outputs, saved)


def restore(gradients, saved, gains, valid_mask, pixel_count):
    partials = []
    for grad_out, pair in zip(gradients, saved):
        partials.append(jnp.sum(grad_out, axis=(0, 1, 2)))
        partials.append(jnp.sum(grad_out * pair[0], axis=(0, 1, 2)))
    totals = reduce_groups(jnp.stack(partials), slope_totals)
    inputs = []
    for member, grad_out in enumerate(gradients):
        centred, inverse = saved[member]
        correction = (
            valid_mask * (totals[2 * member] + centred * totals[2 * member + 1]) / pixel_count
        )
        inputs.append((gains[member] * inverse * (grad_out - correction)).astype(jnp.bfloat16))
    return (inputs, totals)


def local(
    images,
    size_ids,
    shared_conv,
    task_conv,
    task_down,
    task_up,
    shared_gain,
    shared_shift,
    down_gain,
    down_shift,
    up_gain,
    up_shift,
    conv_gain,
    conv_shift,
    cotangent,
):
    slot_count, part_rows, breadth, channels = images.shape
    task_count = task_conv.shape[0]
    heights_all = jnp.where(size_ids == 0, H_BIG, H_SMALL).astype(jnp.int32)
    breadths_all = jnp.where(size_ids == 0, W_BIG, W_SMALL).astype(jnp.int32)
    pixel_count = jnp.sum(heights_all * breadths_all).astype(jnp.float32)
    first_slot = lax.axis_index("dp") * slot_count
    heights = lax.dynamic_slice_in_dim(heights_all, first_slot, slot_count)
    breadths = lax.dynamic_slice_in_dim(breadths_all, first_slot, slot_count)
    row_place = lax.axis_index("rows") * part_rows + jnp.arange(part_rows, dtype=jnp.int32)
    col_place = jnp.arange(breadth, dtype=jnp.int32)
    inside = (row_place[None, :, None] < heights[:, None, None]) & (
        col_place[None, None, :] < breadths[:, None, None]
    )
    valid_mask = inside.astype(jnp.float32)[..., None]
    masked_input = jnp.where(inside[..., None], images, jnp.zeros_like(images))
    first_out, first_pad = conv_apply(masked_input, shared_conv[0])
    first_norm, first_saved = normalize(
        [first_out], shared_gain[0:1], shared_shift[0:1], valid_mask, pixel_count
    )
    hidden = (jax.nn.silu(first_norm[0]) * valid_mask).astype(jnp.bfloat16)
    second_out, second_pad = conv_apply(hidden, shared_conv[1])
    second_norm, second_saved = normalize(
        [second_out], shared_gain[1:2], shared_shift[1:2], valid_mask, pixel_count
    )
    shared_feat = (jax.nn.silu(second_norm[0]) * valid_mask).astype(jnp.bfloat16)
    shared_wide = shared_feat.astype(jnp.float32)
    lowered = [
        jnp.dot(shared_feat, task_down[branch], preferred_element_type=jnp.float32)
        for branch in range(task_count)
    ]
    down_norm, down_saved = normalize(lowered, down_gain, down_shift, valid_mask, pixel_count)
    squeezed = [(jax.nn.silu(element) * valid_mask).astype(jnp.bfloat16) for element in down_norm]
    raised = [
        jnp.dot(squeezed[branch], task_up[branch], preferred_element_type=jnp.float32)
        for branch in range(task_count)
    ]
    up_norm, up_saved = normalize(raised, up_gain, up_shift, valid_mask, pixel_count)
    attention = [jax.nn.sigmoid(element) for element in up_norm]
    gated = [(attention[branch] * shared_wide).astype(jnp.bfloat16) for branch in range(task_count)]
    conv_results = [conv_apply(gated[branch], task_conv[branch]) for branch in range(task_count)]
    conv_norm, conv_saved = normalize(
        [element[0] for element in conv_results], conv_gain, conv_shift, valid_mask, pixel_count
    )
    pooled_maps = []
    for branch in range(task_count):
        active = jax.nn.silu(conv_norm[branch]) * valid_mask
        pooled_maps.append(
            active.reshape(slot_count, part_rows // 2, 2, breadth // 2, 2, channels).mean(
                axis=(2, 4)
            )
        )
    maps_out = jnp.stack(pooled_maps).astype(jnp.bfloat16)
    cot_wide = cotangent.astype(jnp.float32)
    conv_incoming = []
    for branch in range(task_count):
        spread_grad = jnp.repeat(jnp.repeat(cot_wide[branch], 2, axis=1), 2, axis=2) * 0.25
        conv_incoming.append(spread_grad * valid_mask * silu_slope(conv_norm[branch]))
    conv_dz, conv_totals = restore(conv_incoming, conv_saved, conv_gain, valid_mask, pixel_count)
    shared_grad = jnp.zeros(shared_feat.shape, jnp.float32)
    conv_weight_grads = []
    up_incoming = []
    for branch in range(task_count):
        weight_grad, gated_grad = conv_back(
            conv_dz[branch], task_conv[branch], conv_results[branch][1]
        )
        conv_weight_grads.append(weight_grad)
        shared_grad = shared_grad + gated_grad * attention[branch]
        attention_grad = gated_grad * shared_wide
        up_incoming.append(attention_grad * attention[branch] * (1.0 - attention[branch]))
    up_dz, up_totals = restore(up_incoming, up_saved, up_gain, valid_mask, pixel_count)
    up_weight_grads = []
    down_incoming = []
    for branch in range(task_count):
        reduced = squeezed[branch].shape[-1]
        up_weight_grads.append(
            lax.dot_general(
                up_dz[branch].reshape(-1, channels),
                squeezed[branch].reshape(-1, reduced),
                (((0,), (0,)), ((), ())),
                preferred_element_type=jnp.float32,
            )
        )
        squeezed_grad = lax.dot_general(
            up_dz[branch],
            task_up[branch],
            (((3,), (1,)), ((), ())),
            preferred_element_type=jnp.float32,
        )
        down_incoming.append(squeezed_grad * valid_mask * silu_slope(down_norm[branch]))
    down_dz, down_totals = restore(down_incoming, down_saved, down_gain, valid_mask, pixel_count)
    down_weight_grads = []
    flat_shared = shared_feat.reshape(-1, channels)
    for branch in range(task_count):
        reduced = down_dz[branch].shape[-1]
        down_weight_grads.append(
            lax.dot_general(
                flat_shared,
                down_dz[branch].reshape(-1, reduced),
                (((0,), (0,)), ((), ())),
                preferred_element_type=jnp.float32,
            )
        )
        shared_grad = shared_grad + lax.dot_general(
            down_dz[branch],
            task_down[branch],
            (((3,), (1,)), ((), ())),
            preferred_element_type=jnp.float32,
        )
    second_dz, second_totals = restore(
        [shared_grad * valid_mask * silu_slope(second_norm[0])],
        second_saved,
        shared_gain[1:2],
        valid_mask,
        pixel_count,
    )
    second_weight_grad, hidden_grad = conv_back(second_dz[0], shared_conv[1], second_pad)
    first_dz, first_totals = restore(
        [hidden_grad * valid_mask * silu_slope(first_norm[0])],
        first_saved,
        shared_gain[0:1],
        valid_mask,
        pixel_count,
    )
    first_weight_grad, input_back = conv_back(first_dz[0], shared_conv[0], first_pad)
    input_grad = input_back * valid_mask
    shared_stack = jnp.stack([first_weight_grad, second_weight_grad])
    conv_stack = jnp.stack(conv_weight_grads)
    down_stack = jnp.stack(down_weight_grads)
    up_stack = jnp.stack(up_weight_grads)
    spread = (
        lax.psum_scatter(shared_stack, "dp", scatter_dimension=1, tiled=True),
        lax.psum_scatter(conv_stack, "dp", scatter_dimension=1, tiled=True),
        lax.psum_scatter(down_stack, "dp", scatter_dimension=1, tiled=True),
        lax.psum_scatter(up_stack, "dp", scatter_dimension=1, tiled=True),
    )
    shared_part, conv_part, down_part, up_part = (
        lax.psum(spread[0].astype(jnp.bfloat16), "rows").astype(jnp.float32),
        lax.psum(spread[1].astype(jnp.bfloat16), "rows").astype(jnp.float32),
        lax.psum(spread[2].astype(jnp.bfloat16), "rows").astype(jnp.float32),
        lax.psum(spread[3].astype(jnp.bfloat16), "rows").astype(jnp.float32),
    )
    up_grad = up_part.transpose(0, 2, 1)
    shared_gain_grad = jnp.stack([first_totals[1], second_totals[1]])
    shared_shift_grad = jnp.stack([first_totals[0], second_totals[0]])
    return (
        maps_out,
        input_grad,
        shared_part,
        conv_part,
        down_part,
        up_grad,
        shared_gain_grad,
        shared_shift_grad,
        down_totals[1::2],
        down_totals[0::2],
        up_totals[1::2],
        up_totals[0::2],
        conv_totals[1::2],
        conv_totals[0::2],
    )


def solution(mesh):
    placed = (
        P("dp", "rows", None, None),
        P(),
        P(),
        P(),
        P(),
        P(),
        P(),
        P(),
        P(),
        P(),
        P(),
        P(),
        P(),
        P(),
        P(None, "dp", "rows", None, None),
    )
    return jax.shard_map(
        local,
        mesh=mesh,
        in_specs=placed,
        out_specs=(
            P(None, "dp", "rows", None, None),
            P("dp", "rows", None, None),
            P(None, "dp", None),
            P(None, "dp", None),
            P(None, "dp", None),
            P(None, None, "dp"),
            P(),
            P(),
            P(),
            P(),
            P(),
            P(),
            P(),
            P(),
        ),
        check_vma=False,
    )
```

profile of v0, /device:TPU:0, one launch (start us, length us, event | category | flops | bytes accessed | tf_op | source)
XLA Modules:
  0.0 1778.1 jit_solution(11769551774106237272)
XLA Ops:
  19.7 7.9 fusion.127
  27.6 10.9 fusion.126
  43.1 9.1 multiply_reduce_fusion.10
  52.3 43.9 %psum.182 = f32[2,512]{1,0:T(2,128)S(1)} all-reduce(f32[2,512]{1,0:T(2,128)S(1)} %pad_maximum_fusion.28), channel_id=1, replica_groups=mesh['dp'=8,'rows'=4] {'dp','rows'}, use_global_device_ids=true, to_apply=%region_2.3 | all-reduce | flops 1024 | bytes 8192 | tf_op jit(solution)/shard_map/psum | solution.py:82
  115.4 7.0 copy.32
  122.4 6.7 copy.31
  129.1 6.7 copy.29
  135.8 6.7 copy.30
  148.3 9.2 multiply_reduce_fusion.9
  157.5 42.4 %psum.183 = f32[2,512]{1,0:T(2,128)S(1)} all-reduce(f32[2,512]{1,0:T(2,128)S(1)} %pad_maximum_fusion.29), channel_id=1, replica_groups=mesh['dp'=8,'rows'=4] {'dp','rows'}, use_global_device_ids=true, to_apply=%region_6.7 | all-reduce | flops 1024 | bytes 8192 | tf_op jit(solution)/shard_map/psum | solution.py:82
  207.3 40.1 %psum.184 = f32[2,512]{1,0:T(2,128)S(1)} all-reduce(f32[2,512]{1,0:T(2,128)S(1)} %pad_maximum_fusion.30), channel_id=1, replica_groups=mesh['dp'=8,'rows'=4] {'dp','rows'}, use_global_device_ids=true, to_apply=%region_9.10 | all-reduce | flops 1024 | bytes 8192 | tf_op jit(solution)/shard_map/psum | solution.py:82
  252.0 40.2 %psum.185 = f32[2,512]{1,0:T(2,128)S(1)} all-reduce(f32[2,512]{1,0:T(2,128)S(1)} %pad_maximum_fusion.31), channel_id=1, replica_groups=mesh['dp'=8,'rows'=4] {'dp','rows'}, use_global_device_ids=true, to_apply=%region_12.13 | all-reduce | flops 1024 | bytes 8192 | tf_op jit(solution)/shard_map/psum | solution.py:82
  305.6 11.9 multiply_reduce_fusion.6
  317.6 41.0 %psum.187 = f32[2,512]{1,0:T(2,128)S(1)} all-reduce(f32[2,512]{1,0:T(2,128)S(1)} %pad_maximum_fusion.33), channel_id=1, replica_groups=mesh['dp'=8,'rows'=4] {'dp','rows'}, use_global_device_ids=true, to_apply=%region_19.20 | all-reduce | flops 1024 | bytes 8192 | tf_op jit(solution)/shard_map/psum | solution.py:82
  362.6 40.4 %all-reduce.14 = (f32[2,512]{1,0:T(2,128)S(1)}, f32[2,512]{1,0:T(2,128)S(1)}) all-reduce(f32[2,512]{1,0:T(2,128)S(1)} %pad_maximum_fusion.34, f32[2,512]{1,0:T(2,128)S(1)} %pad_maximum_fusion.36), channel_id=1, replica_groups=mesh['dp'=8,'rows'=4] {'dp','rows'}, use_global_device_ids=true, to_apply=%region_22.23 | all-reduce | flops 2048 | bytes 16384 | tf_op jit(solution)/shard_map/psum | solution.py:82
  415.5 11.7 multiply_reduce_fusion.3
  427.2 40.7 %psum.191 = f32[2,512]{1,0:T(2,128)S(1)} all-reduce(f32[2,512]{1,0:T(2,128)S(1)} %pad_maximum_fusion.37), channel_id=1, replica_groups=mesh['dp'=8,'rows'=4] {'dp','rows'}, use_global_device_ids=true, to_apply=%region_32.33 | all-reduce | flops 1024 | bytes 8192 | tf_op jit(solution)/shard_map/psum | solution.py:82
  473.5 4.4 collective-permute-done.9
  480.2 11.5 multiply_reduce_fusion
  491.8 42.0 %all-reduce.13 = (f32[2,512]{1,0:T(2,128)S(1)}, f32[2,512]{1,0:T(2,128)S(1)}, f32[2,512]{1,0:T(2,128)S(1)}) all-reduce(f32[2,512]{1,0:T(2,128)S(1)} %pad_maximum_fusion.38, f32[2,512]{1,0:T(2,128)S(1)} %pad_maximum_fusion.35, f32[2,512]{1,0:T(2,128)S(1)} %pad_maximum_fusion.32), channel_id=1, replica_groups=mesh['dp'=8,'rows'=4] {'dp','rows'}, use_global_device_ids=true, to_apply=%region_35.36 | all-reduce | flops 3072 | bytes 24576 | tf_op jit(solution)/shard_map/psum | solution.py:82
  533.9 5.8 fusion.116
  542.3 39.8 %all-reduce.12 = (f32[2,512]{1,0:T(2,128)S(1)}, f32[2,512]{1,0:T(2,128)S(1)}, f32[2,512]{1,0:T(2,128)S(1)}) all-reduce(f32[2,512]{1,0:T(2,128)S(1)} %pad_maximum_fusion.40, f32[2,512]{1,0:T(2,128)S(1)} %pad_maximum_fusion.39, f32[2,512]{1,0:T(2,128)S(1)} %pad_maximum_fusion.41), channel_id=1, replica_groups=mesh['dp'=8,'rows'=4] {'dp','rows'}, use_global_device_ids=true, to_apply=%region_42.43 | all-reduce | flops 3072 | bytes 24576 | tf_op jit(solution)/shard_map/psum | solution.py:86
  582.1 4.6 multiply_convert_fusion.8
  591.8 5.5 collective-permute-start.10
  601.1 4.3 collective-permute-start.12
  618.1 4.1 copy-done.57
  622.2 7.5 fusion.157
  629.8 12.3 fusion.115
  642.2 10.9 fusion.121
  653.1 42.7 %all-reduce.11 = (f32[2,512]{1,0:T(2,128)S(1)}, f32[2,512]{1,0:T(2,128)S(1)}, f32[2,512]{1,0:T(2,128)S(1)}) all-reduce(f32[2,512]{1,0:T(2,128)S(1)} %pad_maximum_fusion.44, f32[2,512]{1,0:T(2,128)S(1)} %pad_maximum_fusion.42, f32[2,512]{1,0:T(2,128)S(1)} %pad_maximum_fusion.46), channel_id=1, replica_groups=mesh['dp'=8,'rows'=4] {'dp','rows'}, use_global_device_ids=true, to_apply=%region_54.55 | all-reduce | flops 3072 | bytes 24576 | tf_op jit(solution)/shard_map/psum | solution.py:86
  695.9 4.7 multiply_convert_fusion.3
  710.6 40.2 %all-reduce.10 = (f32[2,512]{1,0:T(2,128)S(1)}, f32[2,512]{1,0:T(2,128)S(1)}, f32[2,512]{1,0:T(2,128)S(1)}) all-reduce(f32[2,512]{1,0:T(2,128)S(1)} %pad_maximum_fusion.45, f32[2,512]{1,0:T(2,128)S(1)} %pad_maximum_fusion.43, f32[2,512]{1,0:T(2,128)S(1)} %pad_maximum_fusion.47), channel_id=1, replica_groups=mesh['dp'=8,'rows'=4] {'dp','rows'}, use_global_device_ids=true, to_apply=%region_57.58 | all-reduce | flops 3072 | bytes 24576 | tf_op jit(solution)/shard_map/psum | solution.py:86
  766.0 9.2 fusion.113
  775.2 41.7 %psum.202 = f32[2,512]{1,0:T(2,128)S(1)} all-reduce(f32[2,512]{1,0:T(2,128)S(1)} %pad_maximum_fusion.48), channel_id=1, replica_groups=mesh['dp'=8,'rows'=4] {'dp','rows'}, use_global_device_ids=true, to_apply=%region_66.67 | all-reduce | flops 1024 | bytes 8192 | tf_op jit(solution)/shard_map/psum | solution.py:86
  828.2 7.9 convolution_bitcast_fusion.3
  842.1 6.8 fusion.112
  848.9 43.6 %psum.203 = f32[2,512]{1,0:T(2,128)S(1)} all-reduce(f32[2,512]{1,0:T(2,128)S(1)} %pad_maximum_fusion.49), channel_id=1, replica_groups=mesh['dp'=8,'rows'=4] {'dp','rows'}, use_global_device_ids=true, to_apply=%region_69.70 | all-reduce | flops 1024 | bytes 8192 | tf_op jit(solution)/shard_map/psum | solution.py:86
  895.4 7.8 convolution_bitcast_fusion.4
  903.3 6.9 pad_maximum_fusion.1
  911.5 7.9 convolution_bitcast_fusion
  919.4 7.8 convolution_bitcast_fusion.2
  927.2 7.7 convolution_bitcast_fusion.1
  934.8 10.0 pad_maximum_fusion
  945.0 6.9 copy.33
  994.2 241.8 %reduce-scatter.5.cloned.1.call-done = f32[2,576,512]{2,1,0:T(8,128)} async-done(((f32[2,4608,512]{2,1,0:T(8,128)}), f32[2,576,512]{2,1,0:T(8,128)}) %reduce-scatter.5.cloned.1.call-update) | async-done | bytes 2359312 | tf_op jit(solution)/shard_map/reduce_scatter | solution.py:282
  1238.8 449.7 %reduce-scatter.7.cloned.1.call-done = f32[3,576,512]{2,1,0:T(8,128)} async-done(((f32[3,4608,512]{2,1,0:T(8,128)}), f32[3,576,512]{2,1,0:T(8,128)}) %reduce-scatter.7.cloned.1.call-update) | async-done | bytes 3538960 | tf_op jit(solution)/shard_map/reduce_scatter | solution.py:283
  1695.5 11.5 convolution_multiply_fusion
  1706.9 56.4 %all-reduce.18.cloned.1.call-done = (bf16[2,576,512]{2,1,0:T(8,128)(2,1)}, bf16[3,576,512]{2,1,0:T(8,128)(2,1)}, bf16[3,64,512]{2,1,0:T(8,128)(2,1)}, bf16[3,512,64]{1,2,0:T(8,128)(2,1)}) async-done(((bf16[2,576,512]{2,1,0:T(8,128)(2,1)}, bf16[3,576,512]{2,1,0:T(8,128)(2,1)}, bf16[3,64,512]{2,1,0:T(8,128)(2,1)}, bf16[3,512,64]{1,2,0:T(8,128)(2,1)}), (bf16[2,576,512]{2,1,0:T(8,128)(2,1)}, ...) | async-done | bytes 3342352 | tf_op jit(solution)/shard_map/psum | solution.py:288
  (583 shorter events, 219.6 us)
Async XLA Ops:
  7.2 983.5 %reduce-scatter.9.cloned.1.call-start = ((), (), s32[]{:S(2)}) async-start(), calls=%async_computation.6 | async-start | bytes 3538944 | tf_op jit(solution)/shard_map/reduce_scatter | solution.py:284
  9.0 883.5 %copy-start.28 = (f32[2,10,48]{2,1,0:T(8,128)}, f32[2,10,48]{2,1,0:T(8,128)S(1)}, u32[]{:S(2)}) copy-start(f32[2,10,48]{2,1,0:T(8,128)S(1)} %get-tuple-element.220) | copy-start | bytes 11524
  10.4 29.3 %collective-permute-start = (bf16[2,1,48,512]{3,2,1,0:T(8,128)(2,1)S(1)}, bf16[2,1,48,512]{3,2,1,0:T(8,128)(2,1)S(1)}, u32[]{:S(2)}, u32[]{:S(2)}) collective-permute-start(bf16[2,1,48,512]{3,2,1,0:T(8,128)(2,1)S(1)} %get-tuple-element.123), channel_id=1, source_target_pairs={{0,1},{1,2},{2,3},{4,5},{5,6},{6,7},{8,9},{9,10},{10,11},{12,13},{... | collective-permute-start | bytes 294920 | tf_op jit(solution)/shard_map/ppermute | solution.py:23
  12.8 27.0 %collective-permute-start.1 = (bf16[2,1,48,512]{3,2,1,0:T(8,128)(2,1)S(1)}, bf16[2,1,48,512]{3,2,1,0:T(8,128)(2,1)S(1)}, u32[]{:S(2)}, u32[]{:S(2)}) collective-permute-start(bf16[2,1,48,512]{3,2,1,0:T(8,128)(2,1)S(1)} %get-tuple-element.124), channel_id=1, source_target_pairs={{1,0},{2,1},{3,2},{5,4},{6,5},{7,6},{9,8},{10,9},{11,10},{13,12},{... | collective-permute-start | bytes 294920 | tf_op jit(solution)/shard_map/ppermute | solution.py:25
  15.3 81.5 %copy-start.69 = (f32[1,512]{1,0:T(1,128)}, f32[1,512]{1,0:T(1,128)S(1)}, u32[]{:S(2)}) copy-start(f32[1,512]{1,0:T(1,128)S(1)} %get-tuple-element.213) | copy-start | bytes 6148
  39.1 57.7 %copy-start.82 = (f32[1,512]{1,0:T(1,128)}, f32[1,512]{1,0:T(1,128)S(1)}, u32[]{:S(2)}) copy-start(f32[1,512]{1,0:T(1,128)S(1)} %get-tuple-element.217) | copy-start | bytes 6148
  52.2 52.0 %copy-start.6 = (f32[2,10,48,512]{3,2,1,0:T(8,128)}, f32[2,10,48,512]{3,2,1,0:T(8,128)S(1)}, u32[]{:S(2)}) copy-start(f32[2,10,48,512]{3,2,1,0:T(8,128)S(1)} %get-tuple-element.225) | copy-start | bytes 5898244
  98.2 44.2 %collective-permute-start.2 = (bf16[2,1,48,512]{3,2,1,0:T(8,128)(2,1)}, bf16[2,1,48,512]{3,2,1,0:T(8,128)(2,1)}, u32[]{:S(2)}, u32[]{:S(2)}) collective-permute-start(bf16[2,1,48,512]{3,2,1,0:T(8,128)(2,1)} %get-tuple-element.121), channel_id=1, source_target_pairs={{0,1},{1,2},{2,3},{4,5},{5,6},{6,7},{8,9},{9,10},{10,11},{12,13},{... | collective-permute-start | bytes 294920 | tf_op jit(solution)/shard_map/ppermute | solution.py:23
  100.1 42.3 %collective-permute-start.3 = (bf16[2,1,48,512]{3,2,1,0:T(8,128)(2,1)}, bf16[2,1,48,512]{3,2,1,0:T(8,128)(2,1)S(1)}, u32[]{:S(2)}, u32[]{:S(2)}) collective-permute-start(bf16[2,1,48,512]{3,2,1,0:T(8,128)(2,1)} %get-tuple-element.122), channel_id=1, source_target_pairs={{1,0},{2,1},{3,2},{5,4},{6,5},{7,6},{9,8},{10,9},{11,10},{13,12},{... | collective-permute-start | bytes 294920 | tf_op jit(solution)/shard_map/ppermute | solution.py:25
  148.3 51.7 %copy-start.58 = (f32[1,512]{1,0:T(1,128)S(1)}, f32[1,512]{1,0:T(1,128)}, u32[]{:S(2)}) copy-start(f32[1,512]{1,0:T(1,128)} %get-tuple-element.212) | copy-start | bytes 6148
  148.3 52.3 %copy-start.59 = (f32[1,512]{1,0:T(1,128)S(1)}, f32[1,512]{1,0:T(1,128)}, u32[]{:S(2)}) copy-start(f32[1,512]{1,0:T(1,128)} %get-tuple-element.216) | copy-start | bytes 6148
  204.3 43.1 %copy-start.110 = (f32[1,512]{1,0:T(1,128)S(1)}, f32[1,512]{1,0:T(1,128)}, u32[]{:S(2)}) copy-start(f32[1,512]{1,0:T(1,128)} %get-tuple-element.142) | copy-start | bytes 6148
  204.3 43.7 %copy-start.120 = (f32[1,512]{1,0:T(1,128)S(1)}, f32[1,512]{1,0:T(1,128)}, u32[]{:S(2)}) copy-start(f32[1,512]{1,0:T(1,128)} %get-tuple-element.145) | copy-start | bytes 6148
  248.0 44.3 %copy-start.74 = (f32[1,512]{1,0:T(1,128)S(1)}, f32[1,512]{1,0:T(1,128)}, u32[]{:S(2)}) copy-start(f32[1,512]{1,0:T(1,128)} %get-tuple-element.139) | copy-start | bytes 6148
  248.0 44.3 %copy-start.103 = (f32[1,512]{1,0:T(1,128)S(1)}, f32[1,512]{1,0:T(1,128)}, u32[]{:S(2)}) copy-start(f32[1,512]{1,0:T(1,128)} %get-tuple-element.147) | copy-start | bytes 6148
  295.2 4.3 collective-permute-start.4
  296.5 5.7 collective-permute-start.5
  305.6 53.0 %copy-start.109 = (f32[1,512]{1,0:T(1,128)S(1)}, f32[1,512]{1,0:T(1,128)}, u32[]{:S(2)}) copy-start(f32[1,512]{1,0:T(1,128)} %get-tuple-element.143) | copy-start | bytes 6148
  305.6 53.0 %copy-start.119 = (f32[1,512]{1,0:T(1,128)S(1)}, f32[1,512]{1,0:T(1,128)}, u32[]{:S(2)}) copy-start(f32[1,512]{1,0:T(1,128)} %get-tuple-element.146) | copy-start | bytes 6148
  358.7 44.4 %copy-start.75 = (f32[1,512]{1,0:T(1,128)S(1)}, f32[1,512]{1,0:T(1,128)}, u32[]{:S(2)}) copy-start(f32[1,512]{1,0:T(1,128)} %get-tuple-element.140) | copy-start | bytes 6148
  358.7 44.4 %copy-start.105 = (f32[1,512]{1,0:T(1,128)S(1)}, f32[1,512]{1,0:T(1,128)}, u32[]{:S(2)}) copy-start(f32[1,512]{1,0:T(1,128)} %get-tuple-element.149) | copy-start | bytes 6148
  406.1 5.0 collective-permute-start.6
  407.4 5.7 collective-permute-start.7
  415.4 52.5 %copy-start.73 = (f32[1,512]{1,0:T(1,128)S(1)}, f32[1,512]{1,0:T(1,128)}, u32[]{:S(2)}) copy-start(f32[1,512]{1,0:T(1,128)} %get-tuple-element.138) | copy-start | bytes 6148
  415.5 52.5 %copy-start.104 = (f32[1,512]{1,0:T(1,128)S(1)}, f32[1,512]{1,0:T(1,128)}, u32[]{:S(2)}) copy-start(f32[1,512]{1,0:T(1,128)} %get-tuple-element.148) | copy-start | bytes 6148
  470.8 2.6 collective-permute-start.8
  472.2 5.7 collective-permute-start.9
  480.2 53.6 %copy-start.65 = (f32[1,512]{1,0:T(1,128)S(1)}, f32[1,512]{1,0:T(1,128)}, u32[]{:S(2)}) copy-start(f32[1,512]{1,0:T(1,128)} %get-tuple-element.133) | copy-start | bytes 6148
  480.2 53.6 %copy-start.64 = (f32[1,512]{1,0:T(1,128)S(1)}, f32[1,512]{1,0:T(1,128)}, u32[]{:S(2)}) copy-start(f32[1,512]{1,0:T(1,128)} %get-tuple-element.134) | copy-start | bytes 6148
  480.2 53.6 %copy-start.49 = (f32[2,10,48]{2,1,0:T(8,128)S(1)}, f32[2,10,48]{2,1,0:T(8,128)}, u32[]{:S(2)}) copy-start(f32[2,10,48]{2,1,0:T(8,128)} %and_select_fusion) | copy-start | bytes 11524
  480.2 53.6 %copy-start.76 = (f32[1,512]{1,0:T(1,128)S(1)}, f32[1,512]{1,0:T(1,128)}, u32[]{:S(2)}) copy-start(f32[1,512]{1,0:T(1,128)} %get-tuple-element.137) | copy-start | bytes 6148
  480.2 53.6 %copy-start.77 = (f32[1,512]{1,0:T(1,128)S(1)}, f32[1,512]{1,0:T(1,128)}, u32[]{:S(2)}) copy-start(f32[1,512]{1,0:T(1,128)} %get-tuple-element.136) | copy-start | bytes 6148
  586.8 18.6 %collective-permute-start.14 = (bf16[2,1,48,512]{3,2,1,0:T(8,128)(2,1)S(1)}, bf16[2,1,48,512]{3,2,1,0:T(8,128)(2,1)S(1)}, u32[]{:S(2)}, u32[]{:S(2)}) collective-permute-start(bf16[2,1,48,512]{3,2,1,0:T(8,128)(2,1)S(1)} %get-tuple-element.109), channel_id=1, source_target_pairs={{0,1},{1,2},{2,3},{4,5},{5,6},{6,7},{8,9},{9,10},{10,11},{12,13},{... | collective-permute-start | bytes 294920 | tf_op jit(solution)/shard_map/ppermute | solution.py:23
  588.1 18.8 %collective-permute-start.15 = (bf16[2,1,48,512]{3,2,1,0:T(8,128)(2,1)S(1)}, bf16[2,1,48,512]{3,2,1,0:T(8,128)(2,1)S(1)}, u32[]{:S(2)}, u32[]{:S(2)}) collective-permute-start(bf16[2,1,48,512]{3,2,1,0:T(8,128)(2,1)S(1)} %get-tuple-element.110), channel_id=1, source_target_pairs={{1,0},{2,1},{3,2},{5,4},{6,5},{7,6},{9,8},{10,9},{11,10},{13,12},{... | collective-permute-start | bytes 294920 | tf_op jit(solution)/shard_map/ppermute | solution.py:25
  591.8 17.4 collective-permute-start.10
  597.4 11.9 collective-permute-start.11
  601.1 12.2 collective-permute-start.12
  605.4 7.9 collective-permute-start.13
  764.8 227.6 %reduce-scatter.11.cloned.1.call-start = ((), (), s32[]{:S(2)}) async-start(), calls=%async_computation.7 | async-start | bytes 3538944 | tf_op jit(solution)/shard_map/reduce_scatter | solution.py:285
  766.0 51.0 %copy-start.107 = (f32[512]{0:T(512)S(1)}, f32[512]{0:T(512)}, u32[]{:S(2)}) copy-start(f32[512]{0:T(512)} %get-tuple-element.154) | copy-start | bytes 6148
  819.3 18.8 %collective-permute-start.16 = (bf16[2,1,48,512]{3,2,1,0:T(8,128)(2,1)S(1)}, bf16[2,1,48,512]{3,2,1,0:T(8,128)(2,1)S(1)}, u32[]{:S(2)}, u32[]{:S(2)}) collective-permute-start(bf16[2,1,48,512]{3,2,1,0:T(8,128)(2,1)S(1)} %get-tuple-element.104), channel_id=1, source_target_pairs={{0,1},{1,2},{2,3},{4,5},{5,6},{6,7},{8,9},{9,10},{10,11},{12,13},{... | collective-permute-start | bytes 294920 | tf_op jit(solution)/shard_map/ppermute | solution.py:23
  820.7 17.4 collective-permute-start.17
  838.1 397.9 %reduce-scatter.5.cloned.1.call-start = ((), (), s32[]{:S(2)}) async-start(), calls=%async_computation.4 | async-start | bytes 21233664 | tf_op jit(solution)/shard_map/reduce_scatter | solution.py:282
  842.1 50.4 %copy-start.106 = (f32[512]{0:T(512)S(1)}, f32[512]{0:T(512)}, u32[]{:S(2)}) copy-start(f32[512]{0:T(512)} %get-tuple-element.150) | copy-start | bytes 6148
  910.3 778.2 %reduce-scatter.7.cloned.1.call-start = ((), (), s32[]{:S(2)}) async-start(), calls=%async_computation.5 | async-start | bytes 31850496 | tf_op jit(solution)/shard_map/reduce_scatter | solution.py:283
  944.9 818.5 %all-reduce.18.cloned.1.call-start = ((), (), s32[]{:S(2)}) async-start(), calls=%async_computation.8 | async-start | bytes 6684672 | tf_op jit(solution)/shard_map/psum | solution.py:288
  976.4 4.2 collective-permute-start.18
  977.8 5.3 collective-permute-start.19
  (115 other events, 658.3 us)
Sparse Core Ops, SparseCore 0:
  765.0 75.9 reduce-scatter.8
  844.6 75.0 reduce-scatter.10
  923.5 312.4 reduce-scatter.4
  1239.8 448.6 reduce-scatter.6
  1692.1 71.2 all-reduce.17
where the time goes:
time: 1790 us; the launch traced here: 1780 us
  waiting for transfers between devices  760 us (42%)
  blocking collectives  539 us (30%)
  matrix products  187 us (10%)
  local copies, waits for them, and re-layouts  129 us (7%)
  other arithmetic  110 us (6%)
  starting transfers between devices  36.3 us (2%)
    reduce_scatter x1, waiting for transfers between devices, local(): lax.psum_scatter(conv_stack, 'dp', scatter_dimension=1, tiled=True)  450 us
    psum x8, blocking collectives, moment_totals(): return lax.psum(stacked, ('dp', 'rows'))  331 us
    reduce_scatter x1, waiting for transfers between devices, local(): lax.psum_scatter(shared_stack, 'dp', scatter_dimension=1, tiled=True)  242 us
    psum x5, blocking collectives, slope_totals(): return lax.psum(stacked, ('dp', 'rows'))  208 us
    psum x1, waiting for transfers between devices, local(): lax.psum(spread[0].astype(jnp.bfloat16), 'rows').astype(jnp.float32)  56.4 us
    dot_general x5, matrix products, conv_apply(): result = jnp.dot(columns, weight, preferred_element_type=jnp.float32)  53.5 us
    dot_general x5, matrix products, conv_back(): grad_in = jnp.dot(grad_columns, turned, preferred_element_type=jnp.float32)  49 us
    dot_general x5, matrix products, conv_back(): lax.dot_general(columns, grad_out.reshape(-1, out_channels), (((0,), (0,)...  39.1 us
  transfers between devices with their start and end apart: 25, of which 7 were waited for; matrix products, arithmetic and copies ran while one was open for 13% of the time, Pallas kernels for 0%

commit v1 on v0

--- a/solution.py
+++ b/solution.py
@@ -78,23 +78,73 @@
     return (weight_grad, grad_in.reshape(slot_count, height, breadth, channels))
 
 
-def moment_totals(stacked):
-    return lax.psum(stacked, ("dp", "rows"))
-
-
-def slope_totals(stacked):
-    return lax.psum(stacked, ("dp", "rows"))
-
-
-def reduce_groups(partials, reducer):
-    totals = jnp.concatenate(
-        [
-            reducer(partials[2 * member : 2 * member + 2])
-            for member in range(partials.shape[0] // 2)
-        ],
-        axis=0,
-    )
-    return totals
+AXES = ("dp", "rows")
+
+
+def swapped(values, flip):
+    count = lax.axis_size("dp") * lax.axis_size("rows")
+    return lax.ppermute(values, AXES, [(i, i ^ flip) for i in range(count)])
+
+
+def exchange_sum(values):
+    count = lax.axis_size("dp") * lax.axis_size("rows")
+    bits = count.bit_length() - 1
+    assert count == 1 << bits
+    values = values + swapped(values, 1)
+    place = 1
+    while place < bits:
+        low = 1 << place
+        if place + 1 < bits:
+            high = low * 2
+            values = (values + swapped(values, low)) + (
+                swapped(values, high) + swapped(values, high + low)
+            )
+            place += 2
+        else:
+            values = values + swapped(values, low)
+            place += 1
+    return values
+
+
+def scattered_sum(values):
+    parts, height, breadth = values.shape
+    dp_count = lax.axis_size("dp")
+    row_count = lax.axis_size("rows")
+    dp_bits = dp_count.bit_length() - 1
+    row_bits = row_count.bit_length() - 1
+    place = lax.axis_index("dp") * row_count + lax.axis_index("rows")
+    bits = dp_bits + row_bits
+    folded = values.reshape((parts,) + (2,) * bits + (height >> bits, breadth))
+    left = list(range(bits - 1, -1, -1))
+    halves = jnp.split(folded, 2, axis=-1)
+
+    def halve(piece, left, bit):
+        axis = 1 + left.index(bit)
+        mine = (place >> bit) & 1
+        keep = lax.dynamic_index_in_dim(piece, mine, axis, keepdims=False)
+        send = lax.dynamic_index_in_dim(piece, 1 - mine, axis, keepdims=False)
+        got = swapped(send, 1 << bit)
+        total = keep.astype(jnp.float32) + got.astype(jnp.float32)
+        return total.astype(values.dtype), [b for b in left if b != bit]
+
+    done = []
+    for turn, piece in enumerate(halves):
+        order = list(range(bits))
+        if turn and bits > 2:
+            order[1], order[2] = order[2], order[1]
+        kept = left
+        for bit in order:
+            piece, kept = halve(piece, kept, bit)
+        done.append(piece)
+    piece = jnp.concatenate(done, axis=-1)
+    piece = piece.reshape((parts,) + (1,) * row_bits + piece.shape[1:])
+    for bit in range(row_bits - 1, -1, -1):
+        other = swapped(piece, 1 << bit)
+        mine = (place >> bit) & 1
+        pair = jnp.where(mine == 0, jnp.stack([piece, other]), jnp.stack([other, piece]))
+        axis = row_bits - bit
+        piece = jnp.concatenate([pair[0], pair[1]], axis=axis)
+    return piece.reshape(parts, height // dp_count, breadth).astype(jnp.float32)
 
 
 def normalize(arrays, gains, shifts, valid_mask, pixel_count):
@@ -103,7 +153,7 @@
         masked = values * valid_mask
         partials.append(jnp.sum(masked, axis=(0, 1, 2)))
         partials.append(jnp.sum(masked * values, axis=(0, 1, 2)))
-    totals = reduce_groups(jnp.stack(partials), moment_totals)
+    totals = exchange_sum(jnp.stack(partials))
     outputs = []
     saved = []
     for member, values in enumerate(arrays):
@@ -121,7 +171,7 @@
     for grad_out, pair in zip(gradients, saved):
         partials.append(jnp.sum(grad_out, axis=(0, 1, 2)))
         partials.append(jnp.sum(grad_out * pair[0], axis=(0, 1, 2)))
-    totals = reduce_groups(jnp.stack(partials), slope_totals)
+    totals = exchange_sum(jnp.stack(partials))
     inputs = []
     for member, grad_out in enumerate(gradients):
         centred, inverse = saved[member]
@@ -274,22 +324,15 @@
     )
     first_weight_grad, input_back = conv_back(first_dz[0], shared_conv[0], first_pad)
     input_grad = input_back * valid_mask
-    shared_stack = jnp.stack([first_weight_grad, second_weight_grad])
-    conv_stack = jnp.stack(conv_weight_grads)
-    down_stack = jnp.stack(down_weight_grads)
-    up_stack = jnp.stack(up_weight_grads)
-    spread = (
-        lax.psum_scatter(shared_stack, "dp", scatter_dimension=1, tiled=True),
-        lax.psum_scatter(conv_stack, "dp", scatter_dimension=1, tiled=True),
-        lax.psum_scatter(down_stack, "dp", scatter_dimension=1, tiled=True),
-        lax.psum_scatter(up_stack, "dp", scatter_dimension=1, tiled=True),
-    )
-    shared_part, conv_part, down_part, up_part = (
-        lax.psum(spread[0].astype(jnp.bfloat16), "rows").astype(jnp.float32),
-        lax.psum(spread[1].astype(jnp.bfloat16), "rows").astype(jnp.float32),
-        lax.psum(spread[2].astype(jnp.bfloat16), "rows").astype(jnp.float32),
-        lax.psum(spread[3].astype(jnp.bfloat16), "rows").astype(jnp.float32),
-    )
+    low = jnp.bfloat16
+    conv_part = scattered_sum(jnp.stack([g.astype(low) for g in conv_weight_grads]))
+    thin = scattered_sum(
+        jnp.stack([g.astype(low) for g in down_weight_grads + up_weight_grads])
+    )
+    down_part, up_part = thin[:task_count], thin[task_count:]
+    second_part = scattered_sum(second_weight_grad.astype(low)[None])
+    first_part = scattered_sum(first_weight_grad.astype(low)[None])
+    shared_part = jnp.concatenate([first_part, second_part])
     up_grad = up_part.transpose(0, 2, 1)
     shared_gain_grad = jnp.stack([first_totals[1], second_totals[1]])
     shared_shift_grad = jnp.stack([first_totals[0], second_totals[0]])

time: 1790 us -> 767 us (0.43)
  waiting for transfers between devices: 760 us -> 165 us
  blocking collectives: 539 us -> 0 us
  starting transfers between devices: 36.3 us -> 182 us
  matrix products: 187 us -> 149 us
  local copies, waits for them, and re-layouts: 129 us -> 162 us
    reduce_scatter x4 -> x0, waiting for transfers between devices: 691 us -> none  [the longest x1 450 us: local(): lax.psum_scatter(conv_stack, 'dp', scatter_dimension=1, tiled=True)]
    psum x13 -> x0, blocking collectives: 539 us -> none  [the longest x8 331 us: moment_totals(): return lax.psum(stacked, ('dp', 'rows'))]
    ppermute x0 -> x118, waiting for transfers between devices: none -> 158 us  [swapped(): return lax.ppermute(values, AXES, [(i, i ^ flip) for i in range(count)])]
    ppermute x0 -> x118, starting transfers between devices: none -> 142 us  [swapped(): return lax.ppermute(values, AXES, [(i, i ^ flip) for i in range(count)])]
    psum x1 -> x0, waiting for transfers between devices: 56.4 us -> none  [local(): lax.psum(spread[0].astype(jnp.bfloat16), 'rows').astype(jnp.float32)]
    dot_general x5, matrix products: 53.5 us -> 28.5 us  [conv_apply(): result = jnp.dot(columns, weight, preferred_element_type=jnp.float32)]
    unnamed x334 -> x478, local copies, waits for them, and re-layouts: 38.5 us -> 48.8 us
  transfers between devices with their start and end apart: 25 -> 138, of which waited for: 7 -> 62; matrix products, arithmetic and copies ran while one was open for 13% -> 29% of each run, Pallas kernels for 0% -> 0%
where the time goes in v1:
time: 767 us; the launch traced here: 759 us
  starting transfers between devices  182 us (24%)
  waiting for transfers between devices  165 us (22%)
  local copies, waits for them, and re-layouts  162 us (21%)
  matrix products  149 us (19%)
  other arithmetic  94.8 us (12%)
    ppermute x118, waiting for transfers between devices, swapped(): return lax.ppermute(values, AXES, [(i, i ^ flip) for i in range(count)])  158 us
    ppermute x118, starting transfers between devices, swapped(): return lax.ppermute(values, AXES, [(i, i ^ flip) for i in range(count)])  142 us
    unnamed x478, local copies, waits for them, and re-layouts  48.8 us
    dot_general x5, matrix products, conv_back(): lax.dot_general(columns, grad_out.reshape(-1, out_channels), (((0,), (0,)...  46.6 us
    dot_general x5, matrix products, conv_back(): grad_in = jnp.dot(grad_columns, turned, preferred_element_type=jnp.float32)  43 us
    transpose x5, local copies, waits for them, and re-layouts, conv_back(): turned = weight.reshape(9, channels, out_channels).transpose(0, 2, 1).res...  33.3 us
    dot_general x5, matrix products, conv_apply(): result = jnp.dot(columns, weight, preferred_element_type=jnp.float32)  28.5 us
    ppermute x10, starting transfers between devices, with_halo(): lax.ppermute(tail, axis, [(i, (i + 1) % count) for i in range(ends)])  26.6 us
  transfers between devices with their start and end apart: 138, of which 62 were waited for; matrix products, arithmetic and copies ran while one was open for 29% of the time, Pallas kernels for 0%

profile of v1, /device:TPU:0, one launch (start us, length us, event | category | flops | bytes accessed | tf_op | source)
XLA Modules:
  0.0 759.3 jit_solution(4532428549074976953)
XLA Ops:
  7.7 4.0 collective-permute-done.1
  15.7 4.7 multiply_reduce_fusion.10
  30.7 3.7 collective-permute-start.8
  49.5 4.7 multiply_reduce_fusion.9
  93.9 3.9 multiply_convert_fusion.13
  117.9 4.4 fusion.30
  125.1 4.3 collective-permute-start.34
  130.7 4.3 collective-permute-start.36
  150.1 4.7 fusion.6
  154.8 7.9 %fusion.4 = f32[2,10,48,512]{3,2,1,0:T(8,128)S(1)} fusion(bf16[2,10,48,4608]{3,2,1,0:T(8,128)(2,1)} %slice_dynamic-update-slice_fusion.36, bf16[3,4608,512]{2,1,0:T(8,128)(2,1)S(1)} %bitcast.690), kind=kOutput, calls=%fused_computation.12 | convolution fusion | flops 4529848320 | bytes 15532032 | tf_op jit(solution)/shard_map/dot_general | solution.py:56
  165.2 6.5 fusion.29
  200.1 3.7 reshape.1553
  204.0 4.7 multiply_reduce_fusion.21
  217.2 10.8 %fusion.180 = (bf16[1,4608,512]{2,1,0:T(8,128)(2,1)}, bf16[1,4608,512]{2,1,0:T(8,128)(2,1)}, bf16[1,4608,512]{2,1,0:T(8,128)(2,1)}) fusion(bf16[3,4608,512]{2,1,0:T(8,128)(2,1)} %param.18), kind=kLoop, calls=%fused_computation.608 | loop fusion | bytes 28311552 | tf_op jit(solution)/shard_map/slice | solution.py:241
  232.4 4.2 fusion.181
  236.6 6.7 copy.33
  243.3 6.6 copy.32
  249.9 6.6 copy.31
  256.5 6.7 copy.29
  263.2 6.8 copy.30
  270.6 3.9 multiply_convert_fusion.8
  274.5 11.0 %bitcast_convert_fusion = bf16[4608,512]{1,0:T(8,128)(2,1)} fusion(bf16[2,10,48,4608]{3,2,1,0:T(8,128)(2,1)} %copy-done.70, bf16[2,10,48,512]{3,2,1,0:T(8,128)(2,1)S(1)} %get-tuple-element.97), kind=kOutput, calls=%fused_computation.1 | convolution fusion | flops 4532207616 | bytes 14548992 | tf_op jit(solution)/shard_map/dot_general | solution.py:64
  288.6 10.6 %bitcast_convert_fusion.1 = bf16[4608,512]{1,0:T(8,128)(2,1)} fusion(bf16[2,10,48,4608]{3,2,1,0:T(8,128)(2,1)} %slice_dynamic-update-slice_fusion.36, bf16[2,10,48,512]{3,2,1,0:T(8,128)(2,1)S(1)} %get-tuple-element.101), kind=kOutput, calls=%fused_computation.2 | convolution fusion | flops 4532207616 | bytes 14548992 | tf_op jit(solution)/shard_map/dot_general | solution.py:64
  302.3 6.9 bitcast_convert_fusion.2
  323.7 6.7 pad_maximum_fusion
  351.9 4.0 collective-permute-start.52
  376.2 7.6 fusion.209
  384.0 11.5 %multiply_reduce_fusion.17 = (f32[512]{0:T(512)S(1)}, f32[512]{0:T(512)S(1)}, f32[2,10,48,512]{3,2,1,0:T(8,128)}, f32[2,10,48,512]{3,2,1,0:T(8,128)}) fusion(f32[2,10,48,512]{3,2,1,0:T(8,128)S(1)} %copy-done.14, f32[512]{0:T(512)S(1)} %copy-done.126, f32[512]{0:T(512)S(1)} %bitcast.802, f32[512]{0:T(512)S(1)} %bitcast.918, f32[512]{0:T(512)S(1)} %bitcast.865, ...), kind=kOutput, calls=%fused_computation.105 | convolution fusion | flops 4537220096 | bytes 20459520 | tf_op jit(solution)/shard_map/dot_general | solution.py:77
  395.6 8.7 %multiply_reduce_fusion.16 = (f32[512]{0:T(512)S(1)}, f32[512]{0:T(512)S(1)}, f32[2,10,48,512]{3,2,1,0:T(8,128)}, f32[512]{0:T(512)S(1)}, f32[512]{0:T(512)S(1)}...) fusion(f32[2,10,48,512]{3,2,1,0:T(8,128)S(1)} %copy-done.29, f32[512]{0:T(512)S(1)} %copy-done.120, ...), kind=kOutput, calls=%fused_computation.104 | convolution fusion | flops 4544100352 | bytes 26370048 | tf_op jit(solution)/shard_map/dot_general | solution.py:77
  411.2 4.1 dynamic-slice_bitcast_fusion
  421.9 4.3 copy.107
  472.0 5.2 fusion.175
  501.3 9.0 %bitcast_convert_fusion.3 = bf16[4608,512]{1,0:T(8,128)(2,1)S(1)} fusion(bf16[2,10,48,4608]{3,2,1,0:T(8,128)(2,1)} %copy-done.68, bf16[2,10,48,512]{3,2,1,0:T(8,128)(2,1)S(1)} %multiply_convert_fusion.1), kind=kOutput, calls=%fused_computation.4 | convolution fusion | flops 4532207616 | bytes 14548992 | tf_op jit(solution)/shard_map/dot_general | solution.py:64
  514.2 5.5 fusion.174
  537.2 9.0 %bitcast_convert_fusion.4 = bf16[4608,512]{1,0:T(8,128)(2,1)S(1)} fusion(bf16[2,10,48,4608]{3,2,1,0:T(8,128)(2,1)} %copy-done.67, bf16[2,10,48,512]{3,2,1,0:T(8,128)(2,1)S(1)} %multiply_convert_fusion), kind=kOutput, calls=%fused_computation.5 | convolution fusion | flops 4532207616 | bytes 14548992 | tf_op jit(solution)/shard_map/dot_general | solution.py:64
  563.7 9.7 %convolution_multiply_fusion = f32[2,10,48,512]{3,2,1,0:T(8,128)} fusion(bf16[2,10,48,4608]{3,2,1,0:T(8,128)(2,1)} %copy-done.72, bf16[4608,512,1,1]{1,0,3,2:T(8,128)(2,1)S(1)} %bitcast.702, f32[2,10,48]{2,1,0:T(8,128)S(1)} %get-tuple-element.266), kind=kOutput, calls=%fused_computation.162 | convolution fusion | flops 4530339840 | bytes 15535872 | tf_op jit(solution)/shard_map/dot_general | solution.py:77
  575.5 5.8 collective-permute-done.90
  584.4 4.7 collective-permute-done.128
  608.6 5.7 collective-permute-done.136
  620.0 5.6 collective-permute-done.91
  629.3 4.5 collective-permute-done.104
  669.1 20.9 %collective-permute-done.120 = bf16[3,2,2,2,144,256]{5,4,3,2,1,0:T(8,128)(2,1)S(1)} collective-permute-done((bf16[3,2,2,2,144,256]{5,4,3,2,1,0:T(8,128)(2,1)S(1)}, bf16[3,2,2,2,144,256]{5,4,3,2,1,0:T(8,128)(2,1)S(1)}, u32[]{:S(2)}, u32[]{:S(2)}) %collective-permute-start.120) | collective-permute-done | bytes 1769504 | tf_op jit(solution)/shard_map/ppermute | solution.py:86
  692.4 8.0 %collective-permute-done.115 = bf16[3,2,2,2,144,256]{5,4,0,1,2,3:T(8,128)(2,1)S(1)} collective-permute-done((bf16[3,2,2,2,144,256]{5,4,0,1,2,3:T(8,128)(2,1)S(1)}, bf16[3,2,2,2,144,256]{5,4,0,1,2,3:T(8,128)(2,1)S(1)}, u32[]{:S(2)}, u32[]{:S(2)}) %collective-permute-start.115) | collective-permute-done | bytes 1769504 | tf_op jit(solution)/shard_map/ppermute | solution.py:86
  703.8 12.5 %collective-permute-done.121 = bf16[3,2,2,144,256]{4,3,2,1,0:T(8,128)(2,1)S(1)} collective-permute-done((bf16[3,2,2,144,256]{4,3,2,1,0:T(8,128)(2,1)S(1)}, bf16[3,2,2,144,256]{4,3,2,1,0:T(8,128)(2,1)S(1)}, u32[]{:S(2)}, u32[]{:S(2)}) %collective-permute-start.121) | collective-permute-done | bytes 884768 | tf_op jit(solution)/shard_map/ppermute | solution.py:86
  719.1 7.6 %collective-permute-done.122 = bf16[3,2,144,256]{3,2,1,0:T(8,128)(2,1)S(1)} collective-permute-done((bf16[3,2,144,256]{3,2,1,0:T(8,128)(2,1)S(1)}, bf16[3,2,144,256]{3,2,1,0:T(8,128)(2,1)S(1)}, u32[]{:S(2)}, u32[]{:S(2)}) %collective-permute-start.122) | collective-permute-done | bytes 442400 | tf_op jit(solution)/shard_map/ppermute | solution.py:86
  730.5 5.6 collective-permute-done.117
  736.3 8.1 %collective-permute-done.118 = bf16[3,144,256]{2,1,0:T(8,128)(2,1)S(1)} collective-permute-done((bf16[3,144,256]{2,1,0:T(8,128)(2,1)S(1)}, bf16[3,144,256]{2,1,0:T(8,128)(2,1)S(1)}, u32[]{:S(2)}, u32[]{:S(2)}) %collective-permute-start.118) | collective-permute-done | bytes 221216 | tf_op jit(solution)/shard_map/ppermute | solution.py:86
  747.4 6.0 collective-permute-done.124
  (1051 shorter events, 430.7 us)
Async XLA Ops:
  122.4 12.6 %collective-permute-start.32 = (bf16[2,1,48,512]{3,2,1,0:T(8,128)(2,1)S(1)}, bf16[2,1,48,512]{3,2,1,0:T(8,128)(2,1)S(1)}, u32[]{:S(2)}, u32[]{:S(2)}) collective-permute-start(bf16[2,1,48,512]{3,2,1,0:T(8,128)(2,1)S(1)} %get-tuple-element.123), channel_id=1, source_target_pairs={{0,1},{1,2},{2,3},{4,5},{5,6},{6,7},{8,9},{9,10},{10,11},{12,13},{... | collective-permute-start | bytes 294920 | tf_op jit(solution)/shard_map/ppermute | solution.py:23
  123.8 12.6 %collective-permute-start.33 = (bf16[2,1,48,512]{3,2,1,0:T(8,128)(2,1)S(1)}, bf16[2,1,48,512]{3,2,1,0:T(8,128)(2,1)S(1)}, u32[]{:S(2)}, u32[]{:S(2)}) collective-permute-start(bf16[2,1,48,512]{3,2,1,0:T(8,128)(2,1)S(1)} %get-tuple-element.124), channel_id=1, source_target_pairs={{1,0},{2,1},{3,2},{5,4},{6,5},{7,6},{9,8},{10,9},{11,10},{13,12},{... | collective-permute-start | bytes 294920 | tf_op jit(solution)/shard_map/ppermute | solution.py:25
  125.1 13.6 %collective-permute-start.34 = (bf16[2,1,48,512]{3,2,1,0:T(8,128)(2,1)S(1)}, bf16[2,1,48,512]{3,2,1,0:T(8,128)(2,1)S(1)}, u32[]{:S(2)}, u32[]{:S(2)}) collective-permute-start(bf16[2,1,48,512]{3,2,1,0:T(8,128)(2,1)S(1)} %get-tuple-element.128), channel_id=1, source_target_pairs={{0,1},{1,2},{2,3},{4,5},{5,6},{6,7},{8,9},{9,10},{10,11},{12,13},{... | collective-permute-start | bytes 294920 | tf_op jit(solution)/shard_map/ppermute | solution.py:23
  130.7 32.0 %collective-permute-start.36 = (bf16[2,1,48,512]{3,2,1,0:T(8,128)(2,1)S(1)}, bf16[2,1,48,512]{3,2,1,0:T(8,128)(2,1)S(1)}, u32[]{:S(2)}, u32[]{:S(2)}) collective-permute-start(bf16[2,1,48,512]{3,2,1,0:T(8,128)(2,1)S(1)} %get-tuple-element.130), channel_id=1, source_target_pairs={{0,1},{1,2},{2,3},{4,5},{5,6},{6,7},{8,9},{9,10},{10,11},{12,13},{... | collective-permute-start | bytes 294920 | tf_op jit(solution)/shard_map/ppermute | solution.py:23
  135.0 27.7 %collective-permute-start.37 = (bf16[2,1,48,512]{3,2,1,0:T(8,128)(2,1)S(1)}, bf16[2,1,48,512]{3,2,1,0:T(8,128)(2,1)S(1)}, u32[]{:S(2)}, u32[]{:S(2)}) collective-permute-start(bf16[2,1,48,512]{3,2,1,0:T(8,128)(2,1)S(1)} %get-tuple-element.131), channel_id=1, source_target_pairs={{1,0},{2,1},{3,2},{5,4},{6,5},{7,6},{9,8},{10,9},{11,10},{13,12},{... | collective-permute-start | bytes 294920 | tf_op jit(solution)/shard_map/ppermute | solution.py:25
  182.1 21.8 %collective-permute-start.44 = (f32[6,512]{1,0:T(8,128)S(1)}, f32[6,512]{1,0:T(8,128)S(1)}, u32[]{:S(2)}, u32[]{:S(2)}) collective-permute-start(f32[6,512]{1,0:T(8,128)S(1)} %add_add_fusion.7), channel_id=1, source_target_pairs={{0,24},{1,25},{2,26},{3,27},{4,28},{5,29},{6,30},{7,31},{8,16},{9,... | collective-permute-start | bytes 36872 | tf_op jit(solution)/shard_map/ppermute | solution.py:86
  184.4 19.5 %collective-permute-start.43 = (f32[6,512]{1,0:T(8,128)S(1)}, f32[6,512]{1,0:T(8,128)S(1)}, u32[]{:S(2)}, u32[]{:S(2)}) collective-permute-start(f32[6,512]{1,0:T(8,128)S(1)} %add_add_fusion.7), channel_id=1, source_target_pairs={{0,16},{1,17},{2,18},{3,19},{4,20},{5,21},{6,22},{7,23},{8,24},{9,... | collective-permute-start | bytes 36872 | tf_op jit(solution)/shard_map/ppermute | solution.py:86
  185.3 18.5 %collective-permute-start.42 = (f32[6,512]{1,0:T(8,128)S(1)}, f32[6,512]{1,0:T(8,128)S(1)}, u32[]{:S(2)}, u32[]{:S(2)}) collective-permute-start(f32[6,512]{1,0:T(8,128)S(1)} %add_add_fusion.7), channel_id=1, source_target_pairs={{0,8},{1,9},{2,10},{3,11},{4,12},{5,13},{6,14},{7,15},{8,0},{9,1},... | collective-permute-start | bytes 36872 | tf_op jit(solution)/shard_map/ppermute | solution.py:86
  213.6 14.3 %collective-permute-start.48 = (f32[6,512]{1,0:T(8,128)S(1)}, f32[6,512]{1,0:T(8,128)S(1)}, u32[]{:S(2)}, u32[]{:S(2)}) collective-permute-start(f32[6,512]{1,0:T(8,128)S(1)} %add.1000), channel_id=1, source_target_pairs={{0,6},{1,7},{2,4},{3,5},{4,2},{5,3},{6,0},{7,1},{8,14},{9,15},{10,... | collective-permute-start | bytes 36872 | tf_op jit(solution)/shard_map/ppermute | solution.py:86
  214.7 13.2 %collective-permute-start.47 = (f32[6,512]{1,0:T(8,128)S(1)}, f32[6,512]{1,0:T(8,128)S(1)}, u32[]{:S(2)}, u32[]{:S(2)}) collective-permute-start(f32[6,512]{1,0:T(8,128)S(1)} %add.1000), channel_id=1, source_target_pairs={{0,4},{1,5},{2,6},{3,7},{4,0},{5,1},{6,2},{7,3},{8,12},{9,13},{10,... | collective-permute-start | bytes 36872 | tf_op jit(solution)/shard_map/ppermute | solution.py:86
  215.3 12.7 %collective-permute-start.46 = (f32[6,512]{1,0:T(8,128)S(1)}, f32[6,512]{1,0:T(8,128)S(1)}, u32[]{:S(2)}, u32[]{:S(2)}) collective-permute-start(f32[6,512]{1,0:T(8,128)S(1)} %add.1000), channel_id=1, source_target_pairs={{0,2},{1,3},{2,0},{3,1},{4,6},{5,7},{6,4},{7,5},{8,10},{9,11},{10,... | collective-permute-start | bytes 36872 | tf_op jit(solution)/shard_map/ppermute | solution.py:86
  228.0 42.0 %collective-permute-start.51 = (f32[6,512]{1,0:T(8,128)S(1)}, f32[6,512]{1,0:T(8,128)S(1)}, u32[]{:S(2)}, u32[]{:S(2)}) collective-permute-start(f32[6,512]{1,0:T(8,128)S(1)} %add_add_fusion.5), channel_id=1, source_target_pairs={{0,24},{1,25},{2,26},{3,27},{4,28},{5,29},{6,30},{7,31},{8,16},{9,... | collective-permute-start | bytes 36872 | tf_op jit(solution)/shard_map/ppermute | solution.py:86
  230.2 39.7 %collective-permute-start.50 = (f32[6,512]{1,0:T(8,128)S(1)}, f32[6,512]{1,0:T(8,128)S(1)}, u32[]{:S(2)}, u32[]{:S(2)}) collective-permute-start(f32[6,512]{1,0:T(8,128)S(1)} %add_add_fusion.5), channel_id=1, source_target_pairs={{0,16},{1,17},{2,18},{3,19},{4,20},{5,21},{6,22},{7,23},{8,24},{9,... | collective-permute-start | bytes 36872 | tf_op jit(solution)/shard_map/ppermute | solution.py:86
  230.3 39.6 %collective-permute-start.49 = (f32[6,512]{1,0:T(8,128)S(1)}, f32[6,512]{1,0:T(8,128)S(1)}, u32[]{:S(2)}, u32[]{:S(2)}) collective-permute-start(f32[6,512]{1,0:T(8,128)S(1)} %add_add_fusion.5), channel_id=1, source_target_pairs={{0,8},{1,9},{2,10},{3,11},{4,12},{5,13},{6,14},{7,15},{8,0},{9,1},... | collective-permute-start | bytes 36872 | tf_op jit(solution)/shard_map/ppermute | solution.py:86
  333.9 22.1 %collective-permute-start.56 = (bf16[2,1,48,512]{3,2,1,0:T(8,128)(2,1)}, bf16[2,1,48,512]{3,2,1,0:T(8,128)(2,1)}, u32[]{:S(2)}, u32[]{:S(2)}) collective-permute-start(bf16[2,1,48,512]{3,2,1,0:T(8,128)(2,1)} %get-tuple-element.117), channel_id=1, source_target_pairs={{0,1},{1,2},{2,3},{4,5},{5,6},{6,7},{8,9},{9,10},{10,11},{12,13},{... | collective-permute-start | bytes 294920 | tf_op jit(solution)/shard_map/ppermute | solution.py:23
  335.8 21.7 %collective-permute-start.57 = (bf16[2,1,48,512]{3,2,1,0:T(8,128)(2,1)}, bf16[2,1,48,512]{3,2,1,0:T(8,128)(2,1)}, u32[]{:S(2)}, u32[]{:S(2)}) collective-permute-start(bf16[2,1,48,512]{3,2,1,0:T(8,128)(2,1)} %get-tuple-element.118), channel_id=1, source_target_pairs={{1,0},{2,1},{3,2},{5,4},{6,5},{7,6},{9,8},{10,9},{11,10},{13,12},{... | collective-permute-start | bytes 294920 | tf_op jit(solution)/shard_map/ppermute | solution.py:25
  347.6 14.9 %collective-permute-start.54 = (bf16[2,1,48,512]{3,2,1,0:T(8,128)(2,1)}, bf16[2,1,48,512]{3,2,1,0:T(8,128)(2,1)S(1)}, u32[]{:S(2)}, u32[]{:S(2)}) collective-permute-start(bf16[2,1,48,512]{3,2,1,0:T(8,128)(2,1)} %get-tuple-element.121), channel_id=1, source_target_pairs={{0,1},{1,2},{2,3},{4,5},{5,6},{6,7},{8,9},{9,10},{10,11},{12,13},{... | collective-permute-start | bytes 294920 | tf_op jit(solution)/shard_map/ppermute | solution.py:23
  350.6 11.9 %collective-permute-start.55 = (bf16[2,1,48,512]{3,2,1,0:T(8,128)(2,1)}, bf16[2,1,48,512]{3,2,1,0:T(8,128)(2,1)S(1)}, u32[]{:S(2)}, u32[]{:S(2)}) collective-permute-start(bf16[2,1,48,512]{3,2,1,0:T(8,128)(2,1)} %get-tuple-element.122), channel_id=1, source_target_pairs={{1,0},{2,1},{3,2},{5,4},{6,5},{7,6},{9,8},{10,9},{11,10},{13,12},{... | collective-permute-start | bytes 294920 | tf_op jit(solution)/shard_map/ppermute | solution.py:25
  351.9 12.9 %collective-permute-start.52 = (bf16[2,1,48,512]{3,2,1,0:T(8,128)(2,1)}, bf16[2,1,48,512]{3,2,1,0:T(8,128)(2,1)S(1)}, u32[]{:S(2)}, u32[]{:S(2)}) collective-permute-start(bf16[2,1,48,512]{3,2,1,0:T(8,128)(2,1)} %get-tuple-element.119), channel_id=1, source_target_pairs={{0,1},{1,2},{2,3},{4,5},{5,6},{6,7},{8,9},{9,10},{10,11},{12,13},{... | collective-permute-start | bytes 294920 | tf_op jit(solution)/shard_map/ppermute | solution.py:23
  415.3 11.0 %collective-permute-start.64 = (f32[6,512]{1,0:T(8,128)S(1)}, f32[6,512]{1,0:T(8,128)S(1)}, u32[]{:S(2)}, u32[]{:S(2)}) collective-permute-start(f32[6,512]{1,0:T(8,128)S(1)} %add_add_fusion.3), channel_id=1, source_target_pairs={{0,24},{1,25},{2,26},{3,27},{4,28},{5,29},{6,30},{7,31},{8,16},{9,... | collective-permute-start | bytes 36872 | tf_op jit(solution)/shard_map/ppermute | solution.py:86
  426.2 226.1 %collective-permute-start.119 = (bf16[3,2,2,2,2,144,256]{6,5,4,3,2,1,0:T(8,128)(2,1)}, bf16[3,2,2,2,2,144,256]{6,5,4,3,2,1,0:T(8,128)(2,1)}, u32[]{:S(2)}, u32[]{:S(2)}) collective-permute-start(bf16[3,2,2,2,2,144,256]{6,5,4,3,2,1,0:T(8,128)(2,1)} %dynamic-slice_bitcast_fusion), channel_id=1, source_target_pairs={{0,1},{1,0},{2,3},{3,2},{4,5},{5,4},{6,7},{7,6},{8,9},{9,8},{10,11... | collective-permute-start | bytes 10616840 | tf_op jit(solution)/shard_map/ppermute | solution.py:86
  494.6 63.6 %collective-permute-start.131 = (bf16[6,2,2,2,2,16,256]{6,5,4,3,2,1,0:T(8,128)(2,1)}, bf16[6,2,2,2,2,16,256]{6,5,4,3,2,1,0:T(8,128)(2,1)S(1)}, u32[]{:S(2)}, u32[]{:S(2)}) collective-permute-start(bf16[6,2,2,2,2,16,256]{6,5,4,3,2,1,0:T(8,128)(2,1)} %dynamic-slice_bitcast_fusion.6), channel_id=1, source_target_pairs={{0,1},{1,0},{2,3},{3,2},{4,5},{5,4},{6,7},{7,6},{8,9},{9,8},{10,11... | collective-permute-start | bytes 2359304 | tf_op jit(solution)/shard_map/ppermute | solution.py:86
  497.6 12.7 %collective-permute-start.79 = (bf16[2,1,48,512]{3,2,1,0:T(8,128)(2,1)S(1)}, bf16[2,1,48,512]{3,2,1,0:T(8,128)(2,1)S(1)}, u32[]{:S(2)}, u32[]{:S(2)}) collective-permute-start(bf16[2,1,48,512]{3,2,1,0:T(8,128)(2,1)S(1)} %get-tuple-element.112), channel_id=1, source_target_pairs={{0,1},{1,2},{2,3},{4,5},{5,6},{6,7},{8,9},{9,10},{10,11},{12,13},{... | collective-permute-start | bytes 294920 | tf_op jit(solution)/shard_map/ppermute | solution.py:23
  500.0 10.3 %collective-permute-start.80 = (bf16[2,1,48,512]{3,2,1,0:T(8,128)(2,1)S(1)}, bf16[2,1,48,512]{3,2,1,0:T(8,128)(2,1)S(1)}, u32[]{:S(2)}, u32[]{:S(2)}) collective-permute-start(bf16[2,1,48,512]{3,2,1,0:T(8,128)(2,1)S(1)} %get-tuple-element.113), channel_id=1, source_target_pairs={{1,0},{2,1},{3,2},{5,4},{6,5},{7,6},{9,8},{10,9},{11,10},{13,12},{... | collective-permute-start | bytes 294920 | tf_op jit(solution)/shard_map/ppermute | solution.py:25
  534.7 24.6 %collective-permute-start.126 = (bf16[6,2,2,2,2,16,256]{6,5,0,1,2,3,4:T(8,128)(2,1)S(1)}, bf16[6,2,2,2,2,16,256]{6,5,0,1,2,3,4:T(8,128)(2,1)S(1)}, u32[]{:S(2)}, u32[]{:S(2)}) collective-permute-start(bf16[6,2,2,2,2,16,256]{6,5,0,1,2,3,4:T(8,128)(2,1)S(1)} %bitcast.728), channel_id=1, source_target_pairs={{0,1},{1,0},{2,3},{3,2},{4,5},{5,4},{6,7},{7,6},{8,9},{9,8},{10,11... | collective-permute-start | bytes 2359304 | tf_op jit(solution)/shard_map/ppermute | solution.py:86
  550.8 23.5 %collective-permute-start.102 = (bf16[1,2,2,2,2,144,256]{6,5,1,2,3,4,0:T(8,128)(2,1)S(1)}, bf16[1,2,2,2,2,144,256]{6,5,1,2,3,4,0:T(8,128)(2,1)S(1)}, u32[]{:S(2)}, u32[]{:S(2)}) collective-permute-start(bf16[1,2,2,2,2,144,256]{6,5,1,2,3,4,0:T(8,128)(2,1)S(1)} %bitcast.725), channel_id=1, source_target_pairs={{0,1},{1,0},{2,3},{3,2},{4,5},{5,4},{6,7},{7,6},{8,9},{9,8},{10,11... | collective-permute-start | bytes 3538952 | tf_op jit(solution)/shard_map/ppermute | solution.py:86
  553.1 21.7 %collective-permute-start.107 = (bf16[1,2,2,2,2,144,256]{6,5,1,2,4,3,0:T(8,128)(2,1)S(1)}, bf16[1,2,2,2,2,144,256]{6,5,1,2,4,3,0:T(8,128)(2,1)S(1)}, u32[]{:S(2)}, u32[]{:S(2)}) collective-permute-start(bf16[1,2,2,2,2,144,256]{6,5,1,2,4,3,0:T(8,128)(2,1)S(1)} %bitcast.724), channel_id=1, source_target_pairs={{0,1},{1,0},{2,3},{3,2},{4,5},{5,4},{6,7},{7,6},{8,9},{9,8},{10,11... | collective-permute-start | bytes 3538952 | tf_op jit(solution)/shard_map/ppermute | solution.py:86
  558.6 14.8 %collective-permute-start.132 = (bf16[6,2,2,2,16,256]{5,4,3,2,1,0:T(8,128)(2,1)S(1)}, bf16[6,2,2,2,16,256]{5,4,3,2,1,0:T(8,128)(2,1)S(1)}, u32[]{:S(2)}, u32[]{:S(2)}) collective-permute-start(bf16[6,2,2,2,16,256]{5,4,3,2,1,0:T(8,128)(2,1)S(1)} %dynamic-slice_bitcast_fusion.13), channel_id=1, source_target_pairs={{0,4},{1,5},{2,6},{3,7},{4,0},{5,1},{6,2},{7,3},{8,12},{9,13},{10,... | collective-permute-start | bytes 1179656 | tf_op jit(solution)/shard_map/ppermute | solution.py:86
  560.4 13.1 %collective-permute-start.127 = (bf16[6,2,2,2,16,256]{5,4,0,1,2,3:T(8,128)(2,1)S(1)}, bf16[6,2,2,2,16,256]{5,4,0,1,2,3:T(8,128)(2,1)S(1)}, u32[]{:S(2)}, u32[]{:S(2)}) collective-permute-start(bf16[6,2,2,2,16,256]{5,4,0,1,2,3:T(8,128)(2,1)S(1)} %dynamic-slice_bitcast_fusion.14), channel_id=1, source_target_pairs={{0,2},{1,3},{2,0},{3,1},{4,6},{5,7},{6,4},{7,5},{8,10},{9,11},{10,... | collective-permute-start | bytes 1179656 | tf_op jit(solution)/shard_map/ppermute | solution.py:86
  573.4 83.7 %collective-permute-start.114 = (bf16[3,2,2,2,2,144,256]{6,5,0,1,2,3,4:T(8,128)(2,1)S(1)}, bf16[3,2,2,2,2,144,256]{6,5,0,1,2,3,4:T(8,128)(2,1)S(1)}, u32[]{:S(2)}, u32[]{:S(2)}) collective-permute-start(bf16[3,2,2,2,2,144,256]{6,5,0,1,2,3,4:T(8,128)(2,1)S(1)} %bitcast.720), channel_id=1, source_target_pairs={{0,1},{1,0},{2,3},{3,2},{4,5},{5,4},{6,7},{7,6},{8,9},{9,8},{10,11... | collective-permute-start | bytes 10616840 | tf_op jit(solution)/shard_map/ppermute | solution.py:86
  583.0 31.4 %collective-permute-start.103 = (bf16[1,2,2,2,144,256]{5,4,1,2,3,0:T(8,128)(2,1)S(1)}, bf16[1,2,2,2,144,256]{5,4,1,2,3,0:T(8,128)(2,1)S(1)}, u32[]{:S(2)}, u32[]{:S(2)}) collective-permute-start(bf16[1,2,2,2,144,256]{5,4,1,2,3,0:T(8,128)(2,1)S(1)} %dynamic-slice_bitcast_fusion.8), channel_id=1, source_target_pairs={{0,2},{1,3},{2,0},{3,1},{4,6},{5,7},{6,4},{7,5},{8,10},{9,11},{10,... | collective-permute-start | bytes 1769480 | tf_op jit(solution)/shard_map/ppermute | solution.py:86
  583.4 31.8 %collective-permute-start.108 = (bf16[1,2,2,2,144,256]{5,4,1,2,3,0:T(8,128)(2,1)S(1)}, bf16[1,2,2,2,144,256]{5,4,1,2,3,0:T(8,128)(2,1)S(1)}, u32[]{:S(2)}, u32[]{:S(2)}) collective-permute-start(bf16[1,2,2,2,144,256]{5,4,1,2,3,0:T(8,128)(2,1)S(1)} %dynamic-slice_bitcast_fusion.7), channel_id=1, source_target_pairs={{0,4},{1,5},{2,6},{3,7},{4,0},{5,1},{6,2},{7,3},{8,12},{9,13},{10,... | collective-permute-start | bytes 1769480 | tf_op jit(solution)/shard_map/ppermute | solution.py:86
  614.3 11.3 %collective-permute-start.91 = (bf16[1,2,2,2,144,256]{5,4,1,2,3,0:T(8,128)(2,1)S(1)}, bf16[1,2,2,2,144,256]{5,4,1,2,3,0:T(8,128)(2,1)S(1)}, u32[]{:S(2)}, u32[]{:S(2)}) collective-permute-start(bf16[1,2,2,2,144,256]{5,4,1,2,3,0:T(8,128)(2,1)S(1)} %dynamic-slice_bitcast_fusion.10), channel_id=1, source_target_pairs={{0,2},{1,3},{2,0},{3,1},{4,6},{5,7},{6,4},{7,5},{8,10},{9,11},{10,... | collective-permute-start | bytes 1769480 | tf_op jit(solution)/shard_map/ppermute | solution.py:86
  614.4 14.7 %collective-permute-start.96 = (bf16[1,2,2,2,144,256]{5,4,3,2,1,0:T(8,128)(2,1)S(1)}, bf16[1,2,2,2,144,256]{5,4,3,2,1,0:T(8,128)(2,1)S(1)}, u32[]{:S(2)}, u32[]{:S(2)}) collective-permute-start(bf16[1,2,2,2,144,256]{5,4,3,2,1,0:T(8,128)(2,1)S(1)} %dynamic-slice_bitcast_fusion.9), channel_id=1, source_target_pairs={{0,4},{1,5},{2,6},{3,7},{4,0},{5,1},{6,2},{7,3},{8,12},{9,13},{10,... | collective-permute-start | bytes 1769480 | tf_op jit(solution)/shard_map/ppermute | solution.py:86
  616.8 17.1 %collective-permute-start.104 = (bf16[1,2,2,144,256]{4,3,1,2,0:T(8,128)(2,1)S(1)}, bf16[1,2,2,144,256]{4,3,1,2,0:T(8,128)(2,1)S(1)}, u32[]{:S(2)}, u32[]{:S(2)}) collective-permute-start(bf16[1,2,2,144,256]{4,3,1,2,0:T(8,128)(2,1)S(1)} %dynamic-slice_bitcast_fusion.16), channel_id=1, source_target_pairs={{0,4},{1,5},{2,6},{3,7},{4,0},{5,1},{6,2},{7,3},{8,12},{9,13},{10,... | collective-permute-start | bytes 884744 | tf_op jit(solution)/shard_map/ppermute | solution.py:86
  625.6 10.4 %collective-permute-start.109 = (bf16[1,2,2,144,256]{4,3,1,2,0:T(8,128)(2,1)S(1)}, bf16[1,2,2,144,256]{4,3,1,2,0:T(8,128)(2,1)S(1)}, u32[]{:S(2)}, u32[]{:S(2)}) collective-permute-start(bf16[1,2,2,144,256]{4,3,1,2,0:T(8,128)(2,1)S(1)} %dynamic-slice_bitcast_fusion.15), channel_id=1, source_target_pairs={{0,2},{1,3},{2,0},{3,1},{4,6},{5,7},{6,4},{7,5},{8,10},{9,11},{10,... | collective-permute-start | bytes 884744 | tf_op jit(solution)/shard_map/ppermute | solution.py:86
  640.5 20.5 %collective-permute-start.93 = (bf16[1,2,144,256]{3,2,1,0:T(8,128)(2,1)S(1)}, bf16[1,2,144,256]{3,2,1,0:T(8,128)(2,1)S(1)}, u32[]{:S(2)}, u32[]{:S(2)}) collective-permute-start(bf16[1,2,144,256]{3,2,1,0:T(8,128)(2,1)S(1)} %dynamic-slice_bitcast_fusion.26), channel_id=1, source_target_pairs={{0,8},{1,9},{2,10},{3,11},{4,12},{5,13},{6,14},{7,15},{8,0},{9,1},... | collective-permute-start | bytes 442376 | tf_op jit(solution)/shard_map/ppermute | solution.py:86
  643.2 19.7 %collective-permute-start.98 = (bf16[1,2,144,256]{3,2,1,0:T(8,128)(2,1)S(1)}, bf16[1,2,144,256]{3,2,1,0:T(8,128)(2,1)S(1)}, u32[]{:S(2)}, u32[]{:S(2)}) collective-permute-start(bf16[1,2,144,256]{3,2,1,0:T(8,128)(2,1)S(1)} %dynamic-slice_bitcast_fusion.25), channel_id=1, source_target_pairs={{0,8},{1,9},{2,10},{3,11},{4,12},{5,13},{6,14},{7,15},{8,0},{9,1},... | collective-permute-start | bytes 442376 | tf_op jit(solution)/shard_map/ppermute | solution.py:86
  650.4 9.5 %collective-permute-start.111 = (bf16[1,144,256]{2,1,0:T(8,128)(2,1)S(1)}, bf16[1,144,256]{2,1,0:T(8,128)(2,1)S(1)}, u32[]{:S(2)}, u32[]{:S(2)}) collective-permute-start(bf16[1,144,256]{2,1,0:T(8,128)(2,1)S(1)} %dynamic-slice_bitcast_fusion.29), channel_id=1, source_target_pairs={{0,16},{1,17},{2,18},{3,19},{4,20},{5,21},{6,22},{7,23},{8,24},{9,... | collective-permute-start | bytes 221192 | tf_op jit(solution)/shard_map/ppermute | solution.py:86
  655.9 34.1 %collective-permute-start.120 = (bf16[3,2,2,2,144,256]{5,4,3,2,1,0:T(8,128)(2,1)S(1)}, bf16[3,2,2,2,144,256]{5,4,3,2,1,0:T(8,128)(2,1)S(1)}, u32[]{:S(2)}, u32[]{:S(2)}) collective-permute-start(bf16[3,2,2,2,144,256]{5,4,3,2,1,0:T(8,128)(2,1)S(1)} %dynamic-slice_bitcast_fusion.1), channel_id=1, source_target_pairs={{0,4},{1,5},{2,6},{3,7},{4,0},{5,1},{6,2},{7,3},{8,12},{9,13},{10,... | collective-permute-start | bytes 5308424 | tf_op jit(solution)/shard_map/ppermute | solution.py:86
  658.8 41.6 %collective-permute-start.115 = (bf16[3,2,2,2,144,256]{5,4,0,1,2,3:T(8,128)(2,1)S(1)}, bf16[3,2,2,2,144,256]{5,4,0,1,2,3:T(8,128)(2,1)S(1)}, u32[]{:S(2)}, u32[]{:S(2)}) collective-permute-start(bf16[3,2,2,2,144,256]{5,4,0,1,2,3:T(8,128)(2,1)S(1)} %dynamic-slice_bitcast_fusion.2), channel_id=1, source_target_pairs={{0,2},{1,3},{2,0},{3,1},{4,6},{5,7},{6,4},{7,5},{8,10},{9,11},{10,... | collective-permute-start | bytes 5308424 | tf_op jit(solution)/shard_map/ppermute | solution.py:86
  660.0 43.6 %collective-permute-start.112 = (bf16[1,1,1,144,512]{4,3,2,1,0:T(8,128)(2,1)S(1)}, bf16[1,1,1,144,512]{4,3,2,1,0:T(8,128)(2,1)S(1)}, u32[]{:S(2)}, u32[]{:S(2)}) collective-permute-start(bf16[1,1,1,144,512]{4,3,2,1,0:T(8,128)(2,1)S(1)} %get-tuple-element.165), channel_id=1, source_target_pairs={{0,2},{1,3},{2,0},{3,1},{4,6},{5,7},{6,4},{7,5},{8,10},{9,11},{10,... | collective-permute-start | bytes 442376 | tf_op jit(solution)/shard_map/ppermute | solution.py:86
  690.7 25.6 %collective-permute-start.121 = (bf16[3,2,2,144,256]{4,3,2,1,0:T(8,128)(2,1)S(1)}, bf16[3,2,2,144,256]{4,3,2,1,0:T(8,128)(2,1)S(1)}, u32[]{:S(2)}, u32[]{:S(2)}) collective-permute-start(bf16[3,2,2,144,256]{4,3,2,1,0:T(8,128)(2,1)S(1)} %dynamic-slice_bitcast_fusion.4), channel_id=1, source_target_pairs={{0,2},{1,3},{2,0},{3,1},{4,6},{5,7},{6,4},{7,5},{8,10},{9,11},{10,... | collective-permute-start | bytes 2654216 | tf_op jit(solution)/shard_map/ppermute | solution.py:86
  701.0 15.9 %collective-permute-start.116 = (bf16[3,2,2,144,256]{4,3,0,1,2:T(8,128)(2,1)S(1)}, bf16[3,2,2,144,256]{4,3,0,1,2:T(8,128)(2,1)S(1)}, u32[]{:S(2)}, u32[]{:S(2)}) collective-permute-start(bf16[3,2,2,144,256]{4,3,0,1,2:T(8,128)(2,1)S(1)} %dynamic-slice_bitcast_fusion.5), channel_id=1, source_target_pairs={{0,4},{1,5},{2,6},{3,7},{4,0},{5,1},{6,2},{7,3},{8,12},{9,13},{10,... | collective-permute-start | bytes 2654216 | tf_op jit(solution)/shard_map/ppermute | solution.py:86
  702.3 16.8 %collective-permute-start.100 = (bf16[1,1,1,144,512]{4,3,2,1,0:T(8,128)(2,1)S(1)}, bf16[1,1,1,144,512]{4,3,2,1,0:T(8,128)(2,1)S(1)}, u32[]{:S(2)}, u32[]{:S(2)}) collective-permute-start(bf16[1,1,1,144,512]{4,3,2,1,0:T(8,128)(2,1)S(1)} %get-tuple-element.163), channel_id=1, source_target_pairs={{0,2},{1,3},{2,0},{3,1},{4,6},{5,7},{6,4},{7,5},{8,10},{9,11},{10,... | collective-permute-start | bytes 442376 | tf_op jit(solution)/shard_map/ppermute | solution.py:86
  703.7 43.6 %collective-permute-start.113 = (bf16[1,2,1,144,512]{4,3,1,2,0:T(8,128)(2,1)S(1)}, bf16[1,2,1,144,512]{4,3,1,2,0:T(8,128)(2,1)S(1)}, u32[]{:S(2)}, u32[]{:S(2)}) collective-permute-start(bf16[1,2,1,144,512]{4,3,1,2,0:T(8,128)(2,1)S(1)} %get-tuple-element.155), channel_id=1, source_target_pairs={{0,1},{1,0},{2,3},{3,2},{4,5},{5,4},{6,7},{7,6},{8,9},{9,8},{10,11... | collective-permute-start | bytes 884744 | tf_op jit(solution)/shard_map/ppermute | solution.py:86
  716.6 10.1 %collective-permute-start.122 = (bf16[3,2,144,256]{3,2,1,0:T(8,128)(2,1)S(1)}, bf16[3,2,144,256]{3,2,1,0:T(8,128)(2,1)S(1)}, u32[]{:S(2)}, u32[]{:S(2)}) collective-permute-start(bf16[3,2,144,256]{3,2,1,0:T(8,128)(2,1)S(1)} %dynamic-slice_bitcast_fusion.11), channel_id=1, source_target_pairs={{0,8},{1,9},{2,10},{3,11},{4,12},{5,13},{6,14},{7,15},{8,0},{9,1},... | collective-permute-start | bytes 1327112 | tf_op jit(solution)/shard_map/ppermute | solution.py:86
  717.2 18.8 %collective-permute-start.117 = (bf16[3,2,144,256]{3,2,0,1:T(8,128)(2,1)S(1)}, bf16[3,2,144,256]{3,2,0,1:T(8,128)(2,1)S(1)}, u32[]{:S(2)}, u32[]{:S(2)}) collective-permute-start(bf16[3,2,144,256]{3,2,0,1:T(8,128)(2,1)S(1)} %dynamic-slice_bitcast_fusion.12), channel_id=1, source_target_pairs={{0,8},{1,9},{2,10},{3,11},{4,12},{5,13},{6,14},{7,15},{8,0},{9,1},... | collective-permute-start | bytes 1327112 | tf_op jit(solution)/shard_map/ppermute | solution.py:86
  (295 other events, 2027.0 us)

commit v2 on v1

v2 whole, which is shorter than its diff:
```python
import functools

import jax
import jax.numpy as jnp
from jax import lax
from jax.experimental import pallas as pl
from jax.experimental.pallas import tpu as pltpu
from jax.sharding import PartitionSpec as P

H_BIG = 36
W_BIG = 48
H_SMALL = 18
W_SMALL = 24
EPSILON = 1e-05
AXES = ("dp", "rows")
F32 = jnp.float32
BF16 = jnp.bfloat16
VMEM_BYTES = 56 * 1024 * 1024


def swapped(values, flip):
    count = lax.axis_size("dp") * lax.axis_size("rows")
    return lax.ppermute(values, AXES, [(i, i ^ flip) for i in range(count)])


def exchange_sum(values):
    count = lax.axis_size("dp") * lax.axis_size("rows")
    bits = count.bit_length() - 1
    assert count == 1 << bits
    values = values + swapped(values, 1)
    place = 1
    while place < bits:
        low = 1 << place
        if place + 1 < bits:
            high = low * 2
            values = (values + swapped(values, low)) + (
                swapped(values, high) + swapped(values, high + low)
            )
            place += 2
        else:
            values = values + swapped(values, low)
            place += 1
    return values


def gathered_sum(values):
    count = lax.axis_size("dp") * lax.axis_size("rows")
    spread = jnp.broadcast_to(values[None], (count,) + values.shape)
    return jnp.sum(lax.all_to_all(spread, AXES, 0, 0), axis=0)


def edges_swapped(edges):
    count = lax.axis_size("rows")
    above = lax.ppermute(edges[1], "rows", [(i, i + 1) for i in range(count - 1)])
    below = lax.ppermute(edges[0], "rows", [(i + 1, i) for i in range(count - 1)])
    return above, below


def core_bit():
    return lax.axis_index("rows") & 1


def scattered_sum(values, whole, swap_first=False):
    parts, height, breadth = values.shape
    dp_count = lax.axis_size("dp")
    row_count = lax.axis_size("rows")
    place = lax.axis_index("dp") * row_count + lax.axis_index("rows")
    first = 0 if whole else 1
    bits = (dp_count * row_count).bit_length() - 1
    row_bits = row_count.bit_length() - 1
    left = list(range(bits - 1, first - 1, -1))
    piece = values.reshape((parts,) + (2,) * len(left) + (height >> len(left), breadth))
    order = list(range(first, bits))
    if swap_first and bits > 2:
        low = 1 - first
        order[low], order[low + 1] = order[low + 1], order[low]
    for bit in order:
        axis = 1 + left.index(bit)
        mine = (place >> bit) & 1
        keep = lax.dynamic_index_in_dim(piece, mine, axis, keepdims=False)
        send = lax.dynamic_index_in_dim(piece, 1 - mine, axis, keepdims=False)
        got = swapped(send, 1 << bit)
        piece = (keep.astype(F32) + got.astype(F32)).astype(values.dtype)
        left.remove(bit)
    return piece


def rejoined(piece, whole):
    parts = piece.shape[0]
    row_count = lax.axis_size("rows")
    row_bits = row_count.bit_length() - 1
    first = 0 if whole else 1
    piece = piece.reshape((parts,) + (1,) * (row_bits - first) + piece.shape[-2:])

    def joined(piece, bit, axis):
        other = swapped(piece, 1 << bit)
        mine = (lax.axis_index("rows") >> bit) & 1
        lower = jnp.where(mine == 0, piece, other)
        upper = jnp.where(mine == 0, other, piece)
        return jnp.concatenate([lower, upper], axis=axis)

    for bit in range(row_bits - 1, first - 1, -1):
        piece = joined(piece, bit, row_bits - bit)
    piece = piece.reshape(parts, -1, piece.shape[-1])
    if not whole:
        piece = joined(piece, 0, 2)
    return piece.astype(F32)


def dot(left, right):
    return jnp.dot(left, right, preferred_element_type=F32)


def dot_turned(left, right):
    return lax.dot_general(left, right, (((1,), (1,)), ((), ())), preferred_element_type=F32)


def inside_row(limits, place, breadth, channels):
    return lax.broadcasted_iota(jnp.int32, (breadth, channels), 0) < limits[place]


def moments(totals, member, count):
    average = totals[2 * member : 2 * member + 1, :] / count
    variance = totals[2 * member + 1 : 2 * member + 2, :] / count - average * average
    return average, lax.rsqrt(variance + EPSILON)


def sigmoid(values):
    return 1.0 / (1.0 + jnp.exp(-values))


def silu_slope(values):
    logistic = sigmoid(values)
    return logistic * (1.0 + values * (1.0 - logistic))


def fold(values):
    return jnp.sum(values.reshape(-1, 8, values.shape[-1]), axis=0)


def shifted(values):
    breadth = values.shape[0]
    col = lax.broadcasted_iota(jnp.int32, values.shape, 0)
    before = jnp.where(col == 0, 0.0, pltpu.roll(values, 1, 0))
    after = jnp.where(col == breadth - 1, 0.0, pltpu.roll(values, breadth - 1, 0))
    return before, after


def put_three(ref, slot, row, values, flipped):
    channels = values.shape[1]
    before, after = shifted(values)
    if flipped:
        before, after = after, before
    ref[slot, row, :, 0:channels] = before.astype(BF16)
    ref[slot, row, :, channels : 2 * channels] = values.astype(BF16)
    ref[slot, row, :, 2 * channels :] = after.astype(BF16)


def each_row(slots, rows, body):
    def step(index, carry):
        body(index // rows, index % rows)
        return carry

    lax.fori_loop(0, slots * rows, step, 0)


def each_row_summed(slots, rows, channels, body):
    def step(index, carry):
        one, two = body(index // rows, index % rows)
        return carry[0] + fold(one), carry[1] + fold(two)

    zero = jnp.zeros((8, channels), F32)
    one, two = lax.fori_loop(0, slots * rows, step, (zero, zero))
    return jnp.sum(one, axis=0, keepdims=True), jnp.sum(two, axis=0, keepdims=True)


def put_pair(ref, pair, lead=()):
    ref[lead + (slice(0, 1), slice(None))] = pair[0]
    ref[lead + (slice(1, 2), slice(None))] = pair[1]


def add_taps(step, sums, lead, parts):
    slots = sums.shape[len(lead)]
    shape = sums.shape[len(lead) + 1 :]
    for slot in range(slots):
        part = parts(slot).reshape(shape)

        @pl.when(step == 0)
        def _():
            sums[lead + (slot,)] = part

        @pl.when(step > 0)
        def _():
            sums[lead + (slot,)] += part


def forward_taps(step, three, weight, sums, lead=()):
    rows, breadth, channels = sums.shape[-3:]

    def part(slot):
        window = three[slot, pl.ds(step, rows)].reshape(rows * breadth, -1)
        return dot(window, weight)

    add_taps(step, sums, lead, part)


def backward_taps(step, three, weight, sums):
    rows, breadth, channels = sums.shape[-3:]

    def part(slot):
        window = three[slot, pl.ds(2 - step, rows)].reshape(rows * breadth, -1)
        wide = window.shape[1] // 3
        total = None
        for tap in range(3):
            one = dot_turned(
                window[:, tap * wide : (tap + 1) * wide],
                weight[tap * channels : (tap + 1) * channels],
            )
            total = one if total is None else total + one
        return total

    add_taps(step, sums, (), part)


def conv_sums(sums, lead, limits, stats, edges, stat_lead):
    slots, rows, breadth, channels = sums.shape[-4:]

    def body(slot, row):
        values = sums[lead + (slot, row)]
        kept = jnp.where(
            inside_row(limits, slot * (rows + 2) + row + 1, breadth, channels), values, 0.0
        )
        return kept, kept * values

    put_pair(stats, each_row_summed(slots, rows, channels, body), stat_lead)
    for slot in range(slots):
        edges[stat_lead + (0, slot)] = sums[lead + (slot, 0)]
        edges[stat_lead + (1, slot)] = sums[lead + (slot, rows - 1)]


def first_kernel(limits, images, above, below, weight, sums, stats, edges, three):
    step = pl.program_id(0)
    slots, rows, breadth, channels = images.shape

    @pl.when(step == 0)
    def _():
        def put(slot, row, values):
            inside = inside_row(limits, slot * (rows + 2) + row, breadth, channels)
            put_three(three, slot, row, jnp.where(inside, values.astype(F32), 0.0), False)

        each_row(slots, rows, lambda slot, row: put(slot, row + 1, images[slot, row]))
        for slot in range(slots):
            put(slot, 0, above[slot])
            put(slot, rows + 1, below[slot])

    forward_taps(step, three, weight[...], sums)

    @pl.when(step == 2)
    def _():
        conv_sums(sums, (), limits, stats, edges, ())


def activation(values, inside, average, inverse, gain, shift):
    normed = gain * ((values - average) * inverse) + shift
    return jnp.where(inside, normed * sigmoid(normed), 0.0)


def second_kernel(
    limits, count, source, above, below, totals, gain, shift, weight, sums, stats, edges, hidden, three
):
    step = pl.program_id(0)
    slots, rows, breadth, channels = source.shape

    @pl.when(step == 0)
    def _():
        average, inverse = moments(totals, 0, count[0])

        def act(slot, row, values):
            inside = inside_row(limits, slot * (rows + 2) + row, breadth, channels)
            result = activation(values, inside, average, inverse, gain[...], shift[...])
            put_three(three, slot, row, result, False)
            return result

        def own(slot, row):
            hidden[slot, row] = act(slot, row + 1, source[slot, row]).astype(BF16)

        each_row(slots, rows, own)
        for slot in range(slots):
            act(slot, 0, above[slot])
            act(slot, rows + 1, below[slot])

    forward_taps(step, three, weight[...], sums)

    @pl.when(step == 2)
    def _():
        conv_sums(sums, (), limits, stats, edges, ())


def plain_sums(source, slots, rows, breadth, channels):
    def body(slot, row):
        values = source[pl.ds(pl.multiple_of((slot * rows + row) * breadth, breadth), breadth), :]
        return values, values * values

    return each_row_summed(slots, rows, channels, body)


def lower_kernel(
    limits, count, source, above, below, totals, gain, shift, down, shared, stats, lowered
):
    branch = pl.program_id(0)
    slots, rows, breadth, channels = source.shape

    @pl.when(branch == 0)
    def _():
        average, inverse = moments(totals, 0, count[0])

        def act(slot, row, values):
            inside = inside_row(limits, slot * (rows + 2) + row, breadth, channels)
            result = activation(values, inside, average, inverse, gain[...], shift[...])
            shared[slot, row] = result.astype(BF16)

        each_row(slots, rows, lambda slot, row: act(slot, row + 1, source[slot, row]))
        for slot in range(slots):
            act(slot, 0, above[slot])
            act(slot, rows + 1, below[slot])

    part = rows * breadth
    for slot in range(slots):
        lowered[slot * part : (slot + 1) * part, :] = dot(
            shared[slot, 1 : rows + 1].reshape(part, channels), down[0]
        )
    put_pair(stats, plain_sums(lowered, slots, rows, breadth, channels), (0,))


def raise_kernel(
    limits, count, shared, down, up, totals, gain, shift, squeezed, stats, wide, raised
):
    slots, tall, breadth, channels = shared.shape
    rows = tall - 2
    narrow = down.shape[2]
    wide[...] = dot(shared[...].reshape(slots * tall * breadth, channels), down[0])
    average, inverse = moments(totals[0], 0, count[0])

    def act(slot, row):
        inside = inside_row(limits, slot * tall + row, breadth, narrow)
        values = wide[pl.ds(pl.multiple_of((slot * tall + row) * breadth, breadth), breadth), :]
        result = activation(values, inside, average, inverse, gain[0], shift[0])
        squeezed[0, slot, row] = result.astype(BF16)

    each_row(slots, tall, act)
    part = rows * breadth
    for slot in range(slots):
        raised[slot * part : (slot + 1) * part, :] = dot(
            squeezed[0, slot, 1 : rows + 1].reshape(part, narrow), up[0]
        )
    put_pair(stats, plain_sums(raised, slots, rows, breadth, channels), (0,))


def task_kernel(
    limits, count, squeezed, up, shared, totals, gain, shift, weight, sums, stats, edges, gated, wide, three
):
    step = pl.program_id(1)
    slots, tall, breadth, channels = shared.shape
    rows = tall - 2

    @pl.when(step == 0)
    def _():
        wide[...] = dot(squeezed[0].reshape(slots * tall * breadth, -1), up[0])
        average, inverse = moments(totals[0], 0, count[0])

        def gate(slot, row):
            values = wide[pl.ds(pl.multiple_of((slot * tall + row) * breadth, breadth), breadth), :]
            normed = gain[0] * ((values - average) * inverse) + shift[0]
            result = sigmoid(normed) * shared[slot, row].astype(F32)
            put_three(three, slot, row, result, False)
            return result

        def own(slot, row):
            gated[0, slot, row] = gate(slot, row + 1).astype(BF16)

        each_row(slots, rows, own)
        for slot in range(slots):
            gate(slot, 0)
            gate(slot, rows + 1)

    forward_taps(step, three, weight[0], sums, (0,))

    @pl.when(step == 2)
    def _():
        conv_sums(sums, (0,), limits, stats, edges, (0,))


def pool_kernel(
    limits, count, source, cotangent, totals, gain, shift, maps, slope, stats, edges, spread, pairs
):
    slots, rows, breadth, channels = source.shape[1:]
    average, inverse = moments(totals[0], 0, count[0])
    half = breadth // 2
    groups = channels // 128

    def body(slot, pooled):
        block = cotangent[0, slot, pooled].astype(F32) * 0.25
        for group in range(groups):
            lanes = block[:, group * 128 : (group + 1) * 128]
            spread[group, pl.ds(0, half, stride=2), :] = lanes
            spread[group, pl.ds(1, half, stride=2), :] = lanes
        wide = jnp.concatenate([spread[group] for group in range(groups)], axis=1)
        one = two = total = None
        for parity in range(2):
            row = 2 * pooled + parity
            inside = inside_row(limits, slot * (rows + 2) + row + 1, breadth, channels)
            centred = (source[0, slot, row] - average) * inverse
            normed = gain[0] * centred + shift[0]
            logistic = sigmoid(normed)
            active = jnp.where(inside, normed * logistic, 0.0)
            grad = wide * (logistic * (1.0 + normed * (1.0 - logistic)))
            grad = jnp.where(inside, grad, 0.0)
            slope[0, slot, row] = grad
            along = grad * centred
            if parity == 0:
                one, two, total = grad, along, active
            else:
                one, two, total = one + grad, two + along, total + active
        for group in range(groups):
            pairs[group] = total[:, group * 128 : (group + 1) * 128]
            even = pairs[group, pl.ds(0, half, stride=2), :]
            odd = pairs[group, pl.ds(1, half, stride=2), :]
            lanes = slice(group * 128, (group + 1) * 128)
            maps[0, slot, pooled, :, lanes] = ((even + odd) * 0.25).astype(BF16)
        return one, two

    put_pair(stats, each_row_summed(slots, rows // 2, channels, body), (0,))
    for slot in range(slots):
        edges[0, 0, slot] = slope[0, slot, 0]
        edges[0, 1, slot] = slope[0, slot, rows - 1]


def norm_back(grad, values, inside, average, inverse, gain, back, count):
    centred = (values - average) * inverse
    correction = jnp.where(inside, (back[0:1] + centred * back[1:2]) / count, 0.0)
    return gain * inverse * (grad - correction)


def put_halves(ref, lead, slot, row, values):
    half = values.shape[1] // 2
    ref[lead + (0, slot, row)] = values[:, :half].astype(BF16)
    ref[lead + (1, slot, row)] = values[:, half:].astype(BF16)


def fill_back(
    limits, count, grads, grad_above, grad_below, source, above, below, totals, back, gain, three, halves, lead
):
    slots, rows, breadth, channels = source.shape[-4:]
    average, inverse = moments(totals, 0, count)

    def put(slot, row, grad, values):
        inside = inside_row(limits, slot * (rows + 2) + row, breadth, channels)
        result = norm_back(grad, values, inside, average, inverse, gain, back, count)
        if three is not None:
            put_three(three, slot, row, result, True)
        put_halves(halves, lead, slot, row, result)

    def own(slot, row):
        put(slot, row + 1, grads[lead + (slot, row)], source[lead + (slot, row)])

    each_row(slots, rows, own)
    for slot in range(slots):
        put(slot, 0, grad_above[lead + (slot,)], above[lead + (slot,)])
        put(slot, rows + 1, grad_below[lead + (slot,)], below[lead + (slot,)])


def gate_back_kernel(
    limits, count, grads, grad_above, grad_below, source, above, below, totals, back, gain, weight,
    squeezed, up, shared, up_totals, up_gain, up_shift,
    halves, incoming, shared_grad, stats, three, sums, raised,
):
    branch, step = pl.program_id(0), pl.program_id(1)
    slots, rows, breadth, channels = sums.shape

    @pl.when(step == 0)
    def _():
        fill_back(
            limits, count[0], grads, grad_above, grad_below, source, above, below,
            totals[0], back[0], gain[0], three, halves, (0,),
        )

    backward_taps(step, three, weight[0], sums)

    @pl.when(step == 2)
    def _():
        part = rows * breadth
        for slot in range(slots):
            raised[slot * part : (slot + 1) * part, :] = dot(
                squeezed[0, slot, 1 : rows + 1].reshape(part, -1), up[0]
            )
        average, inverse = moments(up_totals[0], 0, count[0])

        def body(slot, row):
            values = raised[pl.ds(pl.multiple_of((slot * rows + row) * breadth, breadth), breadth), :]
            centred = (values - average) * inverse
            attention = sigmoid(up_gain[0] * centred + up_shift[0])
            grad = sums[slot, row]
            result = grad * shared[slot, row + 1].astype(F32) * attention * (1.0 - attention)
            incoming[0, slot, row] = result
            onward = grad * attention

            @pl.when(branch == 0)
            def _():
                shared_grad[slot, row] = onward

            @pl.when(branch > 0)
            def _():
                shared_grad[slot, row] += onward

            return result, result * centred

        put_pair(stats, each_row_summed(slots, rows, channels, body), (0,))


def raise_back_kernel(
    limits, count, grads, squeezed, up, shared, down, up_totals, up_back, up_gain, down_totals, down_gain,
    down_shift, raised_grad, incoming, stats, wide, sums,
):
    slots, rows, breadth, channels = grads.shape[1:]
    part = rows * breadth
    for slot in range(slots):
        wide[slot * part : (slot + 1) * part, :] = dot(
            squeezed[0, slot, 1 : rows + 1].reshape(part, -1), up[0]
        )
    average, inverse = moments(up_totals[0], 0, count[0])

    def place(slot, row):
        return pl.ds(pl.multiple_of((slot * rows + row) * breadth, breadth), breadth)

    def back(slot, row):
        inside = inside_row(limits, slot * (rows + 2) + row + 1, breadth, channels)
        result = norm_back(
            grads[0, slot, row], wide[place(slot, row), :], inside, average, inverse, up_gain[0],
            up_back[0], count[0],
        )
        raised_grad[0, slot, row] = result.astype(BF16)

    each_row(slots, rows, back)
    for slot in range(slots):
        sums[slot * part : (slot + 1) * part, :] = dot_turned(
            raised_grad[0, slot].reshape(part, channels), up[0]
        )
        wide[slot * part : (slot + 1) * part, :] = dot(
            shared[slot, 1 : rows + 1].reshape(part, channels), down[0]
        )
    average2, inverse2 = moments(down_totals[0], 0, count[0])

    def body(slot, row):
        inside = inside_row(limits, slot * (rows + 2) + row + 1, breadth, channels)
        centred = (wide[place(slot, row), :] - average2) * inverse2
        normed = down_gain[0] * centred + down_shift[0]
        result = jnp.where(inside, sums[place(slot, row), :] * silu_slope(normed), 0.0)
        incoming[0, slot, row] = result
        return result, result * centred

    put_pair(stats, each_row_summed(slots, rows, channels, body), (0,))


def lower_back_kernel(
    limits, count, grads, shared, down, down_totals, down_back, down_gain, shared_grad, source, totals, gain,
    shift, lowered_grad, incoming, stats, edges, wide, sums,
):
    branch = pl.program_id(0)
    slots, rows, breadth, channels = source.shape
    part = rows * breadth
    for slot in range(slots):
        wide[slot * part : (slot + 1) * part, :] = dot(
            shared[slot, 1 : rows + 1].reshape(part, channels), down[0]
        )
    average, inverse = moments(down_totals[0], 0, count[0])

    def place(slot, row):
        return pl.ds(pl.multiple_of((slot * rows + row) * breadth, breadth), breadth)

    def back(slot, row):
        inside = inside_row(limits, slot * (rows + 2) + row + 1, breadth, channels)
        result = norm_back(
            grads[0, slot, row], wide[place(slot, row), :], inside, average, inverse, down_gain[0],
            down_back[0], count[0],
        )
        lowered_grad[0, slot, row] = result.astype(BF16)

    each_row(slots, rows, back)
    for slot in range(slots):
        span = slice(slot * part, (slot + 1) * part)
        term = dot_turned(lowered_grad[0, slot].reshape(part, -1), down[0])

        @pl.when(branch == 0)
        def _():
            sums[span, :] = term + shared_grad[slot].reshape(part, channels)

        @pl.when(branch > 0)
        def _():
            sums[span, :] += term

    @pl.when(branch == pl.num_programs(0) - 1)
    def _():
        average2, inverse2 = moments(totals, 0, count[0])

        def body(slot, row):
            inside = inside_row(limits, slot * (rows + 2) + row + 1, breadth, channels)
            centred = (source[slot, row] - average2) * inverse2
            normed = gain[...] * centred + shift[...]
            result = jnp.where(inside, sums[place(slot, row), :] * silu_slope(normed), 0.0)
            incoming[slot, row] = result
            return result, result * centred

        put_pair(stats, each_row_summed(slots, rows, channels, body))
        for slot in range(slots):
            edges[0, slot] = incoming[slot, 0]
            edges[1, slot] = incoming[slot, rows - 1]


def hidden_back_kernel(
    limits, count, grads, grad_above, grad_below, source, above, below, totals, back, gain, weight,
    first, first_totals, first_gain, first_shift, halves, incoming, stats, edges, three, sums,
):
    step = pl.program_id(0)
    slots, rows, breadth, channels = sums.shape

    @pl.when(step == 0)
    def _():
        fill_back(
            limits, count[0], grads, grad_above, grad_below, source, above, below,
            totals[...], back[...], gain[...], three, halves, (),
        )

    backward_taps(step, three, weight[...], sums)

    @pl.when(step == 2)
    def _():
        average, inverse = moments(first_totals, 0, count[0])

        def body(slot, row):
            inside = inside_row(limits, slot * (rows + 2) + row + 1, breadth, channels)
            centred = (first[slot, row] - average) * inverse
            normed = first_gain[...] * centred + first_shift[...]
            result = jnp.where(inside, sums[slot, row] * silu_slope(normed), 0.0)
            incoming[slot, row] = result
            return result, result * centred

        put_pair(stats, each_row_summed(slots, rows, channels, body))
        for slot in range(slots):
            edges[0, slot] = incoming[slot, 0]
            edges[1, slot] = incoming[slot, rows - 1]


def first_grad_kernel(
    limits, count, grads, grad_above, grad_below, source, above, below, totals, back, gain, halves
):
    fill_back(
        limits, count[0], grads, grad_above, grad_below, source, above, below,
        totals[...], back[...], gain[...], None, halves, (),
    )


def input_back_kernel(limits, halves, weight, out, three):
    step = pl.program_id(0)
    slots, rows, breadth, channels = out.shape

    @pl.when(step == 0)
    def _():
        def put(slot, row):
            values = jnp.concatenate([halves[0, slot, row], halves[1, slot, row]], axis=1)
            put_three(three, slot, row, values.astype(F32), True)

        each_row(slots, rows + 2, put)

    backward_taps(step, three, weight[...], out)

    @pl.when(step == 2)
    def _():
        def mask(slot, row):
            inside = inside_row(limits, slot * (rows + 2) + row + 1, breadth, channels)
            out[slot, row] = jnp.where(inside, out[slot, row], 0.0)

        each_row(slots, rows, mask)


def weight_grad_kernel(half, turned, turned_other, grads, grads_other, out, three):
    step = pl.program_id(0)
    slots, tall, breadth, channels = grads_other.shape
    rows = tall - 2

    @pl.when(step == 0)
    def _():
        def own(slot, row):
            put_three(three, slot, row, grads[0, slot, row].astype(F32), True)

        def other(slot, row):
            put_three(three, slots + slot, row, grads_other[slot, row].astype(F32), True)

        each_row(slots, tall, own)
        each_row(slots, tall, other)

    height = turned.shape[1]
    for tap in range(3):
        total = None
        for slot in range(2 * slots):
            left = turned[slot] if slot < slots else turned_other[slot - slots]
            window = three[slot, pl.ds(2 - step, rows), :, tap * channels : (tap + 1) * channels]
            one = dot(left, window.reshape(rows * breadth, channels))
            total = one if total is None else total + one
        out[tap * height : (tap + 1) * height, :] = total.astype(BF16)


def thin_grad_kernel(turned, right, out):
    slots = turned.shape[1]
    total = None
    for slot in range(slots):
        one = dot(turned[0, slot], right[0, slot])
        total = one if total is None else total + one
    out[0] = total.astype(BF16)


SCALARS = pl.BlockSpec(memory_space=pltpu.SMEM)


def fixed(shape):
    zeros = (0,) * len(shape)
    return pl.BlockSpec(tuple(shape), lambda *_: zeros)


def by_branch(shape):
    zeros = (0,) * (len(shape) - 1)
    return pl.BlockSpec((1,) + tuple(shape[1:]), lambda branch, *_: (branch,) + zeros)


def call(name, body, grid, inputs, outputs, scratch, flops, prefetch=0):
    total = sum(a.size * a.dtype.itemsize for a, _ in inputs)
    spec = dict(
        grid=grid,
        in_specs=[s for _, s in inputs[prefetch:]],
        out_specs=[s for _, _, s in outputs],
        scratch_shapes=scratch,
    )
    if prefetch:
        spec = dict(grid_spec=pltpu.PrefetchScalarGridSpec(num_scalar_prefetch=prefetch, **spec))
    return pl.pallas_call(
        body,
        name=name,
        out_shape=[jax.ShapeDtypeStruct(s, d) for s, d, _ in outputs],
        compiler_params=pltpu.CompilerParams(
            vmem_limit_bytes=VMEM_BYTES, dimension_semantics=("arbitrary",) * len(grid)
        ),
        cost_estimate=pl.CostEstimate(flops=flops, bytes_accessed=total, transcendentals=0),
        **spec,
    )(*[a for a, _ in inputs])


def local(
    images,
    size_ids,
    shared_conv,
    task_conv,
    task_down,
    task_up,
    shared_gain,
    shared_shift,
    down_gain,
    down_shift,
    up_gain,
    up_shift,
    conv_gain,
    conv_shift,
    cotangent,
):
    slots, rows, breadth, channels = images.shape
    tasks = task_conv.shape[0]
    tall = rows + 2
    part = rows * breadth
    heights_all = jnp.where(size_ids == 0, H_BIG, H_SMALL).astype(jnp.int32)
    breadths_all = jnp.where(size_ids == 0, W_BIG, W_SMALL).astype(jnp.int32)
    count = jnp.sum(heights_all * breadths_all).astype(F32).reshape(1)
    first_slot = lax.axis_index("dp") * slots
    heights = lax.dynamic_slice_in_dim(heights_all, first_slot, slots)
    breadths = lax.dynamic_slice_in_dim(breadths_all, first_slot, slots)
    row_place = lax.axis_index("rows") * rows + jnp.arange(-1, rows + 1, dtype=jnp.int32)
    within = (row_place[None, :] >= 0) & (row_place[None, :] < heights[:, None])
    limits = jnp.where(within, breadths[:, None], 0).astype(jnp.int32).reshape(-1)
    scalars = [(limits, SCALARS), (count, SCALARS)]

    map_shape = (slots, rows, breadth, channels)
    tall_shape = (slots, tall, breadth, channels)
    edge_shape = (2, slots, breadth, channels)
    half_shape = (2, slots, tall, breadth, channels // 2)
    pair_shape = (2, channels)
    conv_flops = 2 * slots * part * 9 * channels * channels
    thin_flops = conv_flops // 9

    def whole(a):
        return (a, fixed(a.shape))

    def branch(a):
        return (a, by_branch(a.shape))

    def out(shape, dtype):
        return (shape, dtype, fixed(shape))

    def out_branch(shape, dtype):
        shape = (tasks,) + tuple(shape)
        return (shape, dtype, by_branch(shape))

    def shared_weight(index):
        stacked = shared_conv.reshape(-1, channels)
        block = 3 * channels
        return (stacked, pl.BlockSpec((block, channels), lambda step: (3 * index + step, 0)))

    def task_weight():
        block = 3 * channels
        return (task_conv, pl.BlockSpec((1, block, channels), lambda t, step: (t, step, 0)))

    def pairs(totals):
        return totals.reshape(tasks, 2, channels)

    def triple(gains):
        return gains.reshape(tasks, 1, channels)

    three = pltpu.VMEM((slots, tall, breadth, 3 * channels), BF16)
    flat = pltpu.VMEM((slots * part, channels), F32)
    flat_tall = pltpu.VMEM((slots * tall * breadth, channels), F32)
    square = pltpu.VMEM(map_shape, F32)

    count_rows = lax.axis_size("rows")
    image_above = lax.ppermute(
        images[:, rows - 1], "rows", [(i, i + 1) for i in range(count_rows - 1)]
    )
    image_below = lax.ppermute(images[:, 0], "rows", [(i + 1, i) for i in range(count_rows - 1)])
    first_out, first_stats, first_edges = call(
        "first_conv",
        first_kernel,
        (3,),
        [scalars[0], whole(images), whole(image_above), whole(image_below), shared_weight(0)],
        [out(map_shape, F32), out(pair_shape, F32), out(edge_shape, F32)],
        [three],
        conv_flops,
    )
    first_above, first_below = edges_swapped(first_edges)
    first_totals = gathered_sum(first_stats)

    second_out, second_stats, second_edges, hidden = call(
        "second_conv",
        second_kernel,
        (3,),
        scalars
        + [
            whole(a)
            for a in (
                first_out, first_above, first_below, first_totals, shared_gain[0:1], shared_shift[0:1]
            )
        ]
        + [shared_weight(1)],
        [
            out(map_shape, F32),
            out(pair_shape, F32),
            out(edge_shape, F32),
            out(map_shape, BF16),
        ],
        [three],
        conv_flops,
    )
    second_above, second_below = edges_swapped(second_edges)
    second_totals = gathered_sum(second_stats)

    shared, down_stats = call(
        "lower",
        lower_kernel,
        (tasks,),
        scalars
        + [
            whole(a)
            for a in (
                second_out, second_above, second_below, second_totals, shared_gain[1:2], shared_shift[1:2]
            )
        ]
        + [branch(task_down)],
        [out(tall_shape, BF16), out_branch(pair_shape, F32)],
        [flat],
        3 * thin_flops,
    )
    down_totals = exchange_sum(down_stats.reshape(2 * tasks, channels))

    squeezed, up_stats = call(
        "raise",
        raise_kernel,
        (tasks,),
        scalars
        + [whole(shared), branch(task_down), branch(task_up), branch(pairs(down_totals))]
        + [branch(triple(down_gain)), branch(triple(down_shift))],
        [out_branch(tall_shape, BF16), out_branch(pair_shape, F32)],
        [flat_tall, flat],
        6 * thin_flops,
    )
    up_totals = exchange_sum(up_stats.reshape(2 * tasks, channels))

    conv_out, conv_stats, conv_edges, gated = call(
        "task_conv",
        task_kernel,
        (tasks, 3),
        scalars
        + [branch(squeezed), branch(task_up), whole(shared), branch(pairs(up_totals))]
        + [branch(triple(up_gain)), branch(triple(up_shift)), task_weight()],
        [
            out_branch(map_shape, F32),
            out_branch(pair_shape, F32),
            out_branch(edge_shape, F32),
            out_branch(map_shape, BF16),
        ],
        [flat_tall, three],
        tasks * conv_flops,
    )
    conv_above, conv_below = edges_swapped(jnp.moveaxis(conv_edges, 1, 0))
    conv_totals = exchange_sum(conv_stats.reshape(2 * tasks, channels))

    maps, conv_grad, conv_back_stats, conv_grad_edges = call(
        "pool",
        pool_kernel,
        (tasks,),
        scalars
        + [branch(conv_out), branch(cotangent), branch(pairs(conv_totals))]
        + [branch(triple(conv_gain)), branch(triple(conv_shift))],
        [
            out_branch((slots, rows // 2, breadth // 2, channels), BF16),
            out_branch(map_shape, F32),
            out_branch(pair_shape, F32),
            out_branch(edge_shape, F32),
        ],
        [pltpu.VMEM((channels // 128, breadth, 128), F32)] * 2,
        thin_flops,
    )
    conv_grad_above, conv_grad_below = edges_swapped(jnp.moveaxis(conv_grad_edges, 1, 0))
    conv_back = exchange_sum(conv_back_stats.reshape(2 * tasks, channels))

    conv_halves, up_grad_in, shared_grad, up_back_stats = call(
        "gate_back",
        gate_back_kernel,
        (tasks, 3),
        scalars
        + [
            branch(a)
            for a in (
                conv_grad, conv_grad_above, conv_grad_below, conv_out, conv_above, conv_below,
                pairs(conv_totals), pairs(conv_back), triple(conv_gain),
            )
        ]
        + [task_weight(), branch(squeezed), branch(task_up), whole(shared)]
        + [branch(pairs(up_totals)), branch(triple(up_gain)), branch(triple(up_shift))],
        [
            out_branch(half_shape, BF16),
            out_branch(map_shape, F32),
            out(map_shape, F32),
            out_branch(pair_shape, F32),
        ],
        [three, square, flat],
        tasks * conv_flops,
    )
    up_back = exchange_sum(up_back_stats.reshape(2 * tasks, channels))

    raised_grad, down_grad_in, down_back_stats = call(
        "raise_back",
        raise_back_kernel,
        (tasks,),
        scalars
        + [branch(up_grad_in), branch(squeezed), branch(task_up), whole(shared), branch(task_down)]
        + [
            branch(a)
            for a in (
                pairs(up_totals), pairs(up_back), triple(up_gain), pairs(down_totals), triple(down_gain),
                triple(down_shift),
            )
        ],
        [
            out_branch(map_shape, BF16),
            out_branch(map_shape, F32),
            out_branch(pair_shape, F32),
        ],
        [flat, flat],
        9 * thin_flops,
    )
    down_back = exchange_sum(down_back_stats.reshape(2 * tasks, channels))

    lowered_grad, second_grad, second_back_stats, second_grad_edges = call(
        "lower_back",
        lower_back_kernel,
        (tasks,),
        scalars
        + [branch(down_grad_in), whole(shared), branch(task_down)]
        + [branch(pairs(down_totals)), branch(pairs(down_back)), branch(triple(down_gain))]
        + [whole(a) for a in (shared_grad, second_out, second_totals)]
        + [whole(shared_gain[1:2]), whole(shared_shift[1:2])],
        [
            out_branch(map_shape, BF16),
            out(map_shape, F32),
            out(pair_shape, F32),
            out(edge_shape, F32),
        ],
        [flat, flat],
        6 * thin_flops,
    )
    second_grad_above, second_grad_below = edges_swapped(second_grad_edges)
    second_back = gathered_sum(second_back_stats)

    second_halves, first_grad, first_back_stats, first_grad_edges = call(
        "hidden_back",
        hidden_back_kernel,
        (3,),
        scalars
        + [
            whole(a)
            for a in (
                second_grad, second_grad_above, second_grad_below, second_out, second_above, second_below,
                second_totals, second_back, shared_gain[1:2],
            )
        ]
        + [shared_weight(1)]
        + [whole(a) for a in (first_out, first_totals, shared_gain[0:1], shared_shift[0:1])],
        [
            out(half_shape, BF16),
            out(map_shape, F32),
            out(pair_shape, F32),
            out(edge_shape, F32),
        ],
        [three, square],
        conv_flops,
    )
    first_grad_above, first_grad_below = edges_swapped(first_grad_edges)
    first_back = gathered_sum(first_back_stats)

    (first_halves,) = call(
        "first_grad",
        first_grad_kernel,
        (1,),
        scalars
        + [
            whole(a)
            for a in (
                first_grad, first_grad_above, first_grad_below, first_out, first_above, first_below,
                first_totals, first_back, shared_gain[0:1],
            )
        ],
        [out(half_shape, BF16)],
        [],
        0,
    )

    (input_grad,) = call(
        "input_back",
        input_back_kernel,
        (3,),
        [scalars[0], whole(first_halves), shared_weight(0)],
        [out(map_shape, F32)],
        [three],
        conv_flops,
    )

    core = core_bit()

    def turned(values):
        lead = values.shape[:-3]
        return jnp.swapaxes(values.reshape(lead + (part, values.shape[-1])), -1, -2)

    def wide_grad(source, source_other, halves):
        other = swapped(lax.dynamic_index_in_dim(halves, 1 - core, 0, keepdims=False), 1)
        wide = half_shape[1:]
        return call(
            "weight_grad",
            weight_grad_kernel,
            (3,),
            [
                (core.reshape(1), None),
                whole_p(source),
                whole_p(source_other),
                (halves, pl.BlockSpec((1,) + wide, lambda step, c: (c[0], 0, 0, 0, 0))),
                whole_p(other),
            ],
            [((9 * channels, channels // 2), BF16, pl.BlockSpec((3 * channels, channels // 2), lambda step, c: (step, 0)))],
            [pltpu.VMEM((2 * slots, tall, breadth, 3 * channels // 2), BF16)],
            conv_flops,
            prefetch=1,
        )[0]

    def whole_p(a):
        return (a, fixed(a.shape))

    def thin_grads(left, right):
        return call(
            "thin_grad",
            thin_grad_kernel,
            (tasks,),
            [branch(left), branch(right)],
            [out_branch((channels, channels), BF16)],
            [],
            3 * thin_flops,
        )[0]

    inside = jnp.arange(breadth)[None, None, :] < limits.reshape(slots, tall)[:, 1:-1, None]
    masked = jnp.where(inside[..., None], images, jnp.zeros_like(images))
    masked_turned = turned(masked)
    hidden_turned = turned(hidden)
    gated_turned = turned(gated)
    masked_other = swapped(masked_turned, 1)
    hidden_other = swapped(hidden_turned, 1)
    gated_other = swapped(gated_turned, 1)

    task_parts = [
        scattered_sum(
            wide_grad(gated_turned[t], gated_other[t], conv_halves[t])[None], False, t % 2 == 1
        )
        for t in range(tasks)
    ]
    down_grads = thin_grads(
        jnp.broadcast_to(turned(shared[:, 1:-1])[None], (tasks, slots, channels, part)),
        lowered_grad.reshape(tasks, slots, part, channels),
    )
    up_grads = thin_grads(
        turned(raised_grad), squeezed[:, :, 1:-1].reshape(tasks, slots, part, channels)
    )
    thin_parts = scattered_sum(jnp.concatenate([down_grads, up_grads]), True)
    second_part = scattered_sum(wide_grad(hidden_turned, hidden_other, second_halves)[None], False, True)
    first_part = scattered_sum(wide_grad(masked_turned, masked_other, first_halves)[None], False)
    wide_sums = rejoined(jnp.concatenate([first_part, second_part] + task_parts), False)
    thin_sums = rejoined(thin_parts, True)

    return (
        maps,
        input_grad,
        wide_sums[:2],
        wide_sums[2:],
        thin_sums[:tasks],
        thin_sums[tasks:].transpose(0, 2, 1),
        jnp.stack([first_back[1], second_back[1]]),
        jnp.stack([first_back[0], second_back[0]]),
        down_back[1::2],
        down_back[0::2],
        up_back[1::2],
        up_back[0::2],
        conv_back[1::2],
        conv_back[0::2],
    )


def solution(mesh):
    placed = (P("dp", "rows", None, None),) + (P(),) * 13 + (P(None, "dp", "rows", None, None),)
    return jax.shard_map(
        local,
        mesh=mesh,
        in_specs=placed,
        out_specs=(
            P(None, "dp", "rows", None, None),
            P("dp", "rows", None, None),
            P(None, "dp", None),
            P(None, "dp", None),
            P(None, "dp", None),
            P(None, None, "dp"),
        )
        + (P(),) * 8,
        check_vma=False,
    )
```

time: 767 us -> 649 us (0.85)
  Pallas kernels: 0 us -> 247 us
  matrix products: 149 us -> 0 us
  other arithmetic: 94.8 us -> 23.3 us
  local copies, waits for them, and re-layouts: 162 us -> 97.2 us
  starting transfers between devices: 182 us -> 142 us
  waiting for transfers between devices: 165 us -> 126 us
    pallas_call x0 -> x19, Pallas kernels: none -> 247 us  [call(): pl.pallas_call(body, name=name, out_shape=[jax.ShapeDtypeStruct(s, d) for...]
    dot_general x33 -> x0, matrix products: 149 us -> none  [the longest x5 46.6 us: conv_back(): lax.dot_general(columns, grad_out.reshape(-1, out_channels), (((0,), (0,)...]
    ppermute x118 -> x79, starting transfers between devices: 142 us -> 85.5 us  [swapped(): return lax.ppermute(values, AXES, [(i, i ^ flip) for i in range(count)])]
    ppermute x118 -> x79, waiting for transfers between devices: 158 us -> 117 us  [swapped(): return lax.ppermute(values, AXES, [(i, i ^ flip) for i in range(count)])]
    unnamed x478 -> x63, local copies, waits for them, and re-layouts: 48.8 us -> 9.44 us
    transpose x5 -> x0, local copies, waits for them, and re-layouts: 33.3 us -> none  [conv_back(): turned = weight.reshape(9, channels, out_channels).transpose(0, 2, 1).res...]
    all_to_all x0 -> x4, starting transfers between devices: none -> 30.3 us  [gathered_sum(): return jnp.sum(lax.all_to_all(spread, AXES, 0, 0), axis=0)]
    convert_element_type x57 -> x21, other arithmetic: 38.4 us -> 12.5 us  [the longest x19 10.2 us: scattered_sum(): piece = (keep.astype(F32) + got.astype(F32)).astype(values.dtype)]
  transfers between devices with their start and end apart: 138 -> 97, of which waited for: 62 -> 38; matrix products, arithmetic and copies ran while one was open for 29% -> 16% of each run, Pallas kernels for 0% -> 25%
where the time goes in v2:
time: 649 us; the launch traced here: 638 us
  Pallas kernels  247 us (38%)
  starting transfers between devices  142 us (22%)
  waiting for transfers between devices  126 us (19%)
  local copies, waits for them, and re-layouts  97.2 us (15%)
  other arithmetic  23.3 us (4%)
    pallas_call x19, Pallas kernels, call(): pl.pallas_call(body, name=name, out_shape=[jax.ShapeDtypeStruct(s, d) for...  247 us
    ppermute x79, waiting for transfers between devices, swapped(): return lax.ppermute(values, AXES, [(i, i ^ flip) for i in range(count)])  117 us
    ppermute x79, starting transfers between devices, swapped(): return lax.ppermute(values, AXES, [(i, i ^ flip) for i in range(count)])  85.5 us
    all_to_all x4, starting transfers between devices, gathered_sum(): return jnp.sum(lax.all_to_all(spread, AXES, 0, 0), axis=0)  30.3 us
    ppermute x6, starting transfers between devices, edges_swapped(): lax.ppermute(edges[1], 'rows', [(i, i + 1) for i in range(count - 1)])  14.6 us
    reshape x5, local copies, waits for them, and re-layouts, turned(): return jnp.swapaxes(values.reshape(lead + (part, values.shape[-1])), -1, -2)  13.8 us
  transfers between devices with their start and end apart: 97, of which 38 were waited for; matrix products, arithmetic and copies ran while one was open for 16% of the time, Pallas kernels for 25%

profile of v2, /device:TPU:0, one launch (start us, length us, event | category | flops | bytes accessed | tf_op | source)
XLA Modules:
  0.0 638.5 jit_solution(7787323720947089327)
XLA Ops:
  9.9 10.8 %first_conv.1 = (f32[2,10,48,512]{3,2,1,0:T(8,128)}, f32[2,512]{1,0:T(2,128)}, f32[2,2,48,512]{3,2,1,0:T(8,128)}) custom-call(s32[24]{0:T(128)} %select_n.163.limits, bf16[2,10,48,512]{3,2,1,0:T(8,128)(2,1)} %images.1, bf16[2,48,512]{2,1,0:T(8,128)(2,1)} %copy-done.28, bf16[2,48,512]{2,1,0:T(8,128)(2,1)} %copy-done.29, bf16[9216,512]{1,0:T(8,128)(2,1)} %bitcast.268), custom_call_target="tpu_custom_call" | custom-call | flops 4529848320 | bytes 10616928 | tf_op jit(solution)/shard_map/first_conv/pallas_call | solution.py:744
  22.1 8.0 %all-to-all-start = ((f32[32,2,512]{2,1,0:T(2,128)}), f32[32,2,512]{2,1,0:T(2,128)S(1)}, u32[]{:S(2)}, u32[]{:S(2)}) async-start(f32[32,2,512]{2,1,0:T(2,128)} %broadcast_in_dim.80), calls=%async_computation | async-start | bytes 262144 | tf_op jit(solution)/shard_map/all_to_all | solution.py:49
  35.3 3.1 all-to-all-done
  39.8 12.3 %second_conv.1 = (f32[2,10,48,512]{3,2,1,0:T(8,128)}, f32[2,512]{1,0:T(2,128)}, f32[2,2,48,512]{3,2,1,0:T(8,128)}, bf16[2,10,48,512]{3,2,1,0:T(8,128)(2,1)}) custom-call(s32[24]{0:T(128)} %select_n.163.limits, f32[1]{0:T(128)} %bitcast.count, f32[2,10,48,512]{3,2,1,0:T(8,128)} %get-tuple-element.48.source.first, f32[2,48,512]{2,1,0:T(8,128)} %copy-done.11, ...), custom_call_target="tpu_custom_call" | custom-call | flops 4529848320 | bytes 11804772 | tf_op jit(solution)/shard_map/second_conv/pallas_call | solution.py:744
  53.5 7.1 %all-to-all-start.1 = ((f32[32,2,512]{2,1,0:T(2,128)}), f32[32,2,512]{2,1,0:T(2,128)S(1)}, u32[]{:S(2)}, u32[]{:S(2)}) async-start(f32[32,2,512]{2,1,0:T(2,128)} %broadcast_in_dim.81), calls=%async_computation.1 | async-start | bytes 262144 | tf_op jit(solution)/shard_map/all_to_all | solution.py:49
  65.1 3.7 all-to-all-done.1
  70.3 8.1 %lower.1 = (bf16[2,12,48,512]{3,2,1,0:T(8,128)(2,1)}, f32[3,2,512]{2,1,0:T(2,128)}) custom-call(s32[24]{0:T(128)} %select_n.163.limits, f32[1]{0:T(128)} %bitcast.count, f32[2,10,48,512]{3,2,1,0:T(8,128)} %get-tuple-element.51.source, f32[2,48,512]{2,1,0:T(8,128)} %copy-done.26, f32[2,48,512]{2,1,0:T(8,128)} %copy-done.27, f32[2,512]{1,0:T(2,128)} %reduce_sum.47.totals, ...), custom_call_target="tpu_custom_call" | custom-call | flops 1509949440 | bytes 3940452 | tf_op jit(solution)/shard_map/lower/pallas_call | solution.py:744
  79.1 3.0 collective-permute-start.6
  97.6 13.8 %raise.1 = (bf16[3,2,12,48,512]{4,3,2,1,0:T(8,128)(2,1)}, f32[3,2,512]{2,1,0:T(2,128)}) custom-call(s32[24]{0:T(128)} %select_n.163.limits, f32[1]{0:T(128)} %bitcast.count, bf16[2,12,48,512]{3,2,1,0:T(8,128)(2,1)} %get-tuple-element.54.shared, bf16[3,512,512]{2,1,0:T(8,128)(2,1)} %down.7, bf16[3,512,512]{2,1,0:T(8,128)(2,1)} %up.7, ...), custom_call_target="tpu_custom_call" | custom-call | flops 3019898880 | bytes 4350052 | tf_op jit(solution)/shard_map/raise/pallas_call | solution.py:744
  127.1 32.0 %task_conv.1 = (f32[3,2,10,48,512]{4,3,2,1,0:T(8,128)}, f32[3,2,512]{2,1,0:T(2,128)}, f32[3,2,2,48,512]{4,3,2,1,0:T(8,128)}, bf16[3,2,10,48,512]{4,3,2,1,0:T(8,128)(2,1)}) custom-call(s32[24]{0:T(128)} %select_n.163.limits, f32[1]{0:T(128)} %bitcast.count, bf16[3,2,12,48,512]{4,3,2,1,0:T(8,128)(2,1)} %get-tuple-element.56.squeezed, bf16[3,512,512]{2,1,0:T(8,128)(2,1)} %up.7, ...), custom_call_target="tpu_custom_call" | custom-call | flops 13589544960 | bytes 20471908 | tf_op jit(solution)/shard_map/task_conv/pallas_call | solution.py:744
  174.7 9.6 %pool.1 = (bf16[3,2,5,24,512]{4,3,2,1,0:T(8,128)(2,1)}, f32[3,2,10,48,512]{4,3,2,1,0:T(8,128)}, f32[3,2,512]{2,1,0:T(2,128)}, f32[3,2,2,48,512]{4,3,2,1,0:T(8,128)}) custom-call(s32[24]{0:T(128)} %select_n.163.limits, f32[1]{0:T(128)} %bitcast.count, f32[3,2,10,48,512]{4,3,2,1,0:T(8,128)} %get-tuple-element.58.source, bf16[3,2,5,24,512]{4,3,2,1,0:T(8,128)(2,1)} %cotangent.1, ...), custom_call_target="tpu_custom_call" | custom-call | flops 503316480 | bytes 6660196 | tf_op jit(solution)/shard_map/pool/pallas_call | solution.py:744
  193.9 4.9 collective-permute-start.27
  202.3 3.8 collective-permute-done.37
  211.3 37.9 %gate_back.1 = (bf16[3,2,2,12,48,256]{5,4,3,2,1,0:T(8,128)(2,1)}, f32[3,2,10,48,512]{4,3,2,1,0:T(8,128)}, f32[2,10,48,512]{3,2,1,0:T(8,128)}, f32[3,2,512]{2,1,0:T(2,128)}) custom-call(s32[24]{0:T(128)} %select_n.163.limits, f32[1]{0:T(128)} %bitcast.count, f32[3,2,10,48,512]{4,3,2,1,0:T(8,128)} %get-tuple-element.61.grads, ...), custom_call_target="tpu_custom_call" | custom-call | flops 13589544960 | bytes 34658404 | tf_op jit(solution)/shard_map/gate_back/pallas_call | solution.py:744
  256.6 3.7 slice.175
  260.3 3.2 copy.143
  265.1 3.3 collective-permute-start.41
  277.4 4.6 fusion.32
  282.6 18.7 %raise_back.1 = (bf16[3,2,10,48,512]{4,3,2,1,0:T(8,128)(2,1)}, f32[3,2,10,48,512]{4,3,2,1,0:T(8,128)}, f32[3,2,512]{2,1,0:T(2,128)}) custom-call(s32[24]{0:T(128)} %select_n.163.limits, f32[1]{0:T(128)} %bitcast.count, f32[3,2,10,48,512]{4,3,2,1,0:T(8,128)} %get-tuple-element.65.grads, bf16[3,2,12,48,512]{4,3,2,1,0:T(8,128)(2,1)} %get-tuple-element.56.squeezed, ...), custom_call_target="tpu_custom_call" | custom-call | flops 4529848320 | bytes 13817956 | tf_op jit(solution)/shard_map/raise_back/pallas_call | solution.py:744
  307.6 4.6 copy.154
  315.9 5.6 thin_grad.3
  322.1 15.2 %lower_back.1 = (bf16[3,2,10,48,512]{4,3,2,1,0:T(8,128)(2,1)}, f32[2,10,48,512]{3,2,1,0:T(8,128)}, f32[2,512]{1,0:T(2,128)}, f32[2,2,48,512]{3,2,1,0:T(8,128)}) custom-call(s32[24]{0:T(128)} %select_n.163.limits, f32[1]{0:T(128)} %bitcast.count, f32[3,2,10,48,512]{4,3,2,1,0:T(8,128)} %get-tuple-element.67.grads, ...), custom_call_target="tpu_custom_call" | custom-call | flops 3019898880 | bytes 12621924 | tf_op jit(solution)/shard_map/lower_back/pallas_call | solution.py:744
  343.8 7.2 %all-to-all-start.2 = ((f32[32,2,512]{2,1,0:T(2,128)}), f32[32,2,512]{2,1,0:T(2,128)S(1)}, u32[]{:S(2)}, u32[]{:S(2)}) async-start(f32[32,2,512]{2,1,0:T(2,128)} %broadcast_in_dim.82), calls=%async_computation.2 | async-start | bytes 262144 | tf_op jit(solution)/shard_map/all_to_all | solution.py:49
  352.9 5.7 thin_grad.2
  361.0 14.7 %hidden_back.1 = (bf16[2,2,12,48,256]{4,3,2,1,0:T(8,128)(2,1)}, f32[2,10,48,512]{3,2,1,0:T(8,128)}, f32[2,512]{1,0:T(2,128)}, f32[2,2,48,512]{3,2,1,0:T(8,128)}) custom-call(s32[24]{0:T(128)} %select_n.163.limits, f32[1]{0:T(128)} %bitcast.count, f32[2,10,48,512]{3,2,1,0:T(8,128)} %get-tuple-element.70.grads, ...), custom_call_target="tpu_custom_call" | custom-call | flops 4529848320 | bytes 16140388 | tf_op jit(solution)/shard_map/hidden_back/pallas_call | solution.py:744
  383.9 8.0 %all-to-all-start.3 = ((f32[32,2,512]{2,1,0:T(2,128)}), f32[32,2,512]{2,1,0:T(2,128)S(1)}, u32[]{:S(2)}, u32[]{:S(2)}) async-start(f32[32,2,512]{2,1,0:T(2,128)} %broadcast_in_dim.83), calls=%async_computation.3 | async-start | bytes 262144 | tf_op jit(solution)/shard_map/all_to_all | solution.py:49
  401.4 4.5 first_grad.1.halves.grads
  407.3 9.4 %weight_grad.6 = bf16[4608,256]{1,0:T(8,128)(2,1)} custom-call(s32[1]{0:T(128)} %bitcast.18.half, bf16[2,512,480]{2,1,0:T(8,128)(2,1)} %bitcast.262, bf16[2,512,480]{2,1,0:T(8,128)(2,1)} %copy.140.turned_other, bf16[2,2,12,48,256]{4,3,2,1,0:T(8,128)(2,1)} %get-tuple-element.77.grads, bf16[2,12,48,256]{3,2,1,0:T(8,128)(2,1)} %collective-permute-done.63.grads_other), custom_call_target="tpu_custom_call" | custom-call | flops 4529848320 | bytes 3735556 | tf_op jit(solution)/shard_map/weight_grad/pallas_call | solution.py:744
  420.6 9.4 %weight_grad.5 = bf16[4608,256]{1,0:T(8,128)(2,1)} custom-call(s32[1]{0:T(128)} %bitcast.18.half, bf16[2,512,480]{2,1,0:T(8,128)(2,1)} %bitcast.261, bf16[2,512,480]{2,1,0:T(8,128)(2,1)} %copy.135.turned_other, bf16[2,2,12,48,256]{4,3,2,1,0:T(8,128)(2,1)} %first_grad.1.halves.grads, bf16[2,12,48,256]{3,2,1,0:T(8,128)(2,1)} %collective-permute-done.57.grads_other), custom_call_target="tpu_custom_call" | custom-call | flops 4529848320 | bytes 3735556 | tf_op jit(solution)/shard_map/weight_grad/pallas_call | solution.py:744
  437.6 10.4 %collective-permute-done.64 = bf16[1,2,2,2,288,256]{5,4,1,2,3,0:T(8,128)(2,1)S(1)} collective-permute-done((bf16[1,2,2,2,288,256]{5,4,1,2,3,0:T(8,128)(2,1)}, bf16[1,2,2,2,288,256]{5,4,1,2,3,0:T(8,128)(2,1)S(1)}, u32[]{:S(2)}, u32[]{:S(2)}) %collective-permute-start.64) | collective-permute-done | bytes 1179680 | tf_op jit(solution)/shard_map/ppermute | solution.py:23
  451.3 3.4 fusion.33
  456.8 9.4 %weight_grad.7 = bf16[4608,256]{1,0:T(8,128)(2,1)} custom-call(s32[1]{0:T(128)} %bitcast.18.half, bf16[2,512,480]{2,1,0:T(8,128)(2,1)} %get-tuple-element.90.turned, bf16[2,512,480]{2,1,0:T(8,128)(2,1)} %bitcast.264, bf16[2,2,12,48,256]{4,3,2,1,0:T(8,128)(2,1)} %get-tuple-element.83.grads, bf16[2,12,48,256]{3,2,1,0:T(8,128)(2,1)} %collective-permute-done.69.grads_other), custom_call_target="tpu_custom_call" | custom-call | flops 4529848320 | bytes 3735556 | tf_op jit(solution)/shard_map/weight_grad/pallas_call | solution.py:744
  472.7 9.4 %weight_grad.8 = bf16[4608,256]{1,0:T(8,128)(2,1)} custom-call(s32[1]{0:T(128)} %bitcast.18.half, bf16[2,512,480]{2,1,0:T(8,128)(2,1)} %get-tuple-element.89.turned, bf16[2,512,480]{2,1,0:T(8,128)(2,1)} %bitcast.265, bf16[2,2,12,48,256]{4,3,2,1,0:T(8,128)(2,1)} %get-tuple-element.84.grads, bf16[2,12,48,256]{3,2,1,0:T(8,128)(2,1)} %collective-permute-done.74.grads_other), custom_call_target="tpu_custom_call" | custom-call | flops 4529848320 | bytes 3735556 | tf_op jit(solution)/shard_map/weight_grad/pallas_call | solution.py:744
  488.1 9.6 %weight_grad.9 = bf16[4608,256]{1,0:T(8,128)(2,1)} custom-call(s32[1]{0:T(128)} %bitcast.18.half, bf16[2,512,480]{2,1,0:T(8,128)(2,1)} %get-tuple-element.88.turned, bf16[2,512,480]{2,1,0:T(8,128)(2,1)} %bitcast.263, bf16[2,2,12,48,256]{4,3,2,1,0:T(8,128)(2,1)} %get-tuple-element.85.grads, bf16[2,12,48,256]{3,2,1,0:T(8,128)(2,1)} %collective-permute-done.79.grads_other), custom_call_target="tpu_custom_call" | custom-call | flops 4529848320 | bytes 3735556 | tf_op jit(solution)/shard_map/weight_grad/pallas_call | solution.py:744
  508.8 20.3 %collective-permute-done.59 = bf16[1,2,2,288,256]{4,3,1,2,0:T(8,128)(2,1)S(1)} collective-permute-done((bf16[1,2,2,288,256]{4,3,1,2,0:T(8,128)(2,1)S(1)}, bf16[1,2,2,288,256]{4,3,1,2,0:T(8,128)(2,1)S(1)}, u32[]{:S(2)}, u32[]{:S(2)}) %collective-permute-start.59) | collective-permute-done | bytes 589856 | tf_op jit(solution)/shard_map/ppermute | solution.py:23
  530.0 4.8 collective-permute-done.88
  535.7 6.4 %collective-permute-done.60 = bf16[1,2,288,256]{3,2,1,0:T(8,128)(2,1)S(1)} collective-permute-done((bf16[1,2,288,256]{3,2,1,0:T(8,128)(2,1)S(1)}, bf16[1,2,288,256]{3,2,1,0:T(8,128)(2,1)S(1)}, u32[]{:S(2)}, u32[]{:S(2)}) %collective-permute-start.60) | collective-permute-done | bytes 294944 | tf_op jit(solution)/shard_map/ppermute | solution.py:23
  545.6 3.6 collective-permute-done.61
  551.7 3.7 collective-permute-done.67
  561.5 11.9 %collective-permute-done.71 = bf16[1,2,2,288,256]{4,3,1,2,0:T(8,128)(2,1)S(1)} collective-permute-done((bf16[1,2,2,288,256]{4,3,1,2,0:T(8,128)(2,1)S(1)}, bf16[1,2,2,288,256]{4,3,1,2,0:T(8,128)(2,1)S(1)}, u32[]{:S(2)}, u32[]{:S(2)}) %collective-permute-start.71) | collective-permute-done | bytes 589856 | tf_op jit(solution)/shard_map/ppermute | solution.py:23
  573.7 3.3 collective-permute-start.72
  577.2 6.5 %collective-permute-done.81 = bf16[1,2,2,288,256]{4,3,2,1,0:T(8,128)(2,1)S(1)} collective-permute-done((bf16[1,2,2,288,256]{4,3,2,1,0:T(8,128)(2,1)S(1)}, bf16[1,2,2,288,256]{4,3,2,1,0:T(8,128)(2,1)S(1)}, u32[]{:S(2)}, u32[]{:S(2)}) %collective-permute-start.81) | collective-permute-done | bytes 589856 | tf_op jit(solution)/shard_map/ppermute | solution.py:23
  584.2 6.1 collective-permute-start.73
  590.4 3.8 collective-permute-start.78
  597.4 6.8 %collective-permute-done.78 = bf16[1,288,256]{2,1,0:T(8,128)(2,1)S(1)} collective-permute-done((bf16[1,288,256]{2,1,0:T(8,128)(2,1)S(1)}, bf16[1,288,256]{2,1,0:T(8,128)(2,1)S(1)}, u32[]{:S(2)}, u32[]{:S(2)}) %collective-permute-start.78) | collective-permute-done | bytes 147488 | tf_op jit(solution)/shard_map/ppermute | solution.py:23
  608.3 10.7 %input_back.1 = f32[2,10,48,512]{3,2,1,0:T(8,128)} custom-call(s32[24]{0:T(128)} %select_n.163.limits, bf16[2,2,12,48,256]{4,3,2,1,0:T(8,128)(2,1)} %first_grad.1.halves.grads, bf16[9216,512]{1,0:T(8,128)(2,1)} %bitcast.271), custom_call_target="tpu_custom_call" | custom-call | flops 4529848320 | bytes 10616928 | tf_op jit(solution)/shard_map/input_back/pallas_call | solution.py:744
  619.1 5.8 collective-permute-done.84
  626.9 3.7 collective-permute-done.91
  (388 shorter events, 220.2 us)
Async XLA Ops:
  22.1 16.3 %all-to-all-start = ((f32[32,2,512]{2,1,0:T(2,128)}), f32[32,2,512]{2,1,0:T(2,128)S(1)}, u32[]{:S(2)}, u32[]{:S(2)}) async-start(f32[32,2,512]{2,1,0:T(2,128)} %broadcast_in_dim.80), calls=%async_computation | async-start | bytes 262144 | tf_op jit(solution)/shard_map/all_to_all | solution.py:49
  53.5 15.4 %all-to-all-start.1 = ((f32[32,2,512]{2,1,0:T(2,128)}), f32[32,2,512]{2,1,0:T(2,128)S(1)}, u32[]{:S(2)}, u32[]{:S(2)}) async-start(f32[32,2,512]{2,1,0:T(2,128)} %broadcast_in_dim.81), calls=%async_computation.1 | async-start | bytes 262144 | tf_op jit(solution)/shard_map/all_to_all | solution.py:49
  189.9 20.6 %collective-permute-start.29 = (f32[3,2,48,512]{3,2,1,0:T(8,128)S(1)}, f32[3,2,48,512]{3,2,1,0:T(8,128)S(1)}, u32[]{:S(2)}, u32[]{:S(2)}) collective-permute-start(f32[3,2,48,512]{3,2,1,0:T(8,128)S(1)} %get-tuple-element.107), channel_id=1, source_target_pairs={{0,1},{1,2},{2,3},{4,5},{5,6},{6,7},{8,9},{9,10},{10,11},{12,13},{... | collective-permute-start | bytes 1769480 | tf_op jit(solution)/shard_map/ppermute | solution.py:54
  191.2 19.2 %collective-permute-start.30 = (f32[3,2,48,512]{3,2,1,0:T(8,128)S(1)}, f32[3,2,48,512]{3,2,1,0:T(8,128)}, u32[]{:S(2)}, u32[]{:S(2)}) collective-permute-start(f32[3,2,48,512]{3,2,1,0:T(8,128)S(1)} %get-tuple-element.106), channel_id=1, source_target_pairs={{1,0},{2,1},{3,2},{5,4},{6,5},{7,6},{9,8},{10,9},{11,10},{13,12},{... | collective-permute-start | bytes 1769480 | tf_op jit(solution)/shard_map/ppermute | solution.py:55
  193.9 16.6 %collective-permute-start.27 = (f32[3,2,48,512]{3,2,1,0:T(8,128)S(1)}, f32[3,2,48,512]{3,2,1,0:T(8,128)}, u32[]{:S(2)}, u32[]{:S(2)}) collective-permute-start(f32[3,2,48,512]{3,2,1,0:T(8,128)S(1)} %get-tuple-element.109), channel_id=1, source_target_pairs={{0,1},{1,2},{2,3},{4,5},{5,6},{6,7},{8,9},{9,10},{10,11},{12,13},{... | collective-permute-start | bytes 1769480 | tf_op jit(solution)/shard_map/ppermute | solution.py:54
  198.8 11.7 %collective-permute-start.28 = (f32[3,2,48,512]{3,2,1,0:T(8,128)S(1)}, f32[3,2,48,512]{3,2,1,0:T(8,128)}, u32[]{:S(2)}, u32[]{:S(2)}) collective-permute-start(f32[3,2,48,512]{3,2,1,0:T(8,128)S(1)} %get-tuple-element.108), channel_id=1, source_target_pairs={{1,0},{2,1},{3,2},{5,4},{6,5},{7,6},{9,8},{10,9},{11,10},{13,12},{... | collective-permute-start | bytes 1769480 | tf_op jit(solution)/shard_map/ppermute | solution.py:55
  209.8 61.7 %collective-permute-start.56 = (bf16[2,512,480]{1,2,0:T(8,128)(2,1)}, bf16[2,512,480]{1,2,0:T(8,128)(2,1)}, u32[]{:S(2)}, u32[]{:S(2)}) collective-permute-start(bf16[2,512,480]{1,2,0:T(8,128)(2,1)} %bitcast.21), channel_id=1, source_target_pairs={{0,1},{1,0},{2,3},{3,2},{4,5},{5,4},{6,7},{7,6},{8,9},{9,8},{10,11... | collective-permute-start | bytes 2949128 | tf_op jit(solution)/shard_map/ppermute | solution.py:23
  249.9 13.6 %collective-permute-start.38 = (f32[6,512]{1,0:T(8,128)S(1)}, f32[6,512]{1,0:T(8,128)S(1)}, u32[]{:S(2)}, u32[]{:S(2)}) collective-permute-start(f32[6,512]{1,0:T(8,128)S(1)} %reshape.488), channel_id=1, source_target_pairs={{0,1},{1,0},{2,3},{3,2},{4,5},{5,4},{6,7},{7,6},{8,9},{9,8},{10,11... | collective-permute-start | bytes 36872 | tf_op jit(solution)/shard_map/ppermute | solution.py:23
  255.1 138.2 %collective-permute-start.62 = (bf16[2,512,480]{1,2,0:T(8,128)(2,1)}, bf16[2,512,480]{1,2,0:T(8,128)(2,1)}, u32[]{:S(2)}, u32[]{:S(2)}) collective-permute-start(bf16[2,512,480]{1,2,0:T(8,128)(2,1)} %bitcast.34), channel_id=1, source_target_pairs={{0,1},{1,0},{2,3},{3,2},{4,5},{5,4},{6,7},{7,6},{8,9},{9,8},{10,11... | collective-permute-start | bytes 2949128 | tf_op jit(solution)/shard_map/ppermute | solution.py:23
  263.5 10.2 %collective-permute-start.40 = (f32[6,512]{1,0:T(8,128)S(1)}, f32[6,512]{1,0:T(8,128)S(1)}, u32[]{:S(2)}, u32[]{:S(2)}) collective-permute-start(f32[6,512]{1,0:T(8,128)S(1)} %add.362), channel_id=1, source_target_pairs={{0,4},{1,5},{2,6},{3,7},{4,0},{5,1},{6,2},{7,3},{8,12},{9,13},{10,... | collective-permute-start | bytes 36872 | tf_op jit(solution)/shard_map/ppermute | solution.py:23
  265.1 8.7 %collective-permute-start.41 = (f32[6,512]{1,0:T(8,128)S(1)}, f32[6,512]{1,0:T(8,128)S(1)}, u32[]{:S(2)}, u32[]{:S(2)}) collective-permute-start(f32[6,512]{1,0:T(8,128)S(1)} %add.362), channel_id=1, source_target_pairs={{0,6},{1,7},{2,4},{3,5},{4,2},{5,3},{6,0},{7,1},{8,14},{9,15},{10,... | collective-permute-start | bytes 36872 | tf_op jit(solution)/shard_map/ppermute | solution.py:23
  271.5 178.5 %collective-permute-start.68 = (bf16[3,2,512,480]{2,3,1,0:T(8,128)(2,1)}, bf16[3,2,512,480]{2,3,1,0:T(8,128)(2,1)}, u32[]{:S(2)}, u32[]{:S(2)}) collective-permute-start(bf16[3,2,512,480]{2,3,1,0:T(8,128)(2,1)} %bitcast.250), channel_id=1, source_target_pairs={{0,1},{1,0},{2,3},{3,2},{4,5},{5,4},{6,7},{7,6},{8,9},{9,8},{10,11... | collective-permute-start | bytes 8847368 | tf_op jit(solution)/shard_map/ppermute | solution.py:23
  303.3 9.0 %collective-permute-start.47 = (f32[6,512]{1,0:T(8,128)S(1)}, f32[6,512]{1,0:T(8,128)S(1)}, u32[]{:S(2)}, u32[]{:S(2)}) collective-permute-start(f32[6,512]{1,0:T(8,128)S(1)} %add.369), channel_id=1, source_target_pairs={{0,4},{1,5},{2,6},{3,7},{4,0},{5,1},{6,2},{7,3},{8,12},{9,13},{10,... | collective-permute-start | bytes 36872 | tf_op jit(solution)/shard_map/ppermute | solution.py:23
  312.3 9.2 %collective-permute-start.50 = (f32[6,512]{1,0:T(8,128)S(1)}, f32[6,512]{1,0:T(8,128)S(1)}, u32[]{:S(2)}, u32[]{:S(2)}) collective-permute-start(f32[6,512]{1,0:T(8,128)S(1)} %add_add_fusion.1), channel_id=1, source_target_pairs={{0,16},{1,17},{2,18},{3,19},{4,20},{5,21},{6,22},{7,23},{8,24},{9,... | collective-permute-start | bytes 36872 | tf_op jit(solution)/shard_map/ppermute | solution.py:23
  339.1 21.9 %collective-permute-start.52 = (f32[2,48,512]{2,1,0:T(8,128)}, f32[2,48,512]{2,1,0:T(8,128)}, u32[]{:S(2)}, u32[]{:S(2)}) collective-permute-start(f32[2,48,512]{2,1,0:T(8,128)} %get-tuple-element.119), channel_id=1, source_target_pairs={{0,1},{1,2},{2,3},{4,5},{5,6},{6,7},{8,9},{9,10},{10,11},{12,13},{... | collective-permute-start | bytes 589832 | tf_op jit(solution)/shard_map/ppermute | solution.py:54
  341.1 19.9 %collective-permute-start.53 = (f32[2,48,512]{2,1,0:T(8,128)S(1)}, f32[2,48,512]{2,1,0:T(8,128)}, u32[]{:S(2)}, u32[]{:S(2)}) collective-permute-start(f32[2,48,512]{2,1,0:T(8,128)S(1)} %get-tuple-element.118), channel_id=1, source_target_pairs={{1,0},{2,1},{3,2},{5,4},{6,5},{7,6},{9,8},{10,9},{11,10},{13,12},{... | collective-permute-start | bytes 589832 | tf_op jit(solution)/shard_map/ppermute | solution.py:55
  343.8 16.6 %all-to-all-start.2 = ((f32[32,2,512]{2,1,0:T(2,128)}), f32[32,2,512]{2,1,0:T(2,128)S(1)}, u32[]{:S(2)}, u32[]{:S(2)}) async-start(f32[32,2,512]{2,1,0:T(2,128)} %broadcast_in_dim.82), calls=%async_computation.2 | async-start | bytes 262144 | tf_op jit(solution)/shard_map/all_to_all | solution.py:49
  377.6 29.7 %collective-permute-start.63 = (bf16[2,12,48,256]{3,2,1,0:T(8,128)(2,1)}, bf16[2,12,48,256]{3,2,1,0:T(8,128)(2,1)}, u32[]{:S(2)}, u32[]{:S(2)}) collective-permute-start(bf16[2,12,48,256]{3,2,1,0:T(8,128)(2,1)} %dynamic-slice_bitcast_fusion.10), channel_id=1, source_target_pairs={{0,1},{1,0},{2,3},{3,2},{4,5},{5,4},{6,7},{7,6},{8,9},{9,8},{10,11... | collective-permute-start | bytes 1769480 | tf_op jit(solution)/shard_map/ppermute | solution.py:23
  379.7 21.1 %collective-permute-start.54 = (f32[2,48,512]{2,1,0:T(8,128)}, f32[2,48,512]{2,1,0:T(8,128)S(1)}, u32[]{:S(2)}, u32[]{:S(2)}) collective-permute-start(f32[2,48,512]{2,1,0:T(8,128)} %get-tuple-element.117), channel_id=1, source_target_pairs={{0,1},{1,2},{2,3},{4,5},{5,6},{6,7},{8,9},{9,10},{10,11},{12,13},{... | collective-permute-start | bytes 589832 | tf_op jit(solution)/shard_map/ppermute | solution.py:54
  381.9 19.1 %collective-permute-start.55 = (f32[2,48,512]{2,1,0:T(8,128)}, f32[2,48,512]{2,1,0:T(8,128)}, u32[]{:S(2)}, u32[]{:S(2)}) collective-permute-start(f32[2,48,512]{2,1,0:T(8,128)} %get-tuple-element.116), channel_id=1, source_target_pairs={{1,0},{2,1},{3,2},{5,4},{6,5},{7,6},{9,8},{10,9},{11,10},{13,12},{... | collective-permute-start | bytes 589832 | tf_op jit(solution)/shard_map/ppermute | solution.py:55
  383.9 16.2 %all-to-all-start.3 = ((f32[32,2,512]{2,1,0:T(2,128)}), f32[32,2,512]{2,1,0:T(2,128)S(1)}, u32[]{:S(2)}, u32[]{:S(2)}) async-start(f32[32,2,512]{2,1,0:T(2,128)} %broadcast_in_dim.83), calls=%async_computation.3 | async-start | bytes 262144 | tf_op jit(solution)/shard_map/all_to_all | solution.py:49
  393.3 40.7 %collective-permute-start.86 = (bf16[6,2,2,2,2,16,512]{6,5,4,3,2,1,0:T(8,128)(2,1)}, bf16[6,2,2,2,2,16,512]{6,5,4,3,2,1,0:T(8,128)(2,1)}, u32[]{:S(2)}, u32[]{:S(2)}) collective-permute-start(bf16[6,2,2,2,2,16,512]{6,5,4,3,2,1,0:T(8,128)(2,1)} %dynamic-slice_bitcast_fusion), channel_id=1, source_target_pairs={{0,1},{1,0},{2,3},{3,2},{4,5},{5,4},{6,7},{7,6},{8,9},{9,8},{10,11... | collective-permute-start | bytes 4718600 | tf_op jit(solution)/shard_map/ppermute | solution.py:23
  400.8 55.2 %collective-permute-start.69 = (bf16[2,12,48,256]{3,2,1,0:T(8,128)(2,1)}, bf16[2,12,48,256]{3,2,1,0:T(8,128)(2,1)}, u32[]{:S(2)}, u32[]{:S(2)}) collective-permute-start(bf16[2,12,48,256]{3,2,1,0:T(8,128)(2,1)} %dynamic-slice_bitcast_fusion.8), channel_id=1, source_target_pairs={{0,1},{1,0},{2,3},{3,2},{4,5},{5,4},{6,7},{7,6},{8,9},{9,8},{10,11... | collective-permute-start | bytes 1769480 | tf_op jit(solution)/shard_map/ppermute | solution.py:23
  407.0 13.5 %collective-permute-start.57 = (bf16[2,12,48,256]{3,2,1,0:T(8,128)(2,1)S(1)}, bf16[2,12,48,256]{3,2,1,0:T(8,128)(2,1)}, u32[]{:S(2)}, u32[]{:S(2)}) collective-permute-start(bf16[2,12,48,256]{3,2,1,0:T(8,128)(2,1)S(1)} %dynamic-slice_bitcast_fusion.12), channel_id=1, source_target_pairs={{0,1},{1,0},{2,3},{3,2},{4,5},{5,4},{6,7},{7,6},{8,9},{9,8},{10,11... | collective-permute-start | bytes 1769480 | tf_op jit(solution)/shard_map/ppermute | solution.py:23
  419.6 28.4 %collective-permute-start.64 = (bf16[1,2,2,2,288,256]{5,4,1,2,3,0:T(8,128)(2,1)}, bf16[1,2,2,2,288,256]{5,4,1,2,3,0:T(8,128)(2,1)S(1)}, u32[]{:S(2)}, u32[]{:S(2)}) collective-permute-start(bf16[1,2,2,2,288,256]{5,4,1,2,3,0:T(8,128)(2,1)} %bitcast.235), channel_id=1, source_target_pairs={{0,4},{1,5},{2,6},{3,7},{4,0},{5,1},{6,2},{7,3},{8,12},{9,13},{10,... | collective-permute-start | bytes 3538952 | tf_op jit(solution)/shard_map/ppermute | solution.py:23
  420.6 50.9 %collective-permute-start.74 = (bf16[2,12,48,256]{3,2,1,0:T(8,128)(2,1)}, bf16[2,12,48,256]{3,2,1,0:T(8,128)(2,1)}, u32[]{:S(2)}, u32[]{:S(2)}) collective-permute-start(bf16[2,12,48,256]{3,2,1,0:T(8,128)(2,1)} %dynamic-slice_bitcast_fusion.6), channel_id=1, source_target_pairs={{0,1},{1,0},{2,3},{3,2},{4,5},{5,4},{6,7},{7,6},{8,9},{9,8},{10,11... | collective-permute-start | bytes 1769480 | tf_op jit(solution)/shard_map/ppermute | solution.py:23
  433.9 53.4 %collective-permute-start.79 = (bf16[2,12,48,256]{3,2,1,0:T(8,128)(2,1)}, bf16[2,12,48,256]{3,2,1,0:T(8,128)(2,1)}, u32[]{:S(2)}, u32[]{:S(2)}) collective-permute-start(bf16[2,12,48,256]{3,2,1,0:T(8,128)(2,1)} %dynamic-slice_bitcast_fusion.4), channel_id=1, source_target_pairs={{0,1},{1,0},{2,3},{3,2},{4,5},{5,4},{6,7},{7,6},{8,9},{9,8},{10,11... | collective-permute-start | bytes 1769480 | tf_op jit(solution)/shard_map/ppermute | solution.py:23
  448.0 51.1 %collective-permute-start.58 = (bf16[1,2,2,2,288,256]{5,4,1,2,3,0:T(8,128)(2,1)}, bf16[1,2,2,2,288,256]{5,4,1,2,3,0:T(8,128)(2,1)}, u32[]{:S(2)}, u32[]{:S(2)}) collective-permute-start(bf16[1,2,2,2,288,256]{5,4,1,2,3,0:T(8,128)(2,1)} %bitcast.236), channel_id=1, source_target_pairs={{0,2},{1,3},{2,0},{3,1},{4,6},{5,7},{6,4},{7,5},{8,10},{9,11},{10,... | collective-permute-start | bytes 3538952 | tf_op jit(solution)/shard_map/ppermute | solution.py:23
  450.0 52.4 %collective-permute-start.87 = (bf16[6,2,2,2,16,512]{5,4,3,2,1,0:T(8,128)(2,1)}, bf16[6,2,2,2,16,512]{5,4,3,2,1,0:T(8,128)(2,1)}, u32[]{:S(2)}, u32[]{:S(2)}) collective-permute-start(bf16[6,2,2,2,16,512]{5,4,3,2,1,0:T(8,128)(2,1)} %dynamic-slice_bitcast_fusion.2), channel_id=1, source_target_pairs={{0,2},{1,3},{2,0},{3,1},{4,6},{5,7},{6,4},{7,5},{8,10},{9,11},{10,... | collective-permute-start | bytes 2359304 | tf_op jit(solution)/shard_map/ppermute | solution.py:23
  456.0 50.7 %collective-permute-start.65 = (bf16[1,2,2,288,256]{4,3,1,2,0:T(8,128)(2,1)}, bf16[1,2,2,288,256]{4,3,1,2,0:T(8,128)(2,1)}, u32[]{:S(2)}, u32[]{:S(2)}) collective-permute-start(bf16[1,2,2,288,256]{4,3,1,2,0:T(8,128)(2,1)} %dynamic-slice_bitcast_fusion.9), channel_id=1, source_target_pairs={{0,2},{1,3},{2,0},{3,1},{4,6},{5,7},{6,4},{7,5},{8,10},{9,11},{10,... | collective-permute-start | bytes 1769480 | tf_op jit(solution)/shard_map/ppermute | solution.py:23
  471.4 84.1 %collective-permute-start.70 = (bf16[1,2,2,2,288,256]{5,4,1,2,3,0:T(8,128)(2,1)}, bf16[1,2,2,2,288,256]{5,4,1,2,3,0:T(8,128)(2,1)}, u32[]{:S(2)}, u32[]{:S(2)}) collective-permute-start(bf16[1,2,2,2,288,256]{5,4,1,2,3,0:T(8,128)(2,1)} %bitcast.234), channel_id=1, source_target_pairs={{0,2},{1,3},{2,0},{3,1},{4,6},{5,7},{6,4},{7,5},{8,10},{9,11},{10,... | collective-permute-start | bytes 3538952 | tf_op jit(solution)/shard_map/ppermute | solution.py:23
  487.3 71.4 %collective-permute-start.75 = (bf16[1,2,2,2,288,256]{5,4,1,2,3,0:T(8,128)(2,1)}, bf16[1,2,2,2,288,256]{5,4,1,2,3,0:T(8,128)(2,1)S(1)}, u32[]{:S(2)}, u32[]{:S(2)}) collective-permute-start(bf16[1,2,2,2,288,256]{5,4,1,2,3,0:T(8,128)(2,1)} %bitcast.259), channel_id=1, source_target_pairs={{0,4},{1,5},{2,6},{3,7},{4,0},{5,1},{6,2},{7,3},{8,12},{9,13},{10,... | collective-permute-start | bytes 3538952 | tf_op jit(solution)/shard_map/ppermute | solution.py:23
  499.1 61.4 %collective-permute-start.80 = (bf16[1,2,2,2,288,256]{5,4,3,2,1,0:T(8,128)(2,1)S(1)}, bf16[1,2,2,2,288,256]{5,4,3,2,1,0:T(8,128)(2,1)S(1)}, u32[]{:S(2)}, u32[]{:S(2)}) collective-permute-start(bf16[1,2,2,2,288,256]{5,4,3,2,1,0:T(8,128)(2,1)S(1)} %dynamic-slice_bitcast_fusion.1), channel_id=1, source_target_pairs={{0,2},{1,3},{2,0},{3,1},{4,6},{5,7},{6,4},{7,5},{8,10},{9,11},{10,... | collective-permute-start | bytes 3538952 | tf_op jit(solution)/shard_map/ppermute | solution.py:23
  502.4 26.6 %collective-permute-start.59 = (bf16[1,2,2,288,256]{4,3,1,2,0:T(8,128)(2,1)S(1)}, bf16[1,2,2,288,256]{4,3,1,2,0:T(8,128)(2,1)S(1)}, u32[]{:S(2)}, u32[]{:S(2)}) collective-permute-start(bf16[1,2,2,288,256]{4,3,1,2,0:T(8,128)(2,1)S(1)} %dynamic-slice_bitcast_fusion.11), channel_id=1, source_target_pairs={{0,4},{1,5},{2,6},{3,7},{4,0},{5,1},{6,2},{7,3},{8,12},{9,13},{10,... | collective-permute-start | bytes 1769480 | tf_op jit(solution)/shard_map/ppermute | solution.py:23
  506.7 28.1 %collective-permute-start.88 = (bf16[6,2,2,16,512]{4,3,2,1,0:T(8,128)(2,1)S(1)}, bf16[6,2,2,16,512]{4,3,2,1,0:T(8,128)(2,1)S(1)}, u32[]{:S(2)}, u32[]{:S(2)}) collective-permute-start(bf16[6,2,2,16,512]{4,3,2,1,0:T(8,128)(2,1)S(1)} %dynamic-slice_bitcast_fusion.13), channel_id=1, source_target_pairs={{0,4},{1,5},{2,6},{3,7},{4,0},{5,1},{6,2},{7,3},{8,12},{9,13},{10,... | collective-permute-start | bytes 1179656 | tf_op jit(solution)/shard_map/ppermute | solution.py:23
  529.1 13.9 %collective-permute-start.66 = (bf16[1,2,288,256]{3,2,1,0:T(8,128)(2,1)S(1)}, bf16[1,2,288,256]{3,2,1,0:T(8,128)(2,1)S(1)}, u32[]{:S(2)}, u32[]{:S(2)}) collective-permute-start(bf16[1,2,288,256]{3,2,1,0:T(8,128)(2,1)S(1)} %dynamic-slice_bitcast_fusion.17), channel_id=1, source_target_pairs={{0,8},{1,9},{2,10},{3,11},{4,12},{5,13},{6,14},{7,15},{8,0},{9,1},... | collective-permute-start | bytes 884744 | tf_op jit(solution)/shard_map/ppermute | solution.py:23
  542.1 76.9 %collective-permute-start.89 = (bf16[6,2,16,512]{3,2,1,0:T(8,128)(2,1)S(1)}, bf16[6,2,16,512]{3,2,1,0:T(8,128)(2,1)S(1)}, u32[]{:S(2)}, u32[]{:S(2)}) collective-permute-start(bf16[6,2,16,512]{3,2,1,0:T(8,128)(2,1)S(1)} %dynamic-slice_bitcast_fusion.19), channel_id=1, source_target_pairs={{0,8},{1,9},{2,10},{3,11},{4,12},{5,13},{6,14},{7,15},{8,0},{9,1},... | collective-permute-start | bytes 589832 | tf_op jit(solution)/shard_map/ppermute | solution.py:23
  557.1 16.3 %collective-permute-start.71 = (bf16[1,2,2,288,256]{4,3,1,2,0:T(8,128)(2,1)S(1)}, bf16[1,2,2,288,256]{4,3,1,2,0:T(8,128)(2,1)S(1)}, u32[]{:S(2)}, u32[]{:S(2)}) collective-permute-start(bf16[1,2,2,288,256]{4,3,1,2,0:T(8,128)(2,1)S(1)} %dynamic-slice_bitcast_fusion.7), channel_id=1, source_target_pairs={{0,4},{1,5},{2,6},{3,7},{4,0},{5,1},{6,2},{7,3},{8,12},{9,13},{10,... | collective-permute-start | bytes 1769480 | tf_op jit(solution)/shard_map/ppermute | solution.py:23
  559.0 17.9 %collective-permute-start.76 = (bf16[1,2,2,288,256]{4,3,1,2,0:T(8,128)(2,1)S(1)}, bf16[1,2,2,288,256]{4,3,1,2,0:T(8,128)(2,1)S(1)}, u32[]{:S(2)}, u32[]{:S(2)}) collective-permute-start(bf16[1,2,2,288,256]{4,3,1,2,0:T(8,128)(2,1)S(1)} %dynamic-slice_bitcast_fusion.5), channel_id=1, source_target_pairs={{0,2},{1,3},{2,0},{3,1},{4,6},{5,7},{6,4},{7,5},{8,10},{9,11},{10,... | collective-permute-start | bytes 1769480 | tf_op jit(solution)/shard_map/ppermute | solution.py:23
  561.0 22.8 %collective-permute-start.81 = (bf16[1,2,2,288,256]{4,3,2,1,0:T(8,128)(2,1)S(1)}, bf16[1,2,2,288,256]{4,3,2,1,0:T(8,128)(2,1)S(1)}, u32[]{:S(2)}, u32[]{:S(2)}) collective-permute-start(bf16[1,2,2,288,256]{4,3,2,1,0:T(8,128)(2,1)S(1)} %dynamic-slice_bitcast_fusion.3), channel_id=1, source_target_pairs={{0,4},{1,5},{2,6},{3,7},{4,0},{5,1},{6,2},{7,3},{8,12},{9,13},{10,... | collective-permute-start | bytes 1769480 | tf_op jit(solution)/shard_map/ppermute | solution.py:23
  573.7 10.4 %collective-permute-start.72 = (bf16[1,2,288,256]{3,2,1,0:T(8,128)(2,1)S(1)}, bf16[1,2,288,256]{3,2,1,0:T(8,128)(2,1)S(1)}, u32[]{:S(2)}, u32[]{:S(2)}) collective-permute-start(bf16[1,2,288,256]{3,2,1,0:T(8,128)(2,1)S(1)} %dynamic-slice_bitcast_fusion.16), channel_id=1, source_target_pairs={{0,8},{1,9},{2,10},{3,11},{4,12},{5,13},{6,14},{7,15},{8,0},{9,1},... | collective-permute-start | bytes 884744 | tf_op jit(solution)/shard_map/ppermute | solution.py:23
  577.2 13.2 %collective-permute-start.77 = (bf16[1,2,288,256]{3,2,1,0:T(8,128)(2,1)S(1)}, bf16[1,2,288,256]{3,2,1,0:T(8,128)(2,1)S(1)}, u32[]{:S(2)}, u32[]{:S(2)}) collective-permute-start(bf16[1,2,288,256]{3,2,1,0:T(8,128)(2,1)S(1)} %dynamic-slice_bitcast_fusion.15), channel_id=1, source_target_pairs={{0,8},{1,9},{2,10},{3,11},{4,12},{5,13},{6,14},{7,15},{8,0},{9,1},... | collective-permute-start | bytes 884744 | tf_op jit(solution)/shard_map/ppermute | solution.py:23
  584.0 12.9 %collective-permute-start.82 = (bf16[1,2,288,256]{3,2,1,0:T(8,128)(2,1)S(1)}, bf16[1,2,288,256]{3,2,1,0:T(8,128)(2,1)S(1)}, u32[]{:S(2)}, u32[]{:S(2)}) collective-permute-start(bf16[1,2,288,256]{3,2,1,0:T(8,128)(2,1)S(1)} %dynamic-slice_bitcast_fusion.14), channel_id=1, source_target_pairs={{0,8},{1,9},{2,10},{3,11},{4,12},{5,13},{6,14},{7,15},{8,0},{9,1},... | collective-permute-start | bytes 884744 | tf_op jit(solution)/shard_map/ppermute | solution.py:23
  584.2 13.2 %collective-permute-start.73 = (bf16[1,288,256]{2,1,0:T(8,128)(2,1)S(1)}, bf16[1,288,256]{2,1,0:T(8,128)(2,1)S(1)}, u32[]{:S(2)}, u32[]{:S(2)}) collective-permute-start(bf16[1,288,256]{2,1,0:T(8,128)(2,1)S(1)} %dynamic-slice_bitcast_fusion.22), channel_id=1, source_target_pairs={{0,16},{1,17},{2,18},{3,19},{4,20},{5,21},{6,22},{7,23},{8,24},{9,... | collective-permute-start | bytes 442376 | tf_op jit(solution)/shard_map/ppermute | solution.py:23
  590.4 13.8 %collective-permute-start.78 = (bf16[1,288,256]{2,1,0:T(8,128)(2,1)S(1)}, bf16[1,288,256]{2,1,0:T(8,128)(2,1)S(1)}, u32[]{:S(2)}, u32[]{:S(2)}) collective-permute-start(bf16[1,288,256]{2,1,0:T(8,128)(2,1)S(1)} %dynamic-slice_bitcast_fusion.21), channel_id=1, source_target_pairs={{0,16},{1,17},{2,18},{3,19},{4,20},{5,21},{6,22},{7,23},{8,24},{9,... | collective-permute-start | bytes 442376 | tf_op jit(solution)/shard_map/ppermute | solution.py:23
  597.0 9.9 %collective-permute-start.83 = (bf16[1,288,256]{2,1,0:T(8,128)(2,1)S(1)}, bf16[1,288,256]{2,1,0:T(8,128)(2,1)S(1)}, u32[]{:S(2)}, u32[]{:S(2)}) collective-permute-start(bf16[1,288,256]{2,1,0:T(8,128)(2,1)S(1)} %dynamic-slice_bitcast_fusion.20), channel_id=1, source_target_pairs={{0,16},{1,17},{2,18},{3,19},{4,20},{5,21},{6,22},{7,23},{8,24},{9,... | collective-permute-start | bytes 442376 | tf_op jit(solution)/shard_map/ppermute | solution.py:23
  606.9 18.0 %collective-permute-start.84 = (bf16[5,1,288,256]{3,2,0,1:T(8,128)(2,1)S(1)}, bf16[5,1,288,256]{3,2,0,1:T(8,128)(2,1)S(1)}, u32[]{:S(2)}, u32[]{:S(2)}) collective-permute-start(bf16[5,1,288,256]{3,2,0,1:T(8,128)(2,1)S(1)} %bitcast.260), channel_id=1, source_target_pairs={{0,2},{1,3},{2,0},{3,1},{4,6},{5,7},{6,4},{7,5},{8,10},{9,11},{10,... | collective-permute-start | bytes 2211848 | tf_op jit(solution)/shard_map/ppermute | solution.py:23
  625.3 8.7 %collective-permute-start.85 = (bf16[5,576,256]{2,1,0:T(8,128)(2,1)S(1)}, bf16[5,576,256]{2,1,0:T(8,128)(2,1)S(1)}, u32[]{:S(2)}, u32[]{:S(2)}) collective-permute-start(bf16[5,576,256]{2,1,0:T(8,128)(2,1)S(1)} %bitcast.244), channel_id=1, source_target_pairs={{0,1},{1,0},{2,3},{3,2},{4,5},{5,4},{6,7},{7,6},{8,9},{9,8},{10,11... | collective-permute-start | bytes 4423688 | tf_op jit(solution)/shard_map/ppermute | solution.py:23
  (79 other events, 575.9 us)

commit v3 on v0

v3 whole, which is shorter than its diff:
```python
import functools

import jax
import jax.numpy as jnp
from jax import lax
from jax.experimental import pallas as pl
from jax.experimental.pallas import tpu as pltpu
from jax.sharding import PartitionSpec as P

H_BIG = 36
W_BIG = 48
H_SMALL = 18
W_SMALL = 24
EPSILON = 1e-05
AXES = ("dp", "rows")
F32 = jnp.float32
BF16 = jnp.bfloat16
MIB = 1024 * 1024
SUMS = 8


def places():
    return lax.axis_size("dp") * lax.axis_size("rows")


def swapped(values, flip):
    return lax.ppermute(values, AXES, [(i, i ^ flip) for i in range(places())])


def swapped_far(values):
    count = lax.axis_size("rows")
    pairs = [(i, i + 1) for i in range(1, count - 1, 2)]
    return lax.ppermute(values, "rows", pairs + [(j, i) for i, j in pairs])


def exchange_sum(values, got):
    bits = places().bit_length() - 1
    assert places() == 1 << bits
    values = values + got
    place = 1
    while place < bits:
        low = 1 << place
        if place + 1 < bits:
            high = low * 2
            values = (values + swapped(values, low)) + (
                swapped(values, high) + swapped(values, high + low)
            )
            place += 2
        else:
            values = values + swapped(values, low)
            place += 1
    return values


def norm_totals(packed, far=None):
    got = swapped(packed, 1)
    edges = packed.shape[0] - SUMS
    totals = exchange_sum(packed[edges:], got[edges:])
    if far is None:
        return totals
    return totals, got, swapped_far(far)


def dot(left, right):
    return jnp.dot(left, right, preferred_element_type=F32)


def dot_turned(left, right):
    return lax.dot_general(left, right, (((1,), (1,)), ((), ())), preferred_element_type=F32)


def dot_over_rows(left, right):
    return lax.dot_general(left, right, (((0,), (0,)), ((), ())), preferred_element_type=F32)


class Frame:
    def __init__(self, info, slots, rows, breadth, channels):
        self.info, self.slots, self.rows = info, slots, rows
        self.breadth, self.channels = breadth, channels
        self.tall = rows + 2
        odd = self.bit(0) == 1
        self.near_rim = jnp.where(odd, 0, rows + 1)
        self.far_rim = rows + 1 - self.near_rim
        self.near_row = jnp.where(odd, 0, rows - 1)
        self.far_row = rows - 1 - self.near_row

    def bit(self, index):
        return self.info[self.slots * self.tall + index]

    def inside(self, slot, tall_row):
        shape = (self.breadth, self.channels)
        limit = self.info[slot * self.tall + tall_row]
        return lax.broadcasted_iota(jnp.int32, shape, 0) < limit

    def each(self, body):
        def step(row, carry):
            for slot in range(self.slots):
                body(slot, row)
            return carry

        lax.fori_loop(0, self.rows, step, 0)

    def summed(self, body, rows=None):
        def step(row, carry):
            one, two = carry
            for slot in range(self.slots):
                first, second = body(slot, row)
                one, two = one + fold(first), two + fold(second)
            return one, two

        zero = jnp.zeros((8, self.channels), F32)
        one, two = lax.fori_loop(0, rows or self.rows, step, (zero, zero))
        return jnp.sum(one, axis=0, keepdims=True), jnp.sum(two, axis=0, keepdims=True)

    def rims(self, sources, body, group=0):
        for slot in range(self.slots):
            index = group * self.slots + slot
            start = index * self.breadth
            if not isinstance(start, int):
                start = pl.multiple_of(start, 8)
            body(slot, self.near_rim, *[near[pl.ds(start, self.breadth), :] for near, _ in sources])
            body(slot, self.far_rim, *[far[index].astype(F32) for _, far in sources])

    def pack(self, packed, far, rows_of, sums, group=0):
        edges = packed.shape[0] - SUMS

        @pl.when(jnp.equal(group, 0))
        def _():
            packed[edges:, :] = jnp.zeros((SUMS, self.channels), F32)

        packed[pl.ds(edges + 2 * group, 1), :] = sums[0]
        packed[pl.ds(edges + 2 * group + 1, 1), :] = sums[1]
        if far is None:
            return
        for slot in range(self.slots):
            index = group * self.slots + slot
            start = index * self.breadth
            if not isinstance(start, int):
                start = pl.multiple_of(start, 8)
            packed[pl.ds(start, self.breadth), :] = rows_of(slot, self.near_row)
            far[index] = rows_of(slot, self.far_row).astype(far.dtype)

    def pixels(self, slot, row, rows=None):
        start = (slot * (rows or self.rows) + row) * self.breadth
        return pl.ds(pl.multiple_of(start, 8), self.breadth)

    def span(self, slot, rows=None):
        part = (rows or self.rows) * self.breadth
        return slice(slot * part, (slot + 1) * part)


def moments(totals, member, count):
    average = totals[pl.ds(2 * member, 1), :] / count
    variance = totals[pl.ds(2 * member + 1, 1), :] / count - average * average
    return average, lax.rsqrt(variance + EPSILON)


def line(ref, member):
    return ref[pl.ds(member, 1), :]


def sigmoid(values):
    return 1.0 / (1.0 + jnp.exp(-values))


def silu_slope(values):
    logistic = sigmoid(values)
    return logistic * (1.0 + values * (1.0 - logistic))


def fold(values):
    return jnp.sum(values.reshape(-1, 8, values.shape[-1]), axis=0)


def put_three(ref, slot, row, values, flipped):
    breadth, channels = values.shape
    col = lax.broadcasted_iota(jnp.int32, values.shape, 0)
    before = jnp.where(col == 0, 0.0, pltpu.roll(values, 1, 0))
    after = jnp.where(col == breadth - 1, 0.0, pltpu.roll(values, breadth - 1, 0))
    if flipped:
        before, after = after, before
    ref[slot, row, :, 0:channels] = before.astype(BF16)
    ref[slot, row, :, channels : 2 * channels] = values.astype(BF16)
    ref[slot, row, :, 2 * channels :] = after.astype(BF16)


def weight_copies(source, target, arrived, lead=()):
    third = target.shape[-2] // 3
    return [
        pltpu.make_async_copy(
            source.at[lead + (pl.ds(part * third, third),)],
            target.at[pl.ds(part * third, third)],
            arrived.at[part],
        )
        for part in range(3)
    ]


def forward_conv(three, weight, sums, lead=()):
    slots, rows, breadth, channels = sums.shape[-4:]
    third = weight.shape[0] // 3
    for slot in range(slots):
        total = None
        for step in range(3):
            window = three[slot, step : step + rows].reshape(rows * breadth, third)
            one = dot(window, weight[step * third : (step + 1) * third, :])
            total = one if total is None else total + one
        sums[lead + (slot,)] = total.reshape(rows, breadth, channels)


def backward_conv(three, weight, sums):
    slots, rows, breadth, channels = sums.shape[-4:]
    wide = three.shape[-1] // 3
    for slot in range(slots):
        total = None
        for step in range(3):
            window = three[slot, 2 - step : 2 - step + rows].reshape(rows * breadth, 3 * wide)
            for tap in range(3):
                start = (3 * step + tap) * channels
                one = dot_turned(
                    window[:, tap * wide : (tap + 1) * wide], weight[start : start + channels, :]
                )
                total = one if total is None else total + one
        sums[slot] = total.reshape(rows, breadth, channels)


def conv_sums(frame, sums, lead, packed, far, group=0):
    def body(slot, row):
        values = sums[lead + (slot, row)]
        kept = jnp.where(frame.inside(slot, row + 1), values, 0.0)
        return kept, kept * values

    result = frame.summed(body)
    frame.pack(packed, far, lambda slot, row: sums[lead + (slot, row)], result, group)


def plain_sums(frame, source):
    def body(slot, row):
        values = source[frame.pixels(slot, row), :]
        return values, values * values

    return frame.summed(body)


def activation(values, inside, average, inverse, gain, shift):
    normed = gain * ((values - average) * inverse) + shift
    return jnp.where(inside, normed * sigmoid(normed), 0.0)


class NormBack:
    def __init__(self, totals, back, gain, member, count):
        self.average, self.inverse = moments(totals, member, count)
        self.slope = gain * self.inverse
        self.level = self.slope * back[pl.ds(2 * member, 1), :] / count
        self.along = self.slope * back[pl.ds(2 * member + 1, 1), :] / count

    def __call__(self, grad, values, inside):
        centred = (values - self.average) * self.inverse
        return self.slope * grad - jnp.where(inside, self.level + centred * self.along, 0.0)


def first_kernel(
    info, images, above, below, weight, sums, packed, far, masked, three, held, arrived
):
    slots, rows, breadth, channels = images.shape
    frame = Frame(info, slots, rows, breadth, channels)
    copies = weight_copies(weight, held, arrived, (0,))
    for copy in copies:
        copy.start()

    def put(slot, row, values):
        kept = jnp.where(frame.inside(slot, row), values.astype(F32), 0.0)
        put_three(three, slot, row, kept, False)
        return kept

    def own(slot, row):
        masked[slot, row] = put(slot, row + 1, images[slot, row]).astype(BF16)

    frame.each(own)
    for slot in range(slots):
        put(slot, 0, above[slot])
        put(slot, rows + 1, below[slot])
    for copy in copies:
        copy.wait()
    forward_conv(three, held, sums)
    conv_sums(frame, sums, (), packed, far)


def second_kernel(
    info, count, source, near, outer, totals, gain, shift, weight, sums, packed, far, hidden, three, held, arrived
):
    slots, rows, breadth, channels = source.shape
    frame = Frame(info, slots, rows, breadth, channels)
    copies = weight_copies(weight, held, arrived, (1,))
    for copy in copies:
        copy.start()
    average, inverse = moments(totals, 0, count[0])

    def act(slot, row, values):
        inside = frame.inside(slot, row)
        result = activation(values, inside, average, inverse, line(gain, 0), line(shift, 0))
        put_three(three, slot, row, result, False)
        return result

    def own(slot, row):
        hidden[slot, row] = act(slot, row + 1, source[slot, row]).astype(BF16)

    frame.each(own)
    frame.rims([(near, outer)], act)
    for copy in copies:
        copy.wait()
    forward_conv(three, held, sums)
    conv_sums(frame, sums, (), packed, far)


def lower_kernel(
    info, count, source, near, outer, totals, gain, shift, down, shared, packed, lowered
):
    branch = pl.program_id(0)
    slots, rows, breadth, channels = source.shape
    frame = Frame(info, slots, rows, breadth, channels)

    @pl.when(branch == 0)
    def _():
        average, inverse = moments(totals, 0, count[0])

        def act(slot, row, values):
            inside = frame.inside(slot, row)
            result = activation(values, inside, average, inverse, line(gain, 1), line(shift, 1))
            shared[slot, row] = result.astype(BF16)

        frame.each(lambda slot, row: act(slot, row + 1, source[slot, row]))
        frame.rims([(near, outer)], act)

    for slot in range(slots):
        lowered[frame.span(slot), :] = dot(
            shared[slot, 1 : rows + 1].reshape(rows * breadth, channels), down[0]
        )
    frame.pack(packed, None, None, plain_sums(frame, lowered), branch)


def raise_kernel(
    info, count, shared, down, up, totals, gain, shift, squeezed, packed, wide, raised
):
    branch = pl.program_id(0)
    slots, tall, breadth, channels = shared.shape
    rows = tall - 2
    frame = Frame(info, slots, rows, breadth, channels)
    wide[...] = dot(shared[...].reshape(slots * tall * breadth, channels), down[0])
    average, inverse = moments(totals, branch, count[0])

    def act(row, carry):
        for slot in range(slots):
            values = wide[frame.pixels(slot, row, tall), :]
            result = activation(
                values, frame.inside(slot, row), average, inverse, line(gain, branch), line(shift, branch)
            )
            squeezed[0, slot, row] = result.astype(BF16)
        return carry

    lax.fori_loop(0, tall, act, 0)
    for slot in range(slots):
        raised[frame.span(slot), :] = dot(
            squeezed[0, slot, 1 : rows + 1].reshape(rows * breadth, -1), up[0]
        )
    frame.pack(packed, None, None, plain_sums(frame, raised), branch)


def task_weight(branch, weight, held, arrived):
    def copies(which):
        buffer = which % 2
        return weight_copies(weight, held.at[buffer], arrived.at[buffer], (which,))

    @pl.when(branch == 0)
    def _():
        for copy in copies(branch):
            copy.start()

    def ready():
        for copy in copies(branch):
            copy.wait()

        @pl.when(branch + 1 < pl.num_programs(0))
        def _():
            for copy in copies(branch + 1):
                copy.start()

    return ready


def task_kernel(
    info, count, squeezed, up, shared, totals, gain, shift, weight, sums, packed, far, gated,
    wide, three, held, arrived,
):
    branch = pl.program_id(0)
    slots, tall, breadth, channels = shared.shape
    rows = tall - 2
    frame = Frame(info, slots, rows, breadth, channels)
    ready = task_weight(branch, weight, held, arrived)
    wide[...] = dot(squeezed[0].reshape(slots * tall * breadth, -1), up[0])
    average, inverse = moments(totals, branch, count[0])

    def gate(slot, row):
        values = wide[frame.pixels(slot, row, tall), :]
        normed = line(gain, branch) * ((values - average) * inverse) + line(shift, branch)
        result = sigmoid(normed) * shared[slot, row].astype(F32)
        put_three(three, slot, row, result, False)
        return result

    def own(slot, row):
        gated[0, slot, row] = gate(slot, row + 1).astype(BF16)

    frame.each(own)
    for slot in range(slots):
        gate(slot, 0)
        gate(slot, rows + 1)
    ready()
    forward_conv(three, held.at[branch % 2], sums, (0,))
    conv_sums(frame, sums, (0,), packed, far, branch)


def pool_kernel(
    info, count, source, cotangent, totals, gain, shift, maps, slope, packed, far, spread, pairs
):
    branch = pl.program_id(0)
    slots, rows, breadth, channels = source.shape[1:]
    frame = Frame(info, slots, rows, breadth, channels)
    average, inverse = moments(totals, branch, count[0])
    half = breadth // 2
    groups = channels // 128

    def body(slot, pooled):
        block = cotangent[0, slot, pooled].astype(F32) * 0.25
        for group in range(groups):
            lanes = block[:, group * 128 : (group + 1) * 128]
            spread[slot, group, pl.ds(0, half, stride=2), :] = lanes
            spread[slot, group, pl.ds(1, half, stride=2), :] = lanes
        wide = jnp.concatenate([spread[slot, group] for group in range(groups)], axis=1)
        one = two = total = None
        for parity in range(2):
            row = 2 * pooled + parity
            inside = frame.inside(slot, row + 1)
            centred = (source[0, slot, row] - average) * inverse
            normed = line(gain, branch) * centred + line(shift, branch)
            logistic = sigmoid(normed)
            active = jnp.where(inside, normed * logistic, 0.0)
            grad = wide * (logistic * (1.0 + normed * (1.0 - logistic)))
            grad = jnp.where(inside, grad, 0.0)
            slope[0, slot, row] = grad
            along = grad * centred
            if parity == 0:
                one, two, total = grad, along, active
            else:
                one, two, total = one + grad, two + along, total + active
        for group in range(groups):
            lanes = slice(group * 128, (group + 1) * 128)
            pairs[slot, group] = total[:, lanes]
            even = pairs[slot, group, pl.ds(0, half, stride=2), :]
            odd = pairs[slot, group, pl.ds(1, half, stride=2), :]
            maps[0, slot, pooled, :, lanes] = ((even + odd) * 0.25).astype(BF16)
        return one, two

    sums = frame.summed(body, rows // 2)
    frame.pack(packed, far, lambda slot, row: slope[0, slot, row], sums, branch)


def fill_back(
    frame, count, grads, grad_near, grad_far, source, near, outer, totals, back, gain, three, kept, sent, lead, member
):
    norm = NormBack(totals, back, gain, member, count)
    odd = frame.bit(0) == 1
    half = frame.channels // 2

    def put(slot, row, grad, values):
        result = norm(grad, values, frame.inside(slot, row))
        if three is not None:
            put_three(three, slot, row, result, True)
        low, high = result[:, :half], result[:, half:]
        kept[lead + (slot, row)] = jnp.where(odd, high, low).astype(BF16)
        sent[lead + (slot, row)] = jnp.where(odd, low, high).astype(BF16)

    def own(slot, row):
        put(slot, row + 1, grads[lead + (slot, row)], source[lead + (slot, row)])

    frame.each(own)
    frame.rims([(grad_near, grad_far), (near, outer)], put, member if lead else 0)


def conv_grad_kernel(
    info, count, grads, grad_near, grad_far, source, near, outer, totals, back, gain, kept, sent
):
    branch = pl.program_id(0)
    frame = Frame(info, *source.shape[1:])
    fill_back(
        frame, count[0], grads, grad_near, grad_far, source, near, outer,
        totals, back, line(gain, branch), None, kept, sent, (0,), branch,
    )


def fill_halves(frame, kept, sent, three, lead=()):
    odd = frame.bit(0) == 1

    def put(row, carry):
        for slot in range(frame.slots):
            mine = kept[lead + (slot, row)].astype(F32)
            other = sent[lead + (slot, row)].astype(F32)
            low, high = jnp.where(odd, other, mine), jnp.where(odd, mine, other)
            put_three(three, slot, row, jnp.concatenate([low, high], axis=1), True)
        return carry

    lax.fori_loop(0, frame.tall, put, 0)


def gate_back_kernel(
    info, count, kept, sent, weight, squeezed, up, shared, up_totals, up_gain, up_shift,
    incoming, shared_grad, packed, three, sums, raised, held, arrived,
):
    branch = pl.program_id(0)
    slots, rows, breadth, channels = sums.shape
    frame = Frame(info, slots, rows, breadth, channels)
    ready = task_weight(branch, weight, held, arrived)
    fill_halves(frame, kept, sent, three, (0,))
    for slot in range(slots):
        raised[frame.span(slot), :] = dot(
            squeezed[0, slot, 1 : rows + 1].reshape(rows * breadth, -1), up[0]
        )
    ready()
    backward_conv(three, held.at[branch % 2], sums)
    average, inverse = moments(up_totals, branch, count[0])

    @pl.when(branch == 0)
    def _():
        shared_grad[...] = jnp.zeros(shared_grad.shape, F32)

    def body(slot, row):
        centred = (raised[frame.pixels(slot, row), :] - average) * inverse
        attention = sigmoid(line(up_gain, branch) * centred + line(up_shift, branch))
        onward = sums[slot, row] * attention
        result = onward * shared[slot, row + 1].astype(F32) * (1.0 - attention)
        incoming[0, slot, row] = result
        shared_grad[slot, row] += onward
        return result, result * centred

    frame.pack(packed, None, None, frame.summed(body), branch)


def raise_back_kernel(
    info, count, grads, squeezed, up, shared, down, up_totals, up_back, up_gain, down_totals, down_gain,
    down_shift, raised_grad, incoming, packed, wide, sums,
):
    branch = pl.program_id(0)
    slots, rows, breadth, channels = grads.shape[1:]
    part = rows * breadth
    frame = Frame(info, slots, rows, breadth, channels)
    for slot in range(slots):
        wide[frame.span(slot), :] = dot(squeezed[0, slot, 1 : rows + 1].reshape(part, -1), up[0])
    norm = NormBack(up_totals, up_back, line(up_gain, branch), branch, count[0])

    def back(slot, row):
        result = norm(
            grads[0, slot, row], wide[frame.pixels(slot, row), :], frame.inside(slot, row + 1)
        )
        raised_grad[0, slot, row] = result.astype(BF16)

    frame.each(back)
    for slot in range(slots):
        sums[frame.span(slot), :] = dot_turned(raised_grad[0, slot].reshape(part, channels), up[0])
        wide[frame.span(slot), :] = dot(
            shared[slot, 1 : rows + 1].reshape(part, channels), down[0]
        )
    average2, inverse2 = moments(down_totals, branch, count[0])

    def body(slot, row):
        centred = (wide[frame.pixels(slot, row), :] - average2) * inverse2
        normed = line(down_gain, branch) * centred + line(down_shift, branch)
        result = sums[frame.pixels(slot, row), :] * silu_slope(normed)
        result = jnp.where(frame.inside(slot, row + 1), result, 0.0)
        incoming[0, slot, row] = result
        return result, result * centred

    frame.pack(packed, None, None, frame.summed(body), branch)


def lower_back_kernel(
    info, count, grads, shared, down, down_totals, down_back, down_gain, shared_grad, source, totals, gain,
    shift, lowered_grad, incoming, packed, far, wide, sums,
):
    branch = pl.program_id(0)
    slots, rows, breadth, channels = source.shape
    part = rows * breadth
    frame = Frame(info, slots, rows, breadth, channels)
    for slot in range(slots):
        wide[frame.span(slot), :] = dot(
            shared[slot, 1 : rows + 1].reshape(part, channels), down[0]
        )
    norm = NormBack(down_totals, down_back, line(down_gain, branch), branch, count[0])

    def back(slot, row):
        result = norm(
            grads[0, slot, row], wide[frame.pixels(slot, row), :], frame.inside(slot, row + 1)
        )
        lowered_grad[0, slot, row] = result.astype(BF16)

    frame.each(back)
    for slot in range(slots):
        span = frame.span(slot)
        term = dot_turned(lowered_grad[0, slot].reshape(part, -1), down[0])

        @pl.when(branch == 0)
        def _():
            sums[span, :] = term + shared_grad[slot].reshape(part, channels)

        @pl.when(branch > 0)
        def _():
            sums[span, :] += term

    @pl.when(branch == pl.num_programs(0) - 1)
    def _():
        average2, inverse2 = moments(totals, 0, count[0])

        def body(slot, row):
            centred = (source[slot, row] - average2) * inverse2
            normed = line(gain, 1) * centred + line(shift, 1)
            result = sums[frame.pixels(slot, row), :] * silu_slope(normed)
            result = jnp.where(frame.inside(slot, row + 1), result, 0.0)
            incoming[slot, row] = result
            return result, result * centred

        result = frame.summed(body)
        frame.pack(packed, far, lambda slot, row: incoming[slot, row], result)


def hidden_back_kernel(
    info, count, kept, sent, gain, shift, weight, first, first_totals, incoming, packed, far,
    three, sums, held, arrived,
):
    slots, rows, breadth, channels = sums.shape
    frame = Frame(info, slots, rows, breadth, channels)
    copies = weight_copies(weight, held, arrived, (1,))
    for copy in copies:
        copy.start()
    fill_halves(frame, kept, sent, three)
    for copy in copies:
        copy.wait()
    backward_conv(three, held, sums)
    average, inverse = moments(first_totals, 0, count[0])

    def body(slot, row):
        centred = (first[slot, row] - average) * inverse
        normed = line(gain, 0) * centred + line(shift, 0)
        result = sums[slot, row] * silu_slope(normed)
        result = jnp.where(frame.inside(slot, row + 1), result, 0.0)
        incoming[slot, row] = result
        return result, result * centred

    result = frame.summed(body)
    frame.pack(packed, far, lambda slot, row: incoming[slot, row], result)


def one_grad_kernel(
    info, count, grads, grad_near, grad_far, source, near, outer, totals, back, gain, kept, sent, member
):
    frame = Frame(info, *source.shape)
    fill_back(
        frame, count[0], grads, grad_near, grad_far, source, near, outer,
        totals, back, line(gain, member), None, kept, sent, (), 0,
    )


def input_back_kernel(info, kept, sent, weight, out, three, held, arrived):
    slots, rows, breadth, channels = out.shape
    frame = Frame(info, slots, rows, breadth, channels)
    copies = weight_copies(weight, held, arrived, (0,))
    for copy in copies:
        copy.start()
    fill_halves(frame, kept, sent, three)
    for copy in copies:
        copy.wait()
    backward_conv(three, held, out)

    def mask(slot, row):
        out[slot, row] = jnp.where(frame.inside(slot, row + 1), out[slot, row], 0.0)

    frame.each(mask)


def weight_grad_kernel(source, source_other, grads, grads_other, out, three):
    slots, tall, breadth, channels = grads.shape
    rows = tall - 2

    def put(row, carry):
        for slot in range(slots):
            put_three(three, slot, row, grads[slot, row].astype(F32), True)
            put_three(three, slots + slot, row, grads_other[slot, row].astype(F32), True)
        return carry

    lax.fori_loop(0, tall, put, 0)
    height = source.shape[3]
    for step in range(3):
        for tap in range(3):
            total = None
            for slot in range(2 * slots):
                left = source[slot] if slot < slots else source_other[slot - slots]
                lanes = slice(tap * channels, (tap + 1) * channels)
                window = three[slot, 2 - step : 2 - step + rows, :, lanes]
                one = dot_over_rows(
                    left.reshape(rows * breadth, height), window.reshape(rows * breadth, channels)
                )
                total = one if total is None else total + one
            start = (3 * step + tap) * height
            out[start : start + height, :] = total.astype(BF16)


def split_grad_kernel(info, source, source_other, grads, grads_other, *refs, cuts, bits_at):
    three, whole = refs[-2:]
    weight_grad_kernel(source, source_other, grads, grads_other, whole, three)
    width = whole.shape[1] // len(cuts)
    first = 0
    for index, (low, count) in enumerate(cuts):
        outs = refs[first : first + (1 << count)]
        first += 1 << count
        blocks, height, _ = outs[0].shape
        lanes = slice(index * width, (index + 1) * width)
        for flip, out in enumerate(outs):
            chosen = which_block(info, bits_at, low, count, flip)
            for block in range(blocks):
                start = ((block << count) + chosen) * height
                out[block] = whole[pl.ds(pl.multiple_of(start, 16), height), lanes]


def which_block(info, bits_at, low, count, flip):
    number = 0
    for index in range(count):
        bit = info[bits_at + low + index]
        number = number + ((1 - bit if flip >> index & 1 else bit) << index)
    return number


def spread_kernel(info, *refs, low, count, lanes, members, bits_at):
    terms, outs = refs[: -(1 << count)], refs[-(1 << count) :]
    each = len(terms) // members
    for flip, out in enumerate(outs):
        chosen = which_block(info, bits_at, low, count, flip)
        blocks = out.shape[0] // members
        for member in range(members):
            group = terms[member * each : (member + 1) * each]
            for block in range(blocks):
                place = member * blocks + block
                if each == 1:
                    out[place] = group[0][block, chosen, :, lanes]
                    continue
                total = group[0][block, chosen].astype(F32)
                for term in group[1:]:
                    total = total + term[block, chosen].astype(F32)
                out[place] = total.astype(BF16)


def relay_kernel(value, same):
    pass


def settle_kernel(*refs, plan):
    out = refs[-1]
    start = 0
    for row, height, columns, count in plan:
        terms = refs[start : start + count]
        start += count
        width = terms[0].shape[1]
        for column in range(columns):
            span = slice(column * height, (column + 1) * height)
            total = terms[0][span, :].astype(F32)
            for term in terms[1:]:
                total = total + term[span, :].astype(F32)
            lanes = slice(column * width, (column + 1) * width)
            out[row : row + height, lanes] = total.astype(BF16)


def thin_grad_kernel(info, shared, lowered_grad, raised_grad, squeezed, kept, sent, bits_at):
    slots, tall, _, channels = shared.shape
    odd = info[bits_at] == 1
    half = kept.shape[-1]

    def flat(block):
        return block.reshape(-1, block.shape[-1])

    for index in range(2):
        total = None
        for slot in range(slots):
            if index == 0:
                one = dot_over_rows(flat(shared[slot, 1 : tall - 1]), flat(lowered_grad[0, slot]))
            else:
                one = dot_over_rows(
                    flat(raised_grad[0, slot]), flat(squeezed[0, slot, 1 : tall - 1])
                )
            total = one if total is None else total + one
        low, high = total[:, :half], total[:, half:]
        kept[0, index] = jnp.where(odd, high, low).astype(BF16)
        sent[0, index] = jnp.where(odd, low, high).astype(BF16)


def join_kernel(info, *refs, bits_at):
    gathered = len(refs[0].shape) == 3
    pieces, outs = (refs[:1], refs[1:]) if gathered else (refs[:4], refs[4:])
    odd = info[bits_at] == 1
    upper = info[bits_at + 1]
    half = pieces[0].shape[-1]
    start = 0
    for out in outs:
        height = out.shape[2]
        for member in range(out.shape[0]):
            span = slice(start, start + height)
            for flip in range(2):
                if gathered:
                    for core in range(2):
                        lanes = slice(core * half, (core + 1) * half)
                        out[member, flip, :, lanes] = pieces[0][2 * flip + core, span, :].astype(F32)
                    continue
                mine = pieces[2 * flip][span, :].astype(F32)
                other = pieces[2 * flip + 1][span, :].astype(F32)
                row = jnp.where(upper == flip, 0, 1)
                out[member, row, :, :half] = jnp.where(odd, other, mine)
                out[member, row, :, half:] = jnp.where(odd, mine, other)
            start += height


def outputs_kernel(first, second, down, up, conv, *outs):
    for index in range(2):
        outs[index][0:1, :] = first[1 - index : 2 - index, :]
        outs[index][1:2, :] = second[1 - index : 2 - index, :]
    for place, totals in ((2, down), (4, up), (6, conv)):
        for member in range(outs[place].shape[0]):
            for index in range(2):
                row = 2 * member + 1 - index
                outs[place + index][member : member + 1, :] = totals[row : row + 1, :]


SCALARS = pl.BlockSpec(memory_space=pltpu.SMEM)
ELSEWHERE = pl.BlockSpec(memory_space=pl.ANY)


def fixed(shape):
    zeros = (0,) * len(shape)
    return pl.BlockSpec(tuple(shape), lambda *_: zeros)


def by_branch(shape):
    zeros = (0,) * (len(shape) - 1)
    return pl.BlockSpec((1,) + tuple(shape[1:]), lambda branch, *_: (branch,) + zeros)


def call(name, body, grid, inputs, outputs, scratch, flops, room=16, after=(), aliases={}):
    total = sum(a.size * a.dtype.itemsize for a, _ in inputs)
    if after:
        count, inner = len(inputs), body

        def body(*refs):
            inner(*refs[:count], *refs[count + len(after) :])

        inputs = inputs + [(a, ELSEWHERE) for a in after]
    return pl.pallas_call(
        body,
        name=name,
        grid=grid,
        in_specs=[s for _, s in inputs],
        out_specs=[s for _, _, s in outputs],
        out_shape=[jax.ShapeDtypeStruct(s, d) for s, d, _ in outputs],
        scratch_shapes=scratch,
        compiler_params=pltpu.CompilerParams(
            vmem_limit_bytes=room * MIB, dimension_semantics=("arbitrary",) * len(grid)
        ),
        input_output_aliases=aliases,
        cost_estimate=pl.CostEstimate(flops=flops, bytes_accessed=total, transcendentals=0),
    )(*[a for a, _ in inputs])


def whole(a):
    return (a, fixed(a.shape))


def branch_of(a):
    return (a, by_branch(a.shape))


def out(shape, dtype):
    return (tuple(shape), dtype, fixed(shape))


def out_branch(shape, dtype):
    return (tuple(shape), dtype, by_branch(shape))


def in_hbm(a):
    return (pltpu.with_memory_space_constraint(a, pltpu.HBM), ELSEWHERE)


class Halving:
    def __init__(self, reducer, parts, order, rows):
        self.reducer, self.order, self.rows = reducer, list(order), rows
        self.kept, self.sent = parts[0], parts[1:]
        self.columns = 1

    def received(self):
        low, _ = self.order[0]
        return [swapped(a, (flip + 1) << low) for flip, a in enumerate(self.sent)]

    def terms(self):
        return [self.kept] + self.received()

    def step(self):
        terms = self.terms()
        self.order = self.order[1:]
        self.kept, *self.sent = self.reducer.spread([terms], self.rows, self.order)


def merged(halvings, columns=1):
    first = halvings[0]
    groups = [one.terms() for one in halvings]
    order = first.order[1:]
    parts = first.reducer.spread(groups, first.rows, order)
    result = Halving(first.reducer, parts, order, first.rows)
    result.columns = columns
    return result


class Reducer:
    def __init__(self, info, bits_at):
        self.info = info
        self.bits_at = bits_at
        self.bits = places().bit_length() - 1
        self.dp = lax.axis_size("dp")
        self.last = ()
        assert lax.axis_size("rows") == 4

    def call(self, *args, after=(), **kwargs):
        result = call(*args, after=(*after, *self.last), **kwargs)
        self.last = tuple(result[-1:])
        return result

    def relay(self, value):
        return self.call(
            "relay",
            relay_kernel,
            (1,),
            [(value, ELSEWHERE)],
            [(value.shape, value.dtype, ELSEWHERE)],
            [],
            0,
            room=4,
            aliases={0: 0},
        )[0]

    def spread(self, groups, rows, order, after=(), lanes=None):
        low, count = order[0]
        height, width = self.block_rows(rows, order), groups[0][0].shape[-1]
        lanes = lanes or (0, width)
        view = (-1, 1 << count, height, width)
        terms = [term.reshape(view) for group in groups for term in group]
        blocks = terms[0].shape[0]
        steps = 1
        if len(groups) == 1:
            steps = next(n for n in (4, 3, 2, 1) if blocks % n == 0)

        def cut(shape):
            return pl.BlockSpec(
                (shape[0] // steps,) + shape[1:], lambda step: (step,) + (0,) * (len(shape) - 1)
            )

        result = (blocks * len(groups), height, lanes[1] - lanes[0])
        return self.call(
            "spread",
            functools.partial(
                spread_kernel,
                low=low,
                count=count,
                lanes=slice(*lanes),
                members=len(groups),
                bits_at=self.bits_at,
            ),
            (steps,),
            [(self.info, SCALARS)] + [(term, cut(term.shape)) for term in terms],
            [(result, BF16, cut(result))] * (1 << count),
            [],
            0,
            room=8,
            after=after,
        )

    def settle(self, halvings):
        arrays, plan, row = [], [], 0
        for one in halvings:
            flat = (-1, one.kept.shape[-1])
            terms = [term.reshape(flat) for term in one.terms()]
            height = terms[0].shape[0] // one.columns
            plan.append((row, height, one.columns, len(terms)))
            arrays += terms
            row += height
        width = arrays[0].shape[1] * halvings[0].columns
        return self.call(
            "settle",
            functools.partial(settle_kernel, plan=plan),
            (1,),
            [whole(a) for a in arrays],
            [out((row, width), BF16)],
            [],
            0,
            room=8,
        )[0]

    def order(self, axis):
        if axis == "xy":
            return [(low, min(2, self.bits - low)) for low in range(1, self.bits, 2)]
        rest = list(range(3, self.bits))
        order = {"x": [1, 2] + rest, "y": [2, 1] + rest, "z": rest + [1, 2]}[axis]
        return [(bit, 1) for bit in order]

    def block_rows(self, rows, order):
        below = sum(count for low, count in order if low < order[0][0])
        return rows << below

    def pieces(self, piece):
        beside = swapped(piece, 2)
        return [piece, swapped(piece, 1), beside, swapped(beside, 1)]

    def join(self, pieces, members):
        width = pieces[0].shape[-1]
        shapes = []
        for count, rows in members:
            shapes.append((count, 2, rows // 2, 2 * width))
        results = self.call(
            "join",
            functools.partial(join_kernel, bits_at=self.bits_at),
            (1,),
            [(self.info, SCALARS)] + [whole(piece) for piece in pieces],
            [out(shape, F32) for shape in shapes],
            [],
            0,
            room=12,
        )
        return [r.reshape(r.shape[0], -1, r.shape[-1]) for r in results]


def local(
    images,
    size_ids,
    shared_conv,
    task_conv,
    task_down,
    task_up,
    shared_gain,
    shared_shift,
    down_gain,
    down_shift,
    up_gain,
    up_shift,
    conv_gain,
    conv_shift,
    cotangent,
):
    slots, rows, breadth, channels = images.shape
    tasks = task_conv.shape[0]
    tall = rows + 2
    part = rows * breadth
    half = channels // 2
    heights_all = jnp.where(size_ids == 0, H_BIG, H_SMALL).astype(jnp.int32)
    breadths_all = jnp.where(size_ids == 0, W_BIG, W_SMALL).astype(jnp.int32)
    count = jnp.sum(heights_all * breadths_all).astype(F32).reshape(1)
    first_slot = lax.axis_index("dp") * slots
    heights = lax.dynamic_slice_in_dim(heights_all, first_slot, slots)
    breadths = lax.dynamic_slice_in_dim(breadths_all, first_slot, slots)
    row_place = lax.axis_index("rows") * rows + jnp.arange(-1, rows + 1, dtype=jnp.int32)
    within = (row_place[None, :] >= 0) & (row_place[None, :] < heights[:, None])
    limits = jnp.where(within, breadths[:, None], 0).astype(jnp.int32).reshape(-1)
    bits_at = slots * tall
    place = lax.axis_index("dp") * lax.axis_size("rows") + lax.axis_index("rows")
    bits = (place >> jnp.arange(places().bit_length() - 1, dtype=jnp.int32)) & 1
    info = jnp.concatenate([limits, bits.astype(jnp.int32)])
    scalars = [(info, SCALARS), (count, SCALARS)]

    map_shape = (slots, rows, breadth, channels)
    tall_shape = (slots, tall, breadth, channels)
    half_shape = (slots, tall, breadth, half)
    conv_flops = 2 * slots * part * 9 * channels * channels
    thin_flops = conv_flops // 9

    def all_tasks(shape):
        return (tasks,) + tuple(shape)

    def sums_only():
        return out((SUMS, channels), F32)

    def packed(groups):
        return [
            out((groups * slots * breadth + SUMS, channels), F32),
            out((groups * slots, breadth, channels), F32 if groups == 1 else BF16),
        ]

    three = pltpu.VMEM((slots, tall, breadth, 3 * channels), BF16)
    flat = pltpu.VMEM((slots * part, channels), F32)
    flat_tall = pltpu.VMEM((slots * tall * breadth, channels), F32)
    square = pltpu.VMEM(map_shape, F32)
    one_weight = [pltpu.VMEM((9 * channels, channels), BF16), pltpu.SemaphoreType.DMA((3,))]
    two_weights = [pltpu.VMEM((2, 9 * channels, channels), BF16), pltpu.SemaphoreType.DMA((2, 3))]

    count_rows = lax.axis_size("rows")
    image_above = lax.ppermute(
        images[:, rows - 1], "rows", [(i, i + 1) for i in range(count_rows - 1)]
    )
    image_below = lax.ppermute(images[:, 0], "rows", [(i + 1, i) for i in range(count_rows - 1)])
    first_out, first_packed, first_far, masked = call(
        "first_conv",
        first_kernel,
        (1,),
        [scalars[0], whole(images), whole(image_above), whole(image_below), in_hbm(shared_conv)],
        [out(map_shape, F32)] + packed(1) + [out(map_shape, BF16)],
        [three] + one_weight,
        conv_flops,
    )
    first_totals, first_near, first_outer = norm_totals(first_packed, first_far)

    second_out, second_packed, second_far, hidden = call(
        "second_conv",
        second_kernel,
        (1,),
        scalars
        + [whole(a) for a in (first_out, first_near, first_outer, first_totals)]
        + [whole(shared_gain), whole(shared_shift), in_hbm(shared_conv)],
        [out(map_shape, F32)] + packed(1) + [out(map_shape, BF16)],
        [three] + one_weight,
        conv_flops,
    )
    second_totals, second_near, second_outer = norm_totals(second_packed, second_far)

    shared, down_packed = call(
        "lower",
        lower_kernel,
        (tasks,),
        scalars
        + [whole(a) for a in (second_out, second_near, second_outer, second_totals)]
        + [whole(shared_gain), whole(shared_shift), branch_of(task_down)],
        [out(tall_shape, BF16), sums_only()],
        [flat],
        3 * thin_flops,
    )
    down_totals = norm_totals(down_packed)

    squeezed, up_packed = call(
        "raise",
        raise_kernel,
        (tasks,),
        scalars
        + [whole(shared), branch_of(task_down), branch_of(task_up)]
        + [whole(a) for a in (down_totals, down_gain, down_shift)],
        [out_branch(all_tasks(tall_shape), BF16), sums_only()],
        [flat_tall, flat],
        6 * thin_flops,
    )
    up_totals = norm_totals(up_packed)

    conv_out, conv_packed, conv_far, gated = call(
        "task_conv",
        task_kernel,
        (tasks,),
        scalars
        + [branch_of(squeezed), branch_of(task_up)]
        + [whole(a) for a in (shared, up_totals, up_gain, up_shift)]
        + [in_hbm(task_conv)],
        [out_branch(all_tasks(map_shape), F32)]
        + packed(tasks)
        + [out_branch(all_tasks(map_shape), BF16)],
        [flat_tall, three] + two_weights,
        tasks * conv_flops,
        room=22,
    )
    conv_totals, conv_near, conv_outer = norm_totals(conv_packed, conv_far)

    maps, conv_grad, conv_back_packed, conv_grad_far = call(
        "pool",
        pool_kernel,
        (tasks,),
        scalars
        + [branch_of(conv_out), branch_of(cotangent)]
        + [whole(a) for a in (conv_totals, conv_gain, conv_shift)],
        [
            out_branch(all_tasks((slots, rows // 2, breadth // 2, channels)), BF16),
            out_branch(all_tasks(map_shape), F32),
        ]
        + packed(tasks),
        [pltpu.VMEM((slots, channels // 128, breadth, 128), F32)] * 2,
        thin_flops,
    )
    conv_back, conv_grad_near, conv_grad_outer = norm_totals(conv_back_packed, conv_grad_far)

    reducer = Reducer(info, bits_at)
    dp_count = reducer.dp
    wide_rows = 9 * channels // dp_count

    share_rows = wide_rows // 2

    def weight_whole(source, source_other, kept, sent, after=()):
        return reducer.call(
            "weight_grad",
            weight_grad_kernel,
            (1,),
            [whole(a) for a in (source, source_other, kept, swapped(sent, 1))],
            [out((9 * channels, half), BF16)],
            [pltpu.VMEM((2 * slots, tall, breadth, 3 * half), BF16)],
            conv_flops,
            after=after,
        )[0]

    def weight_sum(source, source_other, kept, sent, axes, after=()):
        orders = [reducer.order(axis) for axis in axes]
        width = half // len(orders)
        if share_rows % 16:
            total = weight_whole(source, source_other, kept, sent, after)
            parts = [
                reducer.spread([[total]], share_rows, order, (), (index * width, (index + 1) * width))
                for index, order in enumerate(orders)
            ]
        else:
            shapes = []
            for order in orders:
                height = reducer.block_rows(share_rows, order)
                shape = ((9 * channels // height) >> order[0][1], height, width)
                shapes += [shape] * (1 << order[0][1])
            results = reducer.call(
                "weight_grad",
                functools.partial(
                    split_grad_kernel, cuts=[order[0] for order in orders], bits_at=bits_at
                ),
                (1,),
                [(info, SCALARS)]
                + [whole(a) for a in (source, source_other, kept, swapped(sent, 1))],
                [out(shape, BF16) for shape in shapes],
                [
                    pltpu.VMEM((2 * slots, tall, breadth, 3 * half), BF16),
                    pltpu.VMEM((9 * channels, half), BF16),
                ],
                conv_flops,
                after=after,
            )
            parts = []
            for order in orders:
                parts.append(results[: 1 << order[0][1]])
                results = results[1 << order[0][1] :]
        return [Halving(reducer, part, order, share_rows) for part, order in zip(parts, orders)]

    masked_other, hidden_other, gated_other = (swapped(a, 1) for a in (masked, hidden, gated))

    conv_kept, conv_sent = reducer.call(
        "conv_grad",
        conv_grad_kernel,
        (tasks,),
        scalars
        + [branch_of(conv_grad), whole(conv_grad_near), whole(conv_grad_outer)]
        + [branch_of(conv_out), whole(conv_near), whole(conv_outer)]
        + [whole(a) for a in (conv_totals, conv_back, conv_gain)],
        [out_branch(all_tasks(half_shape), BF16)] * 2,
        [],
        0,
    )

    def step(*halvings):
        for one in halvings:
            one.step()

    def task_grads(t):
        return gated[t], gated_other[t], conv_kept[t], conv_sent[t]

    early = [weight_sum(*task_grads(t), ["xy"[t]])[0] for t in range(2)]
    up_grad_in, shared_grad, up_back_packed = reducer.call(
        "gate_back",
        gate_back_kernel,
        (tasks,),
        scalars
        + [branch_of(conv_kept), branch_of(conv_sent)]
        + [in_hbm(task_conv), branch_of(squeezed), branch_of(task_up)]
        + [whole(a) for a in (shared, up_totals, up_gain, up_shift)],
        [
            out_branch(all_tasks(map_shape), F32),
            out(map_shape, F32),
            sums_only(),
        ],
        [three, square, flat] + two_weights,
        tasks * conv_flops,
        room=22,
        after=[masked_other, hidden_other],
    )
    step(*early)
    up_back = norm_totals(reducer.relay(up_back_packed))
    raised_grad, down_grad_in, down_back_packed = reducer.call(
        "raise_back",
        raise_back_kernel,
        (tasks,),
        scalars
        + [branch_of(up_grad_in), branch_of(squeezed), branch_of(task_up), whole(shared)]
        + [branch_of(task_down)]
        + [
            whole(a)
            for a in (up_totals, up_back, up_gain, down_totals, down_gain, down_shift)
        ],
        [
            out_branch(all_tasks(map_shape), BF16),
            out_branch(all_tasks(map_shape), F32),
            sums_only(),
        ],
        [flat, flat],
        9 * thin_flops,
    )
    early = merged(early)
    down_back = norm_totals(reducer.relay(down_back_packed))
    late = weight_sum(*task_grads(2), "xy", after=[down_back])

    lowered_grad, second_grad, second_back_packed, second_grad_far = reducer.call(
        "lower_back",
        lower_back_kernel,
        (tasks,),
        scalars
        + [branch_of(down_grad_in), whole(shared), branch_of(task_down)]
        + [whole(a) for a in (down_totals, down_back, down_gain, shared_grad, second_out)]
        + [whole(a) for a in (second_totals, shared_gain, shared_shift)],
        [out_branch(all_tasks(map_shape), BF16), out(map_shape, F32)] + packed(1),
        [flat, flat],
        6 * thin_flops,
    )
    square_shape = (tasks, 2, channels, half)
    thin_kept, thin_sent = reducer.call(
        "thin_grad",
        functools.partial(thin_grad_kernel, bits_at=bits_at),
        (tasks,),
        [(info, SCALARS), whole(shared)]
        + [branch_of(a) for a in (lowered_grad, raised_grad, squeezed)],
        [out_branch(square_shape, BF16)] * 2,
        [],
        6 * thin_flops,
    )
    thin_got = swapped(thin_sent, 1)
    step(early, *late)
    second_back, second_grad_near, second_grad_outer = norm_totals(
        reducer.relay(second_back_packed), second_grad_far
    )

    second_kept, second_sent = reducer.call(
        "second_grad",
        functools.partial(one_grad_kernel, member=1),
        (1,),
        scalars
        + [
            whole(a)
            for a in (
                second_grad, second_grad_near, second_grad_outer, second_out, second_near, second_outer,
                second_totals, second_back, shared_gain,
            )
        ],
        [out(half_shape, BF16)] * 2,
        [],
        0,
    )
    second_sum = weight_sum(hidden, hidden_other, second_kept, second_sent, "xy")
    late = merged(late, 2)
    thin_order = reducer.order("y")
    thin_rows = channels // dp_count // 2
    thin_parts = reducer.spread([[thin_kept, thin_got]], thin_rows, thin_order)
    thin = Halving(reducer, thin_parts, thin_order, thin_rows)
    first_grad, first_back_packed, first_grad_far = reducer.call(
        "hidden_back",
        hidden_back_kernel,
        (1,),
        scalars
        + [whole(second_kept), whole(second_sent), whole(shared_gain), whole(shared_shift)]
        + [in_hbm(shared_conv), whole(first_out), whole(first_totals)],
        [out(map_shape, F32)] + packed(1),
        [three, square] + one_weight,
        conv_flops,
    )
    step(*second_sum, late)
    first_back, first_grad_near, first_grad_outer = norm_totals(
        reducer.relay(first_back_packed), first_grad_far
    )

    first_kept, first_sent = reducer.call(
        "first_grad",
        functools.partial(one_grad_kernel, member=0),
        (1,),
        scalars
        + [
            whole(a)
            for a in (
                first_grad, first_grad_near, first_grad_outer, first_out, first_near, first_outer,
                first_totals, first_back, shared_gain,
            )
        ],
        [out(half_shape, BF16)] * 2,
        [],
        0,
    )
    first_sum = weight_sum(masked, masked_other, first_kept, first_sent, ["xy"])

    task_share = reducer.settle([early, late])
    second_sum = merged(second_sum, 2)
    step(thin, *first_sum)
    step(second_sum, thin)
    (input_grad,) = reducer.call(
        "input_back",
        input_back_kernel,
        (1,),
        [scalars[0], whole(first_kept), whole(first_sent), in_hbm(shared_conv)],
        [out(map_shape, F32)],
        [three] + one_weight,
        conv_flops,
    )

    step(thin)
    shared_sums, thin_sums = reducer.join(
        reducer.pieces(reducer.settle(first_sum + [second_sum, thin])),
        [(2, wide_rows), (2 * tasks, channels // dp_count)],
    )
    (task_sums,) = reducer.join([lax.all_gather(task_share, "rows")], [(tasks, wide_rows)])

    pair_shape = (2, channels)
    many_shape = (tasks, channels)
    small = call(
        "outputs",
        outputs_kernel,
        (1,),
        [whole(a) for a in (first_back, second_back, down_back, up_back, conv_back)],
        [out(pair_shape, F32)] * 2 + [out(many_shape, F32)] * 6,
        [],
        0,
        room=4,
    )
    return (
        maps,
        input_grad,
        shared_sums,
        task_sums,
        thin_sums[0::2],
        thin_sums[1::2].transpose(0, 2, 1),
        *small,
    )


def solution(mesh):
    placed = (P("dp", "rows", None, None),) + (P(),) * 13 + (P(None, "dp", "rows", None, None),)
    return jax.shard_map(
        local,
        mesh=mesh,
        in_specs=placed,
        out_specs=(
            P(None, "dp", "rows", None, None),
            P("dp", "rows", None, None),
            P(None, "dp", None),
            P(None, "dp", None),
            P(None, "dp", None),
            P(None, None, "dp"),
        )
        + (P(),) * 8,
        check_vma=False,
    )
```

time: 1790 us -> 500 us (0.28)
  waiting for transfers between devices: 760 us -> 133 us
  blocking collectives: 539 us -> 0 us
  Pallas kernels: 0 us -> 189 us
  matrix products: 187 us -> 0 us
  local copies, waits for them, and re-layouts: 129 us -> 15.4 us
  other arithmetic: 110 us -> 1.66 us
  starting transfers between devices: 36.3 us -> 139 us
    reduce_scatter x4 -> x0, waiting for transfers between devices: 691 us -> none  [the longest x1 450 us: local(): lax.psum_scatter(conv_stack, 'dp', scatter_dimension=1, tiled=True)]
    psum x13 -> x0, blocking collectives: 539 us -> none  [the longest x8 331 us: moment_totals(): return lax.psum(stacked, ('dp', 'rows'))]
    pallas_call x0 -> x46, Pallas kernels: none -> 189 us  [call(): pl.pallas_call(body, name=name, grid=grid, in_specs=[s for _, s in inputs...]
    dot_general x33 -> x0, matrix products: 187 us -> none  [the longest x5 53.5 us: conv_apply(): result = jnp.dot(columns, weight, preferred_element_type=jnp.float32)]
    ppermute x20 -> x118, waiting for transfers between devices: 11.6 us -> 133 us  [the longest x110 131 us: swapped(): return lax.ppermute(values, AXES, [(i, i ^ flip) for i in range(places())])]
    ppermute x20 -> x118, starting transfers between devices: 36.1 us -> 139 us  [the longest x110 131 us: swapped(): return lax.ppermute(values, AXES, [(i, i ^ flip) for i in range(places())])]
    psum x1 -> x0, waiting for transfers between devices: 56.4 us -> none  [local(): lax.psum(spread[0].astype(jnp.bfloat16), 'rows').astype(jnp.float32)]
    convert_element_type x22 -> x0, other arithmetic: 47.7 us -> none  [the longest x9 23.6 us: restore(): (gains[member] * inverse * (grad_out - correction)).astype(jnp.bfloat16)]
  transfers between devices with their start and end apart: 25 -> 119, of which waited for: 7 -> 72; matrix products, arithmetic and copies ran while one was open for 13% -> 1% of each run, Pallas kernels for 0% -> 26%
where the time goes in v3:
time: 500 us; the launch traced here: 495 us
  Pallas kernels  189 us (38%)
  starting transfers between devices  139 us (28%)
  waiting for transfers between devices  133 us (27%)
  between operations  16.4 us (3%)
  local copies, waits for them, and re-layouts  15.4 us (3%)
    pallas_call x46, Pallas kernels, call(): pl.pallas_call(body, name=name, grid=grid, in_specs=[s for _, s in inputs...  189 us
    ppermute x110, starting transfers between devices, swapped(): return lax.ppermute(values, AXES, [(i, i ^ flip) for i in range(places())])  131 us
    ppermute x110, waiting for transfers between devices, swapped(): return lax.ppermute(values, AXES, [(i, i ^ flip) for i in range(places())])  131 us
    unnamed x102, local copies, waits for them, and re-layouts  10.7 us
  transfers between devices with their start and end apart: 119, of which 72 were waited for; matrix products, arithmetic and copies ran while one was open for 1% of the time, Pallas kernels for 26%

profile of v3, /device:TPU:0, one launch (start us, length us, event | category | flops | bytes accessed | tf_op | source)
XLA Modules:
  0.0 494.6 jit_solution(17636284259594922845)
XLA Ops:
  8.2 2.4 collective-permute-start
  17.1 8.0 %first_conv.1 = (f32[2,10,48,512]{3,2,1,0:T(8,128)S(1)}, f32[104,512]{1,0:T(8,128)S(1)}, f32[2,48,512]{2,1,0:T(8,128)S(1)}, bf16[2,10,48,512]{3,2,1,0:T(8,128)(2,1)S(1)}) custom-call(s32[29]{0:T(128)S(1)} %pad_add_fusion.info.refs_0_, bf16[2,10,48,512]{3,2,1,0:T(8,128)(2,1)S(1)} %copy-done.21, bf16[2,48,512]{2,1,0:T(8,128)(2,1)S(1)} %collective-permute-done.above, ...), custom_call_target="tpu_custom_call" | custom-call | flops 4529848320 | bytes 10616948 | tf_op jit(solution)/shard_map/first_conv/pallas_call | solution.py:860
  26.0 3.2 collective-permute-start.2
  34.1 2.4 collective-permute-done.6
  36.5 2.7 collective-permute-start.8
  42.1 2.6 collective-permute-done.9
  44.8 8.9 %second_conv.1 = (f32[2,10,48,512]{3,2,1,0:T(8,128)S(1)}, f32[104,512]{1,0:T(8,128)S(1)}, f32[2,48,512]{2,1,0:T(8,128)S(1)}, bf16[2,10,48,512]{3,2,1,0:T(8,128)(2,1)}) custom-call(s32[29]{0:T(128)S(1)} %pad_add_fusion.info.refs_0_, f32[1]{0:T(128)} %bitcast.count.refs_1_, f32[2,10,48,512]{3,2,1,0:T(8,128)S(1)} %get-tuple-element.117.source.refs_7_.refs_5_, ...), custom_call_target="tpu_custom_call" | custom-call | flops 4529848320 | bytes 11837560 | tf_op jit(solution)/shard_map/second_conv/pallas_call | solution.py:860
  53.7 3.1 collective-permute-start.10
  61.7 2.4 collective-permute-done.14
  65.1 2.9 collective-permute-start.16
  70.3 3.3 collective-permute-done.17
  73.6 4.5 lower.1
  81.9 2.7 collective-permute-start.21
  88.3 3.1 collective-permute-start.23
  93.1 3.8 collective-permute-done.24
  97.0 9.1 %raise.1 = (bf16[3,2,12,48,512]{4,3,2,1,0:T(8,128)(2,1)S(1)}, f32[8,512]{1,0:T(8,128)S(1)}) custom-call(s32[29]{0:T(128)S(1)} %pad_add_fusion.info.refs_0_, f32[1]{0:T(128)} %bitcast.count.refs_1_, bf16[2,12,48,512]{3,2,1,0:T(8,128)(2,1)S(1)} %get-tuple-element.123.shared.refs_7_.refs_5_.refs_3_.refs_1_, bf16[3,512,512]{2,1,0:T(8,128)(2,1)S(1)} %copy-done.2, ...), custom_call_target="tpu_custom_call" | custom-call | flops 3019898880 | bytes 4354168 | tf_op jit(solution)/shard_map/raise/pallas_call | solution.py:860
  119.1 22.8 %task_conv.1 = (f32[3,2,10,48,512]{4,3,2,1,0:T(8,128)S(1)}, f32[296,512]{1,0:T(8,128)S(1)}, bf16[6,48,512]{2,1,0:T(8,128)(2,1)S(1)}, bf16[3,2,10,48,512]{4,3,2,1,0:T(8,128)(2,1)S(1)}) custom-call(s32[29]{0:T(128)S(1)} %pad_add_fusion.info.refs_0_, f32[1]{0:T(128)} %bitcast.count.refs_1_, ...), custom_call_target="tpu_custom_call" | custom-call | flops 13589544960 | bytes 20476024 | tf_op jit(solution)/shard_map/task_conv/pallas_call | solution.py:860
  156.0 2.4 collective-permute-done.38
  158.5 6.7 %pool.1 = (bf16[3,2,5,24,512]{4,3,2,1,0:T(8,128)(2,1)}, f32[3,2,10,48,512]{4,3,2,1,0:T(8,128)S(1)}, f32[296,512]{1,0:T(8,128)S(1)}, bf16[6,48,512]{2,1,0:T(8,128)(2,1)S(1)}) custom-call(s32[29]{0:T(128)S(1)} %pad_add_fusion.info.refs_0_, f32[1]{0:T(128)} %bitcast.count.refs_1_, f32[3,2,10,48,512]{4,3,2,1,0:T(8,128)S(1)} %get-tuple-element.127.source, ...), custom_call_target="tpu_custom_call" | custom-call | flops 503316480 | bytes 6664312 | tf_op jit(solution)/shard_map/pool/pallas_call | solution.py:860
  178.0 2.3 collective-permute-done.47
  180.4 3.3 collective-permute-start.48
  183.8 3.2 conv_grad.1
  191.2 6.4 %weight_grad.5 = (bf16[8,288,256]{2,1,0:T(8,128)(2,1)S(1)}, bf16[8,288,256]{2,1,0:T(8,128)(2,1)S(1)}) custom-call(s32[29]{0:T(128)S(1)} %pad_add_fusion.info.refs_0_, bf16[2,10,48,512]{3,2,1,0:T(8,128)(2,1)S(1)} %get-tuple-element.224.refs_1_, bf16[2,10,48,512]{3,2,1,0:T(8,128)(2,1)S(1)} %get-tuple-element.221.refs_2_, ...), custom_call_target="tpu_custom_call" | custom-call | flops 4529848320 | bytes 3145844 | tf_op jit(solution)/shard_map/weight_grad/pallas_call | solution.py:860
  199.8 6.4 %weight_grad.6 = (bf16[4,576,256]{2,1,0:T(8,128)(2,1)S(1)}, bf16[4,576,256]{2,1,0:T(8,128)(2,1)S(1)}) custom-call(s32[29]{0:T(128)S(1)} %pad_add_fusion.info.refs_0_, bf16[2,10,48,512]{3,2,1,0:T(8,128)(2,1)S(1)} %get-tuple-element.225.refs_1_, bf16[2,10,48,512]{3,2,1,0:T(8,128)(2,1)S(1)} %get-tuple-element.222.refs_2_, ...), custom_call_target="tpu_custom_call" | custom-call | flops 4529848320 | bytes 3145844 | tf_op jit(solution)/shard_map/weight_grad/pallas_call | solution.py:860
  211.3 24.9 %gate_back.1 = (f32[3,2,10,48,512]{4,3,2,1,0:T(8,128)S(1)}, f32[2,10,48,512]{3,2,1,0:T(8,128)S(1)}, f32[8,512]{1,0:T(8,128)S(1)}) custom-call(s32[29]{0:T(128)S(1)} %pad_add_fusion.info.refs_0_, f32[1]{0:T(128)} %bitcast.count.refs_1_, bf16[3,2,12,48,256]{4,3,2,1,0:T(8,128)(2,1)S(1)} %get-tuple-element.134.refs_2_, ...), custom_call_target="tpu_custom_call" | custom-call | flops 13589544960 | bytes 24014968 | tf_op jit(solution)/shard_map/gate_back/pallas_call | solution.py:860
  252.8 12.1 %raise_back.1 = (bf16[3,2,10,48,512]{4,3,2,1,0:T(8,128)(2,1)S(1)}, f32[3,2,10,48,512]{4,3,2,1,0:T(8,128)S(1)}, f32[8,512]{1,0:T(8,128)S(1)}) custom-call(s32[29]{0:T(128)S(1)} %pad_add_fusion.info.refs_0_, f32[1]{0:T(128)} %bitcast.count.refs_1_, f32[3,2,10,48,512]{4,3,2,1,0:T(8,128)S(1)} %get-tuple-element.141.refs_2_, ...), custom_call_target="tpu_custom_call" | custom-call | flops 4529848320 | bytes 13830264 | tf_op jit(solution)/shard_map/raise_back/pallas_call | solution.py:860
  274.2 2.6 collective-permute-start.69
  282.8 6.9 %weight_grad.7 = (bf16[8,288,128]{2,1,0:T(8,128)(2,1)S(1)}, bf16[8,288,128]{2,1,0:T(8,128)(2,1)S(1)}, bf16[4,576,128]{2,1,0:T(8,128)(2,1)S(1)}, bf16[4,576,128]{2,1,0:T(8,128)(2,1)S(1)}) custom-call(s32[29]{0:T(128)S(1)} %pad_add_fusion.info.refs_0_, bf16[2,10,48,512]{3,2,1,0:T(8,128)(2,1)S(1)} %get-tuple-element.223.refs_1_, ...), custom_call_target="tpu_custom_call" | custom-call | flops 4529848320 | bytes 3145844 | tf_op jit(solution)/shard_map/weight_grad/pallas_call | solution.py:860
  291.2 9.1 %lower_back.1 = (bf16[3,2,10,48,512]{4,3,2,1,0:T(8,128)(2,1)S(1)}, f32[2,10,48,512]{3,2,1,0:T(8,128)S(1)}, f32[104,512]{1,0:T(8,128)S(1)}, f32[2,48,512]{2,1,0:T(8,128)S(1)}) custom-call(s32[29]{0:T(128)S(1)} %pad_add_fusion.info.refs_0_, f32[1]{0:T(128)} %bitcast.count.refs_1_, f32[3,2,10,48,512]{4,3,2,1,0:T(8,128)S(1)} %get-tuple-element.147.refs_2_, ...), custom_call_target="tpu_custom_call" | custom-call | flops 3019898880 | bytes 12646520 | tf_op jit(solution)/shard_map/lower_back/pallas_call | solution.py:860
  300.3 4.5 thin_grad.1
  323.3 3.2 collective-permute-start.86
  329.5 7.3 %weight_grad.8 = (bf16[8,288,128]{2,1,0:T(8,128)(2,1)S(1)}, bf16[8,288,128]{2,1,0:T(8,128)(2,1)S(1)}, bf16[4,576,128]{2,1,0:T(8,128)(2,1)S(1)}, bf16[4,576,128]{2,1,0:T(8,128)(2,1)S(1)}) custom-call(s32[29]{0:T(128)S(1)} %pad_add_fusion.info.refs_0_, bf16[2,10,48,512]{3,2,1,0:T(8,128)(2,1)} %get-tuple-element.137.refs_1_, ...), custom_call_target="tpu_custom_call" | custom-call | flops 4529848320 | bytes 3145844 | tf_op jit(solution)/shard_map/weight_grad/pallas_call | solution.py:860
  342.8 9.0 %hidden_back.1 = (f32[2,10,48,512]{3,2,1,0:T(8,128)S(1)}, f32[104,512]{1,0:T(8,128)S(1)}, f32[2,48,512]{2,1,0:T(8,128)S(1)}) custom-call(s32[29]{0:T(128)S(1)} %pad_add_fusion.info.refs_0_, f32[1]{0:T(128)} %bitcast.count.refs_1_, bf16[2,12,48,256]{3,2,1,0:T(8,128)(2,1)S(1)} %get-tuple-element.167.refs_3_.refs_2_, ...), custom_call_target="tpu_custom_call" | custom-call | flops 4529848320 | bytes 12607608 | tf_op jit(solution)/shard_map/hidden_back/pallas_call | solution.py:860
  366.7 2.5 collective-permute-done.97
  371.0 2.7 collective-permute-start.103
  373.7 2.5 collective-permute-start.101
  377.7 6.4 %weight_grad.9 = (bf16[4,288,256]{2,1,0:T(8,128)(2,1)S(1)}, bf16[4,288,256]{2,1,0:T(8,128)(2,1)S(1)}, bf16[4,288,256]{2,1,0:T(8,128)(2,1)S(1)}, bf16[4,288,256]{2,1,0:T(8,128)(2,1)S(1)}) custom-call(s32[29]{0:T(128)S(1)} %pad_add_fusion.info.refs_0_, bf16[2,10,48,512]{3,2,1,0:T(8,128)(2,1)S(1)} %copy-done.32, bf16[2,10,48,512]{3,2,1,0:T(8,128)(2,1)S(1)} %copy-done.35, ...), custom_call_target="tpu_custom_call" | custom-call | flops 4529848320 | bytes 3145844 | tf_op jit(solution)/shard_map/weight_grad/pallas_call | solution.py:860
  384.2 9.8 %collective-permute-done.101 = bf16[2,288,256]{2,1,0:T(8,128)(2,1)S(1)} collective-permute-done((bf16[2,288,256]{2,1,0:T(8,128)(2,1)S(1)}, bf16[2,288,256]{2,1,0:T(8,128)(2,1)S(1)}, u32[]{:S(2)}, u32[]{:S(2)}) %collective-permute-start.101) | collective-permute-done | bytes 294944 | tf_op jit(solution)/shard_map/ppermute | solution.py:27
  401.4 6.0 %collective-permute-done.99 = bf16[4,288,128]{2,1,0:T(8,128)(2,1)S(1)} collective-permute-done((bf16[4,288,128]{2,1,0:T(8,128)(2,1)}, bf16[4,288,128]{2,1,0:T(8,128)(2,1)S(1)}, u32[]{:S(2)}, u32[]{:S(2)}) %collective-permute-start.99) | collective-permute-done | bytes 294944 | tf_op jit(solution)/shard_map/ppermute | solution.py:27
  407.4 2.5 collective-permute-start.108
  413.4 2.5 collective-permute-start.104
  416.0 14.4 %collective-permute-done.106 = bf16[4,288,256]{2,1,0:T(8,128)(2,1)S(1)} collective-permute-done((bf16[4,288,256]{2,1,0:T(8,128)(2,1)}, bf16[4,288,256]{2,1,0:T(8,128)(2,1)S(1)}, u32[]{:S(2)}, u32[]{:S(2)}) %collective-permute-start.106) | collective-permute-done | bytes 589856 | tf_op jit(solution)/shard_map/ppermute | solution.py:27
  430.4 13.0 %collective-permute-done.108 = bf16[4,288,256]{2,1,0:T(8,128)(2,1)S(1)} collective-permute-done((bf16[4,288,256]{2,1,0:T(8,128)(2,1)S(1)}, bf16[4,288,256]{2,1,0:T(8,128)(2,1)S(1)}, u32[]{:S(2)}, u32[]{:S(2)}) %collective-permute-start.108) | collective-permute-done | bytes 589856 | tf_op jit(solution)/shard_map/ppermute | solution.py:27
  444.4 2.5 collective-permute-start.110
  452.8 9.1 %input_back.1.refs_3_ = f32[2,10,48,512]{3,2,1,0:T(8,128)} custom-call(s32[29]{0:T(128)S(1)} %pad_add_fusion.info.refs_0_, bf16[2,12,48,256]{3,2,1,0:T(8,128)(2,1)S(1)} %copy-done.40, bf16[2,12,48,256]{3,2,1,0:T(8,128)(2,1)S(1)} %copy-done.42, bf16[2,4608,512]{2,1,0:T(8,128)(2,1)} %refs_3_.1, bf16[12,32,256]{2,1,0:T(8,128)(2,1)S(1)} %get-tuple-element.202.refs_4_), custom_call_target="tpu_custom_call" | custom-call | flops 4529848320 | bytes 10616948 | tf_op jit(solution)/shard_map/input_back/pallas_call | solution.py:860
  464.9 5.5 %collective-permute-done.114 = bf16[6,32,256]{2,1,0:T(8,128)(2,1)S(1)} collective-permute-done((bf16[6,32,256]{2,1,0:T(8,128)(2,1)S(1)}, bf16[6,32,256]{2,1,0:T(8,128)(2,1)S(1)}, u32[]{:S(2)}, u32[]{:S(2)}) %collective-permute-start.114) | collective-permute-done | bytes 98336 | tf_op jit(solution)/shard_map/ppermute | solution.py:27
  472.5 5.9 %collective-permute-done.116.refs_3_ = bf16[768,256]{1,0:T(8,128)(2,1)S(1)} collective-permute-done((bf16[768,256]{1,0:T(8,128)(2,1)S(1)}, bf16[768,256]{1,0:T(8,128)(2,1)S(1)}, u32[]{:S(2)}, u32[]{:S(2)}) %collective-permute-start.116) | collective-permute-done | bytes 393248 | tf_op jit(solution)/shard_map/ppermute | solution.py:27
  484.7 2.6 join.3
  (384 shorter events, 191.9 us)
Async XLA Ops:
  7.2 476.1 %all-gather.3.cloned.1.call-start = ((), (), s32[]{:S(2)}) async-start(), calls=%async_computation | async-start | bytes 2211840 | tf_op jit(solution)/shard_map/all_gather | solution.py:1418
  36.5 5.6 %collective-permute-start.8 = (f32[8,512]{1,0:T(8,128)S(1)}, f32[8,512]{1,0:T(8,128)S(1)}, u32[]{:S(2)}, u32[]{:S(2)}) collective-permute-start(f32[8,512]{1,0:T(8,128)S(1)} %add_add_fusion.19), channel_id=1, source_target_pairs={{0,16},{1,17},{2,18},{3,19},{4,20},{5,21},{6,22},{7,23},{8,24},{9,... | collective-permute-start | bytes 49160 | tf_op jit(solution)/shard_map/ppermute | solution.py:27
  142.1 46.9 %collective-permute-start.50 = (bf16[3,2,10,48,512]{4,3,2,1,0:T(8,128)(2,1)S(1)}, bf16[3,2,10,48,512]{4,3,2,1,0:T(8,128)(2,1)}, u32[]{:S(2)}, u32[]{:S(2)}) collective-permute-start(bf16[3,2,10,48,512]{4,3,2,1,0:T(8,128)(2,1)S(1)} %get-tuple-element.138), channel_id=1, source_target_pairs={{0,1},{1,0},{2,3},{3,2},{4,5},{5,4},{6,7},{7,6},{8,9},{9,8},{10,11... | collective-permute-start | bytes 8847368 | tf_op jit(solution)/shard_map/ppermute | solution.py:27
  152.8 5.6 %collective-permute-start.38 = (f32[8,512]{1,0:T(8,128)S(1)}, f32[8,512]{1,0:T(8,128)S(1)}, u32[]{:S(2)}, u32[]{:S(2)}) collective-permute-start(f32[8,512]{1,0:T(8,128)S(1)} %add_add_fusion.11), channel_id=1, source_target_pairs={{0,24},{1,25},{2,26},{3,27},{4,28},{5,29},{6,30},{7,31},{8,16},{9,... | collective-permute-start | bytes 49160 | tf_op jit(solution)/shard_map/ppermute | solution.py:27
  173.3 10.5 %collective-permute-start.41 = (bf16[6,48,512]{2,1,0:T(8,128)(2,1)S(1)}, bf16[6,48,512]{2,1,0:T(8,128)(2,1)S(1)}, u32[]{:S(2)}, u32[]{:S(2)}) collective-permute-start(bf16[6,48,512]{2,1,0:T(8,128)(2,1)S(1)} %get-tuple-element.133), channel_id=1, source_target_pairs={{1,2},{2,1},{5,6},{6,5},{9,10},{10,9},{13,14},{14,13},{17,18},{18,... | collective-permute-start | bytes 884744 | tf_op jit(solution)/shard_map/ppermute | solution.py:33
  173.9 9.8 %collective-permute-start.40 = (bf16[6,48,512]{2,1,0:T(8,128)(2,1)S(1)}, bf16[6,48,512]{2,1,0:T(8,128)(2,1)S(1)}, u32[]{:S(2)}, u32[]{:S(2)}) collective-permute-start(bf16[6,48,512]{2,1,0:T(8,128)(2,1)S(1)} %get-tuple-element.132), channel_id=1, source_target_pairs={{1,2},{2,1},{5,6},{6,5},{9,10},{10,9},{13,14},{14,13},{17,18},{18,... | collective-permute-start | bytes 884744 | tf_op jit(solution)/shard_map/ppermute | solution.py:33
  174.8 5.6 %collective-permute-start.47 = (f32[8,512]{1,0:T(8,128)S(1)}, f32[8,512]{1,0:T(8,128)S(1)}, u32[]{:S(2)}, u32[]{:S(2)}) collective-permute-start(f32[8,512]{1,0:T(8,128)S(1)} %add_add_fusion.9), channel_id=1, source_target_pairs={{0,24},{1,25},{2,26},{3,27},{4,28},{5,29},{6,30},{7,31},{8,16},{9,... | collective-permute-start | bytes 49160 | tf_op jit(solution)/shard_map/ppermute | solution.py:27
  177.3 6.3 %collective-permute-start.45 = (f32[8,512]{1,0:T(8,128)S(1)}, f32[8,512]{1,0:T(8,128)S(1)}, u32[]{:S(2)}, u32[]{:S(2)}) collective-permute-start(f32[8,512]{1,0:T(8,128)S(1)} %add_add_fusion.9), channel_id=1, source_target_pairs={{0,8},{1,9},{2,10},{3,11},{4,12},{5,13},{6,14},{7,15},{8,0},{9,1},... | collective-permute-start | bytes 49160 | tf_op jit(solution)/shard_map/ppermute | solution.py:27
  180.4 26.6 %collective-permute-start.48 = (bf16[2,10,48,512]{3,2,1,0:T(8,128)(2,1)S(1)}, bf16[2,10,48,512]{3,2,1,0:T(8,128)(2,1)S(1)}, u32[]{:S(2)}, u32[]{:S(2)}) collective-permute-start(bf16[2,10,48,512]{3,2,1,0:T(8,128)(2,1)S(1)} %copy-done.31), channel_id=1, source_target_pairs={{0,1},{1,0},{2,3},{3,2},{4,5},{5,4},{6,7},{7,6},{8,9},{9,8},{10,11... | collective-permute-start | bytes 2949128 | tf_op jit(solution)/shard_map/ppermute | solution.py:27
  183.7 24.3 %collective-permute-start.49 = (bf16[2,10,48,512]{3,2,1,0:T(8,128)(2,1)}, bf16[2,10,48,512]{3,2,1,0:T(8,128)(2,1)S(1)}, u32[]{:S(2)}, u32[]{:S(2)}) collective-permute-start(bf16[2,10,48,512]{3,2,1,0:T(8,128)(2,1)} %get-tuple-element.137.refs_1_), channel_id=1, source_target_pairs={{0,1},{1,0},{2,3},{3,2},{4,5},{5,4},{6,7},{7,6},{8,9},{9,8},{10,11... | collective-permute-start | bytes 2949128 | tf_op jit(solution)/shard_map/ppermute | solution.py:27
  187.1 12.6 %collective-permute-start.51 = (bf16[2,12,48,256]{3,2,1,0:T(8,128)(2,1)S(1)}, bf16[2,12,48,256]{3,2,1,0:T(8,128)(2,1)S(1)}, u32[]{:S(2)}, u32[]{:S(2)}) collective-permute-start(bf16[2,12,48,256]{3,2,1,0:T(8,128)(2,1)S(1)} %get-tuple-element.228), channel_id=1, source_target_pairs={{0,1},{1,0},{2,3},{3,2},{4,5},{5,4},{6,7},{7,6},{8,9},{9,8},{10,11... | collective-permute-start | bytes 1769480 | tf_op jit(solution)/shard_map/ppermute | solution.py:27
  197.6 38.6 %collective-permute-start.54 = (bf16[8,288,256]{2,1,0:T(8,128)(2,1)S(1)}, bf16[8,288,256]{2,1,0:T(8,128)(2,1)S(1)}, u32[]{:S(2)}, u32[]{:S(2)}) collective-permute-start(bf16[8,288,256]{2,1,0:T(8,128)(2,1)S(1)} %get-tuple-element.139.refs_5_), channel_id=1, source_target_pairs={{0,2},{1,3},{2,0},{3,1},{4,6},{5,7},{6,4},{7,5},{8,10},{9,11},{10,... | collective-permute-start | bytes 3538952 | tf_op jit(solution)/shard_map/ppermute | solution.py:27
  206.2 31.0 %collective-permute-start.53 = (bf16[4,576,256]{2,1,0:T(8,128)(2,1)S(1)}, bf16[4,576,256]{2,1,0:T(8,128)(2,1)S(1)}, u32[]{:S(2)}, u32[]{:S(2)}) collective-permute-start(bf16[4,576,256]{2,1,0:T(8,128)(2,1)S(1)} %get-tuple-element.140.refs_13_), channel_id=1, source_target_pairs={{0,4},{1,5},{2,6},{3,7},{4,0},{5,1},{6,2},{7,3},{8,12},{9,13},{10,... | collective-permute-start | bytes 3538952 | tf_op jit(solution)/shard_map/ppermute | solution.py:27
  247.0 5.5 %collective-permute-start.61 = (f32[8,512]{1,0:T(8,128)S(1)}, f32[8,512]{1,0:T(8,128)S(1)}, u32[]{:S(2)}, u32[]{:S(2)}) collective-permute-start(f32[8,512]{1,0:T(8,128)S(1)} %add_add_fusion.7), channel_id=1, source_target_pairs={{0,24},{1,25},{2,26},{3,27},{4,28},{5,29},{6,30},{7,31},{8,16},{9,... | collective-permute-start | bytes 49160 | tf_op jit(solution)/shard_map/ppermute | solution.py:27
  248.9 33.9 %collective-permute-start.71 = (bf16[2,12,48,256]{3,2,1,0:T(8,128)(2,1)S(1)}, bf16[2,12,48,256]{3,2,1,0:T(8,128)(2,1)S(1)}, u32[]{:S(2)}, u32[]{:S(2)}) collective-permute-start(bf16[2,12,48,256]{3,2,1,0:T(8,128)(2,1)S(1)} %get-tuple-element.226), channel_id=1, source_target_pairs={{0,1},{1,0},{2,3},{3,2},{4,5},{5,4},{6,7},{7,6},{8,9},{9,8},{10,11... | collective-permute-start | bytes 1769480 | tf_op jit(solution)/shard_map/ppermute | solution.py:27
  248.9 16.0 %collective-permute-start.62 = (bf16[4,288,256]{2,1,0:T(8,128)(2,1)S(1)}, bf16[4,288,256]{2,1,0:T(8,128)(2,1)S(1)}, u32[]{:S(2)}, u32[]{:S(2)}) collective-permute-start(bf16[4,288,256]{2,1,0:T(8,128)(2,1)S(1)} %get-tuple-element.145.refs_3_), channel_id=1, source_target_pairs={{0,4},{1,5},{2,6},{3,7},{4,0},{5,1},{6,2},{7,3},{8,12},{9,13},{10,... | collective-permute-start | bytes 1769480 | tf_op jit(solution)/shard_map/ppermute | solution.py:27
  250.2 15.4 %collective-permute-start.63 = (bf16[4,288,256]{2,1,0:T(8,128)(2,1)S(1)}, bf16[4,288,256]{2,1,0:T(8,128)(2,1)S(1)}, u32[]{:S(2)}, u32[]{:S(2)}) collective-permute-start(bf16[4,288,256]{2,1,0:T(8,128)(2,1)S(1)} %get-tuple-element.146.refs_1_), channel_id=1, source_target_pairs={{0,2},{1,3},{2,0},{3,1},{4,6},{5,7},{6,4},{7,5},{8,10},{9,11},{10,... | collective-permute-start | bytes 1769480 | tf_op jit(solution)/shard_map/ppermute | solution.py:27
  274.2 6.5 %collective-permute-start.69 = (f32[8,512]{1,0:T(8,128)S(1)}, f32[8,512]{1,0:T(8,128)S(1)}, u32[]{:S(2)}, u32[]{:S(2)}) collective-permute-start(f32[8,512]{1,0:T(8,128)S(1)} %add_add_fusion.5), channel_id=1, source_target_pairs={{0,16},{1,17},{2,18},{3,19},{4,20},{5,21},{6,22},{7,23},{8,24},{9,... | collective-permute-start | bytes 49160 | tf_op jit(solution)/shard_map/ppermute | solution.py:27
  276.8 5.7 %collective-permute-start.70 = (f32[8,512]{1,0:T(8,128)S(1)}, f32[8,512]{1,0:T(8,128)S(1)}, u32[]{:S(2)}, u32[]{:S(2)}) collective-permute-start(f32[8,512]{1,0:T(8,128)S(1)} %add_add_fusion.5), channel_id=1, source_target_pairs={{0,24},{1,25},{2,26},{3,27},{4,28},{5,29},{6,30},{7,31},{8,16},{9,... | collective-permute-start | bytes 49160 | tf_op jit(solution)/shard_map/ppermute | solution.py:27
  278.7 26.2 %collective-permute-start.74 = (bf16[4,288,256]{2,1,0:T(8,128)(2,1)S(1)}, bf16[4,288,256]{2,1,0:T(8,128)(2,1)S(1)}, u32[]{:S(2)}, u32[]{:S(2)}) collective-permute-start(bf16[4,288,256]{2,1,0:T(8,128)(2,1)S(1)} %get-tuple-element.151.refs_1_), channel_id=1, source_target_pairs={{0,8},{1,9},{2,10},{3,11},{4,12},{5,13},{6,14},{7,15},{8,0},{9,1},... | collective-permute-start | bytes 1769480 | tf_op jit(solution)/shard_map/ppermute | solution.py:27
  289.7 15.9 %collective-permute-start.73 = (bf16[8,288,128]{2,1,0:T(8,128)(2,1)S(1)}, bf16[8,288,128]{2,1,0:T(8,128)(2,1)S(1)}, u32[]{:S(2)}, u32[]{:S(2)}) collective-permute-start(bf16[8,288,128]{2,1,0:T(8,128)(2,1)S(1)} %get-tuple-element.158), channel_id=1, source_target_pairs={{0,2},{1,3},{2,0},{3,1},{4,6},{5,7},{6,4},{7,5},{8,10},{9,11},{10,... | collective-permute-start | bytes 1769480 | tf_op jit(solution)/shard_map/ppermute | solution.py:27
  290.5 16.0 %collective-permute-start.72 = (bf16[4,576,128]{2,1,0:T(8,128)(2,1)S(1)}, bf16[4,576,128]{2,1,0:T(8,128)(2,1)S(1)}, u32[]{:S(2)}, u32[]{:S(2)}) collective-permute-start(bf16[4,576,128]{2,1,0:T(8,128)(2,1)S(1)} %get-tuple-element.153.refs_13_), channel_id=1, source_target_pairs={{0,4},{1,5},{2,6},{3,7},{4,0},{5,1},{6,2},{7,3},{8,12},{9,13},{10,... | collective-permute-start | bytes 1769480 | tf_op jit(solution)/shard_map/ppermute | solution.py:27
  312.3 28.4 %collective-permute-start.83 = (bf16[3,2,512,256]{3,2,1,0:T(8,128)(2,1)S(1)}, bf16[3,2,512,256]{3,2,1,0:T(8,128)(2,1)S(1)}, u32[]{:S(2)}, u32[]{:S(2)}) collective-permute-start(bf16[3,2,512,256]{3,2,1,0:T(8,128)(2,1)S(1)} %get-tuple-element.163.refs_3_), channel_id=1, source_target_pairs={{0,1},{1,0},{2,3},{3,2},{4,5},{5,4},{6,7},{7,6},{8,9},{9,8},{10,11... | collective-permute-start | bytes 4718600 | tf_op jit(solution)/shard_map/ppermute | solution.py:27
  323.3 6.2 %collective-permute-start.86 = (bf16[2,12,48,256]{3,2,1,0:T(8,128)(2,1)S(1)}, bf16[2,12,48,256]{3,2,1,0:T(8,128)(2,1)S(1)}, u32[]{:S(2)}, u32[]{:S(2)}) collective-permute-start(bf16[2,12,48,256]{3,2,1,0:T(8,128)(2,1)S(1)} %get-tuple-element.168.refs_5_.refs_3_), channel_id=1, source_target_pairs={{0,1},{1,0},{2,3},{3,2},{4,5},{5,4},{6,7},{7,6},{8,9},{9,8},{10,11... | collective-permute-start | bytes 1769480 | tf_op jit(solution)/shard_map/ppermute | solution.py:27
  326.6 12.3 %collective-permute-start.84 = (bf16[4,288,128]{2,1,0:T(8,128)(2,1)S(1)}, bf16[4,288,128]{2,1,0:T(8,128)(2,1)S(1)}, u32[]{:S(2)}, u32[]{:S(2)}) collective-permute-start(bf16[4,288,128]{2,1,0:T(8,128)(2,1)S(1)} %get-tuple-element.165.refs_3_), channel_id=1, source_target_pairs={{0,4},{1,5},{2,6},{3,7},{4,0},{5,1},{6,2},{7,3},{8,12},{9,13},{10,... | collective-permute-start | bytes 884744 | tf_op jit(solution)/shard_map/ppermute | solution.py:27
  327.8 11.0 %collective-permute-start.85 = (bf16[4,288,128]{2,1,0:T(8,128)(2,1)S(1)}, bf16[4,288,128]{2,1,0:T(8,128)(2,1)S(1)}, u32[]{:S(2)}, u32[]{:S(2)}) collective-permute-start(bf16[4,288,128]{2,1,0:T(8,128)(2,1)S(1)} %get-tuple-element.166.refs_1_), channel_id=1, source_target_pairs={{0,2},{1,3},{2,0},{3,1},{4,6},{5,7},{6,4},{7,5},{8,10},{9,11},{10,... | collective-permute-start | bytes 884744 | tf_op jit(solution)/shard_map/ppermute | solution.py:27
  336.8 15.2 %collective-permute-start.89 = (bf16[8,288,128]{2,1,0:T(8,128)(2,1)S(1)}, bf16[8,288,128]{2,1,0:T(8,128)(2,1)S(1)}, u32[]{:S(2)}, u32[]{:S(2)}) collective-permute-start(bf16[8,288,128]{2,1,0:T(8,128)(2,1)S(1)} %get-tuple-element.180), channel_id=1, source_target_pairs={{0,2},{1,3},{2,0},{3,1},{4,6},{5,7},{6,4},{7,5},{8,10},{9,11},{10,... | collective-permute-start | bytes 1769480 | tf_op jit(solution)/shard_map/ppermute | solution.py:27
  337.6 15.2 %collective-permute-start.88 = (bf16[4,576,128]{2,1,0:T(8,128)(2,1)S(1)}, bf16[4,576,128]{2,1,0:T(8,128)(2,1)S(1)}, u32[]{:S(2)}, u32[]{:S(2)}) collective-permute-start(bf16[4,576,128]{2,1,0:T(8,128)(2,1)S(1)} %get-tuple-element.172.refs_5_), channel_id=1, source_target_pairs={{0,4},{1,5},{2,6},{3,7},{4,0},{5,1},{6,2},{7,3},{8,12},{9,13},{10,... | collective-permute-start | bytes 1769480 | tf_op jit(solution)/shard_map/ppermute | solution.py:27
  339.5 14.1 %collective-permute-start.87 = (bf16[4,288,128]{2,1,0:T(8,128)(2,1)S(1)}, bf16[4,288,128]{2,1,0:T(8,128)(2,1)S(1)}, u32[]{:S(2)}, u32[]{:S(2)}) collective-permute-start(bf16[4,288,128]{2,1,0:T(8,128)(2,1)S(1)} %get-tuple-element.173.refs_3_), channel_id=1, source_target_pairs={{0,8},{1,9},{2,10},{3,11},{4,12},{5,13},{6,14},{7,15},{8,0},{9,1},... | collective-permute-start | bytes 884744 | tf_op jit(solution)/shard_map/ppermute | solution.py:27
  371.0 6.7 %collective-permute-start.103 = (bf16[2,12,48,256]{3,2,1,0:T(8,128)(2,1)S(1)}, bf16[2,12,48,256]{3,2,1,0:T(8,128)(2,1)S(1)}, u32[]{:S(2)}, u32[]{:S(2)}) collective-permute-start(bf16[2,12,48,256]{3,2,1,0:T(8,128)(2,1)S(1)} %get-tuple-element.186.refs_5_.refs_2_), channel_id=1, source_target_pairs={{0,1},{1,0},{2,3},{3,2},{4,5},{5,4},{6,7},{7,6},{8,9},{9,8},{10,11... | collective-permute-start | bytes 1769480 | tf_op jit(solution)/shard_map/ppermute | solution.py:27
  373.7 20.2 %collective-permute-start.101 = (bf16[2,288,256]{2,1,0:T(8,128)(2,1)S(1)}, bf16[2,288,256]{2,1,0:T(8,128)(2,1)S(1)}, u32[]{:S(2)}, u32[]{:S(2)}) collective-permute-start(bf16[2,288,256]{2,1,0:T(8,128)(2,1)S(1)} %get-tuple-element.164.refs_3_), channel_id=1, source_target_pairs={{0,16},{1,17},{2,18},{3,19},{4,20},{5,21},{6,22},{7,23},{8,24},{9,... | collective-permute-start | bytes 884744 | tf_op jit(solution)/shard_map/ppermute | solution.py:27
  376.2 36.4 %collective-permute-start.98 = (bf16[24,64,256]{2,1,0:T(8,128)(2,1)}, bf16[24,64,256]{2,1,0:T(8,128)(2,1)S(1)}, u32[]{:S(2)}, u32[]{:S(2)}) collective-permute-start(bf16[24,64,256]{2,1,0:T(8,128)(2,1)} %get-tuple-element.174.refs_9_), channel_id=1, source_target_pairs={{0,4},{1,5},{2,6},{3,7},{4,0},{5,1},{6,2},{7,3},{8,12},{9,13},{10,... | collective-permute-start | bytes 2359304 | tf_op jit(solution)/shard_map/ppermute | solution.py:27
  377.3 19.0 %collective-permute-start.102 = (bf16[2,288,128]{2,1,0:T(8,128)(2,1)S(1)}, bf16[2,288,128]{2,1,0:T(8,128)(2,1)S(1)}, u32[]{:S(2)}, u32[]{:S(2)}) collective-permute-start(bf16[2,288,128]{2,1,0:T(8,128)(2,1)S(1)} %get-tuple-element.184.refs_1_), channel_id=1, source_target_pairs={{0,16},{1,17},{2,18},{3,19},{4,20},{5,21},{6,22},{7,23},{8,24},{9,... | collective-permute-start | bytes 442376 | tf_op jit(solution)/shard_map/ppermute | solution.py:27
  397.2 10.2 %collective-permute-start.99 = (bf16[4,288,128]{2,1,0:T(8,128)(2,1)}, bf16[4,288,128]{2,1,0:T(8,128)(2,1)S(1)}, u32[]{:S(2)}, u32[]{:S(2)}) collective-permute-start(bf16[4,288,128]{2,1,0:T(8,128)(2,1)} %copy-done.6), channel_id=1, source_target_pairs={{0,4},{1,5},{2,6},{3,7},{4,0},{5,1},{6,2},{7,3},{8,12},{9,13},{10,... | collective-permute-start | bytes 884744 | tf_op jit(solution)/shard_map/ppermute | solution.py:27
  398.3 12.6 %collective-permute-start.100 = (bf16[4,288,128]{2,1,0:T(8,128)(2,1)S(1)}, bf16[4,288,128]{2,1,0:T(8,128)(2,1)S(1)}, u32[]{:S(2)}, u32[]{:S(2)}) collective-permute-start(bf16[4,288,128]{2,1,0:T(8,128)(2,1)S(1)} %get-tuple-element.183.refs_3_), channel_id=1, source_target_pairs={{0,2},{1,3},{2,0},{3,1},{4,6},{5,7},{6,4},{7,5},{8,10},{9,11},{10,... | collective-permute-start | bytes 884744 | tf_op jit(solution)/shard_map/ppermute | solution.py:27
  400.4 30.0 %collective-permute-start.106 = (bf16[4,288,256]{2,1,0:T(8,128)(2,1)}, bf16[4,288,256]{2,1,0:T(8,128)(2,1)S(1)}, u32[]{:S(2)}, u32[]{:S(2)}) collective-permute-start(bf16[4,288,256]{2,1,0:T(8,128)(2,1)} %copy-done.44), channel_id=1, source_target_pairs={{0,2},{1,3},{2,0},{3,1},{4,6},{5,7},{6,4},{7,5},{8,10},{9,11},{10,... | collective-permute-start | bytes 1769480 | tf_op jit(solution)/shard_map/ppermute | solution.py:27
  400.4 30.0 %collective-permute-start.107 = (bf16[4,288,256]{2,1,0:T(8,128)(2,1)}, bf16[4,288,256]{2,1,0:T(8,128)(2,1)S(1)}, u32[]{:S(2)}, u32[]{:S(2)}) collective-permute-start(bf16[4,288,256]{2,1,0:T(8,128)(2,1)} %copy-done.43), channel_id=1, source_target_pairs={{0,4},{1,5},{2,6},{3,7},{4,0},{5,1},{6,2},{7,3},{8,12},{9,13},{10,... | collective-permute-start | bytes 1769480 | tf_op jit(solution)/shard_map/ppermute | solution.py:27
  407.4 36.0 %collective-permute-start.108 = (bf16[4,288,256]{2,1,0:T(8,128)(2,1)S(1)}, bf16[4,288,256]{2,1,0:T(8,128)(2,1)S(1)}, u32[]{:S(2)}, u32[]{:S(2)}) collective-permute-start(bf16[4,288,256]{2,1,0:T(8,128)(2,1)S(1)} %get-tuple-element.192.refs_4_), channel_id=1, source_target_pairs={{0,6},{1,7},{2,4},{3,5},{4,2},{5,3},{6,0},{7,1},{8,14},{9,15},{10,... | collective-permute-start | bytes 1769480 | tf_op jit(solution)/shard_map/ppermute | solution.py:27
  413.4 36.7 %collective-permute-start.104 = (bf16[24,32,256]{2,1,0:T(8,128)(2,1)S(1)}, bf16[24,32,256]{2,1,0:T(8,128)(2,1)S(1)}, u32[]{:S(2)}, u32[]{:S(2)}) collective-permute-start(bf16[24,32,256]{2,1,0:T(8,128)(2,1)S(1)} %get-tuple-element.195.refs_5_), channel_id=1, source_target_pairs={{0,2},{1,3},{2,0},{3,1},{4,6},{5,7},{6,4},{7,5},{8,10},{9,11},{10,... | collective-permute-start | bytes 1179656 | tf_op jit(solution)/shard_map/ppermute | solution.py:27
  416.0 32.7 %collective-permute-start.105 = (bf16[4,288,128]{2,1,0:T(8,128)(2,1)S(1)}, bf16[4,288,128]{2,1,0:T(8,128)(2,1)S(1)}, u32[]{:S(2)}, u32[]{:S(2)}) collective-permute-start(bf16[4,288,128]{2,1,0:T(8,128)(2,1)S(1)} %get-tuple-element.193.refs_3_), channel_id=1, source_target_pairs={{0,8},{1,9},{2,10},{3,11},{4,12},{5,13},{6,14},{7,15},{8,0},{9,1},... | collective-permute-start | bytes 884744 | tf_op jit(solution)/shard_map/ppermute | solution.py:27
  444.3 20.6 %collective-permute-start.109 = (bf16[1,288,256]{2,1,0:T(8,128)(2,1)S(1)}, bf16[1,288,256]{2,1,0:T(8,128)(2,1)S(1)}, u32[]{:S(2)}, u32[]{:S(2)}) collective-permute-start(bf16[1,288,256]{2,1,0:T(8,128)(2,1)S(1)} %get-tuple-element.204), channel_id=1, source_target_pairs={{0,8},{1,9},{2,10},{3,11},{4,12},{5,13},{6,14},{7,15},{8,0},{9,1},... | collective-permute-start | bytes 442376 | tf_op jit(solution)/shard_map/ppermute | solution.py:27
  444.4 20.5 %collective-permute-start.110 = (bf16[1,288,256]{2,1,0:T(8,128)(2,1)S(1)}, bf16[1,288,256]{2,1,0:T(8,128)(2,1)S(1)}, u32[]{:S(2)}, u32[]{:S(2)}) collective-permute-start(bf16[1,288,256]{2,1,0:T(8,128)(2,1)S(1)} %get-tuple-element.205), channel_id=1, source_target_pairs={{0,16},{1,17},{2,18},{3,19},{4,20},{5,21},{6,22},{7,23},{8,24},{9,... | collective-permute-start | bytes 442376 | tf_op jit(solution)/shard_map/ppermute | solution.py:27
  446.8 18.0 %collective-permute-start.111 = (bf16[1,288,256]{2,1,0:T(8,128)(2,1)S(1)}, bf16[1,288,256]{2,1,0:T(8,128)(2,1)S(1)}, u32[]{:S(2)}, u32[]{:S(2)}) collective-permute-start(bf16[1,288,256]{2,1,0:T(8,128)(2,1)S(1)} %get-tuple-element.200.refs_3_), channel_id=1, source_target_pairs={{0,24},{1,25},{2,26},{3,27},{4,28},{5,29},{6,30},{7,31},{8,16},{9,... | collective-permute-start | bytes 442376 | tf_op jit(solution)/shard_map/ppermute | solution.py:27
  449.4 15.5 %collective-permute-start.112 = (bf16[2,288,128]{2,1,0:T(8,128)(2,1)S(1)}, bf16[2,288,128]{2,1,0:T(8,128)(2,1)S(1)}, u32[]{:S(2)}, u32[]{:S(2)}) collective-permute-start(bf16[2,288,128]{2,1,0:T(8,128)(2,1)S(1)} %get-tuple-element.201.refs_3_), channel_id=1, source_target_pairs={{0,16},{1,17},{2,18},{3,19},{4,20},{5,21},{6,22},{7,23},{8,24},{9,... | collective-permute-start | bytes 442376 | tf_op jit(solution)/shard_map/ppermute | solution.py:27
  450.9 11.0 %collective-permute-start.113 = (bf16[12,32,256]{2,1,0:T(8,128)(2,1)S(1)}, bf16[12,32,256]{2,1,0:T(8,128)(2,1)S(1)}, u32[]{:S(2)}, u32[]{:S(2)}) collective-permute-start(bf16[12,32,256]{2,1,0:T(8,128)(2,1)S(1)} %get-tuple-element.202.refs_4_), channel_id=1, source_target_pairs={{0,8},{1,9},{2,10},{3,11},{4,12},{5,13},{6,14},{7,15},{8,0},{9,1},... | collective-permute-start | bytes 589832 | tf_op jit(solution)/shard_map/ppermute | solution.py:27
  464.2 6.3 %collective-permute-start.114 = (bf16[6,32,256]{2,1,0:T(8,128)(2,1)S(1)}, bf16[6,32,256]{2,1,0:T(8,128)(2,1)S(1)}, u32[]{:S(2)}, u32[]{:S(2)}) collective-permute-start(bf16[6,32,256]{2,1,0:T(8,128)(2,1)S(1)} %get-tuple-element.209.refs_8_), channel_id=1, source_target_pairs={{0,16},{1,17},{2,18},{3,19},{4,20},{5,21},{6,22},{7,23},{8,24},{9,... | collective-permute-start | bytes 294920 | tf_op jit(solution)/shard_map/ppermute | solution.py:27
  470.6 7.8 %collective-permute-start.116 = (bf16[768,256]{1,0:T(8,128)(2,1)S(1)}, bf16[768,256]{1,0:T(8,128)(2,1)S(1)}, u32[]{:S(2)}, u32[]{:S(2)}) collective-permute-start(bf16[768,256]{1,0:T(8,128)(2,1)S(1)} %settle.3.refs_1_.refs_5_), channel_id=1, source_target_pairs={{0,2},{1,3},{2,0},{3,1},{4,6},{5,7},{6,4},{7,5},{8,10},{9,11},{10,... | collective-permute-start | bytes 1179656 | tf_op jit(solution)/shard_map/ppermute | solution.py:27
  472.5 6.6 %collective-permute-start.115 = (bf16[768,256]{1,0:T(8,128)(2,1)S(1)}, bf16[768,256]{1,0:T(8,128)(2,1)S(1)}, u32[]{:S(2)}, u32[]{:S(2)}) collective-permute-start(bf16[768,256]{1,0:T(8,128)(2,1)S(1)} %settle.3.refs_1_.refs_5_), channel_id=1, source_target_pairs={{0,1},{1,0},{2,3},{3,2},{4,5},{5,4},{6,7},{7,6},{8,9},{9,8},{10,11... | collective-permute-start | bytes 1179656 | tf_op jit(solution)/shard_map/ppermute | solution.py:27
  (122 other events, 1256.4 us)
Sparse Core Ops, SparseCore 0:
  397.3 30.0 all-gather.2

commit v4 on v3

--- a/solution.py
+++ b/solution.py
@@ -93,23 +93,33 @@
         return lax.broadcasted_iota(jnp.int32, shape, 0) < limit
 
     def each(self, body):
-        def step(row, carry):
-            for slot in range(self.slots):
-                body(slot, row)
+        self.rows_of(self.rows, body)
+
+    def rows_of(self, rows, body):
+        group = 2 if rows % 2 == 0 else 1
+
+        def step(index, carry):
+            for part in range(group):
+                for slot in range(self.slots):
+                    body(slot, index * group + part)
             return carry
 
-        lax.fori_loop(0, self.rows, step, 0)
+        lax.fori_loop(0, rows // group, step, 0)
 
     def summed(self, body, rows=None):
-        def step(row, carry):
+        rows = rows or self.rows
+        group = 2 if rows % 2 == 0 else 1
+
+        def step(index, carry):
             one, two = carry
-            for slot in range(self.slots):
-                first, second = body(slot, row)
-                one, two = one + fold(first), two + fold(second)
+            for part in range(group):
+                for slot in range(self.slots):
+                    first, second = body(slot, index * group + part)
+                    one, two = one + fold(first), two + fold(second)
             return one, two
 
         zero = jnp.zeros((8, self.channels), F32)
-        one, two = lax.fori_loop(0, rows or self.rows, step, (zero, zero))
+        one, two = lax.fori_loop(0, rows // group, step, (zero, zero))
         return jnp.sum(one, axis=0, keepdims=True), jnp.sum(two, axis=0, keepdims=True)
 
     def rims(self, sources, body, group=0):
@@ -160,7 +170,7 @@
 
 
 def sigmoid(values):
-    return 1.0 / (1.0 + jnp.exp(-values))
+    return jax.nn.sigmoid(values)
 
 
 def silu_slope(values):
@@ -349,16 +359,14 @@
     wide[...] = dot(shared[...].reshape(slots * tall * breadth, channels), down[0])
     average, inverse = moments(totals, branch, count[0])
 
-    def act(row, carry):
-        for slot in range(slots):
-            values = wide[frame.pixels(slot, row, tall), :]
-            result = activation(
-                values, frame.inside(slot, row), average, inverse, line(gain, branch), line(shift, branch)
-            )
-            squeezed[0, slot, row] = result.astype(BF16)
-        return carry
-
-    lax.fori_loop(0, tall, act, 0)
+    def act(slot, row):
+        values = wide[frame.pixels(slot, row, tall), :]
+        result = activation(
+            values, frame.inside(slot, row), average, inverse, line(gain, branch), line(shift, branch)
+        )
+        squeezed[0, slot, row] = result.astype(BF16)
+
+    frame.rows_of(tall, act)
     for slot in range(slots):
         raised[frame.span(slot), :] = dot(
             squeezed[0, slot, 1 : rows + 1].reshape(rows * breadth, -1), up[0]
@@ -500,15 +508,13 @@
 def fill_halves(frame, kept, sent, three, lead=()):
     odd = frame.bit(0) == 1
 
-    def put(row, carry):
-        for slot in range(frame.slots):
-            mine = kept[lead + (slot, row)].astype(F32)
-            other = sent[lead + (slot, row)].astype(F32)
-            low, high = jnp.where(odd, other, mine), jnp.where(odd, mine, other)
-            put_three(three, slot, row, jnp.concatenate([low, high], axis=1), True)
-        return carry
-
-    lax.fori_loop(0, frame.tall, put, 0)
+    def put(slot, row):
+        mine = kept[lead + (slot, row)].astype(F32)
+        other = sent[lead + (slot, row)].astype(F32)
+        low, high = jnp.where(odd, other, mine), jnp.where(odd, mine, other)
+        put_three(three, slot, row, jnp.concatenate([low, high], axis=1), True)
+
+    frame.rows_of(frame.tall, put)
 
 
 def gate_back_kernel(
@@ -799,28 +805,27 @@
 
 
 def join_kernel(info, *refs, bits_at):
-    gathered = len(refs[0].shape) == 3
-    pieces, outs = (refs[:1], refs[1:]) if gathered else (refs[:4], refs[4:])
     odd = info[bits_at] == 1
     upper = info[bits_at + 1]
-    half = pieces[0].shape[-1]
-    start = 0
-    for out in outs:
-        height = out.shape[2]
-        for member in range(out.shape[0]):
-            span = slice(start, start + height)
-            for flip in range(2):
-                if gathered:
-                    for core in range(2):
-                        lanes = slice(core * half, (core + 1) * half)
-                        out[member, flip, :, lanes] = pieces[0][2 * flip + core, span, :].astype(F32)
-                    continue
-                mine = pieces[2 * flip][span, :].astype(F32)
-                other = pieces[2 * flip + 1][span, :].astype(F32)
-                row = jnp.where(upper == flip, 0, 1)
-                out[member, row, :, :half] = jnp.where(odd, other, mine)
-                out[member, row, :, half:] = jnp.where(odd, mine, other)
-            start += height
+    outs = refs[8:]
+
+    def join(pieces, outs):
+        start = 0
+        half = pieces[0].shape[-1]
+        for out in outs:
+            height = out.shape[2]
+            for member in range(out.shape[0]):
+                span = slice(start, start + height)
+                start += height
+                for flip in range(2):
+                    mine = pieces[2 * flip][span, :].astype(F32)
+                    other = pieces[2 * flip + 1][span, :].astype(F32)
+                    row = jnp.where(upper == flip, 0, 1)
+                    out[member, row, :, :half] = jnp.where(odd, other, mine)
+                    out[member, row, :, half:] = jnp.where(odd, mine, other)
+
+    join(refs[:4], [outs[1]])
+    join(refs[4:8], [outs[0], outs[2]])
 
 
 def outputs_kernel(first, second, down, up, conv, *outs):
@@ -887,6 +892,10 @@
 
 def out_branch(shape, dtype):
     return (tuple(shape), dtype, by_branch(shape))
+
+
+def branch_weight(a):
+    return (pltpu.with_memory_space_constraint(a, pltpu.HBM), by_branch(a.shape))
 
 
 def in_hbm(a):
@@ -1021,20 +1030,17 @@
         beside = swapped(piece, 2)
         return [piece, swapped(piece, 1), beside, swapped(beside, 1)]
 
-    def join(self, pieces, members):
+    def join(self, gathered, pieces, members):
         width = pieces[0].shape[-1]
-        shapes = []
-        for count, rows in members:
-            shapes.append((count, 2, rows // 2, 2 * width))
         results = self.call(
             "join",
             functools.partial(join_kernel, bits_at=self.bits_at),
             (1,),
-            [(self.info, SCALARS)] + [whole(piece) for piece in pieces],
-            [out(shape, F32) for shape in shapes],
+            [(self.info, SCALARS)] + [whole(piece) for piece in [*gathered, *pieces]],
+            [out((count, 2, rows // 2, 2 * width), F32) for count, rows in members],
             [],
             0,
-            room=12,
+            room=24,
         )
         return [r.reshape(r.shape[0], -1, r.shape[-1]) for r in results]
 
@@ -1136,7 +1142,7 @@
         (tasks,),
         scalars
         + [whole(a) for a in (second_out, second_near, second_outer, second_totals)]
-        + [whole(shared_gain), whole(shared_shift), branch_of(task_down)],
+        + [whole(shared_gain), whole(shared_shift), branch_weight(task_down)],
         [out(tall_shape, BF16), sums_only()],
         [flat],
         3 * thin_flops,
@@ -1148,7 +1154,7 @@
         raise_kernel,
         (tasks,),
         scalars
-        + [whole(shared), branch_of(task_down), branch_of(task_up)]
+        + [whole(shared), branch_weight(task_down), branch_weight(task_up)]
         + [whole(a) for a in (down_totals, down_gain, down_shift)],
         [out_branch(all_tasks(tall_shape), BF16), sums_only()],
         [flat_tall, flat],
@@ -1161,7 +1167,7 @@
         task_kernel,
         (tasks,),
         scalars
-        + [branch_of(squeezed), branch_of(task_up)]
+        + [branch_of(squeezed), branch_weight(task_up)]
         + [whole(a) for a in (shared, up_totals, up_gain, up_shift)]
         + [in_hbm(task_conv)],
         [out_branch(all_tasks(map_shape), F32)]
@@ -1274,7 +1280,7 @@
         (tasks,),
         scalars
         + [branch_of(conv_kept), branch_of(conv_sent)]
-        + [in_hbm(task_conv), branch_of(squeezed), branch_of(task_up)]
+        + [in_hbm(task_conv), branch_of(squeezed), branch_weight(task_up)]
         + [whole(a) for a in (shared, up_totals, up_gain, up_shift)],
         [
             out_branch(all_tasks(map_shape), F32),
@@ -1293,8 +1299,8 @@
         raise_back_kernel,
         (tasks,),
         scalars
-        + [branch_of(up_grad_in), branch_of(squeezed), branch_of(task_up), whole(shared)]
-        + [branch_of(task_down)]
+        + [branch_of(up_grad_in), branch_of(squeezed), branch_weight(task_up), whole(shared)]
+        + [branch_weight(task_down)]
         + [
             whole(a)
             for a in (up_totals, up_back, up_gain, down_totals, down_gain, down_shift)
@@ -1316,7 +1322,7 @@
         lower_back_kernel,
         (tasks,),
         scalars
-        + [branch_of(down_grad_in), whole(shared), branch_of(task_down)]
+        + [branch_of(down_grad_in), whole(shared), branch_weight(task_down)]
         + [whole(a) for a in (down_totals, down_back, down_gain, shared_grad, second_out)]
         + [whole(a) for a in (second_totals, shared_gain, shared_shift)],
         [out_branch(all_tasks(map_shape), BF16), out(map_shape, F32)] + packed(1),
@@ -1358,10 +1364,6 @@
     )
     second_sum = weight_sum(hidden, hidden_other, second_kept, second_sent, "xy")
     late = merged(late, 2)
-    thin_order = reducer.order("y")
-    thin_rows = channels // dp_count // 2
-    thin_parts = reducer.spread([[thin_kept, thin_got]], thin_rows, thin_order)
-    thin = Halving(reducer, thin_parts, thin_order, thin_rows)
     first_grad, first_back_packed, first_grad_far = reducer.call(
         "hidden_back",
         hidden_back_kernel,
@@ -1378,6 +1380,10 @@
         reducer.relay(first_back_packed), first_grad_far
     )
 
+    thin_order = reducer.order("y")
+    thin_rows = channels // dp_count // 2
+    thin_parts = reducer.spread([[thin_kept, thin_got]], thin_rows, thin_order, [first_back])
+    thin = Halving(reducer, thin_parts, thin_order, thin_rows)
     first_kept, first_sent = reducer.call(
         "first_grad",
         functools.partial(one_grad_kernel, member=0),
@@ -1394,12 +1400,11 @@
         [],
         0,
     )
+    second_sum = merged(second_sum, 2)
     first_sum = weight_sum(masked, masked_other, first_kept, first_sent, ["xy"])
 
     task_share = reducer.settle([early, late])
-    second_sum = merged(second_sum, 2)
-    step(thin, *first_sum)
-    step(second_sum, thin)
+    beside = swapped(task_share, 2)
     (input_grad,) = reducer.call(
         "input_back",
         input_back_kernel,
@@ -1407,15 +1412,18 @@
         [scalars[0], whole(first_kept), whole(first_sent), in_hbm(shared_conv)],
         [out(map_shape, F32)],
         [three] + one_weight,
-        conv_flops,
-    )
-
-    step(thin)
-    shared_sums, thin_sums = reducer.join(
+        8 * conv_flops,
+    )
+
+    step(thin, *first_sum, second_sum)
+    beside = reducer.relay(beside)
+    step(thin, thin)
+    task_pieces = [task_share, swapped(task_share, 1), beside, swapped(beside, 1)]
+    shared_sums, task_sums, thin_sums = reducer.join(
+        task_pieces,
         reducer.pieces(reducer.settle(first_sum + [second_sum, thin])),
-        [(2, wide_rows), (2 * tasks, channels // dp_count)],
-    )
-    (task_sums,) = reducer.join([lax.all_gather(task_share, "rows")], [(tasks, wide_rows)])
+        [(2, wide_rows), (tasks, wide_rows), (2 * tasks, channels // dp_count)],
+    )
 
     pair_shape = (2, channels)
     many_shape = (tasks, channels)

time: 500 us -> 476 us (0.952)
  between operations: 16.4 us -> 2.72 us
  Pallas kernels: 189 us -> 183 us
  waiting for transfers between devices: 133 us -> 127 us
    pallas_call x46, Pallas kernels: 189 us -> 183 us  [call(): pl.pallas_call(body, name=name, grid=grid, in_specs=[s for _, s in inputs...]
    ppermute x110 -> x113, waiting for transfers between devices: 131 us -> 125 us  [swapped(): return lax.ppermute(values, AXES, [(i, i ^ flip) for i in range(places())])]
    ppermute x110 -> x113, starting transfers between devices: 131 us -> 133 us  [swapped(): return lax.ppermute(values, AXES, [(i, i ^ flip) for i in range(places())])]
    unnamed x102 -> x32, local copies, waits for them, and re-layouts: 10.7 us -> 10 us
  transfers between devices with their start and end apart: 119 -> 121, of which waited for: 72 -> 73; matrix products, arithmetic and copies ran while one was open for 1% -> 1% of each run, Pallas kernels for 26% -> 26%
where the time goes in v4:
time: 476 us; the launch traced here: 470 us
  Pallas kernels  183 us (38%)
  starting transfers between devices  140 us (29%)
  waiting for transfers between devices  127 us (27%)
  local copies, waits for them, and re-layouts  14.7 us (3%)
    pallas_call x46, Pallas kernels, call(): pl.pallas_call(body, name=name, grid=grid, in_specs=[s for _, s in inputs...  183 us
    ppermute x113, starting transfers between devices, swapped(): return lax.ppermute(values, AXES, [(i, i ^ flip) for i in range(places())])  133 us
    ppermute x113, waiting for transfers between devices, swapped(): return lax.ppermute(values, AXES, [(i, i ^ flip) for i in range(places())])  125 us
    unnamed x32, local copies, waits for them, and re-layouts  10 us
  transfers between devices with their start and end apart: 121, of which 73 were waited for; matrix products, arithmetic and copies ran while one was open for 1% of the time, Pallas kernels for 26%

profile of v4, /device:TPU:0, one launch (start us, length us, event | category | flops | bytes accessed | tf_op | source)
XLA Modules:
  0.0 470.0 jit_solution(6947164148845194921)
XLA Ops:
  10.5 8.0 %first_conv.1 = (f32[2,10,48,512]{3,2,1,0:T(8,128)S(1)}, f32[104,512]{1,0:T(8,128)S(1)}, f32[2,48,512]{2,1,0:T(8,128)S(1)}, bf16[2,10,48,512]{3,2,1,0:T(8,128)(2,1)S(1)}) custom-call(s32[29]{0:T(128)S(1)} %pad_add_fusion.info.refs_0_, bf16[2,10,48,512]{3,2,1,0:T(8,128)(2,1)S(1)} %copy-done.2, bf16[2,48,512]{2,1,0:T(8,128)(2,1)S(1)} %collective-permute-done.above, ...), custom_call_target="tpu_custom_call" | custom-call | flops 4529848320 | bytes 10616948 | tf_op jit(solution)/shard_map/first_conv/pallas_call | solution.py:865
  18.5 3.3 collective-permute-start.2
  26.6 2.4 collective-permute-done.6
  29.1 2.7 collective-permute-start.8
  34.6 2.6 collective-permute-done.9
  37.3 8.0 %second_conv.1 = (f32[2,10,48,512]{3,2,1,0:T(8,128)S(1)}, f32[104,512]{1,0:T(8,128)S(1)}, f32[2,48,512]{2,1,0:T(8,128)S(1)}, bf16[2,10,48,512]{3,2,1,0:T(8,128)(2,1)S(1)}) custom-call(s32[29]{0:T(128)S(1)} %pad_add_fusion.info.refs_0_, f32[1]{0:T(128)} %bitcast.count.refs_1_, f32[2,10,48,512]{3,2,1,0:T(8,128)S(1)} %get-tuple-element.118.source.refs_7_.refs_5_, ...), custom_call_target="tpu_custom_call" | custom-call | flops 4529848320 | bytes 11837560 | tf_op jit(solution)/shard_map/second_conv/pallas_call | solution.py:865
  45.3 3.1 collective-permute-start.10
  53.3 2.4 collective-permute-done.14
  56.8 2.9 collective-permute-start.16
  61.9 3.3 collective-permute-done.17
  65.2 4.7 %lower.1 = (bf16[2,12,48,512]{3,2,1,0:T(8,128)(2,1)S(1)}, f32[8,512]{1,0:T(8,128)S(1)}) custom-call(s32[29]{0:T(128)S(1)} %pad_add_fusion.info.refs_0_, f32[1]{0:T(128)} %bitcast.count.refs_1_, f32[2,10,48,512]{3,2,1,0:T(8,128)S(1)} %get-tuple-element.121.source.refs_9_.refs_5_, f32[104,512]{1,0:T(8,128)S(1)} %collective-permute-done.10.near.refs_6_, ...), custom_call_target="tpu_custom_call" | custom-call | flops 1509949440 | bytes 3973240 | tf_op jit(solution)/shard_map/lower/pallas_call | solution.py:865
  73.7 2.7 collective-permute-start.21
  80.1 3.1 collective-permute-start.23
  84.9 3.8 collective-permute-done.24
  88.8 8.5 %raise.1 = (bf16[3,2,12,48,512]{4,3,2,1,0:T(8,128)(2,1)S(1)}, f32[8,512]{1,0:T(8,128)S(1)}) custom-call(s32[29]{0:T(128)S(1)} %pad_add_fusion.info.refs_0_, f32[1]{0:T(128)} %bitcast.count.refs_1_, bf16[2,12,48,512]{3,2,1,0:T(8,128)(2,1)S(1)} %get-tuple-element.124.shared.refs_7_.refs_5_.refs_3_.refs_1_, bf16[3,512,512]{2,1,0:T(8,128)(2,1)} %refs_4_.6, ...), custom_call_target="tpu_custom_call" | custom-call | flops 3019898880 | bytes 4354168 | tf_op jit(solution)/shard_map/raise/pallas_call | solution.py:865
  110.4 22.9 %task_conv.1 = (f32[3,2,10,48,512]{4,3,2,1,0:T(8,128)S(1)}, f32[296,512]{1,0:T(8,128)S(1)}, bf16[6,48,512]{2,1,0:T(8,128)(2,1)S(1)}, bf16[3,2,10,48,512]{4,3,2,1,0:T(8,128)(2,1)S(1)}) custom-call(s32[29]{0:T(128)S(1)} %pad_add_fusion.info.refs_0_, f32[1]{0:T(128)} %bitcast.count.refs_1_, ...), custom_call_target="tpu_custom_call" | custom-call | flops 13589544960 | bytes 20476024 | tf_op jit(solution)/shard_map/task_conv/pallas_call | solution.py:865
  149.9 6.4 %pool.1 = (bf16[3,2,5,24,512]{4,3,2,1,0:T(8,128)(2,1)}, f32[3,2,10,48,512]{4,3,2,1,0:T(8,128)S(1)}, f32[296,512]{1,0:T(8,128)S(1)}, bf16[6,48,512]{2,1,0:T(8,128)(2,1)S(1)}) custom-call(s32[29]{0:T(128)S(1)} %pad_add_fusion.info.refs_0_, f32[1]{0:T(128)} %bitcast.count.refs_1_, f32[3,2,10,48,512]{4,3,2,1,0:T(8,128)S(1)} %get-tuple-element.128.source, ...), custom_call_target="tpu_custom_call" | custom-call | flops 503316480 | bytes 6664312 | tf_op jit(solution)/shard_map/pool/pallas_call | solution.py:865
  171.4 3.3 collective-permute-start.48
  174.7 3.1 conv_grad.1
  182.1 6.4 %weight_grad.5 = (bf16[8,288,256]{2,1,0:T(8,128)(2,1)S(1)}, bf16[8,288,256]{2,1,0:T(8,128)(2,1)S(1)}) custom-call(s32[29]{0:T(128)S(1)} %pad_add_fusion.info.refs_0_, bf16[2,10,48,512]{3,2,1,0:T(8,128)(2,1)S(1)} %get-tuple-element.226.refs_1_, bf16[2,10,48,512]{3,2,1,0:T(8,128)(2,1)S(1)} %get-tuple-element.223.refs_2_, ...), custom_call_target="tpu_custom_call" | custom-call | flops 4529848320 | bytes 3145844 | tf_op jit(solution)/shard_map/weight_grad/pallas_call | solution.py:865
  190.6 6.4 %weight_grad.6 = (bf16[4,576,256]{2,1,0:T(8,128)(2,1)S(1)}, bf16[4,576,256]{2,1,0:T(8,128)(2,1)S(1)}) custom-call(s32[29]{0:T(128)S(1)} %pad_add_fusion.info.refs_0_, bf16[2,10,48,512]{3,2,1,0:T(8,128)(2,1)S(1)} %get-tuple-element.227.refs_1_, bf16[2,10,48,512]{3,2,1,0:T(8,128)(2,1)S(1)} %get-tuple-element.224.refs_2_, ...), custom_call_target="tpu_custom_call" | custom-call | flops 4529848320 | bytes 3145844 | tf_op jit(solution)/shard_map/weight_grad/pallas_call | solution.py:865
  199.9 24.5 %gate_back.1 = (f32[3,2,10,48,512]{4,3,2,1,0:T(8,128)S(1)}, f32[2,10,48,512]{3,2,1,0:T(8,128)S(1)}, f32[8,512]{1,0:T(8,128)S(1)}) custom-call(s32[29]{0:T(128)S(1)} %pad_add_fusion.info.refs_0_, f32[1]{0:T(128)} %bitcast.count.refs_1_, bf16[3,2,12,48,256]{4,3,2,1,0:T(8,128)(2,1)S(1)} %get-tuple-element.135.refs_2_, ...), custom_call_target="tpu_custom_call" | custom-call | flops 13589544960 | bytes 24014968 | tf_op jit(solution)/shard_map/gate_back/pallas_call | solution.py:865
  224.4 2.5 copy-done.14
  243.6 2.7 copy-done.15
  246.3 11.9 %raise_back.1 = (bf16[3,2,10,48,512]{4,3,2,1,0:T(8,128)(2,1)S(1)}, f32[3,2,10,48,512]{4,3,2,1,0:T(8,128)S(1)}, f32[8,512]{1,0:T(8,128)S(1)}) custom-call(s32[29]{0:T(128)S(1)} %pad_add_fusion.info.refs_0_, f32[1]{0:T(128)} %bitcast.count.refs_1_, f32[3,2,10,48,512]{4,3,2,1,0:T(8,128)S(1)} %copy-done.15, bf16[3,2,12,48,512]{4,3,2,1,0:T(8,128)(2,1)S(1)} %copy-done.13, ...), custom_call_target="tpu_custom_call" | custom-call | flops 4529848320 | bytes 13830264 | tf_op jit(solution)/shard_map/raise_back/pallas_call | solution.py:865
  273.7 6.8 %weight_grad.7 = (bf16[8,288,128]{2,1,0:T(8,128)(2,1)S(1)}, bf16[8,288,128]{2,1,0:T(8,128)(2,1)S(1)}, bf16[4,576,128]{2,1,0:T(8,128)(2,1)S(1)}, bf16[4,576,128]{2,1,0:T(8,128)(2,1)S(1)}) custom-call(s32[29]{0:T(128)S(1)} %pad_add_fusion.info.refs_0_, bf16[2,10,48,512]{3,2,1,0:T(8,128)(2,1)S(1)} %get-tuple-element.225.refs_1_, ...), custom_call_target="tpu_custom_call" | custom-call | flops 4529848320 | bytes 3145844 | tf_op jit(solution)/shard_map/weight_grad/pallas_call | solution.py:865
  282.5 9.2 %lower_back.1 = (bf16[3,2,10,48,512]{4,3,2,1,0:T(8,128)(2,1)S(1)}, f32[2,10,48,512]{3,2,1,0:T(8,128)S(1)}, f32[104,512]{1,0:T(8,128)S(1)}, f32[2,48,512]{2,1,0:T(8,128)S(1)}) custom-call(s32[29]{0:T(128)S(1)} %pad_add_fusion.info.refs_0_, f32[1]{0:T(128)} %bitcast.count.refs_1_, f32[3,2,10,48,512]{4,3,2,1,0:T(8,128)S(1)} %get-tuple-element.148.refs_2_, ...), custom_call_target="tpu_custom_call" | custom-call | flops 3019898880 | bytes 12646520 | tf_op jit(solution)/shard_map/lower_back/pallas_call | solution.py:865
  291.7 4.5 thin_grad.1
  315.1 2.8 collective-permute-start.85
  321.3 6.7 %weight_grad.8 = (bf16[8,288,128]{2,1,0:T(8,128)(2,1)S(1)}, bf16[8,288,128]{2,1,0:T(8,128)(2,1)S(1)}, bf16[4,576,128]{2,1,0:T(8,128)(2,1)S(1)}, bf16[4,576,128]{2,1,0:T(8,128)(2,1)S(1)}) custom-call(s32[29]{0:T(128)S(1)} %pad_add_fusion.info.refs_0_, bf16[2,10,48,512]{3,2,1,0:T(8,128)(2,1)S(1)} %get-tuple-element.138.refs_1_, ...), custom_call_target="tpu_custom_call" | custom-call | flops 4529848320 | bytes 3145844 | tf_op jit(solution)/shard_map/weight_grad/pallas_call | solution.py:865
  331.3 8.8 %hidden_back.1 = (f32[2,10,48,512]{3,2,1,0:T(8,128)S(1)}, f32[104,512]{1,0:T(8,128)S(1)}, f32[2,48,512]{2,1,0:T(8,128)S(1)}) custom-call(s32[29]{0:T(128)S(1)} %pad_add_fusion.info.refs_0_, f32[1]{0:T(128)} %bitcast.count.refs_1_, bf16[2,12,48,256]{3,2,1,0:T(8,128)(2,1)S(1)} %get-tuple-element.168.refs_3_.refs_2_, ...), custom_call_target="tpu_custom_call" | custom-call | flops 4529848320 | bytes 12607608 | tf_op jit(solution)/shard_map/hidden_back/pallas_call | solution.py:865
  340.1 2.7 collective-permute-done.88
  357.5 2.6 collective-permute-done.96
  366.8 2.4 collective-permute-start.98
  369.8 3.4 collective-permute-done.101
  374.9 6.4 %weight_grad.9 = (bf16[4,288,256]{2,1,0:T(8,128)(2,1)S(1)}, bf16[4,288,256]{2,1,0:T(8,128)(2,1)S(1)}, bf16[4,288,256]{2,1,0:T(8,128)(2,1)S(1)}, bf16[4,288,256]{2,1,0:T(8,128)(2,1)S(1)}) custom-call(s32[29]{0:T(128)S(1)} %pad_add_fusion.info.refs_0_, bf16[2,10,48,512]{3,2,1,0:T(8,128)(2,1)S(1)} %get-tuple-element.137.refs_1_, ...), custom_call_target="tpu_custom_call" | custom-call | flops 4529848320 | bytes 3145844 | tf_op jit(solution)/shard_map/weight_grad/pallas_call | solution.py:865
  381.3 2.5 collective-permute-start.108
  383.8 3.3 collective-permute-done.98
  392.4 9.1 %input_back.1.refs_3_ = f32[2,10,48,512]{3,2,1,0:T(8,128)} custom-call(s32[29]{0:T(128)S(1)} %pad_add_fusion.info.refs_0_, bf16[2,12,48,256]{3,2,1,0:T(8,128)(2,1)S(1)} %get-tuple-element.186.refs_3_.refs_1_, bf16[2,12,48,256]{3,2,1,0:T(8,128)(2,1)S(1)} %get-tuple-element.187.refs_5_.refs_2_, bf16[2,4608,512]{2,1,0:T(8,128)(2,1)} %refs_3_.1, ...), custom_call_target="tpu_custom_call" | custom-call | flops 36238786560 | bytes 10616948 | tf_op jit(solution)/shard_map/input_back/pallas_call | solution.py:865
  401.5 4.7 %collective-permute-done.109 = bf16[24,64,256]{2,1,0:T(8,128)(2,1)S(1)} collective-permute-done((bf16[24,64,256]{2,1,0:T(8,128)(2,1)S(1)}, bf16[24,64,256]{2,1,0:T(8,128)(2,1)S(1)}, u32[]{:S(2)}, u32[]{:S(2)}) %collective-permute-start.109) | collective-permute-done | bytes 786464 | tf_op jit(solution)/shard_map/ppermute | solution.py:27
  410.7 9.5 %collective-permute-done.106 = bf16[4,288,256]{2,1,0:T(8,128)(2,1)S(1)} collective-permute-done((bf16[4,288,256]{2,1,0:T(8,128)(2,1)S(1)}, bf16[4,288,256]{2,1,0:T(8,128)(2,1)S(1)}, u32[]{:S(2)}, u32[]{:S(2)}) %collective-permute-start.106) | collective-permute-done | bytes 589856 | tf_op jit(solution)/shard_map/ppermute | solution.py:27
  423.1 3.9 collective-permute-done.105
  434.9 2.9 collective-permute-done.116
  439.4 3.2 collective-permute-done.111
  442.7 6.9 %collective-permute-done.112 = bf16[1,288,256]{2,1,0:T(8,128)(2,1)S(1)} collective-permute-done((bf16[1,288,256]{2,1,0:T(8,128)(2,1)S(1)}, bf16[1,288,256]{2,1,0:T(8,128)(2,1)S(1)}, u32[]{:S(2)}, u32[]{:S(2)}) %collective-permute-start.112) | collective-permute-done | bytes 147488 | tf_op jit(solution)/shard_map/ppermute | solution.py:27
  449.6 4.2 collective-permute-done.114
  457.8 5.5 %collective-permute-done.119.refs_7_ = bf16[768,256]{1,0:T(8,128)(2,1)S(1)} collective-permute-done((bf16[768,256]{1,0:T(8,128)(2,1)S(1)}, bf16[768,256]{1,0:T(8,128)(2,1)S(1)}, u32[]{:S(2)}, u32[]{:S(2)}) %collective-permute-start.119) | collective-permute-done | bytes 393248 | tf_op jit(solution)/shard_map/ppermute | solution.py:27
  465.0 3.6 join.1
  (317 shorter events, 200.1 us)
Async XLA Ops:
  29.1 5.6 %collective-permute-start.8 = (f32[8,512]{1,0:T(8,128)S(1)}, f32[8,512]{1,0:T(8,128)S(1)}, u32[]{:S(2)}, u32[]{:S(2)}) collective-permute-start(f32[8,512]{1,0:T(8,128)S(1)} %add_add_fusion.19), channel_id=1, source_target_pairs={{0,16},{1,17},{2,18},{3,19},{4,20},{5,21},{6,22},{7,23},{8,24},{9,... | collective-permute-start | bytes 49160 | tf_op jit(solution)/shard_map/ppermute | solution.py:27
  133.4 46.4 %collective-permute-start.50 = (bf16[3,2,10,48,512]{4,3,2,1,0:T(8,128)(2,1)S(1)}, bf16[3,2,10,48,512]{4,3,2,1,0:T(8,128)(2,1)}, u32[]{:S(2)}, u32[]{:S(2)}) collective-permute-start(bf16[3,2,10,48,512]{4,3,2,1,0:T(8,128)(2,1)S(1)} %get-tuple-element.139), channel_id=1, source_target_pairs={{0,1},{1,0},{2,3},{3,2},{4,5},{5,4},{6,7},{7,6},{8,9},{9,8},{10,11... | collective-permute-start | bytes 8847368 | tf_op jit(solution)/shard_map/ppermute | solution.py:27
  144.1 5.6 %collective-permute-start.38 = (f32[8,512]{1,0:T(8,128)S(1)}, f32[8,512]{1,0:T(8,128)S(1)}, u32[]{:S(2)}, u32[]{:S(2)}) collective-permute-start(f32[8,512]{1,0:T(8,128)S(1)} %add_add_fusion.11), channel_id=1, source_target_pairs={{0,24},{1,25},{2,26},{3,27},{4,28},{5,29},{6,30},{7,31},{8,16},{9,... | collective-permute-start | bytes 49160 | tf_op jit(solution)/shard_map/ppermute | solution.py:27
  164.4 10.3 %collective-permute-start.41 = (bf16[6,48,512]{2,1,0:T(8,128)(2,1)S(1)}, bf16[6,48,512]{2,1,0:T(8,128)(2,1)S(1)}, u32[]{:S(2)}, u32[]{:S(2)}) collective-permute-start(bf16[6,48,512]{2,1,0:T(8,128)(2,1)S(1)} %get-tuple-element.134), channel_id=1, source_target_pairs={{1,2},{2,1},{5,6},{6,5},{9,10},{10,9},{13,14},{14,13},{17,18},{18,... | collective-permute-start | bytes 884744 | tf_op jit(solution)/shard_map/ppermute | solution.py:33
  165.1 9.6 %collective-permute-start.40 = (bf16[6,48,512]{2,1,0:T(8,128)(2,1)S(1)}, bf16[6,48,512]{2,1,0:T(8,128)(2,1)S(1)}, u32[]{:S(2)}, u32[]{:S(2)}) collective-permute-start(bf16[6,48,512]{2,1,0:T(8,128)(2,1)S(1)} %get-tuple-element.133), channel_id=1, source_target_pairs={{1,2},{2,1},{5,6},{6,5},{9,10},{10,9},{13,14},{14,13},{17,18},{18,... | collective-permute-start | bytes 884744 | tf_op jit(solution)/shard_map/ppermute | solution.py:33
  165.8 5.6 %collective-permute-start.47 = (f32[8,512]{1,0:T(8,128)S(1)}, f32[8,512]{1,0:T(8,128)S(1)}, u32[]{:S(2)}, u32[]{:S(2)}) collective-permute-start(f32[8,512]{1,0:T(8,128)S(1)} %add_add_fusion.9), channel_id=1, source_target_pairs={{0,24},{1,25},{2,26},{3,27},{4,28},{5,29},{6,30},{7,31},{8,16},{9,... | collective-permute-start | bytes 49160 | tf_op jit(solution)/shard_map/ppermute | solution.py:27
  168.5 6.2 %collective-permute-start.45 = (f32[8,512]{1,0:T(8,128)S(1)}, f32[8,512]{1,0:T(8,128)S(1)}, u32[]{:S(2)}, u32[]{:S(2)}) collective-permute-start(f32[8,512]{1,0:T(8,128)S(1)} %add_add_fusion.9), channel_id=1, source_target_pairs={{0,8},{1,9},{2,10},{3,11},{4,12},{5,13},{6,14},{7,15},{8,0},{9,1},... | collective-permute-start | bytes 49160 | tf_op jit(solution)/shard_map/ppermute | solution.py:27
  171.4 26.5 %collective-permute-start.48 = (bf16[2,10,48,512]{3,2,1,0:T(8,128)(2,1)S(1)}, bf16[2,10,48,512]{3,2,1,0:T(8,128)(2,1)S(1)}, u32[]{:S(2)}, u32[]{:S(2)}) collective-permute-start(bf16[2,10,48,512]{3,2,1,0:T(8,128)(2,1)S(1)} %get-tuple-element.137.refs_1_), channel_id=1, source_target_pairs={{0,1},{1,0},{2,3},{3,2},{4,5},{5,4},{6,7},{7,6},{8,9},{9,8},{10,11... | collective-permute-start | bytes 2949128 | tf_op jit(solution)/shard_map/ppermute | solution.py:27
  174.6 23.2 %collective-permute-start.49 = (bf16[2,10,48,512]{3,2,1,0:T(8,128)(2,1)S(1)}, bf16[2,10,48,512]{3,2,1,0:T(8,128)(2,1)S(1)}, u32[]{:S(2)}, u32[]{:S(2)}) collective-permute-start(bf16[2,10,48,512]{3,2,1,0:T(8,128)(2,1)S(1)} %get-tuple-element.138.refs_1_), channel_id=1, source_target_pairs={{0,1},{1,0},{2,3},{3,2},{4,5},{5,4},{6,7},{7,6},{8,9},{9,8},{10,11... | collective-permute-start | bytes 2949128 | tf_op jit(solution)/shard_map/ppermute | solution.py:27
  177.9 12.7 %collective-permute-start.51 = (bf16[2,12,48,256]{3,2,1,0:T(8,128)(2,1)S(1)}, bf16[2,12,48,256]{3,2,1,0:T(8,128)(2,1)S(1)}, u32[]{:S(2)}, u32[]{:S(2)}) collective-permute-start(bf16[2,12,48,256]{3,2,1,0:T(8,128)(2,1)S(1)} %get-tuple-element.230), channel_id=1, source_target_pairs={{0,1},{1,0},{2,3},{3,2},{4,5},{5,4},{6,7},{7,6},{8,9},{9,8},{10,11... | collective-permute-start | bytes 1769480 | tf_op jit(solution)/shard_map/ppermute | solution.py:27
  188.5 38.4 %collective-permute-start.54 = (bf16[8,288,256]{2,1,0:T(8,128)(2,1)S(1)}, bf16[8,288,256]{2,1,0:T(8,128)(2,1)S(1)}, u32[]{:S(2)}, u32[]{:S(2)}) collective-permute-start(bf16[8,288,256]{2,1,0:T(8,128)(2,1)S(1)} %get-tuple-element.140.refs_5_), channel_id=1, source_target_pairs={{0,2},{1,3},{2,0},{3,1},{4,6},{5,7},{6,4},{7,5},{8,10},{9,11},{10,... | collective-permute-start | bytes 3538952 | tf_op jit(solution)/shard_map/ppermute | solution.py:27
  197.0 30.8 %collective-permute-start.53 = (bf16[4,576,256]{2,1,0:T(8,128)(2,1)S(1)}, bf16[4,576,256]{2,1,0:T(8,128)(2,1)S(1)}, u32[]{:S(2)}, u32[]{:S(2)}) collective-permute-start(bf16[4,576,256]{2,1,0:T(8,128)(2,1)S(1)} %get-tuple-element.141.refs_13_), channel_id=1, source_target_pairs={{0,4},{1,5},{2,6},{3,7},{4,0},{5,1},{6,2},{7,3},{8,12},{9,13},{10,... | collective-permute-start | bytes 3538952 | tf_op jit(solution)/shard_map/ppermute | solution.py:27
  239.7 33.9 %collective-permute-start.71 = (bf16[2,12,48,256]{3,2,1,0:T(8,128)(2,1)S(1)}, bf16[2,12,48,256]{3,2,1,0:T(8,128)(2,1)S(1)}, u32[]{:S(2)}, u32[]{:S(2)}) collective-permute-start(bf16[2,12,48,256]{3,2,1,0:T(8,128)(2,1)S(1)} %get-tuple-element.228), channel_id=1, source_target_pairs={{0,1},{1,0},{2,3},{3,2},{4,5},{5,4},{6,7},{7,6},{8,9},{9,8},{10,11... | collective-permute-start | bytes 1769480 | tf_op jit(solution)/shard_map/ppermute | solution.py:27
  239.7 18.4 %collective-permute-start.62 = (bf16[4,288,256]{2,1,0:T(8,128)(2,1)S(1)}, bf16[4,288,256]{2,1,0:T(8,128)(2,1)S(1)}, u32[]{:S(2)}, u32[]{:S(2)}) collective-permute-start(bf16[4,288,256]{2,1,0:T(8,128)(2,1)S(1)} %get-tuple-element.146.refs_3_), channel_id=1, source_target_pairs={{0,4},{1,5},{2,6},{3,7},{4,0},{5,1},{6,2},{7,3},{8,12},{9,13},{10,... | collective-permute-start | bytes 1769480 | tf_op jit(solution)/shard_map/ppermute | solution.py:27
  240.8 17.3 %collective-permute-start.63 = (bf16[4,288,256]{2,1,0:T(8,128)(2,1)S(1)}, bf16[4,288,256]{2,1,0:T(8,128)(2,1)S(1)}, u32[]{:S(2)}, u32[]{:S(2)}) collective-permute-start(bf16[4,288,256]{2,1,0:T(8,128)(2,1)S(1)} %get-tuple-element.147.refs_1_), channel_id=1, source_target_pairs={{0,2},{1,3},{2,0},{3,1},{4,6},{5,7},{6,4},{7,5},{8,10},{9,11},{10,... | collective-permute-start | bytes 1769480 | tf_op jit(solution)/shard_map/ppermute | solution.py:27
  267.7 5.8 %collective-permute-start.70 = (f32[8,512]{1,0:T(8,128)S(1)}, f32[8,512]{1,0:T(8,128)S(1)}, u32[]{:S(2)}, u32[]{:S(2)}) collective-permute-start(f32[8,512]{1,0:T(8,128)S(1)} %add_add_fusion.5), channel_id=1, source_target_pairs={{0,24},{1,25},{2,26},{3,27},{4,28},{5,29},{6,30},{7,31},{8,16},{9,... | collective-permute-start | bytes 49160 | tf_op jit(solution)/shard_map/ppermute | solution.py:27
  270.3 25.9 %collective-permute-start.74 = (bf16[4,288,256]{2,1,0:T(8,128)(2,1)S(1)}, bf16[4,288,256]{2,1,0:T(8,128)(2,1)S(1)}, u32[]{:S(2)}, u32[]{:S(2)}) collective-permute-start(bf16[4,288,256]{2,1,0:T(8,128)(2,1)S(1)} %get-tuple-element.152.refs_1_), channel_id=1, source_target_pairs={{0,8},{1,9},{2,10},{3,11},{4,12},{5,13},{6,14},{7,15},{8,0},{9,1},... | collective-permute-start | bytes 1769480 | tf_op jit(solution)/shard_map/ppermute | solution.py:27
  280.5 16.4 %collective-permute-start.73 = (bf16[8,288,128]{2,1,0:T(8,128)(2,1)S(1)}, bf16[8,288,128]{2,1,0:T(8,128)(2,1)S(1)}, u32[]{:S(2)}, u32[]{:S(2)}) collective-permute-start(bf16[8,288,128]{2,1,0:T(8,128)(2,1)S(1)} %get-tuple-element.159), channel_id=1, source_target_pairs={{0,2},{1,3},{2,0},{3,1},{4,6},{5,7},{6,4},{7,5},{8,10},{9,11},{10,... | collective-permute-start | bytes 1769480 | tf_op jit(solution)/shard_map/ppermute | solution.py:27
  281.8 16.0 %collective-permute-start.72 = (bf16[4,576,128]{2,1,0:T(8,128)(2,1)S(1)}, bf16[4,576,128]{2,1,0:T(8,128)(2,1)S(1)}, u32[]{:S(2)}, u32[]{:S(2)}) collective-permute-start(bf16[4,576,128]{2,1,0:T(8,128)(2,1)S(1)} %get-tuple-element.154.refs_13_), channel_id=1, source_target_pairs={{0,4},{1,5},{2,6},{3,7},{4,0},{5,1},{6,2},{7,3},{8,12},{9,13},{10,... | collective-permute-start | bytes 1769480 | tf_op jit(solution)/shard_map/ppermute | solution.py:27
  315.1 6.2 %collective-permute-start.85 = (bf16[2,12,48,256]{3,2,1,0:T(8,128)(2,1)S(1)}, bf16[2,12,48,256]{3,2,1,0:T(8,128)(2,1)S(1)}, u32[]{:S(2)}, u32[]{:S(2)}) collective-permute-start(bf16[2,12,48,256]{3,2,1,0:T(8,128)(2,1)S(1)} %get-tuple-element.169.refs_5_.refs_3_), channel_id=1, source_target_pairs={{0,1},{1,0},{2,3},{3,2},{4,5},{5,4},{6,7},{7,6},{8,9},{9,8},{10,11... | collective-permute-start | bytes 1769480 | tf_op jit(solution)/shard_map/ppermute | solution.py:27
  317.8 42.4 %collective-permute-start.97 = (bf16[3,2,512,256]{3,2,1,0:T(8,128)(2,1)S(1)}, bf16[3,2,512,256]{3,2,1,0:T(8,128)(2,1)S(1)}, u32[]{:S(2)}, u32[]{:S(2)}) collective-permute-start(bf16[3,2,512,256]{3,2,1,0:T(8,128)(2,1)S(1)} %get-tuple-element.164.refs_3_), channel_id=1, source_target_pairs={{0,1},{1,0},{2,3},{3,2},{4,5},{5,4},{6,7},{7,6},{8,9},{9,8},{10,11... | collective-permute-start | bytes 4718600 | tf_op jit(solution)/shard_map/ppermute | solution.py:27
  317.9 11.6 %collective-permute-start.83 = (bf16[4,288,128]{2,1,0:T(8,128)(2,1)S(1)}, bf16[4,288,128]{2,1,0:T(8,128)(2,1)S(1)}, u32[]{:S(2)}, u32[]{:S(2)}) collective-permute-start(bf16[4,288,128]{2,1,0:T(8,128)(2,1)S(1)} %get-tuple-element.166.refs_3_), channel_id=1, source_target_pairs={{0,4},{1,5},{2,6},{3,7},{4,0},{5,1},{6,2},{7,3},{8,12},{9,13},{10,... | collective-permute-start | bytes 884744 | tf_op jit(solution)/shard_map/ppermute | solution.py:27
  319.2 10.3 %collective-permute-start.84 = (bf16[4,288,128]{2,1,0:T(8,128)(2,1)S(1)}, bf16[4,288,128]{2,1,0:T(8,128)(2,1)S(1)}, u32[]{:S(2)}, u32[]{:S(2)}) collective-permute-start(bf16[4,288,128]{2,1,0:T(8,128)(2,1)S(1)} %get-tuple-element.167.refs_1_), channel_id=1, source_target_pairs={{0,2},{1,3},{2,0},{3,1},{4,6},{5,7},{6,4},{7,5},{8,10},{9,11},{10,... | collective-permute-start | bytes 884744 | tf_op jit(solution)/shard_map/ppermute | solution.py:27
  327.9 14.8 %collective-permute-start.88 = (bf16[8,288,128]{2,1,0:T(8,128)(2,1)S(1)}, bf16[8,288,128]{2,1,0:T(8,128)(2,1)S(1)}, u32[]{:S(2)}, u32[]{:S(2)}) collective-permute-start(bf16[8,288,128]{2,1,0:T(8,128)(2,1)S(1)} %get-tuple-element.179), channel_id=1, source_target_pairs={{0,2},{1,3},{2,0},{3,1},{4,6},{5,7},{6,4},{7,5},{8,10},{9,11},{10,... | collective-permute-start | bytes 1769480 | tf_op jit(solution)/shard_map/ppermute | solution.py:27
  328.2 15.3 %collective-permute-start.87 = (bf16[4,576,128]{2,1,0:T(8,128)(2,1)S(1)}, bf16[4,576,128]{2,1,0:T(8,128)(2,1)S(1)}, u32[]{:S(2)}, u32[]{:S(2)}) collective-permute-start(bf16[4,576,128]{2,1,0:T(8,128)(2,1)S(1)} %get-tuple-element.172.refs_5_), channel_id=1, source_target_pairs={{0,4},{1,5},{2,6},{3,7},{4,0},{5,1},{6,2},{7,3},{8,12},{9,13},{10,... | collective-permute-start | bytes 1769480 | tf_op jit(solution)/shard_map/ppermute | solution.py:27
  330.2 14.2 %collective-permute-start.86 = (bf16[4,288,128]{2,1,0:T(8,128)(2,1)S(1)}, bf16[4,288,128]{2,1,0:T(8,128)(2,1)S(1)}, u32[]{:S(2)}, u32[]{:S(2)}) collective-permute-start(bf16[4,288,128]{2,1,0:T(8,128)(2,1)S(1)} %get-tuple-element.173.refs_9_), channel_id=1, source_target_pairs={{0,8},{1,9},{2,10},{3,11},{4,12},{5,13},{6,14},{7,15},{8,0},{9,1},... | collective-permute-start | bytes 884744 | tf_op jit(solution)/shard_map/ppermute | solution.py:27
  362.8 12.1 %collective-permute-start.100 = (bf16[2,12,48,256]{3,2,1,0:T(8,128)(2,1)S(1)}, bf16[2,12,48,256]{3,2,1,0:T(8,128)(2,1)S(1)}, u32[]{:S(2)}, u32[]{:S(2)}) collective-permute-start(bf16[2,12,48,256]{3,2,1,0:T(8,128)(2,1)S(1)} %get-tuple-element.187.refs_5_.refs_2_), channel_id=1, source_target_pairs={{0,1},{1,0},{2,3},{3,2},{4,5},{5,4},{6,7},{7,6},{8,9},{9,8},{10,11... | collective-permute-start | bytes 1769480 | tf_op jit(solution)/shard_map/ppermute | solution.py:27
  364.1 9.0 %collective-permute-start.101 = (bf16[4,288,128]{2,1,0:T(8,128)(2,1)S(1)}, bf16[4,288,128]{2,1,0:T(8,128)(2,1)S(1)}, u32[]{:S(2)}, u32[]{:S(2)}) collective-permute-start(bf16[4,288,128]{2,1,0:T(8,128)(2,1)S(1)} %get-tuple-element.181.refs_3_), channel_id=1, source_target_pairs={{0,4},{1,5},{2,6},{3,7},{4,0},{5,1},{6,2},{7,3},{8,12},{9,13},{10,... | collective-permute-start | bytes 884744 | tf_op jit(solution)/shard_map/ppermute | solution.py:27
  365.2 9.0 %collective-permute-start.102 = (bf16[4,288,128]{2,1,0:T(8,128)(2,1)S(1)}, bf16[4,288,128]{2,1,0:T(8,128)(2,1)S(1)}, u32[]{:S(2)}, u32[]{:S(2)}) collective-permute-start(bf16[4,288,128]{2,1,0:T(8,128)(2,1)S(1)} %get-tuple-element.182.refs_3_), channel_id=1, source_target_pairs={{0,2},{1,3},{2,0},{3,1},{4,6},{5,7},{6,4},{7,5},{8,10},{9,11},{10,... | collective-permute-start | bytes 884744 | tf_op jit(solution)/shard_map/ppermute | solution.py:27
  366.8 20.3 %collective-permute-start.98 = (bf16[2,288,256]{2,1,0:T(8,128)(2,1)S(1)}, bf16[2,288,256]{2,1,0:T(8,128)(2,1)S(1)}, u32[]{:S(2)}, u32[]{:S(2)}) collective-permute-start(bf16[2,288,256]{2,1,0:T(8,128)(2,1)S(1)} %get-tuple-element.165.refs_3_), channel_id=1, source_target_pairs={{0,16},{1,17},{2,18},{3,19},{4,20},{5,21},{6,22},{7,23},{8,24},{9,... | collective-permute-start | bytes 884744 | tf_op jit(solution)/shard_map/ppermute | solution.py:27
  369.3 19.9 %collective-permute-start.99 = (bf16[2,288,128]{2,1,0:T(8,128)(2,1)S(1)}, bf16[2,288,128]{2,1,0:T(8,128)(2,1)S(1)}, u32[]{:S(2)}, u32[]{:S(2)}) collective-permute-start(bf16[2,288,128]{2,1,0:T(8,128)(2,1)S(1)} %get-tuple-element.183.refs_1_), channel_id=1, source_target_pairs={{0,16},{1,17},{2,18},{3,19},{4,20},{5,21},{6,22},{7,23},{8,24},{9,... | collective-permute-start | bytes 442376 | tf_op jit(solution)/shard_map/ppermute | solution.py:27
  373.1 33.1 %collective-permute-start.109 = (bf16[24,64,256]{2,1,0:T(8,128)(2,1)S(1)}, bf16[24,64,256]{2,1,0:T(8,128)(2,1)S(1)}, u32[]{:S(2)}, u32[]{:S(2)}) collective-permute-start(bf16[24,64,256]{2,1,0:T(8,128)(2,1)S(1)} %get-tuple-element.185.refs_11_), channel_id=1, source_target_pairs={{0,4},{1,5},{2,6},{3,7},{4,0},{5,1},{6,2},{7,3},{8,12},{9,13},{10,... | collective-permute-start | bytes 2359304 | tf_op jit(solution)/shard_map/ppermute | solution.py:27
  381.3 40.9 %collective-permute-start.108 = (bf16[4,288,256]{2,1,0:T(8,128)(2,1)S(1)}, bf16[4,288,256]{2,1,0:T(8,128)(2,1)S(1)}, u32[]{:S(2)}, u32[]{:S(2)}) collective-permute-start(bf16[4,288,256]{2,1,0:T(8,128)(2,1)S(1)} %get-tuple-element.193.refs_4_), channel_id=1, source_target_pairs={{0,6},{1,7},{2,4},{3,5},{4,2},{5,3},{6,0},{7,1},{8,14},{9,15},{10,... | collective-permute-start | bytes 1769480 | tf_op jit(solution)/shard_map/ppermute | solution.py:27
  389.3 38.3 %collective-permute-start.104 = (bf16[864,256]{1,0:T(8,128)(2,1)S(1)}, bf16[864,256]{1,0:T(8,128)(2,1)S(1)}, u32[]{:S(2)}, u32[]{:S(2)}) collective-permute-start(bf16[864,256]{1,0:T(8,128)(2,1)S(1)} %settle.2.refs_4_.refs_1_), channel_id=1, source_target_pairs={{0,2},{1,3},{2,0},{3,1},{4,6},{5,7},{6,4},{7,5},{8,10},{9,11},{10,... | collective-permute-start | bytes 1327112 | tf_op jit(solution)/shard_map/ppermute | solution.py:27
  389.6 30.6 %collective-permute-start.106 = (bf16[4,288,256]{2,1,0:T(8,128)(2,1)S(1)}, bf16[4,288,256]{2,1,0:T(8,128)(2,1)S(1)}, u32[]{:S(2)}, u32[]{:S(2)}) collective-permute-start(bf16[4,288,256]{2,1,0:T(8,128)(2,1)S(1)} %get-tuple-element.196), channel_id=1, source_target_pairs={{0,2},{1,3},{2,0},{3,1},{4,6},{5,7},{6,4},{7,5},{8,10},{9,11},{10,... | collective-permute-start | bytes 1769480 | tf_op jit(solution)/shard_map/ppermute | solution.py:27
  391.4 30.8 %collective-permute-start.107 = (bf16[4,288,256]{2,1,0:T(8,128)(2,1)S(1)}, bf16[4,288,256]{2,1,0:T(8,128)(2,1)S(1)}, u32[]{:S(2)}, u32[]{:S(2)}) collective-permute-start(bf16[4,288,256]{2,1,0:T(8,128)(2,1)S(1)} %get-tuple-element.197), channel_id=1, source_target_pairs={{0,4},{1,5},{2,6},{3,7},{4,0},{5,1},{6,2},{7,3},{8,12},{9,13},{10,... | collective-permute-start | bytes 1769480 | tf_op jit(solution)/shard_map/ppermute | solution.py:27
  408.6 19.0 %collective-permute-start.115 = (bf16[24,32,256]{2,1,0:T(8,128)(2,1)S(1)}, bf16[24,32,256]{2,1,0:T(8,128)(2,1)S(1)}, u32[]{:S(2)}, u32[]{:S(2)}) collective-permute-start(bf16[24,32,256]{2,1,0:T(8,128)(2,1)S(1)} %get-tuple-element.199.refs_5_), channel_id=1, source_target_pairs={{0,2},{1,3},{2,0},{3,1},{4,6},{5,7},{6,4},{7,5},{8,10},{9,11},{10,... | collective-permute-start | bytes 1179656 | tf_op jit(solution)/shard_map/ppermute | solution.py:27
  420.2 6.7 %collective-permute-start.105 = (bf16[4,288,128]{2,1,0:T(8,128)(2,1)S(1)}, bf16[4,288,128]{2,1,0:T(8,128)(2,1)S(1)}, u32[]{:S(2)}, u32[]{:S(2)}) collective-permute-start(bf16[4,288,128]{2,1,0:T(8,128)(2,1)S(1)} %get-tuple-element.192.refs_5_), channel_id=1, source_target_pairs={{0,8},{1,9},{2,10},{3,11},{4,12},{5,13},{6,14},{7,15},{8,0},{9,1},... | collective-permute-start | bytes 884744 | tf_op jit(solution)/shard_map/ppermute | solution.py:27
  428.4 9.4 %collective-permute-start.116 = (bf16[12,32,256]{2,1,0:T(8,128)(2,1)S(1)}, bf16[12,32,256]{2,1,0:T(8,128)(2,1)S(1)}, u32[]{:S(2)}, u32[]{:S(2)}) collective-permute-start(bf16[12,32,256]{2,1,0:T(8,128)(2,1)S(1)} %get-tuple-element.208.refs_3_), channel_id=1, source_target_pairs={{0,8},{1,9},{2,10},{3,11},{4,12},{5,13},{6,14},{7,15},{8,0},{9,1},... | collective-permute-start | bytes 589832 | tf_op jit(solution)/shard_map/ppermute | solution.py:27
  430.5 12.2 %collective-permute-start.111 = (bf16[1,288,256]{2,1,0:T(8,128)(2,1)S(1)}, bf16[1,288,256]{2,1,0:T(8,128)(2,1)S(1)}, u32[]{:S(2)}, u32[]{:S(2)}) collective-permute-start(bf16[1,288,256]{2,1,0:T(8,128)(2,1)S(1)} %get-tuple-element.203), channel_id=1, source_target_pairs={{0,8},{1,9},{2,10},{3,11},{4,12},{5,13},{6,14},{7,15},{8,0},{9,1},... | collective-permute-start | bytes 442376 | tf_op jit(solution)/shard_map/ppermute | solution.py:27
  430.5 19.0 %collective-permute-start.112 = (bf16[1,288,256]{2,1,0:T(8,128)(2,1)S(1)}, bf16[1,288,256]{2,1,0:T(8,128)(2,1)S(1)}, u32[]{:S(2)}, u32[]{:S(2)}) collective-permute-start(bf16[1,288,256]{2,1,0:T(8,128)(2,1)S(1)} %get-tuple-element.204), channel_id=1, source_target_pairs={{0,16},{1,17},{2,18},{3,19},{4,20},{5,21},{6,22},{7,23},{8,24},{9,... | collective-permute-start | bytes 442376 | tf_op jit(solution)/shard_map/ppermute | solution.py:27
  432.9 16.7 %collective-permute-start.113 = (bf16[1,288,256]{2,1,0:T(8,128)(2,1)S(1)}, bf16[1,288,256]{2,1,0:T(8,128)(2,1)S(1)}, u32[]{:S(2)}, u32[]{:S(2)}) collective-permute-start(bf16[1,288,256]{2,1,0:T(8,128)(2,1)S(1)} %get-tuple-element.200.refs_3_), channel_id=1, source_target_pairs={{0,24},{1,25},{2,26},{3,27},{4,28},{5,29},{6,30},{7,31},{8,16},{9,... | collective-permute-start | bytes 442376 | tf_op jit(solution)/shard_map/ppermute | solution.py:27
  434.9 18.9 %collective-permute-start.114 = (bf16[2,288,128]{2,1,0:T(8,128)(2,1)S(1)}, bf16[2,288,128]{2,1,0:T(8,128)(2,1)S(1)}, u32[]{:S(2)}, u32[]{:S(2)}) collective-permute-start(bf16[2,288,128]{2,1,0:T(8,128)(2,1)S(1)} %get-tuple-element.201.refs_1_), channel_id=1, source_target_pairs={{0,16},{1,17},{2,18},{3,19},{4,20},{5,21},{6,22},{7,23},{8,24},{9,... | collective-permute-start | bytes 442376 | tf_op jit(solution)/shard_map/ppermute | solution.py:27
  438.5 16.3 %collective-permute-start.117 = (bf16[6,32,256]{2,1,0:T(8,128)(2,1)S(1)}, bf16[6,32,256]{2,1,0:T(8,128)(2,1)S(1)}, u32[]{:S(2)}, u32[]{:S(2)}) collective-permute-start(bf16[6,32,256]{2,1,0:T(8,128)(2,1)S(1)} %get-tuple-element.210.refs_8_), channel_id=1, source_target_pairs={{0,16},{1,17},{2,18},{3,19},{4,20},{5,21},{6,22},{7,23},{8,24},{9,... | collective-permute-start | bytes 294920 | tf_op jit(solution)/shard_map/ppermute | solution.py:27
  455.0 8.3 %collective-permute-start.119 = (bf16[768,256]{1,0:T(8,128)(2,1)S(1)}, bf16[768,256]{1,0:T(8,128)(2,1)S(1)}, u32[]{:S(2)}, u32[]{:S(2)}) collective-permute-start(bf16[768,256]{1,0:T(8,128)(2,1)S(1)} %settle.3.refs_5_.refs_9_), channel_id=1, source_target_pairs={{0,2},{1,3},{2,0},{3,1},{4,6},{5,7},{6,4},{7,5},{8,10},{9,11},{10,... | collective-permute-start | bytes 1179656 | tf_op jit(solution)/shard_map/ppermute | solution.py:27
  457.3 6.6 %collective-permute-start.103 = (bf16[864,256]{1,0:T(8,128)(2,1)S(1)}, bf16[864,256]{1,0:T(8,128)(2,1)S(1)}, u32[]{:S(2)}, u32[]{:S(2)}) collective-permute-start(bf16[864,256]{1,0:T(8,128)(2,1)S(1)} %settle.2.refs_4_.refs_1_), channel_id=1, source_target_pairs={{0,1},{1,0},{2,3},{3,2},{4,5},{5,4},{6,7},{7,6},{8,9},{9,8},{10,11... | collective-permute-start | bytes 1327112 | tf_op jit(solution)/shard_map/ppermute | solution.py:27
  457.3 6.6 %collective-permute-start.110 = (bf16[864,256]{1,0:T(8,128)(2,1)S(1)}, bf16[864,256]{1,0:T(8,128)(2,1)S(1)}, u32[]{:S(2)}, u32[]{:S(2)}) collective-permute-start(bf16[864,256]{1,0:T(8,128)(2,1)S(1)} %relay.9.refs_3_), channel_id=1, source_target_pairs={{0,1},{1,0},{2,3},{3,2},{4,5},{5,4},{6,7},{7,6},{8,9},{9,8},{10,11... | collective-permute-start | bytes 1327112 | tf_op jit(solution)/shard_map/ppermute | solution.py:27
  457.8 6.1 %collective-permute-start.118 = (bf16[768,256]{1,0:T(8,128)(2,1)S(1)}, bf16[768,256]{1,0:T(8,128)(2,1)S(1)}, u32[]{:S(2)}, u32[]{:S(2)}) collective-permute-start(bf16[768,256]{1,0:T(8,128)(2,1)S(1)} %settle.3.refs_5_.refs_9_), channel_id=1, source_target_pairs={{0,1},{1,0},{2,3},{3,2},{4,5},{5,4},{6,7},{7,6},{8,9},{9,8},{10,11... | collective-permute-start | bytes 1179656 | tf_op jit(solution)/shard_map/ppermute | solution.py:27
  (89 other events, 618.5 us)

commit v5 on v4

--- a/solution.py
+++ b/solution.py
@@ -33,7 +33,7 @@
     return lax.ppermute(values, "rows", pairs + [(j, i) for i, j in pairs])
 
 
-def exchange_sum(values, got):
+def exchange_sum(values, got, beside=()):
     bits = places().bit_length() - 1
     assert places() == 1 << bits
     values = values + got
@@ -45,6 +45,8 @@
             values = (values + swapped(values, low)) + (
                 swapped(values, high) + swapped(values, high + low)
             )
+            if place == 1 and beside:
+                values = passed_on(values, beside)
             place += 2
         else:
             values = values + swapped(values, low)
@@ -55,10 +57,10 @@
 def norm_totals(packed, far=None):
     got = swapped(packed, 1)
     edges = packed.shape[0] - SUMS
-    totals = exchange_sum(packed[edges:], got[edges:])
     if far is None:
-        return totals
-    return totals, got, swapped_far(far)
+        return exchange_sum(packed[edges:], got[edges:])
+    outer = swapped_far(far)
+    return exchange_sum(packed[edges:], got[edges:], [outer]), got, outer
 
 
 def dot(left, right):
@@ -543,7 +545,7 @@
         attention = sigmoid(line(up_gain, branch) * centred + line(up_shift, branch))
         onward = sums[slot, row] * attention
         result = onward * shared[slot, row + 1].astype(F32) * (1.0 - attention)
-        incoming[0, slot, row] = result
+        incoming[0, slot, row] = result.astype(BF16)
         shared_grad[slot, row] += onward
         return result, result * centred
 
@@ -564,7 +566,7 @@
 
     def back(slot, row):
         result = norm(
-            grads[0, slot, row], wide[frame.pixels(slot, row), :], frame.inside(slot, row + 1)
+            grads[0, slot, row].astype(F32), wide[frame.pixels(slot, row), :], frame.inside(slot, row + 1)
         )
         raised_grad[0, slot, row] = result.astype(BF16)
 
@@ -882,8 +884,30 @@
     return (a, fixed(a.shape))
 
 
+def passed_on(value, after):
+    return call(
+        "relay",
+        relay_kernel,
+        (1,),
+        [(value, ELSEWHERE)],
+        [(value.shape, value.dtype, ELSEWHERE)],
+        [],
+        0,
+        room=4,
+        after=after,
+        aliases={0: 0},
+    )[0]
+
+
 def branch_of(a):
     return (a, by_branch(a.shape))
+
+
+def one_of(a, index):
+    if index is None:
+        return whole(a)
+    zeros = (0,) * (len(a.shape) - 1)
+    return (a, pl.BlockSpec((None,) + a.shape[1:], lambda *_: (index,) + zeros))
 
 
 def out(shape, dtype):
@@ -1097,7 +1121,7 @@
     def packed(groups):
         return [
             out((groups * slots * breadth + SUMS, channels), F32),
-            out((groups * slots, breadth, channels), F32 if groups == 1 else BF16),
+            out((groups * slots, breadth, channels), BF16),
         ]
 
     three = pltpu.VMEM((slots, tall, breadth, 3 * channels), BF16)
@@ -1202,23 +1226,24 @@
 
     share_rows = wide_rows // 2
 
-    def weight_whole(source, source_other, kept, sent, after=()):
+    def weight_whole(source, source_other, kept, sent, after=(), member=None):
         return reducer.call(
             "weight_grad",
             weight_grad_kernel,
             (1,),
-            [whole(a) for a in (source, source_other, kept, swapped(sent, 1))],
+            [one_of(a, member) for a in (source, source_other, kept)]
+            + [whole(swapped(sent if member is None else sent[member], 1))],
             [out((9 * channels, half), BF16)],
             [pltpu.VMEM((2 * slots, tall, breadth, 3 * half), BF16)],
             conv_flops,
             after=after,
         )[0]
 
-    def weight_sum(source, source_other, kept, sent, axes, after=()):
+    def weight_sum(source, source_other, kept, sent, axes, after=(), member=None):
         orders = [reducer.order(axis) for axis in axes]
         width = half // len(orders)
         if share_rows % 16:
-            total = weight_whole(source, source_other, kept, sent, after)
+            total = weight_whole(source, source_other, kept, sent, after, member)
             parts = [
                 reducer.spread([[total]], share_rows, order, (), (index * width, (index + 1) * width))
                 for index, order in enumerate(orders)
@@ -1236,7 +1261,8 @@
                 ),
                 (1,),
                 [(info, SCALARS)]
-                + [whole(a) for a in (source, source_other, kept, swapped(sent, 1))],
+                + [one_of(a, member) for a in (source, source_other, kept)]
+            + [whole(swapped(sent if member is None else sent[member], 1))],
                 [out(shape, BF16) for shape in shapes],
                 [
                     pltpu.VMEM((2 * slots, tall, breadth, 3 * half), BF16),
@@ -1270,10 +1296,8 @@
         for one in halvings:
             one.step()
 
-    def task_grads(t):
-        return gated[t], gated_other[t], conv_kept[t], conv_sent[t]
-
-    early = [weight_sum(*task_grads(t), ["xy"[t]])[0] for t in range(2)]
+    task_grads = (gated, gated_other, conv_kept, conv_sent)
+    early = [weight_sum(*task_grads, ["xy"[t]], member=t)[0] for t in range(2)]
     up_grad_in, shared_grad, up_back_packed = reducer.call(
         "gate_back",
         gate_back_kernel,
@@ -1283,7 +1307,7 @@
         + [in_hbm(task_conv), branch_of(squeezed), branch_weight(task_up)]
         + [whole(a) for a in (shared, up_totals, up_gain, up_shift)],
         [
-            out_branch(all_tasks(map_shape), F32),
+            out_branch(all_tasks(map_shape), BF16),
             out(map_shape, F32),
             sums_only(),
         ],
@@ -1315,7 +1339,7 @@
     )
     early = merged(early)
     down_back = norm_totals(reducer.relay(down_back_packed))
-    late = weight_sum(*task_grads(2), "xy", after=[down_back])
+    late = weight_sum(*task_grads, "xy", after=[down_back], member=2)
 
     lowered_grad, second_grad, second_back_packed, second_grad_far = reducer.call(
         "lower_back",
@@ -1415,6 +1439,7 @@
         8 * conv_flops,
     )
 
+    reducer.last = (pltpu.with_memory_space_constraint(input_grad, pltpu.HBM),)
     step(thin, *first_sum, second_sum)
     beside = reducer.relay(beside)
     step(thin, thin)

time: 476 us -> 463 us (0.973)
  local copies, waits for them, and re-layouts: 14.7 us -> 5.4 us
    unnamed x32 -> x36, local copies, waits for them, and re-layouts: 10 us -> 3.11 us
    pallas_call x46 -> x52, Pallas kernels: 183 us -> 183 us  [call(): pl.pallas_call(body, name=name, grid=grid, in_specs=[s for _, s in inputs...]
  transfers between devices with their start and end apart: 121 -> 121, of which waited for: 73 -> 82; matrix products, arithmetic and copies ran while one was open for 1% -> 0% of each run, Pallas kernels for 26% -> 26%
where the time goes in v5:
time: 463 us; the launch traced here: 458 us
  Pallas kernels  183 us (40%)
  starting transfers between devices  139 us (30%)
  waiting for transfers between devices  126 us (27%)
  local copies, waits for them, and re-layouts  5.4 us (1%)
    pallas_call x52, Pallas kernels, call(): pl.pallas_call(body, name=name, grid=grid, in_specs=[s for _, s in inputs...  183 us
    ppermute x113, starting transfers between devices, swapped(): return lax.ppermute(values, AXES, [(i, i ^ flip) for i in range(places())])  130 us
    ppermute x113, waiting for transfers between devices, swapped(): return lax.ppermute(values, AXES, [(i, i ^ flip) for i in range(places())])  126 us
  transfers between devices with their start and end apart: 121, of which 82 were waited for; matrix products, arithmetic and copies ran while one was open for 0% of the time, Pallas kernels for 26%

profile of v5, /device:TPU:0, one launch (start us, length us, event | category | flops | bytes accessed | tf_op | source)
XLA Modules:
  0.0 457.6 jit_solution(4850088715870695773)
XLA Ops:
  2.9 3.0 collective-permute-start
  8.9 8.0 %first_conv.1 = (f32[2,10,48,512]{3,2,1,0:T(8,128)S(1)}, f32[104,512]{1,0:T(8,128)S(1)}, bf16[2,48,512]{2,1,0:T(8,128)(2,1)S(1)}, bf16[2,10,48,512]{3,2,1,0:T(8,128)(2,1)S(1)}) custom-call(s32[29]{0:T(128)S(1)} %pad_add_fusion.info.refs_0_, bf16[2,10,48,512]{3,2,1,0:T(8,128)(2,1)S(1)} %copy-done.1, bf16[2,48,512]{2,1,0:T(8,128)(2,1)S(1)} %collective-permute-done.above, ...), custom_call_target="tpu_custom_call" | custom-call | flops 4529848320 | bytes 10616948 | tf_op jit(solution)/shard_map/first_conv/pallas_call | solution.py:867
  16.9 2.6 collective-permute-start.2
  20.6 3.5 collective-permute-start.6
  28.4 3.7 collective-permute-start.9
  34.0 2.7 collective-permute-done.8
  36.7 8.0 %second_conv.1 = (f32[2,10,48,512]{3,2,1,0:T(8,128)S(1)}, f32[104,512]{1,0:T(8,128)S(1)}, bf16[2,48,512]{2,1,0:T(8,128)(2,1)S(1)}, bf16[2,10,48,512]{3,2,1,0:T(8,128)(2,1)S(1)}) custom-call(s32[29]{0:T(128)S(1)} %pad_add_fusion.info.refs_0_, f32[1]{0:T(128)} %bitcast.count.refs_1_, f32[2,10,48,512]{3,2,1,0:T(8,128)S(1)} %get-tuple-element.118.source.refs_7_.refs_5_, ...), custom_call_target="tpu_custom_call" | custom-call | flops 4529848320 | bytes 11739256 | tf_op jit(solution)/shard_map/second_conv/pallas_call | solution.py:867
  47.0 4.4 collective-permute-start.14
  62.0 4.7 %lower.1 = (bf16[2,12,48,512]{3,2,1,0:T(8,128)(2,1)S(1)}, f32[8,512]{1,0:T(8,128)S(1)}) custom-call(s32[29]{0:T(128)S(1)} %pad_add_fusion.info.refs_0_, f32[1]{0:T(128)} %bitcast.count.refs_1_, f32[2,10,48,512]{3,2,1,0:T(8,128)S(1)} %get-tuple-element.121.source.refs_9_.refs_5_, f32[104,512]{1,0:T(8,128)S(1)} %collective-permute-done.10.near.refs_6_, ...), custom_call_target="tpu_custom_call" | custom-call | flops 1509949440 | bytes 3874936 | tf_op jit(solution)/shard_map/lower/pallas_call | solution.py:867
  68.7 4.3 collective-permute-start.21
  77.3 2.5 collective-permute-start.24
  84.6 8.5 %raise.1 = (bf16[3,2,12,48,512]{4,3,2,1,0:T(8,128)(2,1)S(1)}, f32[8,512]{1,0:T(8,128)S(1)}) custom-call(s32[29]{0:T(128)S(1)} %pad_add_fusion.info.refs_0_, f32[1]{0:T(128)} %bitcast.count.refs_1_, bf16[2,12,48,512]{3,2,1,0:T(8,128)(2,1)S(1)} %get-tuple-element.124.shared.refs_7_.refs_5_.refs_3_.refs_1_, bf16[3,512,512]{2,1,0:T(8,128)(2,1)} %refs_4_.6, ...), custom_call_target="tpu_custom_call" | custom-call | flops 3019898880 | bytes 4354168 | tf_op jit(solution)/shard_map/raise/pallas_call | solution.py:867
  106.1 22.9 %task_conv.1 = (f32[3,2,10,48,512]{4,3,2,1,0:T(8,128)S(1)}, f32[296,512]{1,0:T(8,128)S(1)}, bf16[6,48,512]{2,1,0:T(8,128)(2,1)S(1)}, bf16[3,2,10,48,512]{4,3,2,1,0:T(8,128)(2,1)S(1)}) custom-call(s32[29]{0:T(128)S(1)} %pad_add_fusion.info.refs_0_, f32[1]{0:T(128)} %bitcast.count.refs_1_, ...), custom_call_target="tpu_custom_call" | custom-call | flops 13589544960 | bytes 20476024 | tf_op jit(solution)/shard_map/task_conv/pallas_call | solution.py:867
  131.1 3.3 collective-permute-start.35
  135.1 4.5 collective-permute-done.35
  139.6 2.5 collective-permute-start.39
  146.9 6.4 %pool.1 = (bf16[3,2,5,24,512]{4,3,2,1,0:T(8,128)(2,1)}, f32[3,2,10,48,512]{4,3,2,1,0:T(8,128)S(1)}, f32[296,512]{1,0:T(8,128)S(1)}, bf16[6,48,512]{2,1,0:T(8,128)(2,1)S(1)}) custom-call(s32[29]{0:T(128)S(1)} %pad_add_fusion.info.refs_0_, f32[1]{0:T(128)} %bitcast.count.refs_1_, f32[3,2,10,48,512]{4,3,2,1,0:T(8,128)S(1)} %get-tuple-element.128.source, ...), custom_call_target="tpu_custom_call" | custom-call | flops 503316480 | bytes 6664312 | tf_op jit(solution)/shard_map/pool/pallas_call | solution.py:867
  155.4 2.5 collective-permute-start.44
  159.2 3.6 collective-permute-done.44
  169.3 2.9 conv_grad.1
  174.4 6.4 %weight_grad.5 = (bf16[8,288,256]{2,1,0:T(8,128)(2,1)S(1)}, bf16[8,288,256]{2,1,0:T(8,128)(2,1)S(1)}) custom-call(s32[29]{0:T(128)S(1)} %pad_add_fusion.info.refs_0_, bf16[3,2,10,48,512]{4,3,2,1,0:T(8,128)(2,1)S(1)} %get-tuple-element.139.refs_1_, bf16[3,2,10,48,512]{4,3,2,1,0:T(8,128)(2,1)S(1)} %collective-permute-done.50.refs_2_, ...), custom_call_target="tpu_custom_call" | custom-call | flops 4529848320 | bytes 8257652 | tf_op jit(solution)/shard_map/weight_grad/pallas_call | solution.py:867
  180.9 6.4 %weight_grad.6 = (bf16[4,576,256]{2,1,0:T(8,128)(2,1)S(1)}, bf16[4,576,256]{2,1,0:T(8,128)(2,1)S(1)}) custom-call(s32[29]{0:T(128)S(1)} %pad_add_fusion.info.refs_0_, bf16[3,2,10,48,512]{4,3,2,1,0:T(8,128)(2,1)S(1)} %get-tuple-element.139.refs_1_, bf16[3,2,10,48,512]{4,3,2,1,0:T(8,128)(2,1)S(1)} %collective-permute-done.50.refs_2_, ...), custom_call_target="tpu_custom_call" | custom-call | flops 4529848320 | bytes 8257652 | tf_op jit(solution)/shard_map/weight_grad/pallas_call | solution.py:867
  188.6 24.5 %gate_back.1 = (bf16[3,2,10,48,512]{4,3,2,1,0:T(8,128)(2,1)S(1)}, f32[2,10,48,512]{3,2,1,0:T(8,128)S(1)}, f32[8,512]{1,0:T(8,128)S(1)}) custom-call(s32[29]{0:T(128)S(1)} %pad_add_fusion.info.refs_0_, f32[1]{0:T(128)} %bitcast.count.refs_1_, bf16[3,2,12,48,256]{4,3,2,1,0:T(8,128)(2,1)S(1)} %get-tuple-element.135.refs_3_.refs_2_, ...), custom_call_target="tpu_custom_call" | custom-call | flops 13589544960 | bytes 24014968 | tf_op jit(solution)/shard_map/gate_back/pallas_call | solution.py:867
  224.6 2.5 collective-permute-start.61
  233.7 12.0 %raise_back.1 = (bf16[3,2,10,48,512]{4,3,2,1,0:T(8,128)(2,1)S(1)}, f32[3,2,10,48,512]{4,3,2,1,0:T(8,128)S(1)}, f32[8,512]{1,0:T(8,128)S(1)}) custom-call(s32[29]{0:T(128)S(1)} %pad_add_fusion.info.refs_0_, f32[1]{0:T(128)} %bitcast.count.refs_1_, bf16[3,2,10,48,512]{4,3,2,1,0:T(8,128)(2,1)S(1)} %copy-done.17, bf16[3,2,12,48,512]{4,3,2,1,0:T(8,128)(2,1)S(1)} %copy-done.12, ...), custom_call_target="tpu_custom_call" | custom-call | flops 4529848320 | bytes 10881144 | tf_op jit(solution)/shard_map/raise_back/pallas_call | solution.py:867
  253.8 2.5 collective-permute-start.70
  261.0 6.8 %weight_grad.7 = (bf16[8,288,128]{2,1,0:T(8,128)(2,1)S(1)}, bf16[8,288,128]{2,1,0:T(8,128)(2,1)S(1)}, bf16[4,576,128]{2,1,0:T(8,128)(2,1)S(1)}, bf16[4,576,128]{2,1,0:T(8,128)(2,1)S(1)}) custom-call(s32[29]{0:T(128)S(1)} %pad_add_fusion.info.refs_0_, bf16[3,2,10,48,512]{4,3,2,1,0:T(8,128)(2,1)S(1)} %get-tuple-element.139.refs_1_, ...), custom_call_target="tpu_custom_call" | custom-call | flops 4529848320 | bytes 8257652 | tf_op jit(solution)/shard_map/weight_grad/pallas_call | solution.py:867
  269.7 9.4 %lower_back.1 = (bf16[3,2,10,48,512]{4,3,2,1,0:T(8,128)(2,1)S(1)}, f32[2,10,48,512]{3,2,1,0:T(8,128)S(1)}, f32[104,512]{1,0:T(8,128)S(1)}, bf16[2,48,512]{2,1,0:T(8,128)(2,1)S(1)}) custom-call(s32[29]{0:T(128)S(1)} %pad_add_fusion.info.refs_0_, f32[1]{0:T(128)} %bitcast.count.refs_1_, f32[3,2,10,48,512]{4,3,2,1,0:T(8,128)S(1)} %get-tuple-element.148.refs_2_, ...), custom_call_target="tpu_custom_call" | custom-call | flops 3019898880 | bytes 12646520 | tf_op jit(solution)/shard_map/lower_back/pallas_call | solution.py:867
  279.1 4.5 thin_grad.1
  303.6 3.5 collective-permute-start.84
  307.9 6.7 %weight_grad.8 = (bf16[8,288,128]{2,1,0:T(8,128)(2,1)S(1)}, bf16[8,288,128]{2,1,0:T(8,128)(2,1)S(1)}, bf16[4,576,128]{2,1,0:T(8,128)(2,1)S(1)}, bf16[4,576,128]{2,1,0:T(8,128)(2,1)S(1)}) custom-call(s32[29]{0:T(128)S(1)} %pad_add_fusion.info.refs_0_, bf16[2,10,48,512]{3,2,1,0:T(8,128)(2,1)S(1)} %get-tuple-element.138.refs_1_, ...), custom_call_target="tpu_custom_call" | custom-call | flops 4529848320 | bytes 3145844 | tf_op jit(solution)/shard_map/weight_grad/pallas_call | solution.py:867
  318.5 8.8 %hidden_back.1 = (f32[2,10,48,512]{3,2,1,0:T(8,128)S(1)}, f32[104,512]{1,0:T(8,128)S(1)}, bf16[2,48,512]{2,1,0:T(8,128)(2,1)S(1)}) custom-call(s32[29]{0:T(128)S(1)} %pad_add_fusion.info.refs_0_, f32[1]{0:T(128)} %bitcast.count.refs_1_, bf16[2,12,48,256]{3,2,1,0:T(8,128)(2,1)S(1)} %get-tuple-element.168.refs_3_.refs_2_, ...), custom_call_target="tpu_custom_call" | custom-call | flops 4529848320 | bytes 12607608 | tf_op jit(solution)/shard_map/hidden_back/pallas_call | solution.py:867
  339.7 2.3 collective-permute-start.96
  350.4 3.2 collective-permute-start.102
  357.4 3.8 collective-permute-done.102
  363.4 6.4 %weight_grad.9 = (bf16[4,288,256]{2,1,0:T(8,128)(2,1)S(1)}, bf16[4,288,256]{2,1,0:T(8,128)(2,1)S(1)}, bf16[4,288,256]{2,1,0:T(8,128)(2,1)S(1)}, bf16[4,288,256]{2,1,0:T(8,128)(2,1)S(1)}) custom-call(s32[29]{0:T(128)S(1)} %pad_add_fusion.info.refs_0_, bf16[2,10,48,512]{3,2,1,0:T(8,128)(2,1)S(1)} %get-tuple-element.137.refs_1_, ...), custom_call_target="tpu_custom_call" | custom-call | flops 4529848320 | bytes 3145844 | tf_op jit(solution)/shard_map/weight_grad/pallas_call | solution.py:867
  371.6 2.7 collective-permute-done.98
  374.4 2.5 collective-permute-done.99
  380.2 9.1 %input_back.1.refs_3_ = f32[2,10,48,512]{3,2,1,0:T(8,128)} custom-call(s32[29]{0:T(128)S(1)} %pad_add_fusion.info.refs_0_, bf16[2,12,48,256]{3,2,1,0:T(8,128)(2,1)S(1)} %get-tuple-element.186.refs_3_.refs_1_, bf16[2,12,48,256]{3,2,1,0:T(8,128)(2,1)S(1)} %get-tuple-element.187.refs_5_.refs_2_, bf16[2,4608,512]{2,1,0:T(8,128)(2,1)} %refs_3_.1, ...), custom_call_target="tpu_custom_call" | custom-call | flops 36238786560 | bytes 10616948 | tf_op jit(solution)/shard_map/input_back/pallas_call | solution.py:867
  389.3 5.0 %collective-permute-done.109 = bf16[24,64,256]{2,1,0:T(8,128)(2,1)S(1)} collective-permute-done((bf16[24,64,256]{2,1,0:T(8,128)(2,1)S(1)}, bf16[24,64,256]{2,1,0:T(8,128)(2,1)S(1)}, u32[]{:S(2)}, u32[]{:S(2)}) %collective-permute-start.109) | collective-permute-done | bytes 786464 | tf_op jit(solution)/shard_map/ppermute | solution.py:27
  397.0 11.6 %collective-permute-done.106 = bf16[4,288,256]{2,1,0:T(8,128)(2,1)S(1)} collective-permute-done((bf16[4,288,256]{2,1,0:T(8,128)(2,1)S(1)}, bf16[4,288,256]{2,1,0:T(8,128)(2,1)S(1)}, u32[]{:S(2)}, u32[]{:S(2)}) %collective-permute-start.106) | collective-permute-done | bytes 589856 | tf_op jit(solution)/shard_map/ppermute | solution.py:27
  410.6 4.7 %collective-permute-done.105 = bf16[4,288,128]{2,1,0:T(8,128)(2,1)S(1)} collective-permute-done((bf16[4,288,128]{2,1,0:T(8,128)(2,1)S(1)}, bf16[4,288,128]{2,1,0:T(8,128)(2,1)S(1)}, u32[]{:S(2)}, u32[]{:S(2)}) %collective-permute-start.105) | collective-permute-done | bytes 294944 | tf_op jit(solution)/shard_map/ppermute | solution.py:27
  423.5 3.6 collective-permute-done.116
  429.6 8.2 %collective-permute-done.112 = bf16[1,288,256]{2,1,0:T(8,128)(2,1)S(1)} collective-permute-done((bf16[1,288,256]{2,1,0:T(8,128)(2,1)S(1)}, bf16[1,288,256]{2,1,0:T(8,128)(2,1)S(1)}, u32[]{:S(2)}, u32[]{:S(2)}) %collective-permute-start.112) | collective-permute-done | bytes 147488 | tf_op jit(solution)/shard_map/ppermute | solution.py:27
  437.9 2.4 collective-permute-done.114
  440.3 2.6 collective-permute-done.117
  445.1 5.8 %collective-permute-done.119.refs_7_ = bf16[768,256]{1,0:T(8,128)(2,1)S(1)} collective-permute-done((bf16[768,256]{1,0:T(8,128)(2,1)S(1)}, bf16[768,256]{1,0:T(8,128)(2,1)S(1)}, u32[]{:S(2)}, u32[]{:S(2)}) %collective-permute-start.119) | collective-permute-done | bytes 393248 | tf_op jit(solution)/shard_map/ppermute | solution.py:27
  452.6 3.6 join.1
  (324 shorter events, 178.7 us)
Async XLA Ops:
  1.6 6.1 %collective-permute-start.1 = (bf16[2,48,512]{2,1,0:T(8,128)(2,1)S(1)}, bf16[2,48,512]{2,1,0:T(8,128)(2,1)S(1)}, u32[]{:S(2)}, u32[]{:S(2)}) collective-permute-start(bf16[2,48,512]{2,1,0:T(8,128)(2,1)S(1)} %get-tuple-element.225), channel_id=1, source_target_pairs={{1,0},{2,1},{3,2},{5,4},{6,5},{7,6},{9,8},{10,9},{11,10},{13,12},{... | collective-permute-start | bytes 294920 | tf_op jit(solution)/shard_map/ppermute | solution.py:1138
  47.0 6.1 %collective-permute-start.14 = (f32[8,512]{1,0:T(8,128)S(1)}, f32[8,512]{1,0:T(8,128)S(1)}, u32[]{:S(2)}, u32[]{:S(2)}) collective-permute-start(f32[8,512]{1,0:T(8,128)S(1)} %slice_add_fusion.4), channel_id=1, source_target_pairs={{0,6},{1,7},{2,4},{3,5},{4,2},{5,3},{6,0},{7,1},{8,14},{9,15},{10,... | collective-permute-start | bytes 49160 | tf_op jit(solution)/shard_map/ppermute | solution.py:27
  68.7 6.1 %collective-permute-start.21 = (f32[8,512]{1,0:T(8,128)S(1)}, f32[8,512]{1,0:T(8,128)S(1)}, u32[]{:S(2)}, u32[]{:S(2)}) collective-permute-start(f32[8,512]{1,0:T(8,128)S(1)} %add.259), channel_id=1, source_target_pairs={{0,6},{1,7},{2,4},{3,5},{4,2},{5,3},{6,0},{7,1},{8,14},{9,15},{10,... | collective-permute-start | bytes 49160 | tf_op jit(solution)/shard_map/ppermute | solution.py:27
  129.1 45.3 %collective-permute-start.50 = (bf16[3,2,10,48,512]{4,3,2,1,0:T(8,128)(2,1)S(1)}, bf16[3,2,10,48,512]{4,3,2,1,0:T(8,128)(2,1)S(1)}, u32[]{:S(2)}, u32[]{:S(2)}) collective-permute-start(bf16[3,2,10,48,512]{4,3,2,1,0:T(8,128)(2,1)S(1)} %get-tuple-element.139.refs_1_), channel_id=1, source_target_pairs={{0,1},{1,0},{2,3},{3,2},{4,5},{5,4},{6,7},{7,6},{8,9},{9,8},{10,11... | collective-permute-start | bytes 8847368 | tf_op jit(solution)/shard_map/ppermute | solution.py:27
  129.6 10.0 %collective-permute-start.36 = (bf16[6,48,512]{2,1,0:T(8,128)(2,1)S(1)}, bf16[6,48,512]{2,1,0:T(8,128)(2,1)S(1)}, u32[]{:S(2)}, u32[]{:S(2)}) collective-permute-start(bf16[6,48,512]{2,1,0:T(8,128)(2,1)S(1)} %get-tuple-element.130), channel_id=1, source_target_pairs={{1,2},{2,1},{5,6},{6,5},{9,10},{10,9},{13,14},{14,13},{17,18},{18,... | collective-permute-start | bytes 884744 | tf_op jit(solution)/shard_map/ppermute | solution.py:33
  131.1 8.4 %collective-permute-start.35 = (f32[8,512]{1,0:T(8,128)S(1)}, f32[8,512]{1,0:T(8,128)S(1)}, u32[]{:S(2)}, u32[]{:S(2)}) collective-permute-start(f32[8,512]{1,0:T(8,128)S(1)} %slice_add_fusion.3), channel_id=1, source_target_pairs={{0,6},{1,7},{2,4},{3,5},{4,2},{5,3},{6,0},{7,1},{8,14},{9,15},{10,... | collective-permute-start | bytes 49160 | tf_op jit(solution)/shard_map/ppermute | solution.py:27
  153.4 9.6 %collective-permute-start.41 = (bf16[6,48,512]{2,1,0:T(8,128)(2,1)S(1)}, bf16[6,48,512]{2,1,0:T(8,128)(2,1)S(1)}, u32[]{:S(2)}, u32[]{:S(2)}) collective-permute-start(bf16[6,48,512]{2,1,0:T(8,128)(2,1)S(1)} %get-tuple-element.134), channel_id=1, source_target_pairs={{1,2},{2,1},{5,6},{6,5},{9,10},{10,9},{13,14},{14,13},{17,18},{18,... | collective-permute-start | bytes 884744 | tf_op jit(solution)/shard_map/ppermute | solution.py:33
  155.4 7.4 %collective-permute-start.44 = (f32[8,512]{1,0:T(8,128)S(1)}, f32[8,512]{1,0:T(8,128)S(1)}, u32[]{:S(2)}, u32[]{:S(2)}) collective-permute-start(f32[8,512]{1,0:T(8,128)S(1)} %slice_add_fusion.2), channel_id=1, source_target_pairs={{0,6},{1,7},{2,4},{3,5},{4,2},{5,3},{6,0},{7,1},{8,14},{9,15},{10,... | collective-permute-start | bytes 49160 | tf_op jit(solution)/shard_map/ppermute | solution.py:27
  172.4 8.5 %collective-permute-start.51 = (bf16[2,12,48,256]{3,2,1,0:T(8,128)(2,1)S(1)}, bf16[2,12,48,256]{3,2,1,0:T(8,128)(2,1)S(1)}, u32[]{:S(2)}, u32[]{:S(2)}) collective-permute-start(bf16[2,12,48,256]{3,2,1,0:T(8,128)(2,1)S(1)} %get-tuple-element.224), channel_id=1, source_target_pairs={{0,1},{1,0},{2,3},{3,2},{4,5},{5,4},{6,7},{7,6},{8,9},{9,8},{10,11... | collective-permute-start | bytes 1769480 | tf_op jit(solution)/shard_map/ppermute | solution.py:27
  172.9 15.6 %collective-permute-start.48 = (bf16[2,10,48,512]{3,2,1,0:T(8,128)(2,1)S(1)}, bf16[2,10,48,512]{3,2,1,0:T(8,128)(2,1)S(1)}, u32[]{:S(2)}, u32[]{:S(2)}) collective-permute-start(bf16[2,10,48,512]{3,2,1,0:T(8,128)(2,1)S(1)} %get-tuple-element.137.refs_1_), channel_id=1, source_target_pairs={{0,1},{1,0},{2,3},{3,2},{4,5},{5,4},{6,7},{7,6},{8,9},{9,8},{10,11... | collective-permute-start | bytes 2949128 | tf_op jit(solution)/shard_map/ppermute | solution.py:27
  173.0 15.6 %collective-permute-start.49 = (bf16[2,10,48,512]{3,2,1,0:T(8,128)(2,1)S(1)}, bf16[2,10,48,512]{3,2,1,0:T(8,128)(2,1)S(1)}, u32[]{:S(2)}, u32[]{:S(2)}) collective-permute-start(bf16[2,10,48,512]{3,2,1,0:T(8,128)(2,1)S(1)} %get-tuple-element.138.refs_1_), channel_id=1, source_target_pairs={{0,1},{1,0},{2,3},{3,2},{4,5},{5,4},{6,7},{7,6},{8,9},{9,8},{10,11... | collective-permute-start | bytes 2949128 | tf_op jit(solution)/shard_map/ppermute | solution.py:27
  180.9 32.3 %collective-permute-start.54 = (bf16[8,288,256]{2,1,0:T(8,128)(2,1)S(1)}, bf16[8,288,256]{2,1,0:T(8,128)(2,1)S(1)}, u32[]{:S(2)}, u32[]{:S(2)}) collective-permute-start(bf16[8,288,256]{2,1,0:T(8,128)(2,1)S(1)} %get-tuple-element.140.refs_5_), channel_id=1, source_target_pairs={{0,2},{1,3},{2,0},{3,1},{4,6},{5,7},{6,4},{7,5},{8,10},{9,11},{10,... | collective-permute-start | bytes 3538952 | tf_op jit(solution)/shard_map/ppermute | solution.py:27
  187.4 28.1 %collective-permute-start.53 = (bf16[4,576,256]{2,1,0:T(8,128)(2,1)S(1)}, bf16[4,576,256]{2,1,0:T(8,128)(2,1)S(1)}, u32[]{:S(2)}, u32[]{:S(2)}) collective-permute-start(bf16[4,576,256]{2,1,0:T(8,128)(2,1)S(1)} %get-tuple-element.141.refs_13_), channel_id=1, source_target_pairs={{0,4},{1,5},{2,6},{3,7},{4,0},{5,1},{6,2},{7,3},{8,12},{9,13},{10,... | collective-permute-start | bytes 3538952 | tf_op jit(solution)/shard_map/ppermute | solution.py:27
  229.0 32.0 %collective-permute-start.71 = (bf16[2,12,48,256]{3,2,1,0:T(8,128)(2,1)S(1)}, bf16[2,12,48,256]{3,2,1,0:T(8,128)(2,1)S(1)}, u32[]{:S(2)}, u32[]{:S(2)}) collective-permute-start(bf16[2,12,48,256]{3,2,1,0:T(8,128)(2,1)S(1)} %get-tuple-element.222), channel_id=1, source_target_pairs={{0,1},{1,0},{2,3},{3,2},{4,5},{5,4},{6,7},{7,6},{8,9},{9,8},{10,11... | collective-permute-start | bytes 1769480 | tf_op jit(solution)/shard_map/ppermute | solution.py:27
  229.0 16.7 %collective-permute-start.63 = (bf16[4,288,256]{2,1,0:T(8,128)(2,1)S(1)}, bf16[4,288,256]{2,1,0:T(8,128)(2,1)S(1)}, u32[]{:S(2)}, u32[]{:S(2)}) collective-permute-start(bf16[4,288,256]{2,1,0:T(8,128)(2,1)S(1)} %get-tuple-element.147.refs_1_), channel_id=1, source_target_pairs={{0,2},{1,3},{2,0},{3,1},{4,6},{5,7},{6,4},{7,5},{8,10},{9,11},{10,... | collective-permute-start | bytes 1769480 | tf_op jit(solution)/shard_map/ppermute | solution.py:27
  230.2 15.5 %collective-permute-start.62 = (bf16[4,288,256]{2,1,0:T(8,128)(2,1)S(1)}, bf16[4,288,256]{2,1,0:T(8,128)(2,1)S(1)}, u32[]{:S(2)}, u32[]{:S(2)}) collective-permute-start(bf16[4,288,256]{2,1,0:T(8,128)(2,1)S(1)} %get-tuple-element.146.refs_3_), channel_id=1, source_target_pairs={{0,4},{1,5},{2,6},{3,7},{4,0},{5,1},{6,2},{7,3},{8,12},{9,13},{10,... | collective-permute-start | bytes 1769480 | tf_op jit(solution)/shard_map/ppermute | solution.py:27
  253.8 5.8 %collective-permute-start.70 = (f32[8,512]{1,0:T(8,128)S(1)}, f32[8,512]{1,0:T(8,128)S(1)}, u32[]{:S(2)}, u32[]{:S(2)}) collective-permute-start(f32[8,512]{1,0:T(8,128)S(1)} %add_add_fusion.5), channel_id=1, source_target_pairs={{0,24},{1,25},{2,26},{3,27},{4,28},{5,29},{6,30},{7,31},{8,16},{9,... | collective-permute-start | bytes 49160 | tf_op jit(solution)/shard_map/ppermute | solution.py:27
  258.2 25.4 %collective-permute-start.74 = (bf16[4,288,256]{2,1,0:T(8,128)(2,1)S(1)}, bf16[4,288,256]{2,1,0:T(8,128)(2,1)S(1)}, u32[]{:S(2)}, u32[]{:S(2)}) collective-permute-start(bf16[4,288,256]{2,1,0:T(8,128)(2,1)S(1)} %get-tuple-element.152.refs_1_), channel_id=1, source_target_pairs={{0,8},{1,9},{2,10},{3,11},{4,12},{5,13},{6,14},{7,15},{8,0},{9,1},... | collective-permute-start | bytes 1769480 | tf_op jit(solution)/shard_map/ppermute | solution.py:27
  267.9 16.5 %collective-permute-start.73 = (bf16[8,288,128]{2,1,0:T(8,128)(2,1)S(1)}, bf16[8,288,128]{2,1,0:T(8,128)(2,1)S(1)}, u32[]{:S(2)}, u32[]{:S(2)}) collective-permute-start(bf16[8,288,128]{2,1,0:T(8,128)(2,1)S(1)} %get-tuple-element.159), channel_id=1, source_target_pairs={{0,2},{1,3},{2,0},{3,1},{4,6},{5,7},{6,4},{7,5},{8,10},{9,11},{10,... | collective-permute-start | bytes 1769480 | tf_op jit(solution)/shard_map/ppermute | solution.py:27
  268.7 16.5 %collective-permute-start.72 = (bf16[4,576,128]{2,1,0:T(8,128)(2,1)S(1)}, bf16[4,576,128]{2,1,0:T(8,128)(2,1)S(1)}, u32[]{:S(2)}, u32[]{:S(2)}) collective-permute-start(bf16[4,576,128]{2,1,0:T(8,128)(2,1)S(1)} %get-tuple-element.154.refs_13_), channel_id=1, source_target_pairs={{0,4},{1,5},{2,6},{3,7},{4,0},{5,1},{6,2},{7,3},{8,12},{9,13},{10,... | collective-permute-start | bytes 1769480 | tf_op jit(solution)/shard_map/ppermute | solution.py:27
  303.5 43.3 %collective-permute-start.97 = (bf16[3,2,512,256]{3,2,1,0:T(8,128)(2,1)S(1)}, bf16[3,2,512,256]{3,2,1,0:T(8,128)(2,1)S(1)}, u32[]{:S(2)}, u32[]{:S(2)}) collective-permute-start(bf16[3,2,512,256]{3,2,1,0:T(8,128)(2,1)S(1)} %get-tuple-element.164.refs_3_), channel_id=1, source_target_pairs={{0,1},{1,0},{2,3},{3,2},{4,5},{5,4},{6,7},{7,6},{8,9},{9,8},{10,11... | collective-permute-start | bytes 4718600 | tf_op jit(solution)/shard_map/ppermute | solution.py:27
  303.6 12.6 %collective-permute-start.84 = (bf16[4,288,128]{2,1,0:T(8,128)(2,1)S(1)}, bf16[4,288,128]{2,1,0:T(8,128)(2,1)S(1)}, u32[]{:S(2)}, u32[]{:S(2)}) collective-permute-start(bf16[4,288,128]{2,1,0:T(8,128)(2,1)S(1)} %get-tuple-element.167.refs_1_), channel_id=1, source_target_pairs={{0,2},{1,3},{2,0},{3,1},{4,6},{5,7},{6,4},{7,5},{8,10},{9,11},{10,... | collective-permute-start | bytes 884744 | tf_op jit(solution)/shard_map/ppermute | solution.py:27
  307.1 9.1 %collective-permute-start.83 = (bf16[4,288,128]{2,1,0:T(8,128)(2,1)S(1)}, bf16[4,288,128]{2,1,0:T(8,128)(2,1)S(1)}, u32[]{:S(2)}, u32[]{:S(2)}) collective-permute-start(bf16[4,288,128]{2,1,0:T(8,128)(2,1)S(1)} %get-tuple-element.166.refs_3_), channel_id=1, source_target_pairs={{0,4},{1,5},{2,6},{3,7},{4,0},{5,1},{6,2},{7,3},{8,12},{9,13},{10,... | collective-permute-start | bytes 884744 | tf_op jit(solution)/shard_map/ppermute | solution.py:27
  314.6 14.8 %collective-permute-start.88 = (bf16[8,288,128]{2,1,0:T(8,128)(2,1)S(1)}, bf16[8,288,128]{2,1,0:T(8,128)(2,1)S(1)}, u32[]{:S(2)}, u32[]{:S(2)}) collective-permute-start(bf16[8,288,128]{2,1,0:T(8,128)(2,1)S(1)} %get-tuple-element.179), channel_id=1, source_target_pairs={{0,2},{1,3},{2,0},{3,1},{4,6},{5,7},{6,4},{7,5},{8,10},{9,11},{10,... | collective-permute-start | bytes 1769480 | tf_op jit(solution)/shard_map/ppermute | solution.py:27
  315.3 15.1 %collective-permute-start.87 = (bf16[4,576,128]{2,1,0:T(8,128)(2,1)S(1)}, bf16[4,576,128]{2,1,0:T(8,128)(2,1)S(1)}, u32[]{:S(2)}, u32[]{:S(2)}) collective-permute-start(bf16[4,576,128]{2,1,0:T(8,128)(2,1)S(1)} %get-tuple-element.172.refs_5_), channel_id=1, source_target_pairs={{0,4},{1,5},{2,6},{3,7},{4,0},{5,1},{6,2},{7,3},{8,12},{9,13},{10,... | collective-permute-start | bytes 1769480 | tf_op jit(solution)/shard_map/ppermute | solution.py:27
  316.9 14.3 %collective-permute-start.86 = (bf16[4,288,128]{2,1,0:T(8,128)(2,1)S(1)}, bf16[4,288,128]{2,1,0:T(8,128)(2,1)S(1)}, u32[]{:S(2)}, u32[]{:S(2)}) collective-permute-start(bf16[4,288,128]{2,1,0:T(8,128)(2,1)S(1)} %get-tuple-element.173.refs_9_), channel_id=1, source_target_pairs={{0,8},{1,9},{2,10},{3,11},{4,12},{5,13},{6,14},{7,15},{8,0},{9,1},... | collective-permute-start | bytes 884744 | tf_op jit(solution)/shard_map/ppermute | solution.py:27
  349.4 14.0 %collective-permute-start.100 = (bf16[2,12,48,256]{3,2,1,0:T(8,128)(2,1)S(1)}, bf16[2,12,48,256]{3,2,1,0:T(8,128)(2,1)S(1)}, u32[]{:S(2)}, u32[]{:S(2)}) collective-permute-start(bf16[2,12,48,256]{3,2,1,0:T(8,128)(2,1)S(1)} %get-tuple-element.187.refs_5_.refs_2_), channel_id=1, source_target_pairs={{0,1},{1,0},{2,3},{3,2},{4,5},{5,4},{6,7},{7,6},{8,9},{9,8},{10,11... | collective-permute-start | bytes 1769480 | tf_op jit(solution)/shard_map/ppermute | solution.py:27
  350.4 10.8 %collective-permute-start.102 = (bf16[4,288,128]{2,1,0:T(8,128)(2,1)S(1)}, bf16[4,288,128]{2,1,0:T(8,128)(2,1)S(1)}, u32[]{:S(2)}, u32[]{:S(2)}) collective-permute-start(bf16[4,288,128]{2,1,0:T(8,128)(2,1)S(1)} %get-tuple-element.182.refs_3_), channel_id=1, source_target_pairs={{0,2},{1,3},{2,0},{3,1},{4,6},{5,7},{6,4},{7,5},{8,10},{9,11},{10,... | collective-permute-start | bytes 884744 | tf_op jit(solution)/shard_map/ppermute | solution.py:27
  353.6 9.1 %collective-permute-start.101 = (bf16[4,288,128]{2,1,0:T(8,128)(2,1)S(1)}, bf16[4,288,128]{2,1,0:T(8,128)(2,1)S(1)}, u32[]{:S(2)}, u32[]{:S(2)}) collective-permute-start(bf16[4,288,128]{2,1,0:T(8,128)(2,1)S(1)} %get-tuple-element.181.refs_3_), channel_id=1, source_target_pairs={{0,4},{1,5},{2,6},{3,7},{4,0},{5,1},{6,2},{7,3},{8,12},{9,13},{10,... | collective-permute-start | bytes 884744 | tf_op jit(solution)/shard_map/ppermute | solution.py:27
  354.5 19.9 %collective-permute-start.98 = (bf16[2,288,256]{2,1,0:T(8,128)(2,1)S(1)}, bf16[2,288,256]{2,1,0:T(8,128)(2,1)S(1)}, u32[]{:S(2)}, u32[]{:S(2)}) collective-permute-start(bf16[2,288,256]{2,1,0:T(8,128)(2,1)S(1)} %get-tuple-element.165.refs_3_), channel_id=1, source_target_pairs={{0,16},{1,17},{2,18},{3,19},{4,20},{5,21},{6,22},{7,23},{8,24},{9,... | collective-permute-start | bytes 884744 | tf_op jit(solution)/shard_map/ppermute | solution.py:27
  356.5 20.4 %collective-permute-start.99 = (bf16[2,288,128]{2,1,0:T(8,128)(2,1)S(1)}, bf16[2,288,128]{2,1,0:T(8,128)(2,1)S(1)}, u32[]{:S(2)}, u32[]{:S(2)}) collective-permute-start(bf16[2,288,128]{2,1,0:T(8,128)(2,1)S(1)} %get-tuple-element.183.refs_1_), channel_id=1, source_target_pairs={{0,16},{1,17},{2,18},{3,19},{4,20},{5,21},{6,22},{7,23},{8,24},{9,... | collective-permute-start | bytes 442376 | tf_op jit(solution)/shard_map/ppermute | solution.py:27
  361.2 33.1 %collective-permute-start.109 = (bf16[24,64,256]{2,1,0:T(8,128)(2,1)S(1)}, bf16[24,64,256]{2,1,0:T(8,128)(2,1)S(1)}, u32[]{:S(2)}, u32[]{:S(2)}) collective-permute-start(bf16[24,64,256]{2,1,0:T(8,128)(2,1)S(1)} %get-tuple-element.185.refs_11_), channel_id=1, source_target_pairs={{0,4},{1,5},{2,6},{3,7},{4,0},{5,1},{6,2},{7,3},{8,12},{9,13},{10,... | collective-permute-start | bytes 2359304 | tf_op jit(solution)/shard_map/ppermute | solution.py:27
  369.8 39.9 %collective-permute-start.108 = (bf16[4,288,256]{2,1,0:T(8,128)(2,1)S(1)}, bf16[4,288,256]{2,1,0:T(8,128)(2,1)S(1)}, u32[]{:S(2)}, u32[]{:S(2)}) collective-permute-start(bf16[4,288,256]{2,1,0:T(8,128)(2,1)S(1)} %get-tuple-element.193.refs_4_), channel_id=1, source_target_pairs={{0,6},{1,7},{2,4},{3,5},{4,2},{5,3},{6,0},{7,1},{8,14},{9,15},{10,... | collective-permute-start | bytes 1769480 | tf_op jit(solution)/shard_map/ppermute | solution.py:27
  377.0 39.0 %collective-permute-start.104 = (bf16[864,256]{1,0:T(8,128)(2,1)S(1)}, bf16[864,256]{1,0:T(8,128)(2,1)S(1)}, u32[]{:S(2)}, u32[]{:S(2)}) collective-permute-start(bf16[864,256]{1,0:T(8,128)(2,1)S(1)} %settle.2.refs_4_.refs_1_), channel_id=1, source_target_pairs={{0,2},{1,3},{2,0},{3,1},{4,6},{5,7},{6,4},{7,5},{8,10},{9,11},{10,... | collective-permute-start | bytes 1327112 | tf_op jit(solution)/shard_map/ppermute | solution.py:27
  377.3 31.3 %collective-permute-start.106 = (bf16[4,288,256]{2,1,0:T(8,128)(2,1)S(1)}, bf16[4,288,256]{2,1,0:T(8,128)(2,1)S(1)}, u32[]{:S(2)}, u32[]{:S(2)}) collective-permute-start(bf16[4,288,256]{2,1,0:T(8,128)(2,1)S(1)} %get-tuple-element.196), channel_id=1, source_target_pairs={{0,2},{1,3},{2,0},{3,1},{4,6},{5,7},{6,4},{7,5},{8,10},{9,11},{10,... | collective-permute-start | bytes 1769480 | tf_op jit(solution)/shard_map/ppermute | solution.py:27
  379.0 30.7 %collective-permute-start.107 = (bf16[4,288,256]{2,1,0:T(8,128)(2,1)S(1)}, bf16[4,288,256]{2,1,0:T(8,128)(2,1)S(1)}, u32[]{:S(2)}, u32[]{:S(2)}) collective-permute-start(bf16[4,288,256]{2,1,0:T(8,128)(2,1)S(1)} %get-tuple-element.197), channel_id=1, source_target_pairs={{0,4},{1,5},{2,6},{3,7},{4,0},{5,1},{6,2},{7,3},{8,12},{9,13},{10,... | collective-permute-start | bytes 1769480 | tf_op jit(solution)/shard_map/ppermute | solution.py:27
  395.1 20.9 %collective-permute-start.115 = (bf16[24,32,256]{2,1,0:T(8,128)(2,1)S(1)}, bf16[24,32,256]{2,1,0:T(8,128)(2,1)S(1)}, u32[]{:S(2)}, u32[]{:S(2)}) collective-permute-start(bf16[24,32,256]{2,1,0:T(8,128)(2,1)S(1)} %get-tuple-element.199.refs_5_), channel_id=1, source_target_pairs={{0,2},{1,3},{2,0},{3,1},{4,6},{5,7},{6,4},{7,5},{8,10},{9,11},{10,... | collective-permute-start | bytes 1179656 | tf_op jit(solution)/shard_map/ppermute | solution.py:27
  408.6 6.7 %collective-permute-start.105 = (bf16[4,288,128]{2,1,0:T(8,128)(2,1)S(1)}, bf16[4,288,128]{2,1,0:T(8,128)(2,1)S(1)}, u32[]{:S(2)}, u32[]{:S(2)}) collective-permute-start(bf16[4,288,128]{2,1,0:T(8,128)(2,1)S(1)} %get-tuple-element.192.refs_5_), channel_id=1, source_target_pairs={{0,8},{1,9},{2,10},{3,11},{4,12},{5,13},{6,14},{7,15},{8,0},{9,1},... | collective-permute-start | bytes 884744 | tf_op jit(solution)/shard_map/ppermute | solution.py:27
  416.8 10.3 %collective-permute-start.116 = (bf16[12,32,256]{2,1,0:T(8,128)(2,1)S(1)}, bf16[12,32,256]{2,1,0:T(8,128)(2,1)S(1)}, u32[]{:S(2)}, u32[]{:S(2)}) collective-permute-start(bf16[12,32,256]{2,1,0:T(8,128)(2,1)S(1)} %get-tuple-element.208.refs_3_), channel_id=1, source_target_pairs={{0,8},{1,9},{2,10},{3,11},{4,12},{5,13},{6,14},{7,15},{8,0},{9,1},... | collective-permute-start | bytes 589832 | tf_op jit(solution)/shard_map/ppermute | solution.py:27
  418.0 11.7 %collective-permute-start.111 = (bf16[1,288,256]{2,1,0:T(8,128)(2,1)S(1)}, bf16[1,288,256]{2,1,0:T(8,128)(2,1)S(1)}, u32[]{:S(2)}, u32[]{:S(2)}) collective-permute-start(bf16[1,288,256]{2,1,0:T(8,128)(2,1)S(1)} %get-tuple-element.203), channel_id=1, source_target_pairs={{0,8},{1,9},{2,10},{3,11},{4,12},{5,13},{6,14},{7,15},{8,0},{9,1},... | collective-permute-start | bytes 442376 | tf_op jit(solution)/shard_map/ppermute | solution.py:27
  418.9 19.0 %collective-permute-start.112 = (bf16[1,288,256]{2,1,0:T(8,128)(2,1)S(1)}, bf16[1,288,256]{2,1,0:T(8,128)(2,1)S(1)}, u32[]{:S(2)}, u32[]{:S(2)}) collective-permute-start(bf16[1,288,256]{2,1,0:T(8,128)(2,1)S(1)} %get-tuple-element.204), channel_id=1, source_target_pairs={{0,16},{1,17},{2,18},{3,19},{4,20},{5,21},{6,22},{7,23},{8,24},{9,... | collective-permute-start | bytes 442376 | tf_op jit(solution)/shard_map/ppermute | solution.py:27
  420.8 19.4 %collective-permute-start.114 = (bf16[2,288,128]{2,1,0:T(8,128)(2,1)S(1)}, bf16[2,288,128]{2,1,0:T(8,128)(2,1)S(1)}, u32[]{:S(2)}, u32[]{:S(2)}) collective-permute-start(bf16[2,288,128]{2,1,0:T(8,128)(2,1)S(1)} %get-tuple-element.201.refs_1_), channel_id=1, source_target_pairs={{0,16},{1,17},{2,18},{3,19},{4,20},{5,21},{6,22},{7,23},{8,24},{9,... | collective-permute-start | bytes 442376 | tf_op jit(solution)/shard_map/ppermute | solution.py:27
  421.8 18.5 %collective-permute-start.113 = (bf16[1,288,256]{2,1,0:T(8,128)(2,1)S(1)}, bf16[1,288,256]{2,1,0:T(8,128)(2,1)S(1)}, u32[]{:S(2)}, u32[]{:S(2)}) collective-permute-start(bf16[1,288,256]{2,1,0:T(8,128)(2,1)S(1)} %get-tuple-element.200.refs_3_), channel_id=1, source_target_pairs={{0,24},{1,25},{2,26},{3,27},{4,28},{5,29},{6,30},{7,31},{8,16},{9,... | collective-permute-start | bytes 442376 | tf_op jit(solution)/shard_map/ppermute | solution.py:27
  427.8 15.1 %collective-permute-start.117 = (bf16[6,32,256]{2,1,0:T(8,128)(2,1)S(1)}, bf16[6,32,256]{2,1,0:T(8,128)(2,1)S(1)}, u32[]{:S(2)}, u32[]{:S(2)}) collective-permute-start(bf16[6,32,256]{2,1,0:T(8,128)(2,1)S(1)} %get-tuple-element.210.refs_8_), channel_id=1, source_target_pairs={{0,16},{1,17},{2,18},{3,19},{4,20},{5,21},{6,22},{7,23},{8,24},{9,... | collective-permute-start | bytes 294920 | tf_op jit(solution)/shard_map/ppermute | solution.py:27
  443.0 7.8 %collective-permute-start.119 = (bf16[768,256]{1,0:T(8,128)(2,1)S(1)}, bf16[768,256]{1,0:T(8,128)(2,1)S(1)}, u32[]{:S(2)}, u32[]{:S(2)}) collective-permute-start(bf16[768,256]{1,0:T(8,128)(2,1)S(1)} %settle.3.refs_5_.refs_9_), channel_id=1, source_target_pairs={{0,2},{1,3},{2,0},{3,1},{4,6},{5,7},{6,4},{7,5},{8,10},{9,11},{10,... | collective-permute-start | bytes 1179656 | tf_op jit(solution)/shard_map/ppermute | solution.py:27
  444.6 6.9 %collective-permute-start.103 = (bf16[864,256]{1,0:T(8,128)(2,1)S(1)}, bf16[864,256]{1,0:T(8,128)(2,1)S(1)}, u32[]{:S(2)}, u32[]{:S(2)}) collective-permute-start(bf16[864,256]{1,0:T(8,128)(2,1)S(1)} %settle.2.refs_4_.refs_1_), channel_id=1, source_target_pairs={{0,1},{1,0},{2,3},{3,2},{4,5},{5,4},{6,7},{7,6},{8,9},{9,8},{10,11... | collective-permute-start | bytes 1327112 | tf_op jit(solution)/shard_map/ppermute | solution.py:27
  444.6 6.9 %collective-permute-start.110 = (bf16[864,256]{1,0:T(8,128)(2,1)S(1)}, bf16[864,256]{1,0:T(8,128)(2,1)S(1)}, u32[]{:S(2)}, u32[]{:S(2)}) collective-permute-start(bf16[864,256]{1,0:T(8,128)(2,1)S(1)} %relay.21.refs_3_), channel_id=1, source_target_pairs={{0,1},{1,0},{2,3},{3,2},{4,5},{5,4},{6,7},{7,6},{8,9},{9,8},{10,11... | collective-permute-start | bytes 1327112 | tf_op jit(solution)/shard_map/ppermute | solution.py:27
  445.1 6.4 %collective-permute-start.118 = (bf16[768,256]{1,0:T(8,128)(2,1)S(1)}, bf16[768,256]{1,0:T(8,128)(2,1)S(1)}, u32[]{:S(2)}, u32[]{:S(2)}) collective-permute-start(bf16[768,256]{1,0:T(8,128)(2,1)S(1)} %settle.3.refs_5_.refs_9_), channel_id=1, source_target_pairs={{0,1},{1,0},{2,3},{3,2},{4,5},{5,4},{6,7},{7,6},{8,9},{9,8},{10,11... | collective-permute-start | bytes 1179656 | tf_op jit(solution)/shard_map/ppermute | solution.py:27
  (91 other events, 666.0 us)
